TPU v7x, 32 devices: a whole 2x2x4 slice. The times are simulated.
32 devices in a mesh: mix: 2 (over y), dp: 4 (over z), tensor: 4 (over x, core).
Axes of the slice: x: 2, y: 2, z: 4, core: 2. Of those that a mesh axis runs over, the one named last changes fastest.
Arguments:
- grad_gate: bfloat16 [20480, 7168], P(('mix', 'dp'), 'tensor'), parts along dimension 0, may hold values from -640 to 640
- grad_down: bfloat16 [20480, 7168], P(('mix', 'dp'), 'tensor'), parts along dimension 0, may hold values from -640 to 640
- error_gate: bfloat16 [20480, 7168], P(('mix', 'dp'), 'tensor'), parts along dimension 0, may hold values from -3 to 3
- error_down: bfloat16 [20480, 7168], P(('mix', 'dp'), 'tensor'), parts along dimension 0, may hold values from -3 to 3
- start_gate: bfloat16 [64, 7168], P(None, 'tensor'), may hold values from -5 to 5
- start_down: bfloat16 [64, 5120], replicated, may hold values from -5 to 5
Outputs:
- update_gate: bfloat16 [10240, 7168], P(('mix', 'dp'), 'tensor'), parts along dimension 0
- update_down: bfloat16 [10240, 7168], P(('mix', 'dp'), 'tensor'), parts along dimension 0
- new_error_gate: bfloat16 [20480, 7168], P(('mix', 'dp'), 'tensor'), parts along dimension 0
- new_error_down: bfloat16 [20480, 7168], P(('mix', 'dp'), 'tensor'), parts along dimension 0
There are 2 independent parts, one for each index of `mix`. A program takes and returns all parts, laid end to end along the dimension named above; an argument that names none is the same for every part. Nothing has to cross between parts.
All inputs are finite; a program needn't handle non-finite values.
Results may differ from a plain program's by a relative error of at most 0.009.
Values sent between devices are 32-bit elements; how exact they have to be, the bound alone decides.
No kernel may reach another device: no remote copies, remote signals or barrier semaphores. Data moves between devices by JAX's collectives and lax.ppermute only.
A program may use at most 192 MiB of HBM per device.

v0:
```python
import jax
import jax.numpy as jnp
from jax import lax
from jax.sharding import PartitionSpec as P

REPLICAS = 2


def from_partner(shard, axis, stride):
    return lax.ppermute(shard, axis, [(i, i ^ 1 << stride) for i in range(lax.axis_size(axis))])


def corrected(grad, error):
    return (grad.astype(jnp.float32) + error.astype(jnp.float32)).astype(jnp.bfloat16)


def transposed(matrix, ortho):
    return lax.dot_general(
        matrix,
        ortho.astype(jnp.bfloat16),
        (((0,), (0,)), ((), ())),
        preferred_element_type=jnp.float32,
    )


def gram_of(left):
    return jnp.dot(left.T, left, precision=lax.Precision.HIGHEST)


def factored(left, inner):
    lower = jnp.linalg.cholesky(inner)
    return lax.linalg.triangular_solve(lower, left, left_side=False, lower=True, transpose_a=True)


def local(grad_gate, grad_down, error_gate, error_down, start_gate, start_down):
    high = lax.Precision.HIGHEST
    dp_place = lax.axis_index("dp")
    block = dp_place // REPLICAS
    replica = dp_place % REPLICAS
    pair_bits = REPLICAS.bit_length() - 1
    fixed_gate = corrected(grad_gate, error_gate)
    fixed_down = corrected(grad_down, error_down)
    slab = fixed_gate.shape[0]
    cols_down = lax.dynamic_slice_in_dim(start_down, block * slab, slab, 1)
    left_gate = lax.dot_general(
        fixed_gate, start_gate, (((1,), (1,)), ((), ())), preferred_element_type=jnp.float32
    )
    left_down = lax.dot_general(
        fixed_down, cols_down, (((0,), (1,)), ((), ())), preferred_element_type=jnp.float32
    )
    left_gate = lax.psum(left_gate, "tensor")
    bit = 0
    left_gate = left_gate + from_partner(left_gate, "dp", bit)
    left_down = lax.psum(left_down, "dp")
    keep_gate = (replica == 0).astype(jnp.float32)
    inner_gate = lax.psum(gram_of(left_gate) * keep_gate, "dp")
    inner_down = lax.psum(gram_of(left_down), "tensor")
    ortho_gate = factored(left_gate, inner_gate)
    ortho_down = factored(left_down, inner_down)
    right_gate = transposed(fixed_gate, ortho_gate)
    right_gate = lax.psum(right_gate, "dp") / REPLICAS
    right_down = jnp.dot(
        fixed_down, ortho_down.astype(jnp.bfloat16), preferred_element_type=jnp.float32
    )
    right_down = lax.psum(right_down, "tensor")
    bit = 0
    right_down = right_down + from_partner(right_down, "dp", bit)
    right_down = right_down / REPLICAS
    rebuilt_gate = jnp.dot(ortho_gate, right_gate.T, precision=high)
    rebuilt_down = jnp.dot(right_down, ortho_down.T, precision=high)
    share = slab // REPLICAS
    update_gate = lax.dynamic_slice_in_dim(rebuilt_gate, replica * share, share, 0).astype(
        jnp.bfloat16
    )
    update_down = lax.dynamic_slice_in_dim(rebuilt_down, replica * share, share, 0).astype(
        jnp.bfloat16
    )
    new_error_gate = (fixed_gate.astype(jnp.float32) - rebuilt_gate).astype(jnp.bfloat16)
    new_error_down = (fixed_down.astype(jnp.float32) - rebuilt_down).astype(jnp.bfloat16)
    return (update_gate, update_down, new_error_gate, new_error_down)


def solution(mesh):
    in_specs = (
        P(("mix", "dp"), "tensor"),
        P(("mix", "dp"), "tensor"),
        P(("mix", "dp"), "tensor"),
        P(("mix", "dp"), "tensor"),
        P(None, "tensor"),
        P(),
    )
    out_specs = (
        P(("mix", "dp"), "tensor"),
        P(("mix", "dp"), "tensor"),
        P(("mix", "dp"), "tensor"),
        P(("mix", "dp"), "tensor"),
    )
    return jax.shard_map(local, mesh=mesh, in_specs=in_specs, out_specs=out_specs, check_vma=False)
```

profile of v0, /device:TPU:0, one launch (start us, length us, event | category | flops | bytes accessed | tf_op | source)
XLA Modules:
  0.0 278.2 jit_solution(14361388834337673998)
XLA Ops:
  7.2 1.0 copy-done
  8.3 9.6 %fusion.7 = f32[1792,64]{0,1:T(8,128)} fusion(bf16[64,5120]{1,0:T(8,128)(2,1)S(1)} %copy-done, s32[]{:T(128)S(6)} %select_n.24, bf16[2560,1792]{1,0:T(8,128)(2,1)} %param.10, bf16[2560,1792]{1,0:T(8,128)(2,1)} %param.8), kind=kOutput, calls=%fused_computation.14 | convolution fusion | flops 605552640 | bytes 19136516 | tf_op jit(solution)/shard_map/dot_general | solution.py:48
  18.0 10.0 %fusion.24 = f32[2560,64]{0,1:T(8,128)} fusion(bf16[64,1792]{1,0:T(8,128)(2,1)S(1)} %copy-done.3, bf16[2560,1792]{1,0:T(8,128)(2,1)} %param.9, bf16[2560,1792]{1,0:T(8,128)(2,1)} %param.7), kind=kOutput, calls=%fused_computation.41 | convolution fusion | flops 605552640 | bytes 19234816 | tf_op jit(solution)/shard_map/dot_general | solution.py:45
  28.0 30.3 %all-reduce.7.cloned.1.call-done = f32[1792,64]{0,1:T(8,128)} async-done(((f32[1792,64]{0,1:T(8,128)}), f32[1792,64]{0,1:T(8,128)}) %all-reduce.7.cloned.1.call-update) | async-done | bytes 458768 | tf_op jit(solution)/shard_map/psum | solution.py:54
  58.3 1.7 fusion.25
  60.0 10.3 %psum.46 = f32[64,64]{0,1:T(8,128)S(1)} all-reduce(f32[64,64]{0,1:T(8,128)S(1)} %fusion.25), channel_id=1, replica_groups=mesh['mix'=2,'dp'=4,'tensor'=4] {'tensor'}, use_global_device_ids=true, to_apply=%region_6.8 | all-reduce | flops 4096 | bytes 32768 | tf_op jit(solution)/shard_map/psum | solution.py:57
  70.4 5.8 %cholesky.55 = f32[64,64]{1,0:T(8,128)S(1)} custom-call(f32[64,64]{1,0:T(8,128)S(1)} %fusion.17), custom_call_target="Cholesky" | custom-call | tf_op jit(solution)/shard_map/jit(cholesky)/cholesky | solution.py:31
  77.6 4.9 %custom-call.9 = f32[1,64,64]{1,2,0:T(8,128)S(1)} custom-call(f32[1,64,64]{2,1,0:T(8,128)S(1)} %fusion.14), custom_call_target="InvertDiagBlocksLowerTriangular" | custom-call | tf_op jit(solution)/shard_map/triangular_solve | solution.py:32
  82.5 1.6 fusion.15
  84.1 10.0 %fusion.11 = f32[2560,64]{0,1:T(8,128)} fusion(f32[1792,64]{0,1:T(8,128)S(1)} %fusion.15, bf16[2560,1792]{1,0:T(8,128)(2,1)} %param.10, bf16[2560,1792]{1,0:T(8,128)(2,1)} %param.8), kind=kOutput, calls=%fused_computation.18 | convolution fusion | flops 605667328 | bytes 19464192 | tf_op jit(solution)/shard_map/dot_general | solution.py:62
  94.1 39.2 %all-reduce.9.cloned.1.call-done = (f32[2560,64]{0,1:T(8,128)}, f32[2560,64]{0,1:T(8,128)}) async-done(((f32[2560,64]{0,1:T(8,128)}, f32[2560,64]{0,1:T(8,128)}), (f32[2560,64]{0,1:T(8,128)}, f32[2560,64]{0,1:T(8,128)})) %all-reduce.9.cloned.1.call-update) | async-done | bytes 1310736 | tf_op jit(solution)/shard_map/psum | solution.py:51
  133.4 1.5 collective-permute-start
  135.4 15.8 %collective-permute-done = f32[2560,64]{0,1:T(8,128)S(1)} collective-permute-done((f32[2560,64]{0,1:T(8,128)}, f32[2560,64]{0,1:T(8,128)S(1)}, u32[]{:S(2)}, u32[]{:S(2)}) %collective-permute-start) | collective-permute-done | bytes 655392 | tf_op jit(solution)/shard_map/ppermute | solution.py:10
  151.2 1.2 add.48
  153.0 23.5 %psum.43 = f32[64,64]{0,1:T(8,128)S(1)} all-reduce(f32[64,64]{0,1:T(8,128)S(1)} %convolution_multiply_fusion), channel_id=1, replica_groups=mesh['mix'=2,'dp'=4,'tensor'=4] {'dp'}, use_global_device_ids=true, to_apply=%region_1.2 | all-reduce | flops 4096 | bytes 32768 | tf_op jit(solution)/shard_map/psum | solution.py:56
  176.6 5.8 %cholesky.44 = f32[64,64]{1,0:T(8,128)S(1)} custom-call(f32[64,64]{1,0:T(8,128)S(1)} %fusion.20), custom_call_target="Cholesky" | custom-call | tf_op jit(solution)/shard_map/jit(cholesky)/cholesky | solution.py:31
  183.8 4.9 %custom-call.8 = f32[1,64,64]{1,2,0:T(8,128)S(1)} custom-call(f32[1,64,64]{2,1,0:T(8,128)S(1)} %fusion.13), custom_call_target="InvertDiagBlocksLowerTriangular" | custom-call | tf_op jit(solution)/shard_map/triangular_solve | solution.py:32
  188.7 0.7 fusion.18
  189.5 9.8 %fusion.9 = f32[1792,64]{1,0:T(8,128)} fusion(f32[2560,64]{0,1:T(8,128)S(1)} %fusion.18, bf16[2560,1792]{1,0:T(8,128)(2,1)} %param.9, bf16[2560,1792]{1,0:T(8,128)(2,1)} %param.7), kind=kOutput, calls=%fused_computation.16 | convolution fusion | flops 605716480 | bytes 19464192 | tf_op jit(solution)/shard_map/dot_general | solution.py:18
  199.3 21.4 %subtract_convert_fusion = (bf16[2560,1792]{1,0:T(8,128)(2,1)}, bf16[2560,1792]{1,0:T(8,128)(2,1)}) fusion(bf16[2560,1792]{1,0:T(8,128)(2,1)} %param.10, bf16[2560,1792]{1,0:T(8,128)(2,1)} %param.8, f32[1792,64]{0,1:T(8,128)S(1)} %fusion.15, f32[2560,64]{0,1:T(8,128)S(1)} %copy-done.2, f32[2560,64]{0,1:T(8,128)S(1)} %collective-permute-done.1), kind=kOutput, calls=%fused_computation | convolution fusion | flops 3560243200 | bytes 38469632 | tf_op jit(solution)/shard_map/dot_general | solution.py:70
  220.8 4.7 %dynamic-slice_convert_fusion = bf16[1280,1792]{1,0:T(8,128)(2,1)} fusion(bf16[2560,1792]{1,0:T(8,128)(2,1)} %get-tuple-element.10, s32[]{:T(128)S(6)} %select_n.22), kind=kLoop, calls=%fused_computation.4 | loop fusion | bytes 9175044 | tf_op jit(solution)/shard_map/convert_element_type | solution.py:75
  225.5 19.2 %all-reduce.5.cloned.1.call-done = f32[1792,64]{1,0:T(8,128)} async-done(((f32[1792,64]{1,0:T(8,128)}), f32[1792,64]{1,0:T(8,128)}) %all-reduce.5.cloned.1.call-update) | async-done | bytes 458768 | tf_op jit(solution)/shard_map/psum | solution.py:61
  244.6 22.3 %subtract_convert_fusion.1 = (bf16[2560,1792]{1,0:T(8,128)(2,1)}, bf16[2560,1792]{1,0:T(8,128)(2,1)}) fusion(bf16[2560,1792]{1,0:T(8,128)(2,1)} %param.9, bf16[2560,1792]{1,0:T(8,128)(2,1)} %param.7, f32[2560,64]{0,1:T(8,128)S(1)} %fusion.18, f32[1792,64]{1,0:T(8,128)} %all-reduce.5.cloned.1.call-done), kind=kOutput, calls=%fused_computation.1 | convolution fusion | flops 3560030208 | bytes 37814272 | tf_op jit(solution)/shard_map/dot_general | solution.py:69
  267.0 4.7 %dynamic-slice_convert_fusion.1 = bf16[1280,1792]{1,0:T(8,128)(2,1)} fusion(bf16[2560,1792]{1,0:T(8,128)(2,1)} %get-tuple-element.8, s32[]{:T(128)S(6)} %select_n.22), kind=kLoop, calls=%fused_computation.5 | loop fusion | bytes 9175044 | tf_op jit(solution)/shard_map/convert_element_type | solution.py:72
  (26 shorter events, 4.2 us)
Async XLA Ops:
  7.2 1.1 copy-start
  7.2 51.2 %all-reduce.7.cloned.1.call-start = ((), (), s32[]{:S(2)}) async-start(), calls=%async_computation.1 | async-start | bytes 917504 | tf_op jit(solution)/shard_map/psum | solution.py:54
  8.3 9.7 %copy-start.3 = (bf16[64,1792]{1,0:T(8,128)(2,1)S(1)}, bf16[64,1792]{1,0:T(8,128)(2,1)}, u32[]{:S(2)}) copy-start(bf16[64,1792]{1,0:T(8,128)(2,1)} %param.11) | copy-start | bytes 688132
  17.9 115.4 %all-reduce.9.cloned.1.call-start = ((), (), s32[]{:S(2)}) async-start(), calls=%async_computation.2 | async-start | bytes 2621440 | tf_op jit(solution)/shard_map/psum | solution.py:51
  94.1 150.6 %all-reduce.5.cloned.1.call-start = ((), (), s32[]{:S(2)}) async-start(), calls=%async_computation | async-start | bytes 1835008 | tf_op jit(solution)/shard_map/psum | solution.py:61
  133.4 17.8 %collective-permute-start = (f32[2560,64]{0,1:T(8,128)}, f32[2560,64]{0,1:T(8,128)S(1)}, u32[]{:S(2)}, u32[]{:S(2)}) collective-permute-start(f32[2560,64]{0,1:T(8,128)} %get-tuple-element.5), channel_id=1, source_target_pairs={{0,4},{4,0},{8,12},{12,8},{1,5},{5,1},{9,13},{13,9},{2,6},{6,2},{1... | collective-permute-start | bytes 1966088 | tf_op jit(solution)/shard_map/ppermute | solution.py:10
  134.8 64.5 %collective-permute-start.1 = (f32[2560,64]{0,1:T(8,128)}, f32[2560,64]{0,1:T(8,128)S(1)}, u32[]{:S(2)}, u32[]{:S(2)}) collective-permute-start(f32[2560,64]{0,1:T(8,128)} %get-tuple-element.6), channel_id=1, source_target_pairs={{0,4},{4,0},{8,12},{12,8},{1,5},{5,1},{9,13},{13,9},{2,6},{6,2},{1... | collective-permute-start | bytes 1966088 | tf_op jit(solution)/shard_map/ppermute | solution.py:10
  189.5 9.9 %copy-start.2 = (f32[2560,64]{0,1:T(8,128)S(1)}, f32[2560,64]{0,1:T(8,128)}, u32[]{:S(2)}) copy-start(f32[2560,64]{0,1:T(8,128)} %get-tuple-element.6) | copy-start | bytes 1966084
  244.6 27.1 %copy-start.1 = (bf16[64,5120]{1,0:T(8,128)(2,1)S(1)}, bf16[64,5120]{1,0:T(8,128)(2,1)}, u32[]{:S(2)}) copy-start(bf16[64,5120]{1,0:T(8,128)(2,1)} %param.12) | copy-start | bytes 1966084
Sparse Core Ops, SparseCore 0:
  18.1 40.2 all-reduce.6
  94.2 39.0 all-reduce.8
  199.4 45.1 all-reduce.4
where the time goes:
time: 279 us; the launch traced here: 278 us
  waiting for transfers between devices  105 us (38%)
  matrix products  87.9 us (32%)
  blocking collectives  33.8 us (12%)
  other arithmetic  25.3 us (9%)
  between operations  13.9 us (5%)
  local copies, waits for them, and re-layouts  10.7 us (4%)
    psum x1, waiting for transfers between devices, local(): left_gate = lax.psum(left_gate, 'tensor')  39.2 us
    psum x1, waiting for transfers between devices, local(): left_down = lax.psum(left_down, 'dp')  30.3 us
    psum x1, blocking collectives, local(): inner_gate = lax.psum(gram_of(left_gate) * keep_gate, 'dp')  23.5 us
    dot_general x1, matrix products, local(): rebuilt_gate = jnp.dot(ortho_gate, right_gate.T, precision=high)  22.3 us
    dot_general x1, matrix products, local(): rebuilt_down = jnp.dot(right_down, ortho_down.T, precision=high)  21.4 us
    psum x1, waiting for transfers between devices, local(): right_gate = lax.psum(right_gate, 'dp') / REPLICAS  19.2 us
    ppermute x2, waiting for transfers between devices, from_partner(): lax.ppermute(shard, axis, [(i, i ^ 1 << stride) for i in range(lax.axis_s...  15.8 us
    another operation x6, other arithmetic, factored(): lower = jnp.linalg.cholesky(inner)  13 us
  transfers between devices with their start and end apart: 5, of which 4 were waited for; matrix products, arithmetic and copies ran while one was open for 22% of the time, Pallas kernels for 0%

commit v1 on v0

v1 whole, which is shorter than its diff:
```python
import functools

import jax
import jax.numpy as jnp
from jax import lax
from jax.experimental import pallas as pl
from jax.experimental.pallas import tpu as pltpu
from jax.sharding import PartitionSpec as P

REPLICAS = 2
RANK = 64
TILE = 256
MIB = 1 << 20
BF16 = jnp.bfloat16
F32 = jnp.float32

NN = (((1,), (0,)), ((), ()))
NT = (((1,), (1,)), ((), ()))
TN = (((0,), (0,)), ((), ()))


def from_partner(shard, axis, stride):
    return lax.ppermute(shard, axis, [(i, i ^ 1 << stride) for i in range(lax.axis_size(axis))])


def corrected(grad, error):
    return (grad.astype(F32) + error.astype(F32)).astype(BF16)


def transposed(matrix, ortho):
    return lax.dot_general(matrix, ortho.astype(BF16), TN, preferred_element_type=F32)


def gram_of(left):
    return jnp.dot(left.T, left, precision=lax.Precision.HIGHEST)


def factored(left, inner):
    lower = jnp.linalg.cholesky(inner)
    return lax.linalg.triangular_solve(lower, left, left_side=False, lower=True, transpose_a=True)


def local_plain(grad_gate, grad_down, error_gate, error_down, start_gate, start_down):
    high = lax.Precision.HIGHEST
    dp_place = lax.axis_index("dp")
    block = dp_place // REPLICAS
    replica = dp_place % REPLICAS
    fixed_gate = corrected(grad_gate, error_gate)
    fixed_down = corrected(grad_down, error_down)
    slab = fixed_gate.shape[0]
    cols_down = lax.dynamic_slice_in_dim(start_down, block * slab, slab, 1)
    left_gate = lax.dot_general(fixed_gate, start_gate, NT, preferred_element_type=F32)
    left_down = lax.dot_general(
        fixed_down, cols_down, (((0,), (1,)), ((), ())), preferred_element_type=F32
    )
    left_gate = lax.psum(left_gate, "tensor")
    left_gate = left_gate + from_partner(left_gate, "dp", 0)
    left_down = lax.psum(left_down, "dp")
    keep_gate = (replica == 0).astype(F32)
    inner_gate = lax.psum(gram_of(left_gate) * keep_gate, "dp")
    inner_down = lax.psum(gram_of(left_down), "tensor")
    ortho_gate = factored(left_gate, inner_gate)
    ortho_down = factored(left_down, inner_down)
    right_gate = transposed(fixed_gate, ortho_gate)
    right_gate = lax.psum(right_gate, "dp") / REPLICAS
    right_down = jnp.dot(fixed_down, ortho_down.astype(BF16), preferred_element_type=F32)
    right_down = lax.psum(right_down, "tensor")
    right_down = right_down + from_partner(right_down, "dp", 0)
    right_down = right_down / REPLICAS
    rebuilt_gate = jnp.dot(ortho_gate, right_gate.T, precision=high)
    rebuilt_down = jnp.dot(right_down, ortho_down.T, precision=high)
    share = slab // REPLICAS
    update_gate = lax.dynamic_slice_in_dim(rebuilt_gate, replica * share, share, 0).astype(BF16)
    update_down = lax.dynamic_slice_in_dim(rebuilt_down, replica * share, share, 0).astype(BF16)
    new_error_gate = (fixed_gate.astype(F32) - rebuilt_gate).astype(BF16)
    new_error_down = (fixed_down.astype(F32) - rebuilt_down).astype(BF16)
    return (update_gate, update_down, new_error_gate, new_error_down)


def exchange(x, partner):
    n_dp, n_t = lax.axis_size("dp"), lax.axis_size("tensor")
    pairs = []
    for d in range(n_dp):
        for t in range(n_t):
            to_d, to_t = partner(d, t)
            pairs.append((d * n_t + t, to_d * n_t + to_t))
    return lax.ppermute(x, ("dp", "tensor"), pairs)


def bits(n, low):
    out, b = [], low
    while b < n:
        out.append(b)
        b *= 2
    return out


def sum_rows(x, core):
    n_t = lax.axis_size("tensor")
    half = RANK // 2
    keep = lax.dynamic_slice_in_dim(x, core * half, half, 0)
    give = lax.dynamic_slice_in_dim(x, (1 - core) * half, half, 0)
    own = keep + exchange(give, lambda d, t: (d, t ^ 1))
    steps = [(0, b) for b in bits(n_t, 2)] + [(1, 0)]
    for i in range(len(steps)):
        def partner(d, t, i=i):
            r, b = steps[i] if t % 2 == 0 else steps[-1 - i]
            return d ^ r, t ^ b
        own = own + exchange(own, partner)
    return own, exchange(own, lambda d, t: (d, t ^ 1))


def sum_cols(x, replica):
    n_dp = lax.axis_size("dp")
    half = RANK // 2
    keep = lax.dynamic_slice_in_dim(x, replica * half, half, 0)
    give = lax.dynamic_slice_in_dim(x, (1 - replica) * half, half, 0)
    own = keep + exchange(give, lambda d, t: (d ^ 1, t))
    for b in bits(n_dp, 2):
        own = own + exchange(own, lambda d, t, b=b: (d ^ b, t))
    return own, exchange(own, lambda d, t: (d ^ 1, t))


VMEM = pl.BlockSpec(memory_space=pltpu.VMEM)
SMEM = pl.BlockSpec(memory_space=pltpu.SMEM)
ANY = pl.BlockSpec(memory_space=pl.ANY)


def params(mib):
    return pltpu.CompilerParams(vmem_limit_bytes=mib * MIB)


def cost(flops, nbytes):
    return pl.CostEstimate(flops=int(flops), bytes_accessed=int(nbytes), transcendentals=0)


def in_vmem(x):
    return pltpu.with_memory_space_constraint(x, pltpu.VMEM)


def parts_of(x):
    hi = x.astype(BF16)
    lo = (x - hi.astype(F32)).astype(BF16)
    return hi, lo


def gate_left_kernel(grad, error, start, fixed, left):
    rows, cols = grad.shape

    def body(g, e, f, out):
        c = (g[...].astype(F32) + e[...].astype(F32)).astype(BF16)
        f[...] = c
        out[...] = lax.dot_general(start[...], c, NT, preferred_element_type=F32)

    def step(g, e):
        i = pl.program_id(0)
        at = pl.ds(pl.multiple_of(i * TILE, TILE), TILE)
        body(g, e, fixed.at[at, :], left.at[:, at])

    spec = pl.BlockSpec((TILE, cols), lambda i: (i, 0))
    pltpu.emit_pipeline(step, grid=(rows // TILE,), in_specs=[spec, spec])(grad, error)


def down_left_kernel(grad, error, start, fixed, left):
    rows, cols = grad.shape

    def step(g, e):
        i = pl.program_id(0)
        at = pl.ds(pl.multiple_of(i * TILE, TILE), TILE)
        c = (g[...].astype(F32) + e[...].astype(F32)).astype(BF16)
        fixed[at, :] = c
        term = jnp.dot(start[:, at], c, preferred_element_type=F32)

        @pl.when(i == 0)
        def _():
            left[...] = term

        @pl.when(i > 0)
        def _():
            left[...] += term

    spec = pl.BlockSpec((TILE, cols), lambda i: (i, 0))
    pltpu.emit_pipeline(step, grid=(rows // TILE,), in_specs=[spec, spec])(grad, error)


def left_call(kernel, grad, error, start, left_width):
    rows, cols = grad.shape
    return pl.pallas_call(
        kernel,
        out_shape=(
            pltpu.VMEM((rows, cols), BF16),
            jax.ShapeDtypeStruct((RANK, left_width), F32),
        ),
        in_specs=[ANY, ANY, VMEM],
        out_specs=(VMEM, VMEM),
        compiler_params=params(12),
        cost_estimate=cost(2 * rows * cols * RANK, 4 * rows * cols),
    )(grad, error, start)


def gate_right_kernel(own, other, fixed, right, gram, left, stack):
    half = RANK // 2
    left[:half, :] = own[...]
    left[half:, :] = other[...]
    hi, lo = parts_of(left[...])
    stack[:RANK, :] = hi
    stack[RANK:, :] = lo
    gram[...] = lax.dot_general(
        left[...], left[...], NT, preferred_element_type=F32, precision=lax.Precision.HIGHEST
    )
    cols = fixed.shape[1]

    def step(i, _):
        at = pl.ds(pl.multiple_of(i * TILE, TILE), TILE)
        both = jnp.dot(stack[...], fixed[:, at], preferred_element_type=F32)
        right[:, at] = both[:RANK] + both[RANK:]
        return 0

    lax.fori_loop(0, cols // TILE, step, 0)


def down_right_kernel(place, own, other, fixed, right, gram, left, stack):
    half = RANK // 2
    replica = place[1]
    left[pl.ds(pl.multiple_of(replica * half, half), half), :] = own[...]
    left[pl.ds(pl.multiple_of((1 - replica) * half, half), half), :] = other[...]
    hi, lo = parts_of(left[...])
    stack[:RANK, :] = hi
    stack[RANK:, :] = lo
    gram[...] = lax.dot_general(
        left[...], left[...], NT, preferred_element_type=F32, precision=lax.Precision.HIGHEST
    )
    rows = fixed.shape[0]

    def step(i, _):
        at = pl.ds(pl.multiple_of(i * TILE, TILE), TILE)
        both = lax.dot_general(stack[...], fixed[at, :], NT, preferred_element_type=F32)
        right[:, at] = both[:RANK] + both[RANK:]
        return 0

    lax.fori_loop(0, rows // TILE, step, 0)


def right_call(kernel, args, fixed, out_width):
    rows, cols = fixed.shape
    width = args[-1].shape[1]
    return pl.pallas_call(
        kernel,
        out_shape=(
            jax.ShapeDtypeStruct((RANK, out_width), F32),
            jax.ShapeDtypeStruct((RANK, RANK), F32),
            jax.ShapeDtypeStruct((RANK, width), F32),
        ),
        in_specs=[SMEM] * (len(args) - 2) + [VMEM, VMEM, VMEM],
        out_specs=(VMEM, VMEM, VMEM),
        scratch_shapes=[pltpu.VMEM((2 * RANK, width), BF16)],
        compiler_params=params(12),
        cost_estimate=cost(16 * rows * cols * RANK, 2 * rows * cols),
    )(*args, in_vmem(fixed))


def solve_kernel(place, gram, left, out):
    a = gram[...]
    row_at = lax.broadcasted_iota(jnp.int32, (RANK, RANK), 0)
    col_at = lax.broadcasted_iota(jnp.int32, (RANK, RANK), 1)
    for k in range(RANK):
        row = a[k : k + 1, :]
        col = a[:, k : k + 1]
        inv = 1.0 / a[k : k + 1, k : k + 1]
        row_n = row * inv
        col_n = col * inv
        new = a - col * row_n
        new = jnp.where(row_at == k, row_n, new)
        new = jnp.where(col_at == k, col_n, new)
        a = jnp.where((row_at == k) & (col_at == k), -inv, new)
    half = RANK // 2
    turned = jnp.concatenate([a[half:], a[:half]], axis=0)
    a = jnp.where(place[0] == 0, a, turned) * (-1.0 / REPLICAS)
    out[...] = jnp.dot(a, left[...], preferred_element_type=F32, precision=lax.Precision.HIGHEST)


def solve_call(turn, gram, left):
    return pl.pallas_call(
        solve_kernel,
        out_shape=jax.ShapeDtypeStruct(left.shape, F32),
        in_specs=[SMEM, VMEM, VMEM],
        out_specs=VMEM,
        compiler_params=params(8),
        cost_estimate=cost(1 << 30, 1 << 22),
    )(turn, gram, left)


def rebuild_kernel(place, row_a, row_b, col_a, col_b, fixed, update, new_error, row_stack, col_stack):
    half = RANK // 2
    for at, ref in ((0, row_a), (half, row_b)):
        hi, lo = parts_of(ref[...])
        n = ref.shape[0]
        for k, part in enumerate((hi, lo, hi, lo)):
            row_stack[k * RANK + at : k * RANK + at + n, :] = part
    for at, ref in ((0, col_a), (half, col_b)):
        hi, lo = parts_of(ref[...])
        n = ref.shape[0]
        for k, part in enumerate((hi, hi, lo, lo)):
            col_stack[k * RANK + at : k * RANK + at + n, :] = part
    rows, cols = fixed.shape
    tiles = rows // REPLICAS // TILE
    first = place[1] * tiles
    second = (1 - place[1]) * tiles

    def rebuilt(tile):
        at = pl.ds(pl.multiple_of(tile * TILE, TILE), TILE)
        value = lax.dot_general(row_stack[:, at], col_stack[...], TN, preferred_element_type=F32)
        return value, (fixed[at, :].astype(F32) - value).astype(BF16)

    def mine(u, e):
        value, fresh = rebuilt(first + pl.program_id(0))
        u[...] = value.astype(BF16)
        e[...] = fresh

    def theirs(e):
        _, fresh = rebuilt(second + pl.program_id(0))
        e[...] = fresh

    block = (TILE, cols)
    pltpu.emit_pipeline(
        mine,
        grid=(tiles,),
        out_specs=[pl.BlockSpec(block, lambda i: (i, 0)), pl.BlockSpec(block, lambda i: (first + i, 0))],
    )(update, new_error)
    pltpu.emit_pipeline(
        theirs, grid=(tiles,), out_specs=[pl.BlockSpec(block, lambda i: (second + i, 0))]
    )(new_error)


def rebuild_call(place, row_a, row_b, col_a, col_b, fixed):
    rows, cols = fixed.shape
    return pl.pallas_call(
        rebuild_kernel,
        out_shape=(
            jax.ShapeDtypeStruct((rows // REPLICAS, cols), BF16),
            jax.ShapeDtypeStruct((rows, cols), BF16),
        ),
        in_specs=[SMEM] + [VMEM] * 5,
        out_specs=(ANY, ANY),
        scratch_shapes=[pltpu.VMEM((4 * RANK, rows), BF16), pltpu.VMEM((4 * RANK, cols), BF16)],
        compiler_params=params(20),
        cost_estimate=cost(2 * rows * cols * 4 * RANK, 3 * rows * cols),
    )(place, row_a, row_b, col_a, col_b, in_vmem(fixed))


def local(grad_gate, grad_down, error_gate, error_down, start_gate, start_down):
    slab, width = grad_gate.shape
    dp_place = lax.axis_index("dp")
    core = lax.axis_index("tensor") % 2
    block = dp_place // REPLICAS
    replica = dp_place % REPLICAS
    zero = jnp.zeros_like(core)
    place = jnp.stack([core, replica])
    rows_down = lax.dynamic_slice_in_dim(start_down, block * slab, slab, 1)

    fixed_gate, left_gate = left_call(gate_left_kernel, grad_gate, error_gate, start_gate, slab)
    fixed_down, left_down = left_call(down_left_kernel, grad_down, error_down, rows_down, width)

    gate_own, gate_other = sum_rows(left_gate, core)
    down_own, down_other = sum_cols(left_down, replica)

    right_gate, gram_gate, left_gate = right_call(
        gate_right_kernel, (gate_own, gate_other), fixed_gate, width
    )
    right_down, gram_down, left_down = right_call(
        down_right_kernel, (place, down_own, down_other), fixed_down, slab
    )

    for b in bits(lax.axis_size("dp"), REPLICAS):
        gram_gate = gram_gate + exchange(gram_gate, lambda d, t, b=b: (d ^ b, t))
    for b in bits(lax.axis_size("tensor"), 1):
        gram_down = gram_down + exchange(gram_down, lambda d, t, b=b: (d, t ^ b))

    gate_rows = solve_call(jnp.stack([replica]), gram_gate, left_gate)
    down_cols = solve_call(jnp.stack([core]), gram_down, left_down)

    gate_own, gate_other = sum_cols(right_gate, replica)
    down_own, down_other = sum_rows(right_down, core)

    half = RANK // 2
    update_gate, new_error_gate = rebuild_call(
        place, gate_rows[:half], gate_rows[half:], gate_own, gate_other, fixed_gate
    )
    update_down, new_error_down = rebuild_call(
        place, down_own, down_other, down_cols[:half], down_cols[half:], fixed_down
    )
    return (update_gate, update_down, new_error_gate, new_error_down)


def solution(mesh):
    split = P(("mix", "dp"), "tensor")
    in_specs = (split, split, split, split, P(None, "tensor"), P())
    out_specs = (split, split, split, split)

    def run(grad_gate, *rest):
        groups = mesh.shape["mix"] * mesh.shape["dp"]
        slab = grad_gate.shape[0] // groups
        width = grad_gate.shape[1] // mesh.shape["tensor"]
        fits = slab % (REPLICAS * TILE) == 0 and width % TILE == 0
        body = local if fits else local_plain
        return jax.shard_map(
            body, mesh=mesh, in_specs=in_specs, out_specs=out_specs, check_vma=False
        )(grad_gate, *rest)

    return run
```

time: 279 us -> 130 us (0.47)
  matrix products: 87.9 us -> 0 us
  waiting for transfers between devices: 105 us -> 21.7 us
  Pallas kernels: 0 us -> 61.3 us
  blocking collectives: 33.8 us -> 0 us
  other arithmetic: 25.3 us -> 0.42 us
  starting transfers between devices: 2.15 us -> 18.3 us
  local copies, waits for them, and re-layouts: 10.7 us -> 26.6 us
  between operations: 13.9 us -> 1.04 us
    psum x3 -> x0, waiting for transfers between devices: 88.7 us -> none  [the longest x1 39.2 us: local(): left_gate = lax.psum(left_gate, 'tensor')]
    dot_general x8 -> x0, matrix products: 85.5 us -> none  [the longest x1 22.3 us: local(): rebuilt_gate = jnp.dot(ortho_gate, right_gate.T, precision=high)]
    pallas_call x0 -> x8, Pallas kernels: none -> 61.3 us  [the longest x2 19.8 us: rebuild_call(): pl.pallas_call(rebuild_kernel, out_shape=(jax.ShapeDtypeStruct((rows // R...]
    psum x2 -> x0, blocking collectives: 33.8 us -> none  [the longest x1 23.5 us: local(): inner_gate = lax.psum(gram_of(left_gate) * keep_gate, 'dp')]
    unnamed x8 -> x38, local copies, waits for them, and re-layouts: 1.03 us -> 26.4 us
    another operation x10 -> x1, other arithmetic: 24.1 us -> 0.08 us  [local(): place = jnp.stack([core, replica])]
    ppermute x2 -> x17, starting transfers between devices: 2.03 us -> 18.3 us  [exchange(): return lax.ppermute(x, ('dp', 'tensor'), pairs)]
    convert_element_type x2 -> x0, local copies, waits for them, and re-layouts: 9.47 us -> none  [the longest x1 4.74 us: local(): lax.dynamic_slice_in_dim(rebuilt_gate, replica * share, share, 0)]
  transfers between devices with their start and end apart: 5 -> 17, of which waited for: 4 -> 6; matrix products, arithmetic and copies ran while one was open for 22% -> 0% of each run, Pallas kernels for 0% -> 34%
where the time goes in v1:
time: 130 us; the launch traced here: 129 us
  Pallas kernels  61.3 us (47%)
  local copies, waits for them, and re-layouts  26.6 us (20%)
  waiting for transfers between devices  21.7 us (17%)
  starting transfers between devices  18.3 us (14%)
    unnamed x38, local copies, waits for them, and re-layouts  26.4 us
    ppermute x17, waiting for transfers between devices, exchange(): return lax.ppermute(x, ('dp', 'tensor'), pairs)  21.7 us
    pallas_call x2, Pallas kernels, rebuild_call(): pl.pallas_call(rebuild_kernel, out_shape=(jax.ShapeDtypeStruct((rows // R...  19.8 us
    ppermute x17, starting transfers between devices, exchange(): return lax.ppermute(x, ('dp', 'tensor'), pairs)  18.3 us
    pallas_call x2, Pallas kernels, solve_call(): pl.pallas_call(solve_kernel, out_shape=jax.ShapeDtypeStruct(left.shape, F...  17.7 us
    pallas_call x2, Pallas kernels, left_call(): pl.pallas_call(kernel, out_shape=(pltpu.VMEM((rows, cols), BF16), jax.Sha...  14.9 us
    pallas_call x2, Pallas kernels, right_call(): pl.pallas_call(kernel, out_shape=(jax.ShapeDtypeStruct((RANK, out_width),...  8.93 us
  transfers between devices with their start and end apart: 17, of which 6 were waited for; matrix products, arithmetic and copies ran while one was open for 0% of the time, Pallas kernels for 34%

profile of v1, /device:TPU:0, one launch (start us, length us, event | category | flops | bytes accessed | tf_op | source)
XLA Modules:
  0.0 129.4 jit_solution(17736468297239311988)
XLA Ops:
  1.8 3.6 %copy-done.5 = bf16[2560,1792]{1,0:T(8,128)(2,1)S(1)} copy-done((bf16[2560,1792]{1,0:T(8,128)(2,1)S(1)}, bf16[2560,1792]{1,0:T(8,128)(2,1)}, u32[]{:S(2)}) %copy-start.5) | copy-done | bytes 9175064
  5.4 3.6 %copy-done.6 = bf16[2560,1792]{1,0:T(8,128)(2,1)S(1)} copy-done((bf16[2560,1792]{1,0:T(8,128)(2,1)S(1)}, bf16[2560,1792]{1,0:T(8,128)(2,1)}, u32[]{:S(2)}) %copy-start.6) | copy-done | bytes 9175064
  9.0 7.5 %shard_map.97 = (bf16[2560,1792]{1,0:T(8,128)(2,1)S(1)}, f32[64,1792]{1,0:T(8,128)S(1)}) custom-call(bf16[2560,1792]{1,0:T(8,128)(2,1)S(1)} %copy-done.5, bf16[2560,1792]{1,0:T(8,128)(2,1)S(1)} %copy-done.6, bf16[64,2560]{1,0:T(8,128)(2,1)S(1)} %constant_dynamic-slice_fusion.2.start), custom_call_target="tpu_custom_call" | custom-call | flops 587202560 | bytes 18350080 | tf_op jit(solution)/shard_map/pallas_call | solution.py:188
  16.5 3.6 %copy-done.2 = bf16[2560,1792]{1,0:T(8,128)(2,1)} copy-done((bf16[2560,1792]{1,0:T(8,128)(2,1)}, bf16[2560,1792]{1,0:T(8,128)(2,1)S(1)}, u32[]{:S(2)}) %copy-start.2) | copy-done | bytes 9175064
  20.2 3.1 %collective-permute-start.8 = (f32[32,1792]{1,0:T(8,128)S(1)}, f32[32,1792]{1,0:T(8,128)S(1)}, u32[]{:S(2)}, u32[]{:S(2)}) collective-permute-start(f32[32,1792]{1,0:T(8,128)S(1)} %constant_dynamic-slice_fusion.1), channel_id=1, source_target_pairs={{0,4},{1,5},{2,6},{3,7},{4,0},{5,1},{6,2},{7,3},{8,12},{9,13},{10,... | collective-permute-start | bytes 688136 | tf_op jit(solution)/shard_map/ppermute | solution.py:87
  23.3 3.6 %copy-done.7 = bf16[2560,1792]{1,0:T(8,128)(2,1)S(1)} copy-done((bf16[2560,1792]{1,0:T(8,128)(2,1)S(1)}, bf16[2560,1792]{1,0:T(8,128)(2,1)}, u32[]{:S(2)}) %copy-start.7) | copy-done | bytes 9175064
  26.9 3.6 %copy-done.8 = bf16[2560,1792]{1,0:T(8,128)(2,1)S(1)} copy-done((bf16[2560,1792]{1,0:T(8,128)(2,1)S(1)}, bf16[2560,1792]{1,0:T(8,128)(2,1)}, u32[]{:S(2)}) %copy-start.8) | copy-done | bytes 9175064
  30.5 7.4 %shard_map.93 = (bf16[2560,1792]{1,0:T(8,128)(2,1)S(1)}, f32[64,2560]{1,0:T(8,128)S(1)}) custom-call(bf16[2560,1792]{1,0:T(8,128)(2,1)S(1)} %copy-done.7, bf16[2560,1792]{1,0:T(8,128)(2,1)S(1)} %copy-done.8, bf16[64,1792]{1,0:T(8,128)(2,1)S(1)} %copy-done.9), custom_call_target="tpu_custom_call" | custom-call | flops 587202560 | bytes 18350080 | tf_op jit(solution)/shard_map/pallas_call | solution.py:188
  37.8 3.6 %copy-done.4 = bf16[2560,1792]{1,0:T(8,128)(2,1)} copy-done((bf16[2560,1792]{1,0:T(8,128)(2,1)}, bf16[2560,1792]{1,0:T(8,128)(2,1)S(1)}, u32[]{:S(2)}) %copy-start.4) | copy-done | bytes 9175064
  41.7 2.7 %collective-permute-start.9 = (f32[32,1792]{1,0:T(8,128)S(1)}, f32[32,1792]{1,0:T(8,128)S(1)}, u32[]{:S(2)}, u32[]{:S(2)}) collective-permute-start(f32[32,1792]{1,0:T(8,128)S(1)} %dynamic-slice_add_fusion.2), channel_id=1, source_target_pairs={{0,8},{1,9},{2,10},{3,11},{4,12},{5,13},{6,14},{7,15},{8,0},{9,1},... | collective-permute-start | bytes 688136 | tf_op jit(solution)/shard_map/ppermute | solution.py:87
  45.9 9.5 %collective-permute-done.9 = f32[32,1792]{1,0:T(8,128)S(1)} collective-permute-done((f32[32,1792]{1,0:T(8,128)S(1)}, f32[32,1792]{1,0:T(8,128)S(1)}, u32[]{:S(2)}, u32[]{:S(2)}) %collective-permute-start.9) | collective-permute-done | bytes 229408 | tf_op jit(solution)/shard_map/ppermute | solution.py:87
  55.7 2.1 %collective-permute-start.2 = (f32[32,2560]{1,0:T(8,128)S(1)}, f32[32,2560]{1,0:T(8,128)S(1)}, u32[]{:S(2)}, u32[]{:S(2)}) collective-permute-start(f32[32,2560]{1,0:T(8,128)S(1)} %add.71), channel_id=1, source_target_pairs={{0,4},{1,3},{2,6},{3,1},{4,0},{5,7},{6,2},{7,5},{8,12},{9,11},{10,... | collective-permute-start | bytes 983048 | tf_op jit(solution)/shard_map/ppermute | solution.py:87
  57.8 5.3 %collective-permute-done.10.other = f32[32,1792]{1,0:T(8,128)S(1)} collective-permute-done((f32[32,1792]{1,0:T(8,128)S(1)}, f32[32,1792]{1,0:T(8,128)S(1)}, u32[]{:S(2)}, u32[]{:S(2)}) %collective-permute-start.10) | collective-permute-done | bytes 229408 | tf_op jit(solution)/shard_map/ppermute | solution.py:87
  63.1 3.6 %copy-done.3 = bf16[2560,1792]{1,0:T(8,128)(2,1)S(1)} copy-done((bf16[2560,1792]{1,0:T(8,128)(2,1)S(1)}, bf16[2560,1792]{1,0:T(8,128)(2,1)}, u32[]{:S(2)}) %copy-start.3) | copy-done | bytes 9175064
  66.7 5.8 %shard_map.98 = (f32[64,2560]{1,0:T(8,128)S(1)}, f32[64,64]{1,0:T(8,128)S(1)}, f32[64,1792]{1,0:T(8,128)S(1)}) custom-call(s32[2]{0:T(128)S(1)} %pad_add_fusion.place, f32[32,1792]{1,0:T(8,128)S(1)} %add.80.own, f32[32,1792]{1,0:T(8,128)S(1)} %collective-permute-done.10.other, bf16[2560,1792]{1,0:T(8,128)(2,1)S(1)} %copy-done.3), custom_call_target="tpu_custom_call" | custom-call | flops 4697620480 | bytes 9175040 | tf_op jit(solution)/shard_map/pallas_call | solution.py:247
  75.9 3.1 %shard_map.94 = (f32[64,1792]{1,0:T(8,128)S(1)}, f32[64,64]{1,0:T(8,128)S(1)}, f32[64,2560]{1,0:T(8,128)S(1)}) custom-call(f32[32,2560]{1,0:T(8,128)S(1)} %add.72.own, f32[32,2560]{1,0:T(8,128)S(1)} %collective-permute-done.3.other, bf16[2560,1792]{1,0:T(8,128)(2,1)S(1)} %bitcast.5), custom_call_target="tpu_custom_call" | custom-call | flops 4697620480 | bytes 9175040 | tf_op jit(solution)/shard_map/pallas_call | solution.py:247
  81.6 3.0 %collective-permute-done.16 = f32[64,64]{1,0:T(8,128)S(1)} collective-permute-done((f32[64,64]{1,0:T(8,128)S(1)}, f32[64,64]{1,0:T(8,128)S(1)}, u32[]{:S(2)}, u32[]{:S(2)}) %collective-permute-start.16) | collective-permute-done | bytes 16416 | tf_op jit(solution)/shard_map/ppermute | solution.py:87
  84.6 8.8 %shard_map.99 = f32[64,1792]{1,0:T(8,128)S(1)} custom-call(s32[1]{0:T(128)} %bitcast.place, f32[64,64]{1,0:T(8,128)S(1)} %add.85.gram, f32[64,1792]{1,0:T(8,128)S(1)} %get-tuple-element.28.left), custom_call_target="tpu_custom_call" | custom-call | flops 1073741824 | bytes 4194304 | tf_op jit(solution)/shard_map/pallas_call | solution.py:283
  93.3 2.5 %collective-permute-start.4 = (f32[64,64]{1,0:T(8,128)S(1)}, f32[64,64]{1,0:T(8,128)S(1)}, u32[]{:S(2)}, u32[]{:S(2)}) collective-permute-start(f32[64,64]{1,0:T(8,128)S(1)} %get-tuple-element.20), channel_id=1, source_target_pairs={{0,8},{1,9},{2,10},{3,11},{4,12},{5,13},{6,14},{7,15},{8,0},{9,1},... | collective-permute-start | bytes 49160 | tf_op jit(solution)/shard_map/ppermute | solution.py:87
  96.3 2.0 %collective-permute-start.6 = (f32[32,1792]{1,0:T(8,128)S(1)}, f32[32,1792]{1,0:T(8,128)S(1)}, u32[]{:S(2)}, u32[]{:S(2)}) collective-permute-start(f32[32,1792]{1,0:T(8,128)S(1)} %dynamic-slice_add_fusion.3), channel_id=1, source_target_pairs={{0,8},{1,9},{2,10},{3,11},{4,12},{5,13},{6,14},{7,15},{8,0},{9,1},... | collective-permute-start | bytes 688136 | tf_op jit(solution)/shard_map/ppermute | solution.py:87
  98.3 8.9 %shard_map.95 = f32[64,2560]{1,0:T(8,128)S(1)} custom-call(s32[1]{0:T(128)} %bitcast.1.place, f32[64,64]{1,0:T(8,128)S(1)} %add.73.gram, f32[64,2560]{1,0:T(8,128)S(1)} %get-tuple-element.21.left), custom_call_target="tpu_custom_call" | custom-call | flops 1073741824 | bytes 4194304 | tf_op jit(solution)/shard_map/pallas_call | solution.py:283
  107.4 1.6 %collective-permute-done.6 = f32[32,1792]{1,0:T(8,128)S(1)} collective-permute-done((f32[32,1792]{1,0:T(8,128)S(1)}, f32[32,1792]{1,0:T(8,128)S(1)}, u32[]{:S(2)}, u32[]{:S(2)}) %collective-permute-start.6) | collective-permute-done | bytes 229408 | tf_op jit(solution)/shard_map/ppermute | solution.py:87
  109.6 9.9 %shard_map.100 = (bf16[1280,1792]{1,0:T(8,128)(2,1)}, bf16[2560,1792]{1,0:T(8,128)(2,1)}) custom-call(s32[2]{0:T(128)S(1)} %pad_add_fusion.place, f32[32,2560]{1,0:T(8,128)S(1)} %add.83.row_a, f32[32,2560]{1,0:T(8,128)S(1)} %collective-permute-done.14.row_b, f32[32,1792]{1,0:T(8,128)S(1)} %get-tuple-element.35.col_a, ...), custom_call_target="tpu_custom_call" | custom-call | flops 2348810240 | bytes 13762560 | tf_op jit(solution)/shard_map/pallas_call | solution.py:337
  119.5 9.9 %shard_map.96 = (bf16[1280,1792]{1,0:T(8,128)(2,1)}, bf16[2560,1792]{1,0:T(8,128)(2,1)}) custom-call(s32[2]{0:T(128)S(1)} %pad_add_fusion.place, f32[32,2560]{1,0:T(8,128)S(1)} %get-tuple-element.33.row_a, f32[32,2560]{1,0:T(8,128)S(1)} %get-tuple-element.32.row_b, f32[32,1792]{1,0:T(8,128)S(1)} %add.77.col_a, f32[32,1792]{1,0:T(8,128)S(1)} %collective-permute-done.7.col_b, ...), custom_call_target="tpu_custom_call" | custom-call | flops 2348810240 | bytes 13762560 | tf_op jit(solution)/shard_map/pallas_call | solution.py:337
  (80 shorter events, 10.0 us)
Async XLA Ops:
  20.2 21.5 %collective-permute-start.8 = (f32[32,1792]{1,0:T(8,128)S(1)}, f32[32,1792]{1,0:T(8,128)S(1)}, u32[]{:S(2)}, u32[]{:S(2)}) collective-permute-start(f32[32,1792]{1,0:T(8,128)S(1)} %constant_dynamic-slice_fusion.1), channel_id=1, source_target_pairs={{0,4},{1,5},{2,6},{3,7},{4,0},{5,1},{6,2},{7,3},{8,12},{9,13},{10,... | collective-permute-start | bytes 688136 | tf_op jit(solution)/shard_map/ppermute | solution.py:87
  41.5 34.4 %slice-start.3 = ((s8[9175040]{0:T(1024)(128)(4,1)}), s8[786432]{0:T(1024)(128)(4,1)S(1)}, s32[]{:S(2)}) async-start(s8[9175040]{0:T(1024)(128)(4,1)} %bitcast.4), calls=%async_computation.3 | async-start | bytes 1572864
  41.5 2.8 %collective-permute-start = (f32[32,2560]{1,0:T(8,128)S(1)}, f32[32,2560]{1,0:T(8,128)S(1)}, u32[]{:S(2)}, u32[]{:S(2)}) collective-permute-start(f32[32,2560]{1,0:T(8,128)S(1)} %constant_dynamic-slice_fusion.4), channel_id=1, source_target_pairs={{0,1},{1,0},{2,3},{3,2},{4,5},{5,4},{6,7},{7,6},{8,9},{9,8},{10,11... | collective-permute-start | bytes 983048 | tf_op jit(solution)/shard_map/ppermute | solution.py:87
  41.7 13.8 %collective-permute-start.9 = (f32[32,1792]{1,0:T(8,128)S(1)}, f32[32,1792]{1,0:T(8,128)S(1)}, u32[]{:S(2)}, u32[]{:S(2)}) collective-permute-start(f32[32,1792]{1,0:T(8,128)S(1)} %dynamic-slice_add_fusion.2), channel_id=1, source_target_pairs={{0,8},{1,9},{2,10},{3,11},{4,12},{5,13},{6,14},{7,15},{8,0},{9,1},... | collective-permute-start | bytes 688136 | tf_op jit(solution)/shard_map/ppermute | solution.py:87
  44.4 11.3 %collective-permute-start.1 = (f32[32,2560]{1,0:T(8,128)S(1)}, f32[32,2560]{1,0:T(8,128)S(1)}, u32[]{:S(2)}, u32[]{:S(2)}) collective-permute-start(f32[32,2560]{1,0:T(8,128)S(1)} %dynamic-slice_add_fusion.1), channel_id=1, source_target_pairs={{0,2},{1,5},{2,0},{3,7},{4,6},{5,1},{6,4},{7,3},{8,10},{9,13},{10,... | collective-permute-start | bytes 983048 | tf_op jit(solution)/shard_map/ppermute | solution.py:87
  55.5 7.6 %collective-permute-start.10 = (f32[32,1792]{1,0:T(8,128)S(1)}, f32[32,1792]{1,0:T(8,128)S(1)}, u32[]{:S(2)}, u32[]{:S(2)}) collective-permute-start(f32[32,1792]{1,0:T(8,128)S(1)} %add.80.own), channel_id=1, source_target_pairs={{0,4},{1,5},{2,6},{3,7},{4,0},{5,1},{6,2},{7,3},{8,12},{9,13},{10,... | collective-permute-start | bytes 688136 | tf_op jit(solution)/shard_map/ppermute | solution.py:87
  55.7 16.9 %collective-permute-start.2 = (f32[32,2560]{1,0:T(8,128)S(1)}, f32[32,2560]{1,0:T(8,128)S(1)}, u32[]{:S(2)}, u32[]{:S(2)}) collective-permute-start(f32[32,2560]{1,0:T(8,128)S(1)} %add.71), channel_id=1, source_target_pairs={{0,4},{1,3},{2,6},{3,1},{4,0},{5,7},{6,2},{7,5},{8,12},{9,11},{10,... | collective-permute-start | bytes 983048 | tf_op jit(solution)/shard_map/ppermute | solution.py:87
  72.6 1.7 %collective-permute-start.11 = (f32[32,2560]{1,0:T(8,128)S(1)}, f32[32,2560]{1,0:T(8,128)S(1)}, u32[]{:S(2)}, u32[]{:S(2)}) collective-permute-start(f32[32,2560]{1,0:T(8,128)S(1)} %constant_dynamic-slice_fusion), channel_id=1, source_target_pairs={{0,1},{1,0},{2,3},{3,2},{4,5},{5,4},{6,7},{7,6},{8,9},{9,8},{10,11... | collective-permute-start | bytes 983048 | tf_op jit(solution)/shard_map/ppermute | solution.py:87
  72.7 3.2 %collective-permute-start.3 = (f32[32,2560]{1,0:T(8,128)S(1)}, f32[32,2560]{1,0:T(8,128)S(1)}, u32[]{:S(2)}, u32[]{:S(2)}) collective-permute-start(f32[32,2560]{1,0:T(8,128)S(1)} %add.72.own), channel_id=1, source_target_pairs={{0,1},{1,0},{2,3},{3,2},{4,5},{5,4},{6,7},{7,6},{8,9},{9,8},{10,11... | collective-permute-start | bytes 983048 | tf_op jit(solution)/shard_map/ppermute | solution.py:87
  74.3 21.6 %collective-permute-start.12 = (f32[32,2560]{1,0:T(8,128)S(1)}, f32[32,2560]{1,0:T(8,128)S(1)}, u32[]{:S(2)}, u32[]{:S(2)}) collective-permute-start(f32[32,2560]{1,0:T(8,128)S(1)} %dynamic-slice_add_fusion), channel_id=1, source_target_pairs={{0,2},{1,5},{2,0},{3,7},{4,6},{5,1},{6,4},{7,3},{8,10},{9,13},{10,... | collective-permute-start | bytes 983048 | tf_op jit(solution)/shard_map/ppermute | solution.py:87
  75.9 33.6 %slice-start = ((s8[9175040]{0:T(1024)(128)(4,1)}), s8[786432]{0:T(1024)(128)(4,1)S(1)}, s32[]{:S(2)}) async-start(s8[9175040]{0:T(1024)(128)(4,1)} %bitcast.2), calls=%async_computation | async-start | bytes 1572864
  75.9 33.6 %slice-start.1 = ((s8[9175040]{0:T(1024)(128)(4,1)}), s8[4194304]{0:T(1024)(128)(4,1)S(1)}, s32[]{:S(2)}) async-start(s8[9175040]{0:T(1024)(128)(4,1)} %bitcast.2), calls=%async_computation.1 | async-start | bytes 8388608
  79.1 17.2 %collective-permute-start.5 = (f32[32,1792]{1,0:T(8,128)S(1)}, f32[32,1792]{1,0:T(8,128)S(1)}, u32[]{:S(2)}, u32[]{:S(2)}) collective-permute-start(f32[32,1792]{1,0:T(8,128)S(1)} %constant_dynamic-slice_fusion.3), channel_id=1, source_target_pairs={{0,4},{1,5},{2,6},{3,7},{4,0},{5,1},{6,2},{7,3},{8,12},{9,13},{10,... | collective-permute-start | bytes 688136 | tf_op jit(solution)/shard_map/ppermute | solution.py:87
  79.4 1.2 collective-permute-start.15
  80.6 3.9 %collective-permute-start.16 = (f32[64,64]{1,0:T(8,128)S(1)}, f32[64,64]{1,0:T(8,128)S(1)}, u32[]{:S(2)}, u32[]{:S(2)}) collective-permute-start(f32[64,64]{1,0:T(8,128)S(1)} %add.84), channel_id=1, source_target_pairs={{0,2},{1,3},{2,0},{3,1},{4,6},{5,7},{6,4},{7,5},{8,10},{9,11},{10,... | collective-permute-start | bytes 49160 | tf_op jit(solution)/shard_map/ppermute | solution.py:87
  84.6 25.0 %slice-start.2 = ((s8[9175040]{0:T(1024)(128)(4,1)}), s8[4194304]{0:T(1024)(128)(4,1)S(1)}, s32[]{:S(2)}) async-start(s8[9175040]{0:T(1024)(128)(4,1)} %bitcast.2), calls=%async_computation.2 | async-start | bytes 8388608
  93.3 5.0 %collective-permute-start.4 = (f32[64,64]{1,0:T(8,128)S(1)}, f32[64,64]{1,0:T(8,128)S(1)}, u32[]{:S(2)}, u32[]{:S(2)}) collective-permute-start(f32[64,64]{1,0:T(8,128)S(1)} %get-tuple-element.20), channel_id=1, source_target_pairs={{0,8},{1,9},{2,10},{3,11},{4,12},{5,13},{6,14},{7,15},{8,0},{9,1},... | collective-permute-start | bytes 49160 | tf_op jit(solution)/shard_map/ppermute | solution.py:87
  95.9 23.6 %slice-start.6 = ((s8[9175040]{0:T(1024)(128)(4,1)}), s8[4194304]{0:T(1024)(128)(4,1)S(1)}, s32[]{:S(2)}) async-start(s8[9175040]{0:T(1024)(128)(4,1)} %bitcast.6), calls=%async_computation.6 | async-start | bytes 8388608
  95.9 11.4 %collective-permute-start.13 = (f32[32,2560]{1,0:T(8,128)S(1)}, f32[32,2560]{1,0:T(8,128)S(1)}, u32[]{:S(2)}, u32[]{:S(2)}) collective-permute-start(f32[32,2560]{1,0:T(8,128)S(1)} %add.82), channel_id=1, source_target_pairs={{0,4},{1,3},{2,6},{3,1},{4,0},{5,7},{6,2},{7,5},{8,12},{9,11},{10,... | collective-permute-start | bytes 983048 | tf_op jit(solution)/shard_map/ppermute | solution.py:87
  96.3 12.8 %collective-permute-start.6 = (f32[32,1792]{1,0:T(8,128)S(1)}, f32[32,1792]{1,0:T(8,128)S(1)}, u32[]{:S(2)}, u32[]{:S(2)}) collective-permute-start(f32[32,1792]{1,0:T(8,128)S(1)} %dynamic-slice_add_fusion.3), channel_id=1, source_target_pairs={{0,8},{1,9},{2,10},{3,11},{4,12},{5,13},{6,14},{7,15},{8,0},{9,1},... | collective-permute-start | bytes 688136 | tf_op jit(solution)/shard_map/ppermute | solution.py:87
  98.3 21.1 %slice-start.7 = ((s8[9175040]{0:T(1024)(128)(4,1)}), s8[4194304]{0:T(1024)(128)(4,1)S(1)}, s32[]{:S(2)}) async-start(s8[9175040]{0:T(1024)(128)(4,1)} %bitcast.6), calls=%async_computation.7 | async-start | bytes 8388608
  107.3 2.2 %collective-permute-start.14 = (f32[32,2560]{1,0:T(8,128)S(1)}, f32[32,2560]{1,0:T(8,128)S(1)}, u32[]{:S(2)}, u32[]{:S(2)}) collective-permute-start(f32[32,2560]{1,0:T(8,128)S(1)} %add.83.row_a), channel_id=1, source_target_pairs={{0,1},{1,0},{2,3},{3,2},{4,5},{5,4},{6,7},{7,6},{8,9},{9,8},{10,11... | collective-permute-start | bytes 983048 | tf_op jit(solution)/shard_map/ppermute | solution.py:87
  109.1 10.4 %collective-permute-start.7 = (f32[32,1792]{1,0:T(8,128)S(1)}, f32[32,1792]{1,0:T(8,128)S(1)}, u32[]{:S(2)}, u32[]{:S(2)}) collective-permute-start(f32[32,1792]{1,0:T(8,128)S(1)} %add.77.col_a), channel_id=1, source_target_pairs={{0,4},{1,5},{2,6},{3,7},{4,0},{5,1},{6,2},{7,3},{8,12},{9,13},{10,... | collective-permute-start | bytes 688136 | tf_op jit(solution)/shard_map/ppermute | solution.py:87
  109.5 19.9 %copy-start.1 = (bf16[64,5120]{1,0:T(8,128)(2,1)S(1)}, bf16[64,5120]{1,0:T(8,128)(2,1)}, u32[]{:S(2)}) copy-start(bf16[64,5120]{1,0:T(8,128)(2,1)} %param.11) | copy-start | bytes 1966084
  (12 other events, 69.1 us)

commit v2 on v1

--- a/solution.py
+++ b/solution.py
@@ -138,6 +138,10 @@
     return pltpu.with_memory_space_constraint(x, pltpu.VMEM)
 
 
+def in_hbm(x):
+    return pltpu.with_memory_space_constraint(x, pltpu.HBM)
+
+
 def parts_of(x):
     hi = x.astype(BF16)
     lo = (x - hi.astype(F32)).astype(BF16)
@@ -147,15 +151,13 @@
 def gate_left_kernel(grad, error, start, fixed, left):
     rows, cols = grad.shape
 
-    def body(g, e, f, out):
-        c = (g[...].astype(F32) + e[...].astype(F32)).astype(BF16)
-        f[...] = c
-        out[...] = lax.dot_general(start[...], c, NT, preferred_element_type=F32)
-
     def step(g, e):
         i = pl.program_id(0)
         at = pl.ds(pl.multiple_of(i * TILE, TILE), TILE)
-        body(g, e, fixed.at[at, :], left.at[:, at])
+        c = (g[...].astype(F32) + e[...].astype(F32)).astype(BF16)
+        fixed[at, :] = c
+        term = lax.dot_general(c, start[...], NT, preferred_element_type=F32)
+        left[:, at] = term.T
 
     spec = pl.BlockSpec((TILE, cols), lambda i: (i, 0))
     pltpu.emit_pipeline(step, grid=(rows // TILE,), in_specs=[spec, spec])(grad, error)
@@ -195,7 +197,7 @@
         out_specs=(VMEM, VMEM),
         compiler_params=params(12),
         cost_estimate=cost(2 * rows * cols * RANK, 4 * rows * cols),
-    )(grad, error, start)
+    )(in_hbm(grad), in_hbm(error), start)
 
 
 def gate_right_kernel(own, other, fixed, right, gram, left, stack):
@@ -234,8 +236,8 @@
 
     def step(i, _):
         at = pl.ds(pl.multiple_of(i * TILE, TILE), TILE)
-        both = lax.dot_general(stack[...], fixed[at, :], NT, preferred_element_type=F32)
-        right[:, at] = both[:RANK] + both[RANK:]
+        both = lax.dot_general(fixed[at, :], stack[...], NT, preferred_element_type=F32)
+        right[:, at] = (both[:, :RANK] + both[:, RANK:]).T
         return 0
 
     lax.fori_loop(0, rows // TILE, step, 0)
@@ -263,19 +265,15 @@
     a = gram[...]
     row_at = lax.broadcasted_iota(jnp.int32, (RANK, RANK), 0)
     col_at = lax.broadcasted_iota(jnp.int32, (RANK, RANK), 1)
+    lane = lax.broadcasted_iota(jnp.int32, (1, RANK), 1)
     for k in range(RANK):
-        row = a[k : k + 1, :]
-        col = a[:, k : k + 1]
-        inv = 1.0 / a[k : k + 1, k : k + 1]
-        row_n = row * inv
-        col_n = col * inv
-        new = a - col * row_n
-        new = jnp.where(row_at == k, row_n, new)
-        new = jnp.where(col_at == k, col_n, new)
-        a = jnp.where((row_at == k) & (col_at == k), -inv, new)
+        col = jnp.broadcast_to(a[:, k : k + 1], (RANK, RANK))
+        row = jnp.where(lane == k, 1.0, a[k : k + 1, :]) * (1.0 / col[k : k + 1, :])
+        rest = jnp.where((row_at == k) | (col_at == k), 0.0, a)
+        a = rest - jnp.where(row_at == k, -1.0, col) * row
     half = RANK // 2
     turned = jnp.concatenate([a[half:], a[:half]], axis=0)
-    a = jnp.where(place[0] == 0, a, turned) * (-1.0 / REPLICAS)
+    a = jnp.where(place[0] == 0, a, turned) * (1.0 / REPLICAS)
     out[...] = jnp.dot(a, left[...], preferred_element_type=F32, precision=lax.Precision.HIGHEST)
 
 
@@ -305,31 +303,32 @@
     rows, cols = fixed.shape
     tiles = rows // REPLICAS // TILE
     first = place[1] * tiles
-    second = (1 - place[1]) * tiles
-
-    def rebuilt(tile):
-        at = pl.ds(pl.multiple_of(tile * TILE, TILE), TILE)
-        value = lax.dot_general(row_stack[:, at], col_stack[...], TN, preferred_element_type=F32)
-        return value, (fixed[at, :].astype(F32) - value).astype(BF16)
-
-    def mine(u, e):
-        value, fresh = rebuilt(first + pl.program_id(0))
-        u[...] = value.astype(BF16)
-        e[...] = fresh
-
-    def theirs(e):
-        _, fresh = rebuilt(second + pl.program_id(0))
-        e[...] = fresh
+
+    def tile_of(i):
+        return lax.rem(first + i, REPLICAS * tiles)
+
+    def step(u, e):
+        i = pl.program_id(0)
+        at = pl.ds(pl.multiple_of(tile_of(i) * TILE, TILE), TILE)
+        row = row_stack[:, at].T
+        for j in range(0, cols, TILE):
+            here = slice(j, j + TILE)
+            value = jnp.dot(row, col_stack[:, here], preferred_element_type=F32)
+            e[:, here] = (fixed[at, here].astype(F32) - value).astype(BF16)
+
+            @pl.when(i < tiles)
+            def _():
+                u[:, here] = value.astype(BF16)
 
     block = (TILE, cols)
     pltpu.emit_pipeline(
-        mine,
-        grid=(tiles,),
-        out_specs=[pl.BlockSpec(block, lambda i: (i, 0)), pl.BlockSpec(block, lambda i: (first + i, 0))],
+        step,
+        grid=(REPLICAS * tiles,),
+        out_specs=[
+            pl.BlockSpec(block, lambda i: (jnp.minimum(i, tiles - 1), 0)),
+            pl.BlockSpec(block, lambda i: (tile_of(i), 0)),
+        ],
     )(update, new_error)
-    pltpu.emit_pipeline(
-        theirs, grid=(tiles,), out_specs=[pl.BlockSpec(block, lambda i: (second + i, 0))]
-    )(new_error)
 
 
 def rebuild_call(place, row_a, row_b, col_a, col_b, fixed):

time: 130 us -> 135 us (1.038)
  Pallas kernels: 61.3 us -> 78.3 us
  local copies, waits for them, and re-layouts: 26.6 us -> 12.2 us
  waiting for transfers between devices: 21.7 us -> 24.6 us
    pallas_call x2, Pallas kernels: 19.8 us -> 35.7 us  [rebuild_call(): pl.pallas_call(rebuild_kernel, out_shape=(jax.ShapeDtypeStruct((rows // R...]
    unnamed x38 -> x30, local copies, waits for them, and re-layouts: 26.4 us -> 12 us
    pallas_call x2, Pallas kernels: 14.9 us -> 21.2 us  [left_call(): pl.pallas_call(kernel, out_shape=(pltpu.VMEM((rows, cols), BF16), jax.Sha...]
    pallas_call x2, Pallas kernels: 17.7 us -> 11.9 us  [solve_call(): pl.pallas_call(solve_kernel, out_shape=jax.ShapeDtypeStruct(left.shape, F...]
    ppermute x17, waiting for transfers between devices: 21.7 us -> 24.6 us  [exchange(): return lax.ppermute(x, ('dp', 'tensor'), pairs)]
  transfers between devices with their start and end apart: 17 -> 17, of which waited for: 6 -> 7; matrix products, arithmetic and copies ran while one was open for 0% -> 0% of each run, Pallas kernels for 34% -> 37%
where the time goes in v2:
time: 135 us
  Pallas kernels  78.3 us (58%)
  waiting for transfers between devices  24.6 us (18%)
  starting transfers between devices  18.1 us (13%)
  local copies, waits for them, and re-layouts  12.2 us (9%)
    pallas_call x2, Pallas kernels, rebuild_call(): pl.pallas_call(rebuild_kernel, out_shape=(jax.ShapeDtypeStruct((rows // R...  35.7 us
    ppermute x17, waiting for transfers between devices, exchange(): return lax.ppermute(x, ('dp', 'tensor'), pairs)  24.6 us
    pallas_call x2, Pallas kernels, left_call(): pl.pallas_call(kernel, out_shape=(pltpu.VMEM((rows, cols), BF16), jax.Sha...  21.2 us
    ppermute x17, starting transfers between devices, exchange(): return lax.ppermute(x, ('dp', 'tensor'), pairs)  18.1 us
    unnamed x30, local copies, waits for them, and re-layouts  12 us
    pallas_call x2, Pallas kernels, solve_call(): pl.pallas_call(solve_kernel, out_shape=jax.ShapeDtypeStruct(left.shape, F...  11.9 us
    pallas_call x2, Pallas kernels, right_call(): pl.pallas_call(kernel, out_shape=(jax.ShapeDtypeStruct((RANK, out_width),...  9.55 us
  transfers between devices with their start and end apart: 17, of which 7 were waited for; matrix products, arithmetic and copies ran while one was open for 0% of the time, Pallas kernels for 37%

profile of v2, /device:TPU:0, one launch (start us, length us, event | category | flops | bytes accessed | tf_op | source)
XLA Modules:
  0.0 134.7 jit_solution(11709156383534090634)
XLA Ops:
  1.8 10.7 %shard_map.97 = (bf16[2560,1792]{1,0:T(8,128)(2,1)S(1)}, f32[64,1792]{1,0:T(8,128)S(1)}) custom-call(bf16[2560,1792]{1,0:T(8,128)(2,1)} %grad.3, bf16[2560,1792]{1,0:T(8,128)(2,1)} %error.3, bf16[64,2560]{1,0:T(8,128)(2,1)S(1)} %constant_dynamic-slice_fusion.2.start), custom_call_target="tpu_custom_call" | custom-call | flops 587202560 | bytes 18350080 | tf_op jit(solution)/shard_map/pallas_call | solution.py:190
  12.4 3.6 %copy-done.2 = bf16[2560,1792]{1,0:T(8,128)(2,1)} copy-done((bf16[2560,1792]{1,0:T(8,128)(2,1)}, bf16[2560,1792]{1,0:T(8,128)(2,1)S(1)}, u32[]{:S(2)}) %copy-start.2) | copy-done | bytes 9175064
  16.1 3.1 %collective-permute-start.8 = (f32[32,1792]{1,0:T(8,128)S(1)}, f32[32,1792]{1,0:T(8,128)S(1)}, u32[]{:S(2)}, u32[]{:S(2)}) collective-permute-start(f32[32,1792]{1,0:T(8,128)S(1)} %constant_dynamic-slice_fusion.1), channel_id=1, source_target_pairs={{0,4},{1,5},{2,6},{3,7},{4,0},{5,1},{6,2},{7,3},{8,12},{9,13},{10,... | collective-permute-start | bytes 688136 | tf_op jit(solution)/shard_map/ppermute | solution.py:87
  19.2 10.6 %shard_map.93 = (bf16[2560,1792]{1,0:T(8,128)(2,1)S(1)}, f32[64,2560]{1,0:T(8,128)S(1)}) custom-call(bf16[2560,1792]{1,0:T(8,128)(2,1)} %grad.2, bf16[2560,1792]{1,0:T(8,128)(2,1)} %error.2, bf16[64,1792]{1,0:T(8,128)(2,1)S(1)} %copy-done.5), custom_call_target="tpu_custom_call" | custom-call | flops 587202560 | bytes 18350080 | tf_op jit(solution)/shard_map/pallas_call | solution.py:190
  29.8 3.7 %copy-done.4 = bf16[2560,1792]{1,0:T(8,128)(2,1)} copy-done((bf16[2560,1792]{1,0:T(8,128)(2,1)}, bf16[2560,1792]{1,0:T(8,128)(2,1)S(1)}, u32[]{:S(2)}) %copy-start.4) | copy-done | bytes 9175064
  33.6 2.7 %collective-permute-start.9 = (f32[32,1792]{1,0:T(8,128)S(1)}, f32[32,1792]{1,0:T(8,128)S(1)}, u32[]{:S(2)}, u32[]{:S(2)}) collective-permute-start(f32[32,1792]{1,0:T(8,128)S(1)} %dynamic-slice_add_fusion.2), channel_id=1, source_target_pairs={{0,8},{1,9},{2,10},{3,11},{4,12},{5,13},{6,14},{7,15},{8,0},{9,1},... | collective-permute-start | bytes 688136 | tf_op jit(solution)/shard_map/ppermute | solution.py:87
  36.3 1.6 %collective-permute-start.1 = (f32[32,2560]{1,0:T(8,128)S(1)}, f32[32,2560]{1,0:T(8,128)S(1)}, u32[]{:S(2)}, u32[]{:S(2)}) collective-permute-start(f32[32,2560]{1,0:T(8,128)S(1)} %dynamic-slice_add_fusion.1), channel_id=1, source_target_pairs={{0,2},{1,5},{2,0},{3,7},{4,6},{5,1},{6,4},{7,3},{8,10},{9,13},{10,... | collective-permute-start | bytes 983048 | tf_op jit(solution)/shard_map/ppermute | solution.py:87
  37.9 9.5 %collective-permute-done.9 = f32[32,1792]{1,0:T(8,128)S(1)} collective-permute-done((f32[32,1792]{1,0:T(8,128)S(1)}, f32[32,1792]{1,0:T(8,128)S(1)}, u32[]{:S(2)}, u32[]{:S(2)}) %collective-permute-start.9) | collective-permute-done | bytes 229408 | tf_op jit(solution)/shard_map/ppermute | solution.py:87
  47.7 2.1 %collective-permute-start.2 = (f32[32,2560]{1,0:T(8,128)S(1)}, f32[32,2560]{1,0:T(8,128)S(1)}, u32[]{:S(2)}, u32[]{:S(2)}) collective-permute-start(f32[32,2560]{1,0:T(8,128)S(1)} %add.71), channel_id=1, source_target_pairs={{0,4},{1,3},{2,6},{3,1},{4,0},{5,7},{6,2},{7,5},{8,12},{9,11},{10,... | collective-permute-start | bytes 983048 | tf_op jit(solution)/shard_map/ppermute | solution.py:87
  49.7 5.3 %collective-permute-done.10.other = f32[32,1792]{1,0:T(8,128)S(1)} collective-permute-done((f32[32,1792]{1,0:T(8,128)S(1)}, f32[32,1792]{1,0:T(8,128)S(1)}, u32[]{:S(2)}, u32[]{:S(2)}) %collective-permute-start.10) | collective-permute-done | bytes 229408 | tf_op jit(solution)/shard_map/ppermute | solution.py:87
  55.0 3.6 %copy-done.3 = bf16[2560,1792]{1,0:T(8,128)(2,1)S(1)} copy-done((bf16[2560,1792]{1,0:T(8,128)(2,1)S(1)}, bf16[2560,1792]{1,0:T(8,128)(2,1)}, u32[]{:S(2)}) %copy-start.3) | copy-done | bytes 9175064
  58.6 6.5 %shard_map.98 = (f32[64,2560]{1,0:T(8,128)S(1)}, f32[64,64]{1,0:T(8,128)S(1)}, f32[64,1792]{1,0:T(8,128)S(1)}) custom-call(s32[2]{0:T(128)S(1)} %pad_add_fusion.place, f32[32,1792]{1,0:T(8,128)S(1)} %add.80.own, f32[32,1792]{1,0:T(8,128)S(1)} %collective-permute-done.10.other, bf16[2560,1792]{1,0:T(8,128)(2,1)S(1)} %copy-done.3), custom_call_target="tpu_custom_call" | custom-call | flops 4697620480 | bytes 9175040 | tf_op jit(solution)/shard_map/pallas_call | solution.py:249
  66.9 1.6 %collective-permute-start.12 = (f32[32,2560]{1,0:T(8,128)S(1)}, f32[32,2560]{1,0:T(8,128)S(1)}, u32[]{:S(2)}, u32[]{:S(2)}) collective-permute-start(f32[32,2560]{1,0:T(8,128)S(1)} %dynamic-slice_add_fusion), channel_id=1, source_target_pairs={{0,2},{1,5},{2,0},{3,7},{4,6},{5,1},{6,4},{7,3},{8,10},{9,13},{10,... | collective-permute-start | bytes 983048 | tf_op jit(solution)/shard_map/ppermute | solution.py:87
  68.5 3.1 %shard_map.94 = (f32[64,1792]{1,0:T(8,128)S(1)}, f32[64,64]{1,0:T(8,128)S(1)}, f32[64,2560]{1,0:T(8,128)S(1)}) custom-call(f32[32,2560]{1,0:T(8,128)S(1)} %add.72.own, f32[32,2560]{1,0:T(8,128)S(1)} %collective-permute-done.3.other, bf16[2560,1792]{1,0:T(8,128)(2,1)S(1)} %bitcast.5), custom_call_target="tpu_custom_call" | custom-call | flops 4697620480 | bytes 9175040 | tf_op jit(solution)/shard_map/pallas_call | solution.py:249
  72.0 1.2 collective-permute-done.15
  74.2 2.9 %collective-permute-done.16 = f32[64,64]{1,0:T(8,128)S(1)} collective-permute-done((f32[64,64]{1,0:T(8,128)S(1)}, f32[64,64]{1,0:T(8,128)S(1)}, u32[]{:S(2)}, u32[]{:S(2)}) %collective-permute-start.16) | collective-permute-done | bytes 16416 | tf_op jit(solution)/shard_map/ppermute | solution.py:87
  77.1 5.8 %shard_map.99 = f32[64,1792]{1,0:T(8,128)S(1)} custom-call(s32[1]{0:T(128)} %bitcast.place, f32[64,64]{1,0:T(8,128)S(1)} %add.85.gram, f32[64,1792]{1,0:T(8,128)S(1)} %get-tuple-element.28.left), custom_call_target="tpu_custom_call" | custom-call | flops 1073741824 | bytes 4194304 | tf_op jit(solution)/shard_map/pallas_call | solution.py:281
  83.0 2.5 %collective-permute-start.4 = (f32[64,64]{1,0:T(8,128)S(1)}, f32[64,64]{1,0:T(8,128)S(1)}, u32[]{:S(2)}, u32[]{:S(2)}) collective-permute-start(f32[64,64]{1,0:T(8,128)S(1)} %get-tuple-element.20), channel_id=1, source_target_pairs={{0,8},{1,9},{2,10},{3,11},{4,12},{5,13},{6,14},{7,15},{8,0},{9,1},... | collective-permute-start | bytes 49160 | tf_op jit(solution)/shard_map/ppermute | solution.py:87
  85.9 2.0 %collective-permute-start.6 = (f32[32,1792]{1,0:T(8,128)S(1)}, f32[32,1792]{1,0:T(8,128)S(1)}, u32[]{:S(2)}, u32[]{:S(2)}) collective-permute-start(f32[32,1792]{1,0:T(8,128)S(1)} %dynamic-slice_add_fusion.3), channel_id=1, source_target_pairs={{0,8},{1,9},{2,10},{3,11},{4,12},{5,13},{6,14},{7,15},{8,0},{9,1},... | collective-permute-start | bytes 688136 | tf_op jit(solution)/shard_map/ppermute | solution.py:87
  88.0 6.0 %shard_map.95 = f32[64,2560]{1,0:T(8,128)S(1)} custom-call(s32[1]{0:T(128)} %bitcast.1.place, f32[64,64]{1,0:T(8,128)S(1)} %add.73.gram, f32[64,2560]{1,0:T(8,128)S(1)} %get-tuple-element.21.left), custom_call_target="tpu_custom_call" | custom-call | flops 1073741824 | bytes 4194304 | tf_op jit(solution)/shard_map/pallas_call | solution.py:281
  94.0 2.1 %collective-permute-done.13 = f32[32,2560]{1,0:T(8,128)S(1)} collective-permute-done((f32[32,2560]{1,0:T(8,128)S(1)}, f32[32,2560]{1,0:T(8,128)S(1)}, u32[]{:S(2)}, u32[]{:S(2)}) %collective-permute-start.13) | collective-permute-done | bytes 327712 | tf_op jit(solution)/shard_map/ppermute | solution.py:87
  96.3 2.4 %collective-permute-done.6 = f32[32,1792]{1,0:T(8,128)S(1)} collective-permute-done((f32[32,1792]{1,0:T(8,128)S(1)}, f32[32,1792]{1,0:T(8,128)S(1)}, u32[]{:S(2)}, u32[]{:S(2)}) %collective-permute-start.6) | collective-permute-done | bytes 229408 | tf_op jit(solution)/shard_map/ppermute | solution.py:87
  99.0 17.8 %shard_map.100 = (bf16[1280,1792]{1,0:T(8,128)(2,1)}, bf16[2560,1792]{1,0:T(8,128)(2,1)}) custom-call(s32[2]{0:T(128)S(1)} %pad_add_fusion.place, f32[32,2560]{1,0:T(8,128)S(1)} %add.83.row_a, f32[32,2560]{1,0:T(8,128)S(1)} %collective-permute-done.14.row_b, f32[32,1792]{1,0:T(8,128)S(1)} %get-tuple-element.35.col_a, ...), custom_call_target="tpu_custom_call" | custom-call | flops 2348810240 | bytes 13762560 | tf_op jit(solution)/shard_map/pallas_call | solution.py:336
  116.8 17.8 %shard_map.96 = (bf16[1280,1792]{1,0:T(8,128)(2,1)}, bf16[2560,1792]{1,0:T(8,128)(2,1)}) custom-call(s32[2]{0:T(128)S(1)} %pad_add_fusion.place, f32[32,2560]{1,0:T(8,128)S(1)} %get-tuple-element.33.row_a, f32[32,2560]{1,0:T(8,128)S(1)} %get-tuple-element.32.row_b, f32[32,1792]{1,0:T(8,128)S(1)} %add.77.col_a, f32[32,1792]{1,0:T(8,128)S(1)} %collective-permute-done.7.col_b, ...), custom_call_target="tpu_custom_call" | custom-call | flops 2348810240 | bytes 13762560 | tf_op jit(solution)/shard_map/pallas_call | solution.py:336
  (72 shorter events, 5.3 us)
Async XLA Ops:
  16.1 17.5 %collective-permute-start.8 = (f32[32,1792]{1,0:T(8,128)S(1)}, f32[32,1792]{1,0:T(8,128)S(1)}, u32[]{:S(2)}, u32[]{:S(2)}) collective-permute-start(f32[32,1792]{1,0:T(8,128)S(1)} %constant_dynamic-slice_fusion.1), channel_id=1, source_target_pairs={{0,4},{1,5},{2,6},{3,7},{4,0},{5,1},{6,2},{7,3},{8,12},{9,13},{10,... | collective-permute-start | bytes 688136 | tf_op jit(solution)/shard_map/ppermute | solution.py:87
  33.5 35.0 %slice-start.3 = ((s8[9175040]{0:T(1024)(128)(4,1)}), s8[786432]{0:T(1024)(128)(4,1)S(1)}, s32[]{:S(2)}) async-start(s8[9175040]{0:T(1024)(128)(4,1)} %bitcast.4), calls=%async_computation.3 | async-start | bytes 1572864
  33.5 2.8 %collective-permute-start = (f32[32,2560]{1,0:T(8,128)S(1)}, f32[32,2560]{1,0:T(8,128)S(1)}, u32[]{:S(2)}, u32[]{:S(2)}) collective-permute-start(f32[32,2560]{1,0:T(8,128)S(1)} %constant_dynamic-slice_fusion.4), channel_id=1, source_target_pairs={{0,1},{1,0},{2,3},{3,2},{4,5},{5,4},{6,7},{7,6},{8,9},{9,8},{10,11... | collective-permute-start | bytes 983048 | tf_op jit(solution)/shard_map/ppermute | solution.py:87
  33.6 13.8 %collective-permute-start.9 = (f32[32,1792]{1,0:T(8,128)S(1)}, f32[32,1792]{1,0:T(8,128)S(1)}, u32[]{:S(2)}, u32[]{:S(2)}) collective-permute-start(f32[32,1792]{1,0:T(8,128)S(1)} %dynamic-slice_add_fusion.2), channel_id=1, source_target_pairs={{0,8},{1,9},{2,10},{3,11},{4,12},{5,13},{6,14},{7,15},{8,0},{9,1},... | collective-permute-start | bytes 688136 | tf_op jit(solution)/shard_map/ppermute | solution.py:87
  36.3 11.3 %collective-permute-start.1 = (f32[32,2560]{1,0:T(8,128)S(1)}, f32[32,2560]{1,0:T(8,128)S(1)}, u32[]{:S(2)}, u32[]{:S(2)}) collective-permute-start(f32[32,2560]{1,0:T(8,128)S(1)} %dynamic-slice_add_fusion.1), channel_id=1, source_target_pairs={{0,2},{1,5},{2,0},{3,7},{4,6},{5,1},{6,4},{7,3},{8,10},{9,13},{10,... | collective-permute-start | bytes 983048 | tf_op jit(solution)/shard_map/ppermute | solution.py:87
  47.5 7.6 %collective-permute-start.10 = (f32[32,1792]{1,0:T(8,128)S(1)}, f32[32,1792]{1,0:T(8,128)S(1)}, u32[]{:S(2)}, u32[]{:S(2)}) collective-permute-start(f32[32,1792]{1,0:T(8,128)S(1)} %add.80.own), channel_id=1, source_target_pairs={{0,4},{1,5},{2,6},{3,7},{4,0},{5,1},{6,2},{7,3},{8,12},{9,13},{10,... | collective-permute-start | bytes 688136 | tf_op jit(solution)/shard_map/ppermute | solution.py:87
  47.7 17.6 %collective-permute-start.2 = (f32[32,2560]{1,0:T(8,128)S(1)}, f32[32,2560]{1,0:T(8,128)S(1)}, u32[]{:S(2)}, u32[]{:S(2)}) collective-permute-start(f32[32,2560]{1,0:T(8,128)S(1)} %add.71), channel_id=1, source_target_pairs={{0,4},{1,3},{2,6},{3,1},{4,0},{5,7},{6,2},{7,5},{8,12},{9,11},{10,... | collective-permute-start | bytes 983048 | tf_op jit(solution)/shard_map/ppermute | solution.py:87
  65.1 1.7 %collective-permute-start.11 = (f32[32,2560]{1,0:T(8,128)S(1)}, f32[32,2560]{1,0:T(8,128)S(1)}, u32[]{:S(2)}, u32[]{:S(2)}) collective-permute-start(f32[32,2560]{1,0:T(8,128)S(1)} %constant_dynamic-slice_fusion), channel_id=1, source_target_pairs={{0,1},{1,0},{2,3},{3,2},{4,5},{5,4},{6,7},{7,6},{8,9},{9,8},{10,11... | collective-permute-start | bytes 983048 | tf_op jit(solution)/shard_map/ppermute | solution.py:87
  65.3 3.2 %collective-permute-start.3 = (f32[32,2560]{1,0:T(8,128)S(1)}, f32[32,2560]{1,0:T(8,128)S(1)}, u32[]{:S(2)}, u32[]{:S(2)}) collective-permute-start(f32[32,2560]{1,0:T(8,128)S(1)} %add.72.own), channel_id=1, source_target_pairs={{0,1},{1,0},{2,3},{3,2},{4,5},{5,4},{6,7},{7,6},{8,9},{9,8},{10,11... | collective-permute-start | bytes 983048 | tf_op jit(solution)/shard_map/ppermute | solution.py:87
  66.9 18.6 %collective-permute-start.12 = (f32[32,2560]{1,0:T(8,128)S(1)}, f32[32,2560]{1,0:T(8,128)S(1)}, u32[]{:S(2)}, u32[]{:S(2)}) collective-permute-start(f32[32,2560]{1,0:T(8,128)S(1)} %dynamic-slice_add_fusion), channel_id=1, source_target_pairs={{0,2},{1,5},{2,0},{3,7},{4,6},{5,1},{6,4},{7,3},{8,10},{9,13},{10,... | collective-permute-start | bytes 983048 | tf_op jit(solution)/shard_map/ppermute | solution.py:87
  68.5 30.4 %slice-start = ((s8[9175040]{0:T(1024)(128)(4,1)}), s8[786432]{0:T(1024)(128)(4,1)S(1)}, s32[]{:S(2)}) async-start(s8[9175040]{0:T(1024)(128)(4,1)} %bitcast.2), calls=%async_computation | async-start | bytes 1572864
  68.5 30.4 %slice-start.1 = ((s8[9175040]{0:T(1024)(128)(4,1)}), s8[4194304]{0:T(1024)(128)(4,1)S(1)}, s32[]{:S(2)}) async-start(s8[9175040]{0:T(1024)(128)(4,1)} %bitcast.2), calls=%async_computation.1 | async-start | bytes 8388608
  71.7 14.3 %collective-permute-start.5 = (f32[32,1792]{1,0:T(8,128)S(1)}, f32[32,1792]{1,0:T(8,128)S(1)}, u32[]{:S(2)}, u32[]{:S(2)}) collective-permute-start(f32[32,1792]{1,0:T(8,128)S(1)} %constant_dynamic-slice_fusion.3), channel_id=1, source_target_pairs={{0,4},{1,5},{2,6},{3,7},{4,0},{5,1},{6,2},{7,3},{8,12},{9,13},{10,... | collective-permute-start | bytes 688136 | tf_op jit(solution)/shard_map/ppermute | solution.py:87
  72.0 1.2 collective-permute-start.15
  73.2 3.9 %collective-permute-start.16 = (f32[64,64]{1,0:T(8,128)S(1)}, f32[64,64]{1,0:T(8,128)S(1)}, u32[]{:S(2)}, u32[]{:S(2)}) collective-permute-start(f32[64,64]{1,0:T(8,128)S(1)} %add.84), channel_id=1, source_target_pairs={{0,2},{1,3},{2,0},{3,1},{4,6},{5,7},{6,4},{7,5},{8,10},{9,11},{10,... | collective-permute-start | bytes 49160 | tf_op jit(solution)/shard_map/ppermute | solution.py:87
  77.1 21.8 %slice-start.2 = ((s8[9175040]{0:T(1024)(128)(4,1)}), s8[4194304]{0:T(1024)(128)(4,1)S(1)}, s32[]{:S(2)}) async-start(s8[9175040]{0:T(1024)(128)(4,1)} %bitcast.2), calls=%async_computation.2 | async-start | bytes 8388608
  83.0 5.0 %collective-permute-start.4 = (f32[64,64]{1,0:T(8,128)S(1)}, f32[64,64]{1,0:T(8,128)S(1)}, u32[]{:S(2)}, u32[]{:S(2)}) collective-permute-start(f32[64,64]{1,0:T(8,128)S(1)} %get-tuple-element.20), channel_id=1, source_target_pairs={{0,8},{1,9},{2,10},{3,11},{4,12},{5,13},{6,14},{7,15},{8,0},{9,1},... | collective-permute-start | bytes 49160 | tf_op jit(solution)/shard_map/ppermute | solution.py:87
  85.5 31.3 %slice-start.6 = ((s8[9175040]{0:T(1024)(128)(4,1)}), s8[4194304]{0:T(1024)(128)(4,1)S(1)}, s32[]{:S(2)}) async-start(s8[9175040]{0:T(1024)(128)(4,1)} %bitcast.6), calls=%async_computation.6 | async-start | bytes 8388608
  85.6 10.6 %collective-permute-start.13 = (f32[32,2560]{1,0:T(8,128)S(1)}, f32[32,2560]{1,0:T(8,128)S(1)}, u32[]{:S(2)}, u32[]{:S(2)}) collective-permute-start(f32[32,2560]{1,0:T(8,128)S(1)} %add.82), channel_id=1, source_target_pairs={{0,4},{1,3},{2,6},{3,1},{4,0},{5,7},{6,2},{7,5},{8,12},{9,11},{10,... | collective-permute-start | bytes 983048 | tf_op jit(solution)/shard_map/ppermute | solution.py:87
  85.9 12.8 %collective-permute-start.6 = (f32[32,1792]{1,0:T(8,128)S(1)}, f32[32,1792]{1,0:T(8,128)S(1)}, u32[]{:S(2)}, u32[]{:S(2)}) collective-permute-start(f32[32,1792]{1,0:T(8,128)S(1)} %dynamic-slice_add_fusion.3), channel_id=1, source_target_pairs={{0,8},{1,9},{2,10},{3,11},{4,12},{5,13},{6,14},{7,15},{8,0},{9,1},... | collective-permute-start | bytes 688136 | tf_op jit(solution)/shard_map/ppermute | solution.py:87
  88.0 28.8 %slice-start.7 = ((s8[9175040]{0:T(1024)(128)(4,1)}), s8[4194304]{0:T(1024)(128)(4,1)S(1)}, s32[]{:S(2)}) async-start(s8[9175040]{0:T(1024)(128)(4,1)} %bitcast.6), calls=%async_computation.7 | async-start | bytes 8388608
  96.2 2.7 %collective-permute-start.14 = (f32[32,2560]{1,0:T(8,128)S(1)}, f32[32,2560]{1,0:T(8,128)S(1)}, u32[]{:S(2)}, u32[]{:S(2)}) collective-permute-start(f32[32,2560]{1,0:T(8,128)S(1)} %add.83.row_a), channel_id=1, source_target_pairs={{0,1},{1,0},{2,3},{3,2},{4,5},{5,4},{6,7},{7,6},{8,9},{9,8},{10,11... | collective-permute-start | bytes 983048 | tf_op jit(solution)/shard_map/ppermute | solution.py:87
  98.7 18.0 %collective-permute-start.7 = (f32[32,1792]{1,0:T(8,128)S(1)}, f32[32,1792]{1,0:T(8,128)S(1)}, u32[]{:S(2)}, u32[]{:S(2)}) collective-permute-start(f32[32,1792]{1,0:T(8,128)S(1)} %add.77.col_a), channel_id=1, source_target_pairs={{0,4},{1,5},{2,6},{3,7},{4,0},{5,1},{6,2},{7,3},{8,12},{9,13},{10,... | collective-permute-start | bytes 688136 | tf_op jit(solution)/shard_map/ppermute | solution.py:87
  98.9 35.8 %copy-start.1 = (bf16[64,5120]{1,0:T(8,128)(2,1)S(1)}, bf16[64,5120]{1,0:T(8,128)(2,1)}, u32[]{:S(2)}) copy-start(bf16[64,5120]{1,0:T(8,128)(2,1)} %param.11) | copy-start | bytes 1966084
  (8 other events, 67.0 us)

commit v3 on v2

v3 whole, which is shorter than its diff:
```python
import functools

import jax
import jax.numpy as jnp
from jax import lax
from jax.experimental import pallas as pl
from jax.experimental.pallas import tpu as pltpu
from jax.sharding import PartitionSpec as P

REPLICAS = 2
RANK = 64
TILE = 256
MIB = 1 << 20
BF16 = jnp.bfloat16
F32 = jnp.float32

NN = (((1,), (0,)), ((), ()))
NT = (((1,), (1,)), ((), ()))
TN = (((0,), (0,)), ((), ()))


def from_partner(shard, axis, stride):
    return lax.ppermute(shard, axis, [(i, i ^ 1 << stride) for i in range(lax.axis_size(axis))])


def corrected(grad, error):
    return (grad.astype(F32) + error.astype(F32)).astype(BF16)


def transposed(matrix, ortho):
    return lax.dot_general(matrix, ortho.astype(BF16), TN, preferred_element_type=F32)


def gram_of(left):
    return jnp.dot(left.T, left, precision=lax.Precision.HIGHEST)


def factored(left, inner):
    lower = jnp.linalg.cholesky(inner)
    return lax.linalg.triangular_solve(lower, left, left_side=False, lower=True, transpose_a=True)


def local_plain(grad_gate, grad_down, error_gate, error_down, start_gate, start_down):
    high = lax.Precision.HIGHEST
    dp_place = lax.axis_index("dp")
    block = dp_place // REPLICAS
    replica = dp_place % REPLICAS
    fixed_gate = corrected(grad_gate, error_gate)
    fixed_down = corrected(grad_down, error_down)
    slab = fixed_gate.shape[0]
    cols_down = lax.dynamic_slice_in_dim(start_down, block * slab, slab, 1)
    left_gate = lax.dot_general(fixed_gate, start_gate, NT, preferred_element_type=F32)
    left_down = lax.dot_general(
        fixed_down, cols_down, (((0,), (1,)), ((), ())), preferred_element_type=F32
    )
    left_gate = lax.psum(left_gate, "tensor")
    left_gate = left_gate + from_partner(left_gate, "dp", 0)
    left_down = lax.psum(left_down, "dp")
    keep_gate = (replica == 0).astype(F32)
    inner_gate = lax.psum(gram_of(left_gate) * keep_gate, "dp")
    inner_down = lax.psum(gram_of(left_down), "tensor")
    ortho_gate = factored(left_gate, inner_gate)
    ortho_down = factored(left_down, inner_down)
    right_gate = transposed(fixed_gate, ortho_gate)
    right_gate = lax.psum(right_gate, "dp") / REPLICAS
    right_down = jnp.dot(fixed_down, ortho_down.astype(BF16), preferred_element_type=F32)
    right_down = lax.psum(right_down, "tensor")
    right_down = right_down + from_partner(right_down, "dp", 0)
    right_down = right_down / REPLICAS
    rebuilt_gate = jnp.dot(ortho_gate, right_gate.T, precision=high)
    rebuilt_down = jnp.dot(right_down, ortho_down.T, precision=high)
    share = slab // REPLICAS
    update_gate = lax.dynamic_slice_in_dim(rebuilt_gate, replica * share, share, 0).astype(BF16)
    update_down = lax.dynamic_slice_in_dim(rebuilt_down, replica * share, share, 0).astype(BF16)
    new_error_gate = (fixed_gate.astype(F32) - rebuilt_gate).astype(BF16)
    new_error_down = (fixed_down.astype(F32) - rebuilt_down).astype(BF16)
    return (update_gate, update_down, new_error_gate, new_error_down)


def core_of():
    return lax.rem(lax.axis_index("tensor"), 2)


def replica_of():
    return lax.rem(lax.axis_index("dp"), REPLICAS)


def exchange(x, partner):
    n_dp, n_t = lax.axis_size("dp"), lax.axis_size("tensor")
    pairs = []
    for d in range(n_dp):
        for t in range(n_t):
            to_d, to_t = partner(d, t)
            pairs.append((d * n_t + t, to_d * n_t + to_t))
    return lax.ppermute(x, ("dp", "tensor"), pairs)


def bits(n, low):
    out, b = [], low
    while b < n:
        out.append(b)
        b *= 2
    return out


def sum_rows(keep, give):
    n_t = lax.axis_size("tensor")
    own = add_call(keep, exchange(give, lambda d, t: (d, t ^ 1)))
    steps = [(0, b) for b in bits(n_t, 2)] + [(1, 0)]
    for i in range(len(steps)):
        def partner(d, t, i=i):
            r, b = steps[i] if t % 2 == 0 else steps[-1 - i]
            return d ^ r, t ^ b
        own = add_call(own, exchange(own, partner))
    return own, exchange(own, lambda d, t: (d, t ^ 1))


def sum_cols(keep, give):
    n_dp = lax.axis_size("dp")
    own = add_call(keep, exchange(give, lambda d, t: (d ^ 1, t)))
    for b in bits(n_dp, REPLICAS):
        own = add_call(own, exchange(own, lambda d, t, b=b: (d ^ b, t)))
    return own, exchange(own, lambda d, t: (d ^ 1, t))


VMEM = pl.BlockSpec(memory_space=pltpu.VMEM)
HBM = pl.BlockSpec(memory_space=pltpu.HBM)


def params(mib):
    return pltpu.CompilerParams(vmem_limit_bytes=mib * MIB)


def cost(micros):
    return pl.CostEstimate(flops=int(micros * 1.1e9), bytes_accessed=0, transcendentals=0)


def in_vmem(*xs):
    return [pltpu.with_memory_space_constraint(x, pltpu.VMEM) for x in xs]


def in_hbm(x):
    return pltpu.with_memory_space_constraint(x, pltpu.HBM)


def parts_of(x):
    hi = x.astype(BF16)
    lo = (x - hi.astype(F32)).astype(BF16)
    return hi, lo


def add_kernel(x, y, out):
    out[...] = x[...] + y[...]


def add_call(x, y):
    return pl.pallas_call(
        add_kernel,
        out_shape=pltpu.VMEM(x.shape, F32),
        in_specs=[VMEM, VMEM],
        out_specs=VMEM,
        compiler_params=params(4),
        cost_estimate=cost(0.2),
    )(*in_vmem(x, y))


def halve(whole, place, keep, give):
    half = RANK // 2
    keep[...] = whole[pl.ds(pl.multiple_of(place * half, half), half), :]
    give[...] = whole[pl.ds(pl.multiple_of((1 - place) * half, half), half), :]


def gate_left_kernel(grad, error, start, fixed, keep, give, left):
    rows, cols = grad.shape

    def step(g, e):
        at = pl.ds(pl.multiple_of(pl.program_id(0) * TILE, TILE), TILE)
        term = jnp.zeros((TILE, RANK), F32)
        for j in range(0, cols, TILE):
            here = slice(j, j + TILE)
            c = g[:, here] + e[:, here]
            fixed[at, here] = c
            term += lax.dot_general(c, start[:, here], NT, preferred_element_type=F32)
        left[:, at] = term.T

    spec = pl.BlockSpec((TILE, cols), lambda i: (i, 0), pipeline_mode=pl.Buffered(3))
    pltpu.emit_pipeline(step, grid=(rows // TILE,), in_specs=[spec, spec])(grad, error)
    halve(left, core_of(), keep, give)


def down_left_kernel(grad, error, start, fixed, keep, give, left):
    rows, cols = grad.shape
    block = lax.div(lax.axis_index("dp"), REPLICAS) * (rows // TILE)
    left[...] = jnp.zeros_like(left)

    def step(g, e, s):
        at = pl.ds(pl.multiple_of(pl.program_id(0) * TILE, TILE), TILE)
        for j in range(0, cols, TILE):
            here = slice(j, j + TILE)
            c = g[:, here] + e[:, here]
            fixed[at, here] = c
            left[:, here] += jnp.dot(s[...], c, preferred_element_type=F32)

    spec = pl.BlockSpec((TILE, cols), lambda i: (i, 0), pipeline_mode=pl.Buffered(3))
    part = pl.BlockSpec((RANK, TILE), lambda i: (0, block + i))
    pltpu.emit_pipeline(step, grid=(rows // TILE,), in_specs=[spec, spec, part])(grad, error, start)
    halve(left, replica_of(), keep, give)


def left_call(kernel, grad, error, start, start_spec, width):
    rows, cols = grad.shape
    half = RANK // 2
    start = in_hbm(start) if start_spec is HBM else in_vmem(start)[0]
    return pl.pallas_call(
        kernel,
        out_shape=(
            pltpu.VMEM((rows, cols), BF16),
            pltpu.VMEM((half, width), F32),
            pltpu.VMEM((half, width), F32),
        ),
        in_specs=[HBM, HBM, start_spec],
        out_specs=(VMEM, VMEM, VMEM),
        scratch_shapes=[pltpu.VMEM((RANK, width), F32)],
        compiler_params=params(12),
        cost_estimate=cost(7),
    )(in_hbm(grad), in_hbm(error), start)


def load_left(own, other, place, left, stack, gram):
    half = RANK // 2
    left[pl.ds(pl.multiple_of(place * half, half), half), :] = own[...]
    left[pl.ds(pl.multiple_of((1 - place) * half, half), half), :] = other[...]
    hi, lo = parts_of(left[...])
    stack[:RANK, :] = hi
    stack[RANK:, :] = lo
    gram[...] = lax.dot_general(
        left[...], left[...], NT, preferred_element_type=F32, precision=lax.Precision.HIGHEST
    )


def gate_right_kernel(own, other, fixed, keep, give, gram, left, stack, right):
    load_left(own, other, core_of(), left, stack, gram)
    cols = fixed.shape[1]

    def step(i, _):
        at = pl.ds(pl.multiple_of(i * TILE, TILE), TILE)
        both = jnp.dot(stack[...], fixed[:, at], preferred_element_type=F32)
        right[:, at] = both[:RANK] + both[RANK:]
        return 0

    lax.fori_loop(0, cols // TILE, step, 0)
    halve(right, replica_of(), keep, give)


def down_right_kernel(own, other, fixed, keep, give, gram, left, stack, right):
    load_left(own, other, replica_of(), left, stack, gram)
    rows = fixed.shape[0]

    def step(i, _):
        at = pl.ds(pl.multiple_of(i * TILE, TILE), TILE)
        both = lax.dot_general(stack[...], fixed[at, :], NT, preferred_element_type=F32)
        right[:, at] = both[:RANK] + both[RANK:]
        return 0

    lax.fori_loop(0, rows // TILE, step, 0)
    halve(right, core_of(), keep, give)


def right_call(kernel, own, other, fixed, out_width):
    width = own.shape[1]
    half = RANK // 2
    return pl.pallas_call(
        kernel,
        out_shape=(
            pltpu.VMEM((half, out_width), F32),
            pltpu.VMEM((half, out_width), F32),
            pltpu.VMEM((RANK, RANK), F32),
            pltpu.VMEM((RANK, width), F32),
        ),
        in_specs=[VMEM, VMEM, VMEM],
        out_specs=(VMEM, VMEM, VMEM, VMEM),
        scratch_shapes=[pltpu.VMEM((2 * RANK, width), BF16), pltpu.VMEM((RANK, out_width), F32)],
        compiler_params=params(8),
        cost_estimate=cost(4),
    )(*in_vmem(own, other, fixed))


def solve_kernel(place_of, n, *refs):
    left, out = refs[n:]
    a = refs[0][...]
    for ref in refs[1:n]:
        a += ref[...]
    row_at = lax.broadcasted_iota(jnp.int32, (RANK, RANK), 0)
    col_at = lax.broadcasted_iota(jnp.int32, (RANK, RANK), 1)
    lane = lax.broadcasted_iota(jnp.int32, (1, RANK), 1)
    for k in range(RANK):
        col = jnp.broadcast_to(a[:, k : k + 1], (RANK, RANK))
        row = jnp.where(lane == k, 1.0, a[k : k + 1, :]) * (1.0 / col[k : k + 1, :])
        rest = jnp.where((row_at == k) | (col_at == k), 0.0, a)
        a = rest - jnp.where(row_at == k, -1.0, col) * row
    half = RANK // 2
    turned = jnp.concatenate([a[half:], a[:half]], axis=0)
    a = jnp.where(place_of() == 0, a, turned) * (1.0 / REPLICAS)
    out[...] = jnp.dot(a, left[...], preferred_element_type=F32, precision=lax.Precision.HIGHEST)


def solve_call(place_of, grams, left):
    n = len(grams)
    return pl.pallas_call(
        functools.partial(solve_kernel, place_of, n),
        out_shape=pltpu.VMEM(left.shape, F32),
        in_specs=[VMEM] * (n + 1),
        out_specs=VMEM,
        compiler_params=params(4),
        cost_estimate=cost(6),
    )(*in_vmem(*grams, left))


def rebuild_kernel(n_row, *refs):
    row_refs, col_refs = refs[:n_row], refs[n_row:3]
    fixed, update, new_error, row_stack, col_stack = refs[3:]
    for sources, stack, order in ((row_refs, row_stack, (0, 1, 0, 1)), (col_refs, col_stack, (0, 0, 1, 1))):
        at = 0
        for ref in sources:
            parts = parts_of(ref[...])
            n = ref.shape[0]
            for k, which in enumerate(order):
                stack[k * RANK + at : k * RANK + at + n, :] = parts[which]
            at += n
    rows, cols = fixed.shape
    tiles = rows // REPLICAS // TILE
    first = replica_of() * tiles

    def tile_of(i):
        return lax.rem(first + i, REPLICAS * tiles)

    def step(u, e):
        i = pl.program_id(0)
        at = pl.ds(pl.multiple_of(tile_of(i) * TILE, TILE), TILE)

        def tile(with_update):
            row = row_stack[:, at].T
            for j in range(0, cols, TILE):
                here = slice(j, j + TILE)
                value = jnp.dot(row, col_stack[:, here], preferred_element_type=F32)
                e[:, here] = (fixed[at, here].astype(F32) - value).astype(BF16)
                if with_update:
                    u[:, here] = value.astype(BF16)

        pl.when(i < tiles)(lambda: tile(True))
        pl.when(i >= tiles)(lambda: tile(False))

    block = (TILE, cols)
    pltpu.emit_pipeline(
        step,
        grid=(REPLICAS * tiles,),
        out_specs=[
            pl.BlockSpec(block, lambda i: (jnp.minimum(i, tiles - 1), 0)),
            pl.BlockSpec(block, lambda i: (tile_of(i), 0)),
        ],
    )(update, new_error)


def rebuild_call(rows_in, cols_in, fixed):
    rows, cols = fixed.shape
    return pl.pallas_call(
        functools.partial(rebuild_kernel, len(rows_in)),
        out_shape=(
            pltpu.HBM((rows // REPLICAS, cols), BF16),
            pltpu.HBM((rows, cols), BF16),
        ),
        in_specs=[VMEM] * 4,
        out_specs=(HBM, HBM),
        scratch_shapes=[pltpu.VMEM((4 * RANK, rows), BF16), pltpu.VMEM((4 * RANK, cols), BF16)],
        compiler_params=params(12),
        cost_estimate=cost(6),
    )(*in_vmem(*rows_in, *cols_in, fixed))


def local(grad_gate, grad_down, error_gate, error_down, start_gate, start_down):
    slab, width = grad_gate.shape
    n_dp, n_t = lax.axis_size("dp"), lax.axis_size("tensor")

    fixed_down, *down = left_call(down_left_kernel, grad_down, error_down, start_down, HBM, width)
    fixed_gate, *gate = left_call(gate_left_kernel, grad_gate, error_gate, start_gate, VMEM, slab)

    *down, gram_down, left_down = right_call(down_right_kernel, *sum_cols(*down), fixed_down, slab)
    *gate, gram_gate, left_gate = right_call(gate_right_kernel, *sum_rows(*gate), fixed_gate, width)

    grams_down = [gram_down] + [
        exchange(gram_down, lambda d, t, b=b: (d, t ^ b)) for b in range(1, n_t)
    ]
    grams_gate = [gram_gate] + [
        exchange(gram_gate, lambda d, t, b=b: (d ^ b, t)) for b in range(REPLICAS, n_dp, REPLICAS)
    ]
    down_cols = solve_call(core_of, grams_down, left_down)
    gate_rows = solve_call(replica_of, grams_gate, left_gate)

    update_down, new_error_down = rebuild_call(sum_rows(*down), [down_cols], fixed_down)
    update_gate, new_error_gate = rebuild_call([gate_rows], sum_cols(*gate), fixed_gate)
    return (update_gate, update_down, new_error_gate, new_error_down)


def solution(mesh):
    split = P(("mix", "dp"), "tensor")
    in_specs = (split, split, split, split, P(None, "tensor"), P())
    out_specs = (split, split, split, split)

    def run(grad_gate, *rest):
        groups = mesh.shape["mix"] * mesh.shape["dp"]
        slab = grad_gate.shape[0] // groups
        width = grad_gate.shape[1] // mesh.shape["tensor"]
        fits = slab % (REPLICAS * TILE) == 0 and width % TILE == 0
        body = local if fits else local_plain
        return jax.shard_map(
            body, mesh=mesh, in_specs=in_specs, out_specs=out_specs, check_vma=False
        )(grad_gate, *rest)

    return run
```

time: 135 us -> 97.1 us (0.72)
  Pallas kernels: 78.3 us -> 55.3 us
  local copies, waits for them, and re-layouts: 12.2 us -> 0.01 us
  waiting for transfers between devices: 24.6 us -> 22.7 us
    pallas_call x8 -> x18, Pallas kernels: 78.3 us -> 55.3 us  [the longest x2 17.5 us: left_call(): pl.pallas_call(kernel, out_shape=(pltpu.VMEM((rows, cols), BF16), pltpu.V...]
    unnamed x30 -> x2, local copies, waits for them, and re-layouts: 12 us -> 0.01 us
    ppermute x17 -> x18, waiting for transfers between devices: 24.6 us -> 22.7 us  [exchange(): return lax.ppermute(x, ('dp', 'tensor'), pairs)]
    ppermute x17 -> x18, starting transfers between devices: 18.1 us -> 17.5 us  [exchange(): return lax.ppermute(x, ('dp', 'tensor'), pairs)]
  transfers between devices with their start and end apart: 17 -> 18, of which waited for: 7 -> 5; matrix products, arithmetic and copies ran while one was open for 0% -> 0% of each run, Pallas kernels for 37% -> 39%
where the time goes in v3:
time: 97.1 us; the launch traced here: 96.4 us
  Pallas kernels  55.3 us (57%)
  waiting for transfers between devices  22.7 us (23%)
  starting transfers between devices  17.5 us (18%)
    ppermute x18, waiting for transfers between devices, exchange(): return lax.ppermute(x, ('dp', 'tensor'), pairs)  22.7 us
    ppermute x18, starting transfers between devices, exchange(): return lax.ppermute(x, ('dp', 'tensor'), pairs)  17.5 us
    pallas_call x2, Pallas kernels, left_call(): pl.pallas_call(kernel, out_shape=(pltpu.VMEM((rows, cols), BF16), pltpu.V...  17.5 us
    pallas_call x2, Pallas kernels, rebuild_call(): pl.pallas_call(functools.partial(rebuild_kernel, len(rows_in)), out_shape...  17.2 us
    pallas_call x2, Pallas kernels, solve_call(): pl.pallas_call(functools.partial(solve_kernel, place_of, n), out_shape=pl...  11.8 us
    pallas_call x2, Pallas kernels, right_call(): pl.pallas_call(kernel, out_shape=(pltpu.VMEM((half, out_width), F32), plt...  8.45 us
  transfers between devices with their start and end apart: 18, of which 5 were waited for; matrix products, arithmetic and copies ran while one was open for 0% of the time, Pallas kernels for 39%

profile of v3, /device:TPU:0, one launch (start us, length us, event | category | flops | bytes accessed | tf_op | source)
XLA Modules:
  0.0 96.4 jit_solution(17191122108709316042)
XLA Ops:
  0.6 9.3 %shard_map.102 = (bf16[2560,1792]{1,0:T(8,128)(2,1)S(1)}, f32[32,1792]{1,0:T(8,128)S(1)}, f32[32,1792]{1,0:T(8,128)S(1)}) custom-call(bf16[2560,1792]{1,0:T(8,128)(2,1)} %grad.3, bf16[2560,1792]{1,0:T(8,128)(2,1)} %error.3, bf16[64,5120]{1,0:T(8,128)(2,1)} %start.3), custom_call_target="tpu_custom_call" | custom-call | flops 7699999744 | tf_op jit(solution)/shard_map/pallas_call | solution.py:214
  10.0 3.1 %collective-permute-start.8 = (f32[32,1792]{1,0:T(8,128)S(1)}, f32[32,1792]{1,0:T(8,128)S(1)}, u32[]{:S(2)}, u32[]{:S(2)}) collective-permute-start(f32[32,1792]{1,0:T(8,128)S(1)} %get-tuple-element.31), channel_id=1, source_target_pairs={{0,4},{1,5},{2,6},{3,7},{4,0},{5,1},{6,2},{7,3},{8,12},{9,13},{10,... | collective-permute-start | bytes 688136 | tf_op jit(solution)/shard_map/ppermute | solution.py:95
  13.1 8.1 %shard_map.93 = (bf16[2560,1792]{1,0:T(8,128)(2,1)S(1)}, f32[32,2560]{1,0:T(8,128)S(1)}, f32[32,2560]{1,0:T(8,128)S(1)}) custom-call(bf16[2560,1792]{1,0:T(8,128)(2,1)} %grad.2, bf16[2560,1792]{1,0:T(8,128)(2,1)} %error.2, bf16[64,1792]{1,0:T(8,128)(2,1)S(1)} %copy-done), custom_call_target="tpu_custom_call" | custom-call | flops 7699999744 | tf_op jit(solution)/shard_map/pallas_call | solution.py:214
  21.4 2.6 %collective-permute-start.9 = (f32[32,1792]{1,0:T(8,128)S(1)}, f32[32,1792]{1,0:T(8,128)S(1)}, u32[]{:S(2)}, u32[]{:S(2)}) collective-permute-start(f32[32,1792]{1,0:T(8,128)S(1)} %shard_map.103.x), channel_id=1, source_target_pairs={{0,8},{1,9},{2,10},{3,11},{4,12},{5,13},{6,14},{7,15},{8,0},{9,1},... | collective-permute-start | bytes 688136 | tf_op jit(solution)/shard_map/ppermute | solution.py:95
  24.1 1.6 %collective-permute-start.1 = (f32[32,2560]{1,0:T(8,128)S(1)}, f32[32,2560]{1,0:T(8,128)S(1)}, u32[]{:S(2)}, u32[]{:S(2)}) collective-permute-start(f32[32,2560]{1,0:T(8,128)S(1)} %shard_map.94.x), channel_id=1, source_target_pairs={{0,2},{1,5},{2,0},{3,7},{4,6},{5,1},{6,4},{7,3},{8,10},{9,13},{10,... | collective-permute-start | bytes 983048 | tf_op jit(solution)/shard_map/ppermute | solution.py:95
  25.6 9.6 %collective-permute-done.9.y = f32[32,1792]{1,0:T(8,128)S(1)} collective-permute-done((f32[32,1792]{1,0:T(8,128)S(1)}, f32[32,1792]{1,0:T(8,128)S(1)}, u32[]{:S(2)}, u32[]{:S(2)}) %collective-permute-start.9) | collective-permute-done | bytes 229408 | tf_op jit(solution)/shard_map/ppermute | solution.py:95
  35.3 2.1 %collective-permute-start.2 = (f32[32,2560]{1,0:T(8,128)S(1)}, f32[32,2560]{1,0:T(8,128)S(1)}, u32[]{:S(2)}, u32[]{:S(2)}) collective-permute-start(f32[32,2560]{1,0:T(8,128)S(1)} %shard_map.95.x), channel_id=1, source_target_pairs={{0,4},{1,3},{2,6},{3,1},{4,0},{5,7},{6,2},{7,5},{8,12},{9,11},{10,... | collective-permute-start | bytes 983048 | tf_op jit(solution)/shard_map/ppermute | solution.py:95
  37.4 5.4 %collective-permute-done.10.other = f32[32,1792]{1,0:T(8,128)S(1)} collective-permute-done((f32[32,1792]{1,0:T(8,128)S(1)}, f32[32,1792]{1,0:T(8,128)S(1)}, u32[]{:S(2)}, u32[]{:S(2)}) %collective-permute-start.10) | collective-permute-done | bytes 229408 | tf_op jit(solution)/shard_map/ppermute | solution.py:95
  42.8 5.2 %shard_map.105 = (f32[32,2560]{1,0:T(8,128)S(1)}, f32[32,2560]{1,0:T(8,128)S(1)}, f32[64,64]{1,0:T(8,128)S(1)}, f32[64,1792]{1,0:T(8,128)S(1)}) custom-call(f32[32,1792]{1,0:T(8,128)S(1)} %shard_map.104.own, f32[32,1792]{1,0:T(8,128)S(1)} %collective-permute-done.10.other, bf16[2560,1792]{1,0:T(8,128)(2,1)S(1)} %get-tuple-element.32.fixed.refs_3_), custom_call_target="tpu_custom_call" | custom-call | flops 4400000000 | tf_op jit(solution)/shard_map/pallas_call | solution.py:272
  48.1 0.5 collective-permute-start.3
  48.7 1.2 %collective-permute-start.17 = (f32[64,64]{1,0:T(8,128)S(1)}, f32[64,64]{1,0:T(8,128)S(1)}, u32[]{:S(2)}, u32[]{:S(2)}) collective-permute-start(f32[64,64]{1,0:T(8,128)S(1)} %get-tuple-element.35.refs_0_), channel_id=1, source_target_pairs={{0,3},{1,2},{2,1},{3,0},{4,7},{5,6},{6,5},{7,4},{8,11},{9,10},{10,... | collective-permute-start | bytes 49160 | tf_op jit(solution)/shard_map/ppermute | solution.py:95
  49.9 0.5 collective-permute-start.16
  50.6 1.6 %collective-permute-start.12 = (f32[32,2560]{1,0:T(8,128)S(1)}, f32[32,2560]{1,0:T(8,128)S(1)}, u32[]{:S(2)}, u32[]{:S(2)}) collective-permute-start(f32[32,2560]{1,0:T(8,128)S(1)} %shard_map.106.x), channel_id=1, source_target_pairs={{0,2},{1,5},{2,0},{3,7},{4,6},{5,1},{6,4},{7,3},{8,10},{9,13},{10,... | collective-permute-start | bytes 983048 | tf_op jit(solution)/shard_map/ppermute | solution.py:95
  52.2 3.2 %shard_map.97 = (f32[32,1792]{1,0:T(8,128)S(1)}, f32[32,1792]{1,0:T(8,128)S(1)}, f32[64,64]{1,0:T(8,128)S(1)}, f32[64,2560]{1,0:T(8,128)S(1)}) custom-call(f32[32,2560]{1,0:T(8,128)S(1)} %shard_map.96.own, f32[32,2560]{1,0:T(8,128)S(1)} %collective-permute-done.3.other, bf16[2560,1792]{1,0:T(8,128)(2,1)S(1)} %get-tuple-element.24.fixed.refs_3_), custom_call_target="tpu_custom_call" | custom-call | flops 4400000000 | tf_op jit(solution)/shard_map/pallas_call | solution.py:272
  55.5 0.4 collective-permute-start.5
  55.8 1.9 %collective-permute-done.12.y = f32[32,2560]{1,0:T(8,128)S(1)} collective-permute-done((f32[32,2560]{1,0:T(8,128)S(1)}, f32[32,2560]{1,0:T(8,128)S(1)}, u32[]{:S(2)}, u32[]{:S(2)}) %collective-permute-start.12) | collective-permute-done | bytes 327712 | tf_op jit(solution)/shard_map/ppermute | solution.py:95
  58.1 5.9 %shard_map.109.refs_2_ = f32[64,1792]{1,0:T(8,128)S(1)} custom-call(f32[64,64]{1,0:T(8,128)S(1)} %get-tuple-element.35.refs_0_, f32[64,64]{1,0:T(8,128)S(1)} %collective-permute-done.15.refs_1_, f32[64,64]{1,0:T(8,128)S(1)} %collective-permute-done.16.refs_2_, f32[64,64]{1,0:T(8,128)S(1)} %collective-permute-done.17.refs_3_, ...), custom_call_target="tpu_custom_call" | custom-call | flops 6600000000 | tf_op jit(solution)/shard_map/pallas_call | solution.py:309
  64.0 2.6 %collective-permute-start.4 = (f32[64,64]{1,0:T(8,128)S(1)}, f32[64,64]{1,0:T(8,128)S(1)}, u32[]{:S(2)}, u32[]{:S(2)}) collective-permute-start(f32[64,64]{1,0:T(8,128)S(1)} %get-tuple-element.25.refs_0_), channel_id=1, source_target_pairs={{0,8},{1,9},{2,10},{3,11},{4,12},{5,13},{6,14},{7,15},{8,0},{9,1},... | collective-permute-start | bytes 49160 | tf_op jit(solution)/shard_map/ppermute | solution.py:95
  66.6 0.5 collective-permute-start.6
  67.2 1.7 %collective-permute-done.4.refs_1_ = f32[64,64]{1,0:T(8,128)S(1)} collective-permute-done((f32[64,64]{1,0:T(8,128)S(1)}, f32[64,64]{1,0:T(8,128)S(1)}, u32[]{:S(2)}, u32[]{:S(2)}) %collective-permute-start.4) | collective-permute-done | bytes 16416 | tf_op jit(solution)/shard_map/ppermute | solution.py:95
  68.9 6.0 %shard_map.98.refs_0_ = f32[64,2560]{1,0:T(8,128)S(1)} custom-call(f32[64,64]{1,0:T(8,128)S(1)} %get-tuple-element.25.refs_0_, f32[64,64]{1,0:T(8,128)S(1)} %collective-permute-done.4.refs_1_, f32[64,2560]{1,0:T(8,128)S(1)} %get-tuple-element.26.refs_2_), custom_call_target="tpu_custom_call" | custom-call | flops 6600000000 | tf_op jit(solution)/shard_map/pallas_call | solution.py:309
  74.9 4.2 %collective-permute-done.6.y = f32[32,1792]{1,0:T(8,128)S(1)} collective-permute-done((f32[32,1792]{1,0:T(8,128)S(1)}, f32[32,1792]{1,0:T(8,128)S(1)}, u32[]{:S(2)}, u32[]{:S(2)}) %collective-permute-start.6) | collective-permute-done | bytes 229408 | tf_op jit(solution)/shard_map/ppermute | solution.py:95
  79.2 8.6 %shard_map.110 = (bf16[1280,1792]{1,0:T(8,128)(2,1)}, bf16[2560,1792]{1,0:T(8,128)(2,1)}) custom-call(f32[32,2560]{1,0:T(8,128)S(1)} %shard_map.108.refs_0_, f32[32,2560]{1,0:T(8,128)S(1)} %collective-permute-done.14.refs_1_, f32[64,1792]{1,0:T(8,128)S(1)} %shard_map.109.refs_2_, bf16[2560,1792]{1,0:T(8,128)(2,1)S(1)} %get-tuple-element.32.fixed.refs_3_), custom_call_target="tpu_custom_call" | custom-call | flops 6600000000 | tf_op jit(solution)/shard_map/pallas_call | solution.py:366
  87.8 8.6 %shard_map.101 = (bf16[1280,1792]{1,0:T(8,128)(2,1)}, bf16[2560,1792]{1,0:T(8,128)(2,1)}) custom-call(f32[64,2560]{1,0:T(8,128)S(1)} %shard_map.98.refs_0_, f32[32,1792]{1,0:T(8,128)S(1)} %shard_map.100.refs_1_, f32[32,1792]{1,0:T(8,128)S(1)} %collective-permute-done.7.refs_2_, bf16[2560,1792]{1,0:T(8,128)(2,1)S(1)} %get-tuple-element.24.fixed.refs_3_), custom_call_target="tpu_custom_call" | custom-call | flops 6600000000 | tf_op jit(solution)/shard_map/pallas_call | solution.py:366
  (32 shorter events, 1.2 us)
Async XLA Ops:
  0.6 12.5 %copy-start = (bf16[64,1792]{1,0:T(8,128)(2,1)S(1)}, bf16[64,1792]{1,0:T(8,128)(2,1)}, u32[]{:S(2)}) copy-start(bf16[64,1792]{1,0:T(8,128)(2,1)} %start.2) | copy-start | bytes 688132
  10.0 11.3 %collective-permute-start.8 = (f32[32,1792]{1,0:T(8,128)S(1)}, f32[32,1792]{1,0:T(8,128)S(1)}, u32[]{:S(2)}, u32[]{:S(2)}) collective-permute-start(f32[32,1792]{1,0:T(8,128)S(1)} %get-tuple-element.31), channel_id=1, source_target_pairs={{0,4},{1,5},{2,6},{3,7},{4,0},{5,1},{6,2},{7,3},{8,12},{9,13},{10,... | collective-permute-start | bytes 688136 | tf_op jit(solution)/shard_map/ppermute | solution.py:95
  21.2 2.8 %collective-permute-start = (f32[32,2560]{1,0:T(8,128)S(1)}, f32[32,2560]{1,0:T(8,128)S(1)}, u32[]{:S(2)}, u32[]{:S(2)}) collective-permute-start(f32[32,2560]{1,0:T(8,128)S(1)} %get-tuple-element.23), channel_id=1, source_target_pairs={{0,1},{1,0},{2,3},{3,2},{4,5},{5,4},{6,7},{7,6},{8,9},{9,8},{10,11... | collective-permute-start | bytes 983048 | tf_op jit(solution)/shard_map/ppermute | solution.py:95
  21.4 13.8 %collective-permute-start.9 = (f32[32,1792]{1,0:T(8,128)S(1)}, f32[32,1792]{1,0:T(8,128)S(1)}, u32[]{:S(2)}, u32[]{:S(2)}) collective-permute-start(f32[32,1792]{1,0:T(8,128)S(1)} %shard_map.103.x), channel_id=1, source_target_pairs={{0,8},{1,9},{2,10},{3,11},{4,12},{5,13},{6,14},{7,15},{8,0},{9,1},... | collective-permute-start | bytes 688136 | tf_op jit(solution)/shard_map/ppermute | solution.py:95
  24.1 11.2 %collective-permute-start.1 = (f32[32,2560]{1,0:T(8,128)S(1)}, f32[32,2560]{1,0:T(8,128)S(1)}, u32[]{:S(2)}, u32[]{:S(2)}) collective-permute-start(f32[32,2560]{1,0:T(8,128)S(1)} %shard_map.94.x), channel_id=1, source_target_pairs={{0,2},{1,5},{2,0},{3,7},{4,6},{5,1},{6,4},{7,3},{8,10},{9,13},{10,... | collective-permute-start | bytes 983048 | tf_op jit(solution)/shard_map/ppermute | solution.py:95
  35.2 7.6 %collective-permute-start.10 = (f32[32,1792]{1,0:T(8,128)S(1)}, f32[32,1792]{1,0:T(8,128)S(1)}, u32[]{:S(2)}, u32[]{:S(2)}) collective-permute-start(f32[32,1792]{1,0:T(8,128)S(1)} %shard_map.104.own), channel_id=1, source_target_pairs={{0,4},{1,5},{2,6},{3,7},{4,0},{5,1},{6,2},{7,3},{8,12},{9,13},{10,... | collective-permute-start | bytes 688136 | tf_op jit(solution)/shard_map/ppermute | solution.py:95
  35.3 12.7 %collective-permute-start.2 = (f32[32,2560]{1,0:T(8,128)S(1)}, f32[32,2560]{1,0:T(8,128)S(1)}, u32[]{:S(2)}, u32[]{:S(2)}) collective-permute-start(f32[32,2560]{1,0:T(8,128)S(1)} %shard_map.95.x), channel_id=1, source_target_pairs={{0,4},{1,3},{2,6},{3,1},{4,0},{5,7},{6,2},{7,5},{8,12},{9,11},{10,... | collective-permute-start | bytes 983048 | tf_op jit(solution)/shard_map/ppermute | solution.py:95
  48.0 2.6 %collective-permute-start.11 = (f32[32,2560]{1,0:T(8,128)S(1)}, f32[32,2560]{1,0:T(8,128)S(1)}, u32[]{:S(2)}, u32[]{:S(2)}) collective-permute-start(f32[32,2560]{1,0:T(8,128)S(1)} %get-tuple-element.34), channel_id=1, source_target_pairs={{0,1},{1,0},{2,3},{3,2},{4,5},{5,4},{6,7},{7,6},{8,9},{9,8},{10,11... | collective-permute-start | bytes 983048 | tf_op jit(solution)/shard_map/ppermute | solution.py:95
  48.1 4.1 %collective-permute-start.3 = (f32[32,2560]{1,0:T(8,128)S(1)}, f32[32,2560]{1,0:T(8,128)S(1)}, u32[]{:S(2)}, u32[]{:S(2)}) collective-permute-start(f32[32,2560]{1,0:T(8,128)S(1)} %shard_map.96.own), channel_id=1, source_target_pairs={{0,1},{1,0},{2,3},{3,2},{4,5},{5,4},{6,7},{7,6},{8,9},{9,8},{10,11... | collective-permute-start | bytes 983048 | tf_op jit(solution)/shard_map/ppermute | solution.py:95
  48.7 9.4 %collective-permute-start.17 = (f32[64,64]{1,0:T(8,128)S(1)}, f32[64,64]{1,0:T(8,128)S(1)}, u32[]{:S(2)}, u32[]{:S(2)}) collective-permute-start(f32[64,64]{1,0:T(8,128)S(1)} %get-tuple-element.35.refs_0_), channel_id=1, source_target_pairs={{0,3},{1,2},{2,1},{3,0},{4,7},{5,6},{6,5},{7,4},{8,11},{9,10},{10,... | collective-permute-start | bytes 49160 | tf_op jit(solution)/shard_map/ppermute | solution.py:95
  49.9 8.2 %collective-permute-start.16 = (f32[64,64]{1,0:T(8,128)S(1)}, f32[64,64]{1,0:T(8,128)S(1)}, u32[]{:S(2)}, u32[]{:S(2)}) collective-permute-start(f32[64,64]{1,0:T(8,128)S(1)} %get-tuple-element.35.refs_0_), channel_id=1, source_target_pairs={{0,2},{1,3},{2,0},{3,1},{4,6},{5,7},{6,4},{7,5},{8,10},{9,11},{10,... | collective-permute-start | bytes 49160 | tf_op jit(solution)/shard_map/ppermute | solution.py:95
  50.4 7.7 %collective-permute-start.15 = (f32[64,64]{1,0:T(8,128)S(1)}, f32[64,64]{1,0:T(8,128)S(1)}, u32[]{:S(2)}, u32[]{:S(2)}) collective-permute-start(f32[64,64]{1,0:T(8,128)S(1)} %get-tuple-element.35.refs_0_), channel_id=1, source_target_pairs={{0,1},{1,0},{2,3},{3,2},{4,5},{5,4},{6,7},{7,6},{8,9},{9,8},{10,11... | collective-permute-start | bytes 49160 | tf_op jit(solution)/shard_map/ppermute | solution.py:95
  50.6 7.1 %collective-permute-start.12 = (f32[32,2560]{1,0:T(8,128)S(1)}, f32[32,2560]{1,0:T(8,128)S(1)}, u32[]{:S(2)}, u32[]{:S(2)}) collective-permute-start(f32[32,2560]{1,0:T(8,128)S(1)} %shard_map.106.x), channel_id=1, source_target_pairs={{0,2},{1,5},{2,0},{3,7},{4,6},{5,1},{6,4},{7,3},{8,10},{9,13},{10,... | collective-permute-start | bytes 983048 | tf_op jit(solution)/shard_map/ppermute | solution.py:95
  55.5 11.1 %collective-permute-start.5 = (f32[32,1792]{1,0:T(8,128)S(1)}, f32[32,1792]{1,0:T(8,128)S(1)}, u32[]{:S(2)}, u32[]{:S(2)}) collective-permute-start(f32[32,1792]{1,0:T(8,128)S(1)} %get-tuple-element.28), channel_id=1, source_target_pairs={{0,4},{1,5},{2,6},{3,7},{4,0},{5,1},{6,2},{7,3},{8,12},{9,13},{10,... | collective-permute-start | bytes 688136 | tf_op jit(solution)/shard_map/ppermute | solution.py:95
  57.8 9.3 %collective-permute-start.13 = (f32[32,2560]{1,0:T(8,128)S(1)}, f32[32,2560]{1,0:T(8,128)S(1)}, u32[]{:S(2)}, u32[]{:S(2)}) collective-permute-start(f32[32,2560]{1,0:T(8,128)S(1)} %shard_map.107.x), channel_id=1, source_target_pairs={{0,4},{1,3},{2,6},{3,1},{4,0},{5,7},{6,2},{7,5},{8,12},{9,11},{10,... | collective-permute-start | bytes 983048 | tf_op jit(solution)/shard_map/ppermute | solution.py:95
  64.0 4.9 %collective-permute-start.4 = (f32[64,64]{1,0:T(8,128)S(1)}, f32[64,64]{1,0:T(8,128)S(1)}, u32[]{:S(2)}, u32[]{:S(2)}) collective-permute-start(f32[64,64]{1,0:T(8,128)S(1)} %get-tuple-element.25.refs_0_), channel_id=1, source_target_pairs={{0,8},{1,9},{2,10},{3,11},{4,12},{5,13},{6,14},{7,15},{8,0},{9,1},... | collective-permute-start | bytes 49160 | tf_op jit(solution)/shard_map/ppermute | solution.py:95
  66.6 12.4 %collective-permute-start.6 = (f32[32,1792]{1,0:T(8,128)S(1)}, f32[32,1792]{1,0:T(8,128)S(1)}, u32[]{:S(2)}, u32[]{:S(2)}) collective-permute-start(f32[32,1792]{1,0:T(8,128)S(1)} %shard_map.99.x), channel_id=1, source_target_pairs={{0,8},{1,9},{2,10},{3,11},{4,12},{5,13},{6,14},{7,15},{8,0},{9,1},... | collective-permute-start | bytes 688136 | tf_op jit(solution)/shard_map/ppermute | solution.py:95
  67.1 12.0 %collective-permute-start.14 = (f32[32,2560]{1,0:T(8,128)S(1)}, f32[32,2560]{1,0:T(8,128)S(1)}, u32[]{:S(2)}, u32[]{:S(2)}) collective-permute-start(f32[32,2560]{1,0:T(8,128)S(1)} %shard_map.108.refs_0_), channel_id=1, source_target_pairs={{0,1},{1,0},{2,3},{3,2},{4,5},{5,4},{6,7},{7,6},{8,9},{9,8},{10,11... | collective-permute-start | bytes 983048 | tf_op jit(solution)/shard_map/ppermute | solution.py:95
  79.1 8.7 %collective-permute-start.7 = (f32[32,1792]{1,0:T(8,128)S(1)}, f32[32,1792]{1,0:T(8,128)S(1)}, u32[]{:S(2)}, u32[]{:S(2)}) collective-permute-start(f32[32,1792]{1,0:T(8,128)S(1)} %shard_map.100.refs_1_), channel_id=1, source_target_pairs={{0,4},{1,5},{2,6},{3,7},{4,0},{5,1},{6,2},{7,3},{8,12},{9,13},{10,... | collective-permute-start | bytes 688136 | tf_op jit(solution)/shard_map/ppermute | solution.py:95

commit v4 on v0

v4 whole, which is shorter than its diff:
```python
import functools

import jax
import jax.numpy as jnp
from jax import lax
from jax.experimental import pallas as pl
from jax.experimental.pallas import tpu as pltpu
from jax.sharding import PartitionSpec as P

REPLICAS = 2
RANK = 64
TILE = 256
FLOPS = 1.15e9
WEIGHTS = (8.0, 8.0, 1.0, 1.0, 1.0, 1.0, 1.0, 4.0, 4.0, 1.0, 1.0, 1.0, 6.0, 1.0, 1.0, 8.0, 8.0)
MIB = 1 << 20
BF16 = jnp.bfloat16
F32 = jnp.float32

NN = (((1,), (0,)), ((), ()))
NT = (((1,), (1,)), ((), ()))
TN = (((0,), (0,)), ((), ()))


def from_partner(shard, axis, stride):
    return lax.ppermute(shard, axis, [(i, i ^ 1 << stride) for i in range(lax.axis_size(axis))])


def corrected(grad, error):
    return (grad.astype(F32) + error.astype(F32)).astype(BF16)


def transposed(matrix, ortho):
    return lax.dot_general(matrix, ortho.astype(BF16), TN, preferred_element_type=F32)


def gram_of(left):
    return jnp.dot(left.T, left, precision=lax.Precision.HIGHEST)


def factored(left, inner):
    lower = jnp.linalg.cholesky(inner)
    return lax.linalg.triangular_solve(lower, left, left_side=False, lower=True, transpose_a=True)


def local_plain(grad_gate, grad_down, error_gate, error_down, start_gate, start_down):
    high = lax.Precision.HIGHEST
    dp_place = lax.axis_index("dp")
    block = dp_place // REPLICAS
    replica = dp_place % REPLICAS
    fixed_gate = corrected(grad_gate, error_gate)
    fixed_down = corrected(grad_down, error_down)
    slab = fixed_gate.shape[0]
    cols_down = lax.dynamic_slice_in_dim(start_down, block * slab, slab, 1)
    left_gate = lax.dot_general(fixed_gate, start_gate, NT, preferred_element_type=F32)
    left_down = lax.dot_general(
        fixed_down, cols_down, (((0,), (1,)), ((), ())), preferred_element_type=F32
    )
    left_gate = lax.psum(left_gate, "tensor")
    left_gate = left_gate + from_partner(left_gate, "dp", 0)
    left_down = lax.psum(left_down, "dp")
    keep_gate = (replica == 0).astype(F32)
    inner_gate = lax.psum(gram_of(left_gate) * keep_gate, "dp")
    inner_down = lax.psum(gram_of(left_down), "tensor")
    ortho_gate = factored(left_gate, inner_gate)
    ortho_down = factored(left_down, inner_down)
    right_gate = transposed(fixed_gate, ortho_gate)
    right_gate = lax.psum(right_gate, "dp") / REPLICAS
    right_down = jnp.dot(fixed_down, ortho_down.astype(BF16), preferred_element_type=F32)
    right_down = lax.psum(right_down, "tensor")
    right_down = right_down + from_partner(right_down, "dp", 0)
    right_down = right_down / REPLICAS
    rebuilt_gate = jnp.dot(ortho_gate, right_gate.T, precision=high)
    rebuilt_down = jnp.dot(right_down, ortho_down.T, precision=high)
    share = slab // REPLICAS
    update_gate = lax.dynamic_slice_in_dim(rebuilt_gate, replica * share, share, 0).astype(BF16)
    update_down = lax.dynamic_slice_in_dim(rebuilt_down, replica * share, share, 0).astype(BF16)
    new_error_gate = (fixed_gate.astype(F32) - rebuilt_gate).astype(BF16)
    new_error_down = (fixed_down.astype(F32) - rebuilt_down).astype(BF16)
    return (update_gate, update_down, new_error_gate, new_error_down)


def core_of():
    return lax.rem(lax.axis_index("tensor"), 2)


def replica_of():
    return lax.rem(lax.axis_index("dp"), REPLICAS)


def exchange(x, partner):
    n_dp, n_t = lax.axis_size("dp"), lax.axis_size("tensor")
    pairs = []
    for d in range(n_dp):
        for t in range(n_t):
            to_d, to_t = partner(d, t)
            pairs.append((d * n_t + t, to_d * n_t + to_t))
    return lax.ppermute(x, ("dp", "tensor"), pairs)


def bits(n, low):
    out, b = [], low
    while b < n:
        out.append(b)
        b *= 2
    return out


def row_steps():
    steps = [(0, b) for b in bits(lax.axis_size("tensor"), 2)] + [(1, 0)]

    def partner(i, d, t):
        r, b = steps[i] if t % 2 == 0 else steps[-1 - i]
        return d ^ r, t ^ b

    return [functools.partial(partner, i) for i in range(len(steps))]


def col_steps():
    return [lambda d, t, b=b: (d ^ b, t) for b in bits(lax.axis_size("dp"), REPLICAS)]


def other_core(d, t):
    return d, t ^ 1


def other_replica(d, t):
    return d ^ 1, t


VMEM = pl.BlockSpec(memory_space=pltpu.VMEM)
HBM = pl.BlockSpec(memory_space=pltpu.HBM)
ANY = pl.BlockSpec(memory_space=pl.ANY)
HALF = RANK // 2


class Order:
    def __init__(self):
        self.token = None
        self.calls = 0

    def __call__(self, kernel, args, outs, scratch=(), mib=8, aliases=None):
        args = list(args)
        n_in, n_tok = len(args), 0 if self.token is None else 1
        operands = [
            pltpu.with_memory_space_constraint(x, pltpu.VMEM if spec is VMEM else pltpu.HBM)
            for x, spec in args
        ]
        specs = [spec for _, spec in args]
        if n_tok:
            operands.append(self.token)
            specs.append(ANY)

        def body(*refs):
            kernel(*refs[:n_in], *refs[n_in + n_tok :])

        out = pl.pallas_call(
            body,
            out_shape=tuple(
                (pltpu.VMEM if spec is VMEM else pltpu.HBM)(shape, kind) for shape, kind, spec in outs
            ),
            in_specs=specs,
            out_specs=tuple(spec for *_, spec in outs),
            scratch_shapes=list(scratch),
            input_output_aliases=aliases or {},
            compiler_params=pltpu.CompilerParams(vmem_limit_bytes=mib * MIB),
            cost_estimate=pl.CostEstimate(
                flops=int(WEIGHTS[self.calls] * FLOPS), bytes_accessed=1 << 10, transcendentals=0
            ),
        )(*operands)
        small = [x for x, (*_, spec) in zip(out, outs) if spec is VMEM]
        self.token = min(small, key=lambda x: x.size)
        self.calls += 1
        return out


def parts_of(x):
    hi = x.astype(BF16)
    lo = (x - hi.astype(F32)).astype(BF16)
    return hi, lo


def add_kernel(x, y, out):
    out[...] = x[...] + y[...]


def add(run, x, y):
    return run(add_kernel, [(x, VMEM), (y, VMEM)], [(x.shape, F32, VMEM)], mib=2)[0]


def halve(whole, place, keep, give):
    keep[...] = whole[pl.ds(pl.multiple_of(place * HALF, HALF), HALF), :]
    give[...] = whole[pl.ds(pl.multiple_of((1 - place) * HALF, HALF), HALF), :]


def tile_at(i):
    return pl.ds(pl.multiple_of(i * TILE, TILE), TILE)


def gate_left(run, grad, error, start, first, count, before=None):
    rows, cols = grad.shape
    last = (first + count) * TILE == rows

    def kernel(grad, error, start, *refs):
        if before is not None:
            refs = refs[2:]
        left, fixed = refs[:2]

        def step(g, e):
            at = tile_at(first + pl.program_id(0))
            term = jnp.zeros((TILE, RANK), F32)
            for j in range(0, cols, TILE):
                here = slice(j, j + TILE)
                c = g[:, here] + e[:, here]
                fixed[at, here] = c
                term += lax.dot_general(c, start[:, here], NT, preferred_element_type=F32)
            left[:, at] = term.T

        spec = pl.BlockSpec((TILE, cols), lambda i: (first + i, 0), pipeline_mode=pl.Buffered(3))
        pltpu.emit_pipeline(step, grid=(count,), in_specs=[spec, spec])(grad, error)
        if last:
            halve(left, core_of(), *refs[2:])

    args = [(grad, HBM), (error, HBM), (start, VMEM)]
    outs = [((RANK, rows), F32, VMEM), ((rows, cols), BF16, VMEM)]
    if last:
        outs += [((HALF, rows), F32, VMEM)] * 2
    aliases = None
    if before is not None:
        args += [(x, VMEM) for x in before]
        aliases = {3: 0, 4: 1}
    return run(kernel, args, outs, mib=8, aliases=aliases)


def down_left(run, grad, error, start, first, count, before=None):
    rows, cols = grad.shape
    width = count * TILE

    def kernel(grad, error, start, *refs):
        if before is not None:
            refs = refs[1:]
        keep, give, fixed, left = refs
        block = lax.div(lax.axis_index("dp"), REPLICAS) * (rows // TILE)
        left[...] = jnp.zeros_like(left)

        def step(g, e, s):
            at = tile_at(pl.program_id(0))
            for j in range(0, width, TILE):
                here = slice(j, j + TILE)
                c = g[:, here] + e[:, here]
                fixed[at, first * TILE + j : first * TILE + j + TILE] = c
                left[:, here] += jnp.dot(s[...], c, preferred_element_type=F32)

        spec = pl.BlockSpec((TILE, width), lambda i: (i, 0), pipeline_mode=pl.Buffered(3))
        part = pl.BlockSpec((RANK, TILE), lambda i: (0, block + i))
        columns = pl.ds(first * TILE, width)
        pltpu.emit_pipeline(step, grid=(rows // TILE,), in_specs=[spec, spec, part])(
            grad.at[:, columns], error.at[:, columns], start
        )
        halve(left, replica_of(), keep, give)

    args = [(grad, HBM), (error, HBM), (start, HBM)]
    aliases = None
    if before is not None:
        args += [(before, VMEM)]
        aliases = {3: 2}
    outs = [((HALF, width), F32, VMEM)] * 2 + [((rows, cols), BF16, VMEM)]
    return run(kernel, args, outs, [pltpu.VMEM((RANK, width), F32)], mib=8, aliases=aliases)


def load_left(own, other, place, left, stack, gram):
    left[pl.ds(pl.multiple_of(place * HALF, HALF), HALF), :] = own[...]
    left[pl.ds(pl.multiple_of((1 - place) * HALF, HALF), HALF), :] = other[...]
    hi, lo = parts_of(left[...])
    stack[:RANK, :] = hi
    stack[RANK:, :] = lo
    gram[...] = lax.dot_general(
        left[...], left[...], NT, preferred_element_type=F32, precision=lax.Precision.HIGHEST
    )


def gate_right(run, own, other, fixed):
    rows, cols = fixed.shape

    def kernel(own, other, fixed, keep, give, gram, left, stack, right):
        load_left(own, other, core_of(), left, stack, gram)

        def step(i, _):
            both = jnp.dot(stack[...], fixed[:, tile_at(i)], preferred_element_type=F32)
            right[:, tile_at(i)] = both[:RANK] + both[RANK:]
            return 0

        lax.fori_loop(0, cols // TILE, step, 0)
        halve(right, replica_of(), keep, give)

    return right_call(run, kernel, own, other, fixed, cols)


def down_right(run, own, other, fixed):
    rows, cols = fixed.shape

    def kernel(own, other, fixed, keep, give, gram, left, stack, right):
        load_left(own, other, replica_of(), left, stack, gram)

        def step(i, _):
            both = lax.dot_general(stack[...], fixed[tile_at(i), :], NT, preferred_element_type=F32)
            right[:, tile_at(i)] = both[:RANK] + both[RANK:]
            return 0

        lax.fori_loop(0, rows // TILE, step, 0)
        halve(right, core_of(), keep, give)

    return right_call(run, kernel, own, other, fixed, rows)


def right_call(run, kernel, own, other, fixed, out_width):
    width = own.shape[1]
    return run(
        kernel,
        [(own, VMEM), (other, VMEM), (fixed, VMEM)],
        [((HALF, out_width), F32, VMEM)] * 2 + [((RANK, RANK), F32, VMEM), ((RANK, width), F32, VMEM)],
        [pltpu.VMEM((2 * RANK, width), BF16), pltpu.VMEM((RANK, out_width), F32)],
        mib=4,
    )


def inverses(grams):
    row_at = lax.broadcasted_iota(jnp.int32, (RANK, RANK), 0)
    col_at = lax.broadcasted_iota(jnp.int32, (RANK, RANK), 1)
    lane = lax.broadcasted_iota(jnp.int32, (1, RANK), 1)

    def scaled(a):
        diagonal = jnp.where(row_at == col_at, a, 0.0)
        down = lax.rsqrt(jnp.sum(diagonal, axis=1, keepdims=True))
        across = lax.rsqrt(jnp.sum(diagonal, axis=0, keepdims=True))
        return a * down * across, down, across

    def sweep(a, k):
        one, two = (row_at == k, row_at == k + 1)
        here = one | two | (col_at == k) | (col_at == k + 1)
        col_1 = jnp.broadcast_to(a[:, k : k + 1], (RANK, RANK))
        col_2 = jnp.broadcast_to(a[:, k + 1 : k + 2], (RANK, RANK))
        p, q, r = col_1[k : k + 1], col_2[k : k + 1], col_2[k + 1 : k + 2]
        row_1 = jnp.where(lane == k, 1.0, jnp.where(lane == k + 1, 0.0, a[k : k + 1]))
        row_2 = jnp.where(lane == k + 1, 1.0, jnp.where(lane == k, 0.0, a[k + 1 : k + 2]))
        inv = 1.0 / (p * r - q * q)
        new_1 = (r * row_1 - q * row_2) * inv
        new_2 = (p * row_2 - q * row_1) * inv
        col_1 = jnp.where(one, -1.0, jnp.where(two, 0.0, col_1))
        col_2 = jnp.where(two, -1.0, jnp.where(one, 0.0, col_2))
        return jnp.where(here, 0.0, a) - col_1 * new_1 - col_2 * new_2

    systems = [scaled(a) for a in grams]
    values = [a for a, _, _ in systems]
    for k in range(0, RANK, 2):
        values = [sweep(a, k) for a in values]
    return [a * down * across for a, (_, down, across) in zip(values, systems)]


def solve(run, systems):
    counts = [(len(grams), len(lefts)) for _, grams, lefts in systems]
    widths = [sum(x.shape[1] for x in lefts) for _, _, lefts in systems]

    def kernel(*refs):
        outs = refs[-len(systems) :]
        totals, left_refs = [], []
        for n_gram, n_left in counts:
            total = refs[0][...]
            for ref in refs[1:n_gram]:
                total += ref[...]
            totals.append(total)
            left_refs.append(refs[n_gram : n_gram + n_left])
            refs = refs[n_gram + n_left :]
        for (place, _, _), a, lefts, out in zip(systems, inverses(totals), left_refs, outs):
            turned = jnp.concatenate([a[HALF:], a[:HALF]], axis=0)
            a = jnp.where(place() == 0, a, turned) * (1.0 / REPLICAS)
            at = 0
            for left in lefts:
                n = left.shape[1]
                out[:, at : at + n] = jnp.dot(
                    a, left[...], preferred_element_type=F32, precision=lax.Precision.HIGHEST
                )
                at += n

    args = [(x, VMEM) for _, grams, lefts in systems for x in (*grams, *lefts)]
    return run(kernel, args, [((RANK, n), F32, VMEM) for n in widths], mib=4)


def rebuild(run, rows_in, cols_in, fixed, height):
    rows, cols = fixed.shape
    tiles = rows // REPLICAS // height
    n_row, n_col = len(rows_in), len(cols_in)

    def kernel(*refs):
        row_refs, col_refs = refs[:n_row], refs[n_row : n_row + n_col]
        fixed, new_error, update, done, row_stack, col_stack, row_turned = refs[n_row + n_col :]
        done[...] = jnp.zeros_like(done)
        for sources, stack, order in (
            (row_refs, row_stack, (0, 1, 0, 1)),
            (col_refs, col_stack, (0, 0, 1, 1)),
        ):
            at = 0
            for ref in sources:
                parts = parts_of(ref[...])
                n = ref.shape[0]
                for k, which in enumerate(order):
                    stack[k * RANK + at : k * RANK + at + n, :] = parts[which]
                at += n
        for i in range(0, rows, TILE):
            row_turned[i : i + TILE, :] = row_stack[:, i : i + TILE].T
        replica = replica_of()
        mine, theirs = replica * tiles, (1 - replica) * tiles

        def tile(i, e, u):
            at = pl.ds(pl.multiple_of(i * height, height), height)
            row = row_turned[at, :]
            for j in range(0, cols, TILE):
                here = slice(j, j + TILE)
                value = jnp.dot(row, col_stack[:, here], preferred_element_type=F32)
                e[:, here] = (fixed[at, here].astype(F32) - value).astype(BF16)
                if u is not None:
                    u[:, here] = value.astype(BF16)

        def tile_of(i):
            return jnp.where(i < tiles, mine + i, theirs + i - tiles)

        def step(e, u):
            i = pl.program_id(0)
            pl.when(i < tiles)(lambda: tile(tile_of(i), e, u))
            pl.when(i >= tiles)(lambda: tile(tile_of(i), e, None))

        block = (height, cols)
        pltpu.emit_pipeline(
            step,
            grid=(REPLICAS * tiles,),
            out_specs=[
                pl.BlockSpec(block, lambda i: (tile_of(i), 0)),
                pl.BlockSpec(block, lambda i: (jnp.minimum(i, tiles - 1), 0)),
            ],
        )(new_error, update)

    return run(
        kernel,
        [(x, VMEM) for x in (*rows_in, *cols_in)] + [(fixed, VMEM)],
        [
            ((rows, cols), BF16, HBM),
            ((rows // REPLICAS, cols), BF16, HBM),
            ((8, 128), F32, VMEM),
        ],
        [
            pltpu.VMEM((4 * RANK, rows), BF16),
            pltpu.VMEM((4 * RANK, cols), BF16),
            pltpu.VMEM((rows, 4 * RANK), BF16),
        ],
        mib=18,
    )[:2]


def local(grad_gate, grad_down, error_gate, error_down, start_gate, start_down):
    slab, width = grad_gate.shape
    n_dp, n_t = lax.axis_size("dp"), lax.axis_size("tensor")
    run = Order()
    hops, steps = row_steps(), col_steps()

    keep, give, fixed_down = down_left(run, grad_down, error_down, start_down, 0, width // TILE)
    got = exchange(give, other_replica)
    _, fixed_gate, keep_gate, give = gate_left(run, grad_gate, error_gate, start_gate, 0, slab // TILE)
    got_gate = exchange(give, other_core)
    down = add(run, keep, got)
    got = exchange(down, steps[0])
    gate = add(run, keep_gate, got_gate)
    for hop in hops:
        gate = add(run, gate, exchange(gate, hop))
    other_gate = exchange(gate, other_core)
    for i in range(len(steps)):
        down = add(run, down, got)
        if i + 1 < len(steps):
            got = exchange(down, steps[i + 1])
    other_down = exchange(down, other_replica)

    keep_gate, give, gram_gate, left_gate = gate_right(run, gate, other_gate, fixed_gate)
    got_gate = exchange(give, other_replica)
    grams_gate = [gram_gate] + [
        exchange(gram_gate, lambda d, t, b=b: (d ^ b, t)) for b in range(REPLICAS, n_dp, REPLICAS)
    ]
    keep, give, gram_down, left_down = down_right(run, down, other_down, fixed_down)
    got = exchange(give, other_core)
    grams_down = [gram_down] + [
        exchange(gram_down, lambda d, t, b=b: (d, t ^ b)) for b in range(1, n_t)
    ]
    gate = add(run, keep_gate, got_gate)
    got_gate = exchange(gate, steps[0])
    down = add(run, keep, got)
    for hop in hops[:-1]:
        down = add(run, down, exchange(down, hop))
    got = exchange(down, hops[-1])
    down_cols, gate_rows = solve(
        run, [(core_of, grams_down, (left_down,)), (replica_of, grams_gate, (left_gate,))]
    )
    for i in range(len(steps)):
        gate = add(run, gate, got_gate)
        if i + 1 < len(steps):
            got_gate = exchange(gate, steps[i + 1])
    other_gate = exchange(gate, other_replica)
    down = add(run, down, got)
    other_down = exchange(down, other_core)

    new_error_down, update_down = rebuild(run, [down, other_down], [down_cols], fixed_down, TILE)
    new_error_gate, update_gate = rebuild(
        run, [gate_rows], [gate, other_gate], fixed_gate, slab // REPLICAS // 2
    )
    return (update_gate, update_down, new_error_gate, new_error_down)


def solution(mesh):
    split = P(("mix", "dp"), "tensor")
    in_specs = (split, split, split, split, P(None, "tensor"), P())
    out_specs = (split, split, split, split)

    def run(grad_gate, *rest):
        groups = mesh.shape["mix"] * mesh.shape["dp"]
        slab = grad_gate.shape[0] // groups
        width = grad_gate.shape[1] // mesh.shape["tensor"]
        fits = slab % (REPLICAS * TILE) == 0 and width % TILE == 0
        body = local if fits else local_plain
        return jax.shard_map(
            body, mesh=mesh, in_specs=in_specs, out_specs=out_specs, check_vma=False
        )(grad_gate, *rest)

    return run
```

time: 279 us -> 98.7 us (0.35)
  matrix products: 87.9 us -> 0 us
  waiting for transfers between devices: 105 us -> 33.1 us
  Pallas kernels: 0 us -> 48.4 us
  blocking collectives: 33.8 us -> 0 us
  other arithmetic: 25.3 us -> 0 us
  starting transfers between devices: 2.15 us -> 16.1 us
  between operations: 13.9 us -> 0.8 us
  local copies, waits for them, and re-layouts: 10.7 us -> 0.01 us
    psum x3 -> x0, waiting for transfers between devices: 88.7 us -> none  [the longest x1 39.2 us: local(): left_gate = lax.psum(left_gate, 'tensor')]
    dot_general x8 -> x0, matrix products: 85.5 us -> none  [the longest x1 22.3 us: local(): rebuilt_gate = jnp.dot(ortho_gate, right_gate.T, precision=high)]
    pallas_call x0 -> x17, Pallas kernels: none -> 48.4 us  [__call__(): pl.pallas_call(body, out_shape=tuple(((pltpu.VMEM if spec is VMEM else pl...]
    psum x2 -> x0, blocking collectives: 33.8 us -> none  [the longest x1 23.5 us: local(): inner_gate = lax.psum(gram_of(left_gate) * keep_gate, 'dp')]
    another operation x10 -> x0, other arithmetic: 24.1 us -> none  [the longest x6 13 us: factored(): lower = jnp.linalg.cholesky(inner)]
    ppermute x2 -> x18, waiting for transfers between devices: 15.8 us -> 33.1 us  [exchange(): return lax.ppermute(x, ('dp', 'tensor'), pairs)]
    ppermute x2 -> x18, starting transfers between devices: 2.03 us -> 16.1 us  [exchange(): return lax.ppermute(x, ('dp', 'tensor'), pairs)]
    convert_element_type x2 -> x0, local copies, waits for them, and re-layouts: 9.47 us -> none  [the longest x1 4.74 us: local(): lax.dynamic_slice_in_dim(rebuilt_gate, replica * share, share, 0)]
  transfers between devices with their start and end apart: 5 -> 18, of which waited for: 4 -> 10; matrix products, arithmetic and copies ran while one was open for 22% -> 0% of each run, Pallas kernels for 0% -> 32%
where the time goes in v4:
time: 98.7 us; the launch traced here: 98.4 us
  Pallas kernels  48.4 us (49%)
  waiting for transfers between devices  33.1 us (34%)
  starting transfers between devices  16.1 us (16%)
    pallas_call x17, Pallas kernels, __call__(): pl.pallas_call(body, out_shape=tuple(((pltpu.VMEM if spec is VMEM else pl...  48.4 us
    ppermute x18, waiting for transfers between devices, exchange(): return lax.ppermute(x, ('dp', 'tensor'), pairs)  33.1 us
    ppermute x18, starting transfers between devices, exchange(): return lax.ppermute(x, ('dp', 'tensor'), pairs)  16.1 us
  transfers between devices with their start and end apart: 18, of which 10 were waited for; matrix products, arithmetic and copies ran while one was open for 0% of the time, Pallas kernels for 32%

profile of v4, /device:TPU:0, one launch (start us, length us, event | category | flops | bytes accessed | tf_op | source)
XLA Modules:
  0.0 98.4 jit_solution(3115569471148407878)
XLA Ops:
  0.6 9.3 %shard_map.93 = (f32[32,1792]{1,0:T(8,128)S(1)}, f32[32,1792]{1,0:T(8,128)S(1)}, bf16[2560,1792]{1,0:T(8,128)(2,1)S(1)}) custom-call(bf16[2560,1792]{1,0:T(8,128)(2,1)} %refs_0_.2, bf16[2560,1792]{1,0:T(8,128)(2,1)} %refs_1_.2, bf16[64,5120]{1,0:T(8,128)(2,1)} %refs_2_.2), custom_call_target="tpu_custom_call" | custom-call | flops 9200000000 | bytes 1024 | tf_op jit(solution)/shard_map/pallas_call | solution.py:156
  10.0 3.1 %collective-permute-start = (f32[32,1792]{1,0:T(8,128)S(1)}, f32[32,1792]{1,0:T(8,128)S(1)}, u32[]{:S(2)}, u32[]{:S(2)}) collective-permute-start(f32[32,1792]{1,0:T(8,128)S(1)} %get-tuple-element.26), channel_id=1, source_target_pairs={{0,4},{1,5},{2,6},{3,7},{4,0},{5,1},{6,2},{7,3},{8,12},{9,13},{10,... | collective-permute-start | bytes 688136 | tf_op jit(solution)/shard_map/ppermute | solution.py:97
  13.1 8.9 %shard_map.94 = (f32[64,2560]{1,0:T(8,128)}, bf16[2560,1792]{1,0:T(8,128)(2,1)S(1)}, f32[32,2560]{1,0:T(8,128)S(1)}, f32[32,2560]{1,0:T(8,128)S(1)}) custom-call(bf16[2560,1792]{1,0:T(8,128)(2,1)} %refs_0_.3, bf16[2560,1792]{1,0:T(8,128)(2,1)} %refs_1_.3, bf16[64,1792]{1,0:T(8,128)(2,1)S(1)} %copy-done, f32[32,1792]{1,0:T(8,128)S(1)} %get-tuple-element.25.refs_3_.refs_0_), custom_call_target="tpu_custom_call" | custom-call | flops 9200000000 | bytes 1024 | tf_op jit(solution)/shard_map/pallas_call | solution.py:156
  22.1 1.6 %collective-permute-done.2.refs_1_ = f32[32,2560]{1,0:T(8,128)S(1)} collective-permute-done((f32[32,2560]{1,0:T(8,128)S(1)}, f32[32,2560]{1,0:T(8,128)S(1)}, u32[]{:S(2)}, u32[]{:S(2)}) %collective-permute-start.2) | collective-permute-done | bytes 327712 | tf_op jit(solution)/shard_map/ppermute | solution.py:97
  23.7 1.5 %collective-permute-start.3 = (f32[32,2560]{1,0:T(8,128)S(1)}, f32[32,2560]{1,0:T(8,128)S(1)}, u32[]{:S(2)}, u32[]{:S(2)}) collective-permute-start(f32[32,2560]{1,0:T(8,128)S(1)} %shard_map.96.refs_0_.refs_2_), channel_id=1, source_target_pairs={{0,2},{1,5},{2,0},{3,7},{4,6},{5,1},{6,4},{7,3},{8,10},{9,13},{10,... | collective-permute-start | bytes 983048 | tf_op jit(solution)/shard_map/ppermute | solution.py:97
  25.2 5.6 %collective-permute-done.3.refs_1_ = f32[32,2560]{1,0:T(8,128)S(1)} collective-permute-done((f32[32,2560]{1,0:T(8,128)S(1)}, f32[32,2560]{1,0:T(8,128)S(1)}, u32[]{:S(2)}, u32[]{:S(2)}) %collective-permute-start.3) | collective-permute-done | bytes 327712 | tf_op jit(solution)/shard_map/ppermute | solution.py:97
  31.0 3.0 %collective-permute-start.1 = (f32[32,1792]{1,0:T(8,128)S(1)}, f32[32,1792]{1,0:T(8,128)S(1)}, u32[]{:S(2)}, u32[]{:S(2)}) collective-permute-start(f32[32,1792]{1,0:T(8,128)S(1)} %shard_map.95.refs_2_.refs_0_), channel_id=1, source_target_pairs={{0,8},{1,9},{2,10},{3,11},{4,12},{5,13},{6,14},{7,15},{8,0},{9,1},... | collective-permute-start | bytes 688136 | tf_op jit(solution)/shard_map/ppermute | solution.py:97
  34.0 7.6 %collective-permute-done.4.refs_1_ = f32[32,2560]{1,0:T(8,128)S(1)} collective-permute-done((f32[32,2560]{1,0:T(8,128)S(1)}, f32[32,2560]{1,0:T(8,128)S(1)}, u32[]{:S(2)}, u32[]{:S(2)}) %collective-permute-start.4) | collective-permute-done | bytes 327712 | tf_op jit(solution)/shard_map/ppermute | solution.py:97
  41.7 2.9 %collective-permute-done.1.refs_1_ = f32[32,1792]{1,0:T(8,128)S(1)} collective-permute-done((f32[32,1792]{1,0:T(8,128)S(1)}, f32[32,1792]{1,0:T(8,128)S(1)}, u32[]{:S(2)}, u32[]{:S(2)}) %collective-permute-start.1) | collective-permute-done | bytes 229408 | tf_op jit(solution)/shard_map/ppermute | solution.py:97
  44.8 3.3 %shard_map.100 = (f32[32,1792]{1,0:T(8,128)S(1)}, f32[32,1792]{1,0:T(8,128)S(1)}, f32[64,64]{1,0:T(8,128)S(1)}, f32[64,2560]{1,0:T(8,128)S(1)}) custom-call(f32[32,2560]{1,0:T(8,128)S(1)} %shard_map.98.refs_2_.refs_0_, f32[32,2560]{1,0:T(8,128)S(1)} %collective-permute-done.6.refs_1_, bf16[2560,1792]{1,0:T(8,128)(2,1)S(1)} %get-tuple-element.30.refs_2_.refs_3_, ...), custom_call_target="tpu_custom_call" | custom-call | flops 4600000000 | bytes 1024 | tf_op jit(solution)/shard_map/pallas_call | solution.py:156
  48.0 2.1 %collective-permute-start.12 = (f32[32,1792]{1,0:T(8,128)S(1)}, f32[32,1792]{1,0:T(8,128)S(1)}, u32[]{:S(2)}, u32[]{:S(2)}) collective-permute-start(f32[32,1792]{1,0:T(8,128)S(1)} %get-tuple-element.38), channel_id=1, source_target_pairs={{0,4},{1,5},{2,6},{3,7},{4,0},{5,1},{6,2},{7,3},{8,12},{9,13},{10,... | collective-permute-start | bytes 688136 | tf_op jit(solution)/shard_map/ppermute | solution.py:97
  50.1 3.1 %collective-permute-done.5.refs_1_ = f32[32,1792]{1,0:T(8,128)S(1)} collective-permute-done((f32[32,1792]{1,0:T(8,128)S(1)}, f32[32,1792]{1,0:T(8,128)S(1)}, u32[]{:S(2)}, u32[]{:S(2)}) %collective-permute-start.5) | collective-permute-done | bytes 229408 | tf_op jit(solution)/shard_map/ppermute | solution.py:97
  53.2 5.3 %shard_map.101 = (f32[32,2560]{1,0:T(8,128)S(1)}, f32[32,2560]{1,0:T(8,128)S(1)}, f32[64,64]{1,0:T(8,128)S(1)}, f32[64,1792]{1,0:T(8,128)S(1)}) custom-call(f32[32,1792]{1,0:T(8,128)S(1)} %shard_map.99.refs_3_.refs_0_, f32[32,1792]{1,0:T(8,128)S(1)} %collective-permute-done.5.refs_1_, bf16[2560,1792]{1,0:T(8,128)(2,1)S(1)} %get-tuple-element.29.refs_2_.refs_3_, ...), custom_call_target="tpu_custom_call" | custom-call | flops 4600000000 | bytes 1024 | tf_op jit(solution)/shard_map/pallas_call | solution.py:156
  58.6 1.6 %collective-permute-done.11.refs_1_ = f32[32,2560]{1,0:T(8,128)S(1)} collective-permute-done((f32[32,2560]{1,0:T(8,128)S(1)}, f32[32,2560]{1,0:T(8,128)S(1)}, u32[]{:S(2)}, u32[]{:S(2)}) %collective-permute-start.11) | collective-permute-done | bytes 327712 | tf_op jit(solution)/shard_map/ppermute | solution.py:97
  60.2 0.6 collective-permute-start.13
  60.8 0.7 collective-permute-start.9
  61.5 2.3 %collective-permute-start.8 = (f32[64,64]{1,0:T(8,128)S(1)}, f32[64,64]{1,0:T(8,128)S(1)}, u32[]{:S(2)}, u32[]{:S(2)}) collective-permute-start(f32[64,64]{1,0:T(8,128)S(1)} %get-tuple-element.32.refs_2_.refs_0_), channel_id=1, source_target_pairs={{0,2},{1,3},{2,0},{3,1},{4,6},{5,7},{6,4},{7,5},{8,10},{9,11},{10,... | collective-permute-start | bytes 49160 | tf_op jit(solution)/shard_map/ppermute | solution.py:97
  63.8 4.2 %collective-permute-done.13.refs_1_ = f32[32,2560]{1,0:T(8,128)S(1)} collective-permute-done((f32[32,2560]{1,0:T(8,128)S(1)}, f32[32,2560]{1,0:T(8,128)S(1)}, u32[]{:S(2)}, u32[]{:S(2)}) %collective-permute-start.13) | collective-permute-done | bytes 327712 | tf_op jit(solution)/shard_map/ppermute | solution.py:97
  68.1 2.4 %collective-permute-start.16 = (f32[32,2560]{1,0:T(8,128)S(1)}, f32[32,2560]{1,0:T(8,128)S(1)}, u32[]{:S(2)}, u32[]{:S(2)}) collective-permute-start(f32[32,2560]{1,0:T(8,128)S(1)} %shard_map.104.refs_8_.refs_0_), channel_id=1, source_target_pairs={{0,4},{1,3},{2,6},{3,1},{4,0},{5,7},{6,2},{7,5},{8,12},{9,11},{10,... | collective-permute-start | bytes 983048 | tf_op jit(solution)/shard_map/ppermute | solution.py:97
  70.5 4.9 %shard_map.105 = (f32[64,1792]{1,0:T(8,128)S(1)}, f32[64,2560]{1,0:T(8,128)S(1)}) custom-call(f32[64,64]{1,0:T(8,128)S(1)} %get-tuple-element.32.refs_2_.refs_0_, f32[64,64]{1,0:T(8,128)S(1)} %collective-permute-done.7.refs_1_, f32[64,64]{1,0:T(8,128)S(1)} %collective-permute-done.8.refs_2_, f32[64,64]{1,0:T(8,128)S(1)} %collective-permute-done.9.refs_3_, ...), custom_call_target="tpu_custom_call" | custom-call | flops 6899999744 | bytes 1024 | tf_op jit(solution)/shard_map/pallas_call | solution.py:156
  75.4 4.8 %collective-permute-done.14.refs_1_ = f32[32,1792]{1,0:T(8,128)S(1)} collective-permute-done((f32[32,1792]{1,0:T(8,128)S(1)}, f32[32,1792]{1,0:T(8,128)S(1)}, u32[]{:S(2)}, u32[]{:S(2)}) %collective-permute-start.14) | collective-permute-done | bytes 229408 | tf_op jit(solution)/shard_map/ppermute | solution.py:97
  80.5 1.5 %collective-permute-done.17.refs_1_ = f32[32,2560]{1,0:T(8,128)S(1)} collective-permute-done((f32[32,2560]{1,0:T(8,128)S(1)}, f32[32,2560]{1,0:T(8,128)S(1)}, u32[]{:S(2)}, u32[]{:S(2)}) %collective-permute-start.17) | collective-permute-done | bytes 327712 | tf_op jit(solution)/shard_map/ppermute | solution.py:97
  82.1 8.7 %shard_map.108 = (bf16[2560,1792]{1,0:T(8,128)(2,1)}, bf16[1280,1792]{1,0:T(8,128)(2,1)}, f32[8,128]{1,0:T(8,128)S(1)}) custom-call(f32[32,2560]{1,0:T(8,128)S(1)} %shard_map.107.refs_0_.refs_4_, f32[32,2560]{1,0:T(8,128)S(1)} %collective-permute-done.17.refs_1_, f32[64,1792]{1,0:T(8,128)S(1)} %get-tuple-element.40.refs_2_, ...), custom_call_target="tpu_custom_call" | custom-call | flops 9200000000 | bytes 1024 | tf_op jit(solution)/shard_map/pallas_call | solution.py:156
  90.7 7.7 %shard_map.109 = (bf16[2560,1792]{1,0:T(8,128)(2,1)}, bf16[1280,1792]{1,0:T(8,128)(2,1)}, f32[8,128]{1,0:T(8,128)}) custom-call(f32[64,2560]{1,0:T(8,128)S(1)} %get-tuple-element.39.refs_0_, f32[32,1792]{1,0:T(8,128)S(1)} %shard_map.106.refs_2_.refs_1_, f32[32,1792]{1,0:T(8,128)S(1)} %collective-permute-done.15.refs_2_, ...), custom_call_target="tpu_custom_call" | custom-call | flops 9200000000 | bytes 1024 | tf_op jit(solution)/shard_map/pallas_call | solution.py:156
  (31 shorter events, 0.9 us)
Async XLA Ops:
  0.6 12.5 %copy-start = (bf16[64,1792]{1,0:T(8,128)(2,1)S(1)}, bf16[64,1792]{1,0:T(8,128)(2,1)}, u32[]{:S(2)}) copy-start(bf16[64,1792]{1,0:T(8,128)(2,1)} %refs_2_.3) | copy-start | bytes 688132
  10.0 12.0 %collective-permute-start = (f32[32,1792]{1,0:T(8,128)S(1)}, f32[32,1792]{1,0:T(8,128)S(1)}, u32[]{:S(2)}, u32[]{:S(2)}) collective-permute-start(f32[32,1792]{1,0:T(8,128)S(1)} %get-tuple-element.26), channel_id=1, source_target_pairs={{0,4},{1,5},{2,6},{3,7},{4,0},{5,1},{6,2},{7,3},{8,12},{9,13},{10,... | collective-permute-start | bytes 688136 | tf_op jit(solution)/shard_map/ppermute | solution.py:97
  22.0 1.6 %collective-permute-start.2 = (f32[32,2560]{1,0:T(8,128)S(1)}, f32[32,2560]{1,0:T(8,128)S(1)}, u32[]{:S(2)}, u32[]{:S(2)}) collective-permute-start(f32[32,2560]{1,0:T(8,128)S(1)} %get-tuple-element.28), channel_id=1, source_target_pairs={{0,1},{1,0},{2,3},{3,2},{4,5},{5,4},{6,7},{7,6},{8,9},{9,8},{10,11... | collective-permute-start | bytes 983048 | tf_op jit(solution)/shard_map/ppermute | solution.py:97
  23.7 7.1 %collective-permute-start.3 = (f32[32,2560]{1,0:T(8,128)S(1)}, f32[32,2560]{1,0:T(8,128)S(1)}, u32[]{:S(2)}, u32[]{:S(2)}) collective-permute-start(f32[32,2560]{1,0:T(8,128)S(1)} %shard_map.96.refs_0_.refs_2_), channel_id=1, source_target_pairs={{0,2},{1,5},{2,0},{3,7},{4,6},{5,1},{6,4},{7,3},{8,10},{9,13},{10,... | collective-permute-start | bytes 983048 | tf_op jit(solution)/shard_map/ppermute | solution.py:97
  30.9 10.7 %collective-permute-start.4 = (f32[32,2560]{1,0:T(8,128)S(1)}, f32[32,2560]{1,0:T(8,128)S(1)}, u32[]{:S(2)}, u32[]{:S(2)}) collective-permute-start(f32[32,2560]{1,0:T(8,128)S(1)} %shard_map.97.refs_0_.refs_2_), channel_id=1, source_target_pairs={{0,4},{1,3},{2,6},{3,1},{4,0},{5,7},{6,2},{7,5},{8,12},{9,11},{10,... | collective-permute-start | bytes 983048 | tf_op jit(solution)/shard_map/ppermute | solution.py:97
  31.0 13.7 %collective-permute-start.1 = (f32[32,1792]{1,0:T(8,128)S(1)}, f32[32,1792]{1,0:T(8,128)S(1)}, u32[]{:S(2)}, u32[]{:S(2)}) collective-permute-start(f32[32,1792]{1,0:T(8,128)S(1)} %shard_map.95.refs_2_.refs_0_), channel_id=1, source_target_pairs={{0,8},{1,9},{2,10},{3,11},{4,12},{5,13},{6,14},{7,15},{8,0},{9,1},... | collective-permute-start | bytes 688136 | tf_op jit(solution)/shard_map/ppermute | solution.py:97
  41.6 3.1 %collective-permute-start.6 = (f32[32,2560]{1,0:T(8,128)S(1)}, f32[32,2560]{1,0:T(8,128)S(1)}, u32[]{:S(2)}, u32[]{:S(2)}) collective-permute-start(f32[32,2560]{1,0:T(8,128)S(1)} %shard_map.98.refs_2_.refs_0_), channel_id=1, source_target_pairs={{0,1},{1,0},{2,3},{3,2},{4,5},{5,4},{6,7},{7,6},{8,9},{9,8},{10,11... | collective-permute-start | bytes 983048 | tf_op jit(solution)/shard_map/ppermute | solution.py:97
  44.7 8.5 %collective-permute-start.5 = (f32[32,1792]{1,0:T(8,128)S(1)}, f32[32,1792]{1,0:T(8,128)S(1)}, u32[]{:S(2)}, u32[]{:S(2)}) collective-permute-start(f32[32,1792]{1,0:T(8,128)S(1)} %shard_map.99.refs_3_.refs_0_), channel_id=1, source_target_pairs={{0,4},{1,5},{2,6},{3,7},{4,0},{5,1},{6,2},{7,3},{8,12},{9,13},{10,... | collective-permute-start | bytes 688136 | tf_op jit(solution)/shard_map/ppermute | solution.py:97
  48.0 10.5 %collective-permute-start.12 = (f32[32,1792]{1,0:T(8,128)S(1)}, f32[32,1792]{1,0:T(8,128)S(1)}, u32[]{:S(2)}, u32[]{:S(2)}) collective-permute-start(f32[32,1792]{1,0:T(8,128)S(1)} %get-tuple-element.38), channel_id=1, source_target_pairs={{0,4},{1,5},{2,6},{3,7},{4,0},{5,1},{6,2},{7,3},{8,12},{9,13},{10,... | collective-permute-start | bytes 688136 | tf_op jit(solution)/shard_map/ppermute | solution.py:97
  58.5 1.7 %collective-permute-start.11 = (f32[32,2560]{1,0:T(8,128)S(1)}, f32[32,2560]{1,0:T(8,128)S(1)}, u32[]{:S(2)}, u32[]{:S(2)}) collective-permute-start(f32[32,2560]{1,0:T(8,128)S(1)} %get-tuple-element.36), channel_id=1, source_target_pairs={{0,1},{1,0},{2,3},{3,2},{4,5},{5,4},{6,7},{7,6},{8,9},{9,8},{10,11... | collective-permute-start | bytes 983048 | tf_op jit(solution)/shard_map/ppermute | solution.py:97
  60.2 7.8 %collective-permute-start.13 = (f32[32,2560]{1,0:T(8,128)S(1)}, f32[32,2560]{1,0:T(8,128)S(1)}, u32[]{:S(2)}, u32[]{:S(2)}) collective-permute-start(f32[32,2560]{1,0:T(8,128)S(1)} %shard_map.103.refs_0_.refs_2_), channel_id=1, source_target_pairs={{0,2},{1,5},{2,0},{3,7},{4,6},{5,1},{6,4},{7,3},{8,10},{9,13},{10,... | collective-permute-start | bytes 983048 | tf_op jit(solution)/shard_map/ppermute | solution.py:97
  60.8 7.3 %collective-permute-start.10 = (f32[64,64]{1,0:T(8,128)S(1)}, f32[64,64]{1,0:T(8,128)S(1)}, u32[]{:S(2)}, u32[]{:S(2)}) collective-permute-start(f32[64,64]{1,0:T(8,128)S(1)} %get-tuple-element.31.refs_3_.refs_5_), channel_id=1, source_target_pairs={{0,8},{1,9},{2,10},{3,11},{4,12},{5,13},{6,14},{7,15},{8,0},{9,1},... | collective-permute-start | bytes 49160 | tf_op jit(solution)/shard_map/ppermute | solution.py:97
  60.8 9.7 %collective-permute-start.9 = (f32[64,64]{1,0:T(8,128)S(1)}, f32[64,64]{1,0:T(8,128)S(1)}, u32[]{:S(2)}, u32[]{:S(2)}) collective-permute-start(f32[64,64]{1,0:T(8,128)S(1)} %get-tuple-element.32.refs_2_.refs_0_), channel_id=1, source_target_pairs={{0,3},{1,2},{2,1},{3,0},{4,7},{5,6},{6,5},{7,4},{8,11},{9,10},{10,... | collective-permute-start | bytes 49160 | tf_op jit(solution)/shard_map/ppermute | solution.py:97
  61.5 9.0 %collective-permute-start.8 = (f32[64,64]{1,0:T(8,128)S(1)}, f32[64,64]{1,0:T(8,128)S(1)}, u32[]{:S(2)}, u32[]{:S(2)}) collective-permute-start(f32[64,64]{1,0:T(8,128)S(1)} %get-tuple-element.32.refs_2_.refs_0_), channel_id=1, source_target_pairs={{0,2},{1,3},{2,0},{3,1},{4,6},{5,7},{6,4},{7,5},{8,10},{9,11},{10,... | collective-permute-start | bytes 49160 | tf_op jit(solution)/shard_map/ppermute | solution.py:97
  63.8 6.7 %collective-permute-start.7 = (f32[64,64]{1,0:T(8,128)S(1)}, f32[64,64]{1,0:T(8,128)S(1)}, u32[]{:S(2)}, u32[]{:S(2)}) collective-permute-start(f32[64,64]{1,0:T(8,128)S(1)} %get-tuple-element.32.refs_2_.refs_0_), channel_id=1, source_target_pairs={{0,1},{1,0},{2,3},{3,2},{4,5},{5,4},{6,7},{7,6},{8,9},{9,8},{10,11... | collective-permute-start | bytes 49160 | tf_op jit(solution)/shard_map/ppermute | solution.py:97
  68.0 12.2 %collective-permute-start.14 = (f32[32,1792]{1,0:T(8,128)S(1)}, f32[32,1792]{1,0:T(8,128)S(1)}, u32[]{:S(2)}, u32[]{:S(2)}) collective-permute-start(f32[32,1792]{1,0:T(8,128)S(1)} %shard_map.102.refs_2_.refs_0_), channel_id=1, source_target_pairs={{0,8},{1,9},{2,10},{3,11},{4,12},{5,13},{6,14},{7,15},{8,0},{9,1},... | collective-permute-start | bytes 688136 | tf_op jit(solution)/shard_map/ppermute | solution.py:97
  68.1 12.3 %collective-permute-start.16 = (f32[32,2560]{1,0:T(8,128)S(1)}, f32[32,2560]{1,0:T(8,128)S(1)}, u32[]{:S(2)}, u32[]{:S(2)}) collective-permute-start(f32[32,2560]{1,0:T(8,128)S(1)} %shard_map.104.refs_8_.refs_0_), channel_id=1, source_target_pairs={{0,4},{1,3},{2,6},{3,1},{4,0},{5,7},{6,2},{7,5},{8,12},{9,11},{10,... | collective-permute-start | bytes 983048 | tf_op jit(solution)/shard_map/ppermute | solution.py:97
  80.4 1.7 %collective-permute-start.17 = (f32[32,2560]{1,0:T(8,128)S(1)}, f32[32,2560]{1,0:T(8,128)S(1)}, u32[]{:S(2)}, u32[]{:S(2)}) collective-permute-start(f32[32,2560]{1,0:T(8,128)S(1)} %shard_map.107.refs_0_.refs_4_), channel_id=1, source_target_pairs={{0,1},{1,0},{2,3},{3,2},{4,5},{5,4},{6,7},{7,6},{8,9},{9,8},{10,11... | collective-permute-start | bytes 983048 | tf_op jit(solution)/shard_map/ppermute | solution.py:97
  80.5 10.3 %collective-permute-start.15 = (f32[32,1792]{1,0:T(8,128)S(1)}, f32[32,1792]{1,0:T(8,128)S(1)}, u32[]{:S(2)}, u32[]{:S(2)}) collective-permute-start(f32[32,1792]{1,0:T(8,128)S(1)} %shard_map.106.refs_2_.refs_1_), channel_id=1, source_target_pairs={{0,4},{1,5},{2,6},{3,7},{4,0},{5,1},{6,2},{7,3},{8,12},{9,13},{10,... | collective-permute-start | bytes 688136 | tf_op jit(solution)/shard_map/ppermute | solution.py:97

commit v5 on v4

v5 whole, which is shorter than its diff:
```python
import functools

import jax
import jax.numpy as jnp
from jax import lax
from jax.experimental import pallas as pl
from jax.experimental.pallas import tpu as pltpu
from jax.sharding import PartitionSpec as P

REPLICAS = 2
RANK = 64
TILE = 256
FLOPS = 1.15e9
WEIGHTS = (8.0, 2.0, 1.0, 7.0, 1.0, 5.0, 1.0, 4.0, 5.0, 1.0, 5.0, 5.0, 1.0, 6.0, 1.0, 8.0, 1.0, 8.0)
MIB = 1 << 20
BF16 = jnp.bfloat16
F32 = jnp.float32

NN = (((1,), (0,)), ((), ()))
NT = (((1,), (1,)), ((), ()))
TN = (((0,), (0,)), ((), ()))


def from_partner(shard, axis, stride):
    return lax.ppermute(shard, axis, [(i, i ^ 1 << stride) for i in range(lax.axis_size(axis))])


def corrected(grad, error):
    return (grad.astype(F32) + error.astype(F32)).astype(BF16)


def transposed(matrix, ortho):
    return lax.dot_general(matrix, ortho.astype(BF16), TN, preferred_element_type=F32)


def gram_of(left):
    return jnp.dot(left.T, left, precision=lax.Precision.HIGHEST)


def factored(left, inner):
    lower = jnp.linalg.cholesky(inner)
    return lax.linalg.triangular_solve(lower, left, left_side=False, lower=True, transpose_a=True)


def local_plain(grad_gate, grad_down, error_gate, error_down, start_gate, start_down):
    high = lax.Precision.HIGHEST
    dp_place = lax.axis_index("dp")
    block = dp_place // REPLICAS
    replica = dp_place % REPLICAS
    fixed_gate = corrected(grad_gate, error_gate)
    fixed_down = corrected(grad_down, error_down)
    slab = fixed_gate.shape[0]
    cols_down = lax.dynamic_slice_in_dim(start_down, block * slab, slab, 1)
    left_gate = lax.dot_general(fixed_gate, start_gate, NT, preferred_element_type=F32)
    left_down = lax.dot_general(
        fixed_down, cols_down, (((0,), (1,)), ((), ())), preferred_element_type=F32
    )
    left_gate = lax.psum(left_gate, "tensor")
    left_gate = left_gate + from_partner(left_gate, "dp", 0)
    left_down = lax.psum(left_down, "dp")
    keep_gate = (replica == 0).astype(F32)
    inner_gate = lax.psum(gram_of(left_gate) * keep_gate, "dp")
    inner_down = lax.psum(gram_of(left_down), "tensor")
    ortho_gate = factored(left_gate, inner_gate)
    ortho_down = factored(left_down, inner_down)
    right_gate = transposed(fixed_gate, ortho_gate)
    right_gate = lax.psum(right_gate, "dp") / REPLICAS
    right_down = jnp.dot(fixed_down, ortho_down.astype(BF16), preferred_element_type=F32)
    right_down = lax.psum(right_down, "tensor")
    right_down = right_down + from_partner(right_down, "dp", 0)
    right_down = right_down / REPLICAS
    rebuilt_gate = jnp.dot(ortho_gate, right_gate.T, precision=high)
    rebuilt_down = jnp.dot(right_down, ortho_down.T, precision=high)
    share = slab // REPLICAS
    update_gate = lax.dynamic_slice_in_dim(rebuilt_gate, replica * share, share, 0).astype(BF16)
    update_down = lax.dynamic_slice_in_dim(rebuilt_down, replica * share, share, 0).astype(BF16)
    new_error_gate = (fixed_gate.astype(F32) - rebuilt_gate).astype(BF16)
    new_error_down = (fixed_down.astype(F32) - rebuilt_down).astype(BF16)
    return (update_gate, update_down, new_error_gate, new_error_down)


def core_of():
    return lax.rem(lax.axis_index("tensor"), 2)


def replica_of():
    return lax.rem(lax.axis_index("dp"), REPLICAS)


def exchange(x, partner):
    n_dp, n_t = lax.axis_size("dp"), lax.axis_size("tensor")
    pairs = []
    for d in range(n_dp):
        for t in range(n_t):
            to_d, to_t = partner(d, t)
            pairs.append((d * n_t + t, to_d * n_t + to_t))
    return lax.ppermute(x, ("dp", "tensor"), pairs)


def bits(n, low):
    out, b = [], low
    while b < n:
        out.append(b)
        b *= 2
    return out


def row_steps():
    steps = [(0, b) for b in bits(lax.axis_size("tensor"), 2)] + [(1, 0)]

    def partner(i, d, t):
        r, b = steps[i] if t % 2 == 0 else steps[-1 - i]
        return d ^ r, t ^ b

    return [functools.partial(partner, i) for i in range(len(steps))]


def col_steps():
    return [lambda d, t, b=b: (d ^ b, t) for b in bits(lax.axis_size("dp"), REPLICAS)]


def other_core(d, t):
    return d, t ^ 1


def other_replica(d, t):
    return d ^ 1, t


VMEM = pl.BlockSpec(memory_space=pltpu.VMEM)
HBM = pl.BlockSpec(memory_space=pltpu.HBM)
ANY = pl.BlockSpec(memory_space=pl.ANY)
HALF = RANK // 2


class Calls:
    def __init__(self):
        self.count = 0

    def __call__(self, kernel, args, outs, scratch=(), mib=8, aliases=None, after=()):
        n_in, n_after = len(args), len(after)
        operands = [
            pltpu.with_memory_space_constraint(x, pltpu.VMEM if spec is VMEM else pltpu.HBM)
            for x, spec in args
        ]

        def body(*refs):
            kernel(*refs[:n_in], *refs[n_in + n_after :])

        out = pl.pallas_call(
            body,
            out_shape=tuple(
                (pltpu.VMEM if spec is VMEM else pltpu.HBM)(shape, kind) for shape, kind, spec in outs
            ),
            in_specs=[spec for _, spec in args] + [ANY] * n_after,
            out_specs=tuple(spec for *_, spec in outs),
            scratch_shapes=list(scratch),
            input_output_aliases=aliases or {},
            compiler_params=pltpu.CompilerParams(vmem_limit_bytes=mib * MIB),
            cost_estimate=pl.CostEstimate(
                flops=int(WEIGHTS[self.count] * FLOPS), bytes_accessed=1 << 10, transcendentals=0
            ),
        )(*operands, *after)
        self.count += 1
        return out


def parts_of(x):
    hi = x.astype(BF16)
    lo = (x - hi.astype(F32)).astype(BF16)
    return hi, lo


def add_kernel(x, y, out):
    out[...] = x[...] + y[...]


def add(run, x, y, after=()):
    return run(add_kernel, [(x, VMEM), (y, VMEM)], [(x.shape, F32, VMEM)], mib=2, after=after)[0]


def add_split_kernel(x, y, own, rest):
    n = own.shape[1]
    own[...] = x[:, :n] + y[:, :n]
    rest[...] = x[:, n:] + y[:, n:]


def add_split(run, x, y, after=()):
    outs = [((HALF, x.shape[1] - 2 * RANK), F32, VMEM), ((HALF, 2 * RANK), F32, VMEM)]
    return run(add_split_kernel, [(x, VMEM), (y, VMEM)], outs, mib=2, after=after)


def halve(whole, place, keep, give):
    keep[...] = whole[pl.ds(pl.multiple_of(place * HALF, HALF), HALF), :]
    give[...] = whole[pl.ds(pl.multiple_of((1 - place) * HALF, HALF), HALF), :]


def tile_at(i):
    return pl.ds(pl.multiple_of(i * TILE, TILE), TILE)


def gate_left(run, grad, error, start, first, count, before=None, after=()):
    rows, cols = grad.shape
    last = (first + count) * TILE == rows

    def kernel(grad, error, start, *refs):
        if before is not None:
            refs = refs[2:]
        left, fixed = refs[:2]

        def step(g, e):
            at = tile_at(first + pl.program_id(0))
            term = jnp.zeros((TILE, RANK), F32)
            for j in range(0, cols, TILE):
                here = slice(j, j + TILE)
                c = g[:, here] + e[:, here]
                fixed[at, here] = c
                term += lax.dot_general(c, start[:, here], NT, preferred_element_type=F32)
            left[:, at] = term.T

        spec = pl.BlockSpec((TILE, cols), lambda i: (first + i, 0), pipeline_mode=pl.Buffered(3))
        pltpu.emit_pipeline(step, grid=(count,), in_specs=[spec, spec])(grad, error)
        if last:
            halve(left, core_of(), *refs[2:])

    args = [(grad, HBM), (error, HBM), (start, VMEM)]
    outs = [((RANK, rows), F32, VMEM), ((rows, cols), BF16, VMEM)]
    if last:
        outs += [((HALF, rows), F32, VMEM)] * 2
    aliases = None
    if before is not None:
        args += [(x, VMEM) for x in before]
        aliases = {3: 0, 4: 1}
    return run(kernel, args, outs, mib=8, aliases=aliases, after=after)


def down_left(run, grad, error, start, first, count, before=None, after=()):
    rows, cols = grad.shape
    last = (first + count) * TILE == rows

    def kernel(grad, error, start, *refs):
        if before is not None:
            refs = refs[2:]
        left, fixed = refs[:2]
        block = lax.div(lax.axis_index("dp"), REPLICAS) * (rows // TILE) + first
        if before is None:
            left[...] = jnp.zeros_like(left)

        def step(g, e, s):
            at = tile_at(first + pl.program_id(0))
            for j in range(0, cols, TILE):
                here = slice(j, j + TILE)
                c = g[:, here] + e[:, here]
                fixed[at, here] = c
                left[:, here] += jnp.dot(s[...], c, preferred_element_type=F32)

        spec = pl.BlockSpec((TILE, cols), lambda i: (first + i, 0), pipeline_mode=pl.Buffered(3))
        part = pl.BlockSpec((RANK, TILE), lambda i: (0, block + i))
        pltpu.emit_pipeline(step, grid=(count,), in_specs=[spec, spec, part])(grad, error, start)
        if last:
            halve(left, replica_of(), *refs[2:])

    args = [(grad, HBM), (error, HBM), (start, HBM)]
    outs = [((RANK, cols), F32, VMEM), ((rows, cols), BF16, VMEM)]
    if last:
        outs += [((HALF, cols), F32, VMEM)] * 2
    aliases = None
    if before is not None:
        args += [(x, VMEM) for x in before]
        aliases = {3: 0, 4: 1}
    return run(kernel, args, outs, mib=8, aliases=aliases, after=after)


def load_left(own, other, place, left, stack):
    left[pl.ds(pl.multiple_of(place * HALF, HALF), HALF), :] = own[...]
    left[pl.ds(pl.multiple_of((1 - place) * HALF, HALF), HALF), :] = other[...]
    hi, lo = parts_of(left[...])
    stack[:RANK, :] = hi
    stack[RANK:, :] = lo
    return lax.dot_general(
        left[...], left[...], NT, preferred_element_type=F32, precision=lax.Precision.HIGHEST
    )


def gate_right(run, own, other, fixed, after=()):
    rows, cols = fixed.shape

    def kernel(own, other, fixed, keep, give, gram, left, stack, right):
        gram[...] = load_left(own, other, core_of(), left, stack)

        def step(i, _):
            both = jnp.dot(stack[...], fixed[:, tile_at(i)], preferred_element_type=F32)
            right[:, tile_at(i)] = both[:RANK] + both[RANK:]
            return 0

        lax.fori_loop(0, cols // TILE, step, 0)
        halve(right, replica_of(), keep, give)

    return run(
        kernel,
        [(own, VMEM), (other, VMEM), (fixed, VMEM)],
        [((HALF, cols), F32, VMEM)] * 2 + [((RANK, RANK), F32, VMEM), ((RANK, rows), F32, VMEM)],
        [pltpu.VMEM((2 * RANK, rows), BF16), pltpu.VMEM((RANK, cols), F32)],
        mib=4,
        after=after,
    )


def down_right(run, own, other, fixed, after=()):
    rows, cols = fixed.shape

    def kernel(own, other, fixed, keep, give, left, stack, right):
        gram = load_left(own, other, replica_of(), left, stack)

        def step(i, _):
            both = lax.dot_general(stack[...], fixed[tile_at(i), :], NT, preferred_element_type=F32)
            right[:, tile_at(i)] = both[:RANK] + both[RANK:]
            return 0

        lax.fori_loop(0, rows // TILE, step, 0)
        halve(right, core_of(), keep.at[:, :rows], give.at[:, :rows])
        packed = jnp.concatenate([gram[:HALF], gram[HALF:]], axis=1)
        keep[:, rows:] = packed
        give[:, rows:] = packed

    return run(
        kernel,
        [(own, VMEM), (other, VMEM), (fixed, VMEM)],
        [((HALF, rows + 2 * RANK), F32, VMEM)] * 2 + [((RANK, cols), F32, VMEM)],
        [pltpu.VMEM((2 * RANK, cols), BF16), pltpu.VMEM((RANK, rows), F32)],
        mib=4,
        after=after,
    )


def inverses(grams):
    row_at = lax.broadcasted_iota(jnp.int32, (RANK, RANK), 0)
    col_at = lax.broadcasted_iota(jnp.int32, (RANK, RANK), 1)
    lane = lax.broadcasted_iota(jnp.int32, (1, RANK), 1)

    def scaled(a):
        diagonal = jnp.where(row_at == col_at, a, 0.0)
        down = lax.rsqrt(jnp.sum(diagonal, axis=1, keepdims=True))
        across = lax.rsqrt(jnp.sum(diagonal, axis=0, keepdims=True))
        return a * down * across, down, across

    def sweep(a, k):
        one, two = (row_at == k, row_at == k + 1)
        here = one | two | (col_at == k) | (col_at == k + 1)
        col_1 = jnp.broadcast_to(a[:, k : k + 1], (RANK, RANK))
        col_2 = jnp.broadcast_to(a[:, k + 1 : k + 2], (RANK, RANK))
        p, q, r = col_1[k : k + 1], col_2[k : k + 1], col_2[k + 1 : k + 2]
        row_1 = jnp.where(lane == k, 1.0, jnp.where(lane == k + 1, 0.0, a[k : k + 1]))
        row_2 = jnp.where(lane == k + 1, 1.0, jnp.where(lane == k, 0.0, a[k + 1 : k + 2]))
        inv = 1.0 / (p * r - q * q)
        new_1 = (r * row_1 - q * row_2) * inv
        new_2 = (p * row_2 - q * row_1) * inv
        col_1 = jnp.where(one, -1.0, jnp.where(two, 0.0, col_1))
        col_2 = jnp.where(two, -1.0, jnp.where(one, 0.0, col_2))
        return jnp.where(here, 0.0, a) - col_1 * new_1 - col_2 * new_2

    systems = [scaled(a) for a in grams]
    values = [a for a, _, _ in systems]
    for k in range(0, RANK, 2):
        values = [sweep(a, k) for a in values]
    return [a * down * across for a, (_, down, across) in zip(values, systems)]


def stacked(refs, order, stack):
    at = 0
    for ref in refs:
        parts = parts_of(ref[...])
        n = ref.shape[0]
        for k, which in enumerate(order):
            stack[k * RANK + at : k * RANK + at + n, :] = parts[which]
        at += n


ROW_ORDER, COL_ORDER = (0, 1, 0, 1), (0, 0, 1, 1)


def turn(stack, turned):
    for i in range(0, stack.shape[1], TILE):
        turned[i : i + TILE, :] = stack[:, i : i + TILE].T


def solve(run, grams_down, left_down, grams_gate, left_gate, after=()):
    n_down, n_gate = len(grams_down), len(grams_gate)
    cols, rows = left_down.shape[1], left_gate.shape[1]

    def kernel(*refs):
        down, gate = refs[:n_down], refs[n_down : n_down + n_gate]
        left_down, left_gate, col_stack, row_turned, col, row, row_stack = refs[n_down + n_gate :]
        a = sum((ref[...] for ref in down[1:]), down[0][...])
        a = jnp.concatenate([a[:, :RANK], a[:, RANK:]], axis=0)
        b = sum((ref[...] for ref in gate[1:]), gate[0][...])
        for place, a, left, out in zip(
            (core_of(), replica_of()), inverses([a, b]), (left_down, left_gate), (col, row)
        ):
            other = jnp.concatenate([a[HALF:], a[:HALF]], axis=0)
            a = jnp.where(place == 0, a, other) * (1.0 / REPLICAS)
            out[...] = jnp.dot(
                a, left[...], preferred_element_type=F32, precision=lax.Precision.HIGHEST
            )
        stacked([col], COL_ORDER, col_stack)
        stacked([row], ROW_ORDER, row_stack)
        turn(row_stack, row_turned)

    return run(
        kernel,
        [(x, VMEM) for x in (*grams_down, *grams_gate, left_down, left_gate)],
        [((4 * RANK, cols), BF16, VMEM), ((rows, 4 * RANK), BF16, VMEM)],
        [
            pltpu.VMEM((RANK, cols), F32),
            pltpu.VMEM((RANK, rows), F32),
            pltpu.VMEM((4 * RANK, rows), BF16),
        ],
        mib=6,
        after=after,
    )


def rebuild(run, row_turned, col_stack, halves, fixed, after=()):
    rows, cols = fixed.shape
    share, tiles = rows // REPLICAS, cols // TILE
    rows_late = row_turned is None
    scratch = [pltpu.VMEM((4 * RANK, rows if rows_late else cols), BF16)]
    if rows_late:
        scratch.append(pltpu.VMEM((rows, 4 * RANK), BF16))

    def kernel(ready, own, other, fixed, new_error, update, done, late, *turned):
        done[...] = jnp.zeros_like(done)
        stacked([own, other], ROW_ORDER if rows_late else COL_ORDER, late)
        row, col = ready, late
        if rows_late:
            row, col = turned[0], ready
            turn(late, row)
        replica = replica_of()

        def share_of(i):
            return jnp.where(i < tiles, replica, 1 - replica)

        def step(e, u):
            i = pl.program_id(0)
            at = pl.ds(pl.multiple_of(share_of(i) * share, share), share)
            here = tile_at(lax.rem(i, tiles))

            def tile(with_update):
                value = jnp.dot(row[at, :], col[:, here], preferred_element_type=F32)
                e[...] = (fixed[at, here].astype(F32) - value).astype(BF16)
                if with_update:
                    u[...] = value.astype(BF16)

            pl.when(i < tiles)(lambda: tile(True))
            pl.when(i >= tiles)(lambda: tile(False))

        block = (share, TILE)
        pltpu.emit_pipeline(
            step,
            grid=(REPLICAS * tiles,),
            out_specs=[
                pl.BlockSpec(block, lambda i: (share_of(i), lax.rem(i, tiles))),
                pl.BlockSpec(block, lambda i: (0, jnp.minimum(i, tiles - 1))),
            ],
        )(new_error, update)

    return run(
        kernel,
        [(x, VMEM) for x in (col_stack if rows_late else row_turned, *halves, fixed)],
        [((rows, cols), BF16, HBM), ((share, cols), BF16, HBM), ((8, 128), F32, VMEM)],
        scratch,
        mib=12,
        after=after,
    )


def local(grad_gate, grad_down, error_gate, error_down, start_gate, start_down):
    slab, width = grad_gate.shape
    n_dp, n_t = lax.axis_size("dp"), lax.axis_size("tensor")
    run = Calls()
    hops, steps = row_steps(), col_steps()
    tiles = slab // TILE

    _, fixed_gate, keep_gate, give = gate_left(run, grad_gate, error_gate, start_gate, 0, tiles)
    got_gate = exchange(give, other_core)
    cut = tiles // 5
    down_args = (run, grad_down, error_down, start_down)
    first = down_left(*down_args, 0, cut, after=(keep_gate,))
    gate = add(run, keep_gate, got_gate, after=(first[0],))
    got_gate = exchange(gate, hops[0])
    _, fixed_down, keep, give = down_left(*down_args, cut, tiles - cut, first, after=(gate,))
    got = exchange(give, other_replica)
    for hop in hops[1:]:
        gate = add(run, gate, got_gate, after=(keep,))
        got_gate = exchange(gate, hop)
    down = add(run, keep, got, after=(gate,))
    got = exchange(down, steps[0])
    gate = add(run, gate, got_gate, after=(down,))
    other_gate = exchange(gate, other_core)

    keep_gate, give_gate, gram_gate, left_gate = gate_right(run, gate, other_gate, fixed_gate)
    got_gate = exchange(give_gate, other_replica)
    grams_gate = [gram_gate] + [
        exchange(gram_gate, lambda d, t, b=b: (d ^ b, t)) for b in range(REPLICAS, n_dp, REPLICAS)
    ]
    for i in range(len(steps)):
        down = add(run, down, got, after=(gram_gate,))
        if i + 1 < len(steps):
            got = exchange(down, steps[i + 1])
    other_down = exchange(down, other_replica)
    gate = add(run, keep_gate, got_gate, after=(down,))
    got_gate = exchange(gate, steps[0])

    keep, give, left_down = down_right(run, down, other_down, fixed_down, after=(gate,))
    got = exchange(give, other_core)
    for i in range(len(steps)):
        gate = add(run, gate, got_gate, after=(keep,))
        if i + 1 < len(steps):
            got_gate = exchange(gate, steps[i + 1])
    other_gate = exchange(gate, other_replica)
    down, gram_down = add_split(run, keep, got, after=(gate,))
    grams_down = [gram_down] + [
        exchange(gram_down, lambda d, t, b=b: (d, t ^ b)) for b in range(2, n_t, 2)
    ]
    got = exchange(down, hops[0])
    col_stack, row_turned = solve(run, grams_down, left_down, grams_gate, left_gate)
    for hop in hops[1:]:
        down = add(run, down, got, after=(col_stack,))
        got = exchange(down, hop)
    new_error_gate, update_gate, done = rebuild(
        run, row_turned, None, (gate, other_gate), fixed_gate, after=(down,)
    )
    down = add(run, down, got, after=(done,))
    other_down = exchange(down, other_core)
    new_error_down, update_down, _ = rebuild(run, None, col_stack, (down, other_down), fixed_down)
    return (update_gate, update_down, new_error_gate, new_error_down)


def solution(mesh):
    split = P(("mix", "dp"), "tensor")
    in_specs = (split, split, split, split, P(None, "tensor"), P())
    out_specs = (split, split, split, split)

    def run(grad_gate, *rest):
        groups = mesh.shape["mix"] * mesh.shape["dp"]
        slab = grad_gate.shape[0] // groups
        width = grad_gate.shape[1] // mesh.shape["tensor"]
        fits = slab % (REPLICAS * TILE) == 0 and width % TILE == 0
        body = local if fits else local_plain
        return jax.shard_map(
            body, mesh=mesh, in_specs=in_specs, out_specs=out_specs, check_vma=False
        )(grad_gate, *rest)

    return run
```

time: 98.7 us -> 101 us (1.023)
  Pallas kernels: 48.4 us -> 52.7 us
  waiting for transfers between devices: 33.1 us -> 29.1 us
  starting transfers between devices: 16.1 us -> 17.2 us
    pallas_call x17 -> x18, Pallas kernels: 48.4 us -> 52.7 us  [__call__(): pl.pallas_call(body, out_shape=tuple(((pltpu.VMEM if spec is VMEM else pl...]
    ppermute x18 -> x16, waiting for transfers between devices: 33.1 us -> 29.1 us  [exchange(): return lax.ppermute(x, ('dp', 'tensor'), pairs)]
    ppermute x18 -> x16, starting transfers between devices: 16.1 us -> 17.2 us  [exchange(): return lax.ppermute(x, ('dp', 'tensor'), pairs)]
  transfers between devices with their start and end apart: 18 -> 16, of which waited for: 10 -> 8; matrix products, arithmetic and copies ran while one was open for 0% -> 0% of each run, Pallas kernels for 32% -> 33%
where the time goes in v5:
time: 101 us
  Pallas kernels  52.7 us (52%)
  waiting for transfers between devices  29.1 us (29%)
  starting transfers between devices  17.2 us (17%)
    pallas_call x18, Pallas kernels, __call__(): pl.pallas_call(body, out_shape=tuple(((pltpu.VMEM if spec is VMEM else pl...  52.7 us
    ppermute x16, waiting for transfers between devices, exchange(): return lax.ppermute(x, ('dp', 'tensor'), pairs)  29.1 us
    ppermute x16, starting transfers between devices, exchange(): return lax.ppermute(x, ('dp', 'tensor'), pairs)  17.2 us
  transfers between devices with their start and end apart: 16, of which 8 were waited for; matrix products, arithmetic and copies ran while one was open for 0% of the time, Pallas kernels for 33%

profile of v5, /device:TPU:0, one launch (start us, length us, event | category | flops | bytes accessed | tf_op | source)
XLA Modules:
  0.0 100.6 jit_solution(8284448119216888816)
XLA Ops:
  1.6 8.9 %shard_map.93 = (f32[64,2560]{1,0:T(8,128)}, bf16[2560,1792]{1,0:T(8,128)(2,1)S(1)}, f32[32,2560]{1,0:T(8,128)S(1)}, f32[32,2560]{1,0:T(8,128)S(1)}) custom-call(bf16[2560,1792]{1,0:T(8,128)(2,1)} %refs_0_.3, bf16[2560,1792]{1,0:T(8,128)(2,1)} %refs_1_.3, bf16[64,1792]{1,0:T(8,128)(2,1)S(1)} %copy-done), custom_call_target="tpu_custom_call" | custom-call | flops 9200000000 | bytes 1024 | tf_op jit(solution)/shard_map/pallas_call | solution.py:150
  11.0 2.4 %shard_map.94 = (f32[64,1792]{1,0:T(8,128)S(1)}, bf16[2560,1792]{1,0:T(8,128)(2,1)S(1)}) custom-call(bf16[2560,1792]{1,0:T(8,128)(2,1)} %refs_0_.5, bf16[2560,1792]{1,0:T(8,128)(2,1)} %refs_1_.5, bf16[64,5120]{1,0:T(8,128)(2,1)} %refs_2_.5, f32[32,2560]{1,0:T(8,128)S(1)} %get-tuple-element.28.refs_3_.refs_0_), custom_call_target="tpu_custom_call" | custom-call | flops 2300000000 | bytes 1024 | tf_op jit(solution)/shard_map/pallas_call | solution.py:150
  13.4 2.6 %collective-permute-start.2 = (f32[32,2560]{1,0:T(8,128)S(1)}, f32[32,2560]{1,0:T(8,128)S(1)}, u32[]{:S(2)}, u32[]{:S(2)}) collective-permute-start(f32[32,2560]{1,0:T(8,128)S(1)} %shard_map.95.refs_5_.refs_0_), channel_id=1, source_target_pairs={{0,2},{1,5},{2,0},{3,7},{4,6},{5,1},{6,4},{7,3},{8,10},{9,13},{10,... | collective-permute-start | bytes 983048 | tf_op jit(solution)/shard_map/ppermute | solution.py:97
  15.9 7.5 %shard_map.96 = (f32[64,1792]{1,0:T(8,128)S(1)}, bf16[2560,1792]{1,0:T(8,128)(2,1)S(1)}, f32[32,1792]{1,0:T(8,128)S(1)}, f32[32,1792]{1,0:T(8,128)S(1)}) custom-call(bf16[2560,1792]{1,0:T(8,128)(2,1)} %refs_0_.5, bf16[2560,1792]{1,0:T(8,128)(2,1)} %refs_1_.5, bf16[64,5120]{1,0:T(8,128)(2,1)} %refs_2_.5, ...), custom_call_target="tpu_custom_call", output_to_operand_aliasing={{0}: (3, {}), {1}: (4, {})} | custom-call | flops 8049999872 | bytes 1024 | tf_op jit(solution)/shard_map/pallas_call | solution.py:150
  23.4 1.6 %collective-permute-start.1 = (f32[32,1792]{1,0:T(8,128)S(1)}, f32[32,1792]{1,0:T(8,128)S(1)}, u32[]{:S(2)}, u32[]{:S(2)}) collective-permute-start(f32[32,1792]{1,0:T(8,128)S(1)} %get-tuple-element.33), channel_id=1, source_target_pairs={{0,4},{1,5},{2,6},{3,7},{4,0},{5,1},{6,2},{7,3},{8,12},{9,13},{10,... | collective-permute-start | bytes 688136 | tf_op jit(solution)/shard_map/ppermute | solution.py:97
  25.6 5.7 %collective-permute-done.1.refs_1_ = f32[32,1792]{1,0:T(8,128)S(1)} collective-permute-done((f32[32,1792]{1,0:T(8,128)S(1)}, f32[32,1792]{1,0:T(8,128)S(1)}, u32[]{:S(2)}, u32[]{:S(2)}) %collective-permute-start.1) | collective-permute-done | bytes 229408 | tf_op jit(solution)/shard_map/ppermute | solution.py:97
  31.3 3.5 %collective-permute-done.4.refs_1_ = f32[32,2560]{1,0:T(8,128)S(1)} collective-permute-done((f32[32,2560]{1,0:T(8,128)S(1)}, f32[32,2560]{1,0:T(8,128)S(1)}, u32[]{:S(2)}, u32[]{:S(2)}) %collective-permute-start.4) | collective-permute-done | bytes 327712 | tf_op jit(solution)/shard_map/ppermute | solution.py:97
  34.9 2.7 %collective-permute-start.3 = (f32[32,1792]{1,0:T(8,128)S(1)}, f32[32,1792]{1,0:T(8,128)S(1)}, u32[]{:S(2)}, u32[]{:S(2)}) collective-permute-start(f32[32,1792]{1,0:T(8,128)S(1)} %shard_map.98.refs_2_.refs_0_), channel_id=1, source_target_pairs={{0,8},{1,9},{2,10},{3,11},{4,12},{5,13},{6,14},{7,15},{8,0},{9,1},... | collective-permute-start | bytes 688136 | tf_op jit(solution)/shard_map/ppermute | solution.py:97
  37.6 3.2 %shard_map.100 = (f32[32,1792]{1,0:T(8,128)S(1)}, f32[32,1792]{1,0:T(8,128)S(1)}, f32[64,64]{1,0:T(8,128)S(1)}, f32[64,2560]{1,0:T(8,128)S(1)}) custom-call(f32[32,2560]{1,0:T(8,128)S(1)} %shard_map.99.refs_0_, f32[32,2560]{1,0:T(8,128)S(1)} %collective-permute-done.5.refs_1_, bf16[2560,1792]{1,0:T(8,128)(2,1)S(1)} %get-tuple-element.34.refs_2_.refs_3_), custom_call_target="tpu_custom_call" | custom-call | flops 4600000000 | bytes 1024 | tf_op jit(solution)/shard_map/pallas_call | solution.py:150
  41.4 7.3 %collective-permute-done.3.refs_1_ = f32[32,1792]{1,0:T(8,128)S(1)} collective-permute-done((f32[32,1792]{1,0:T(8,128)S(1)}, f32[32,1792]{1,0:T(8,128)S(1)}, u32[]{:S(2)}, u32[]{:S(2)}) %collective-permute-start.3) | collective-permute-done | bytes 229408 | tf_op jit(solution)/shard_map/ppermute | solution.py:97
  48.8 3.2 %collective-permute-start.11 = (f32[64,64]{1,0:T(8,128)S(1)}, f32[64,64]{1,0:T(8,128)S(1)}, u32[]{:S(2)}, u32[]{:S(2)}) collective-permute-start(f32[64,64]{1,0:T(8,128)S(1)} %get-tuple-element.35.refs_2_), channel_id=1, source_target_pairs={{0,8},{1,9},{2,10},{3,11},{4,12},{5,13},{6,14},{7,15},{8,0},{9,1},... | collective-permute-start | bytes 49160 | tf_op jit(solution)/shard_map/ppermute | solution.py:97
  52.0 2.3 %collective-permute-done.7.refs_1_ = f32[32,1792]{1,0:T(8,128)S(1)} collective-permute-done((f32[32,1792]{1,0:T(8,128)S(1)}, f32[32,1792]{1,0:T(8,128)S(1)}, u32[]{:S(2)}, u32[]{:S(2)}) %collective-permute-start.7) | collective-permute-done | bytes 229408 | tf_op jit(solution)/shard_map/ppermute | solution.py:97
  54.4 5.0 %collective-permute-done.6.refs_1_ = f32[32,1792]{1,0:T(8,128)S(1)} collective-permute-done((f32[32,1792]{1,0:T(8,128)S(1)}, f32[32,1792]{1,0:T(8,128)S(1)}, u32[]{:S(2)}, u32[]{:S(2)}) %collective-permute-start.6) | collective-permute-done | bytes 229408 | tf_op jit(solution)/shard_map/ppermute | solution.py:97
  59.4 5.2 %shard_map.103 = (f32[32,2688]{1,0:T(8,128)S(1)}, f32[32,2688]{1,0:T(8,128)S(1)}, f32[64,1792]{1,0:T(8,128)S(1)}) custom-call(f32[32,1792]{1,0:T(8,128)S(1)} %shard_map.101.refs_2_.refs_0_, f32[32,1792]{1,0:T(8,128)S(1)} %collective-permute-done.6.refs_1_, bf16[2560,1792]{1,0:T(8,128)(2,1)S(1)} %get-tuple-element.36.refs_2_.refs_3_, ...), custom_call_target="tpu_custom_call" | custom-call | flops 5750000128 | bytes 1024 | tf_op jit(solution)/shard_map/pallas_call | solution.py:150
  64.8 2.3 %collective-permute-done.9.refs_1_ = f32[32,1792]{1,0:T(8,128)S(1)} collective-permute-done((f32[32,1792]{1,0:T(8,128)S(1)}, f32[32,1792]{1,0:T(8,128)S(1)}, u32[]{:S(2)}, u32[]{:S(2)}) %collective-permute-start.9) | collective-permute-done | bytes 229408 | tf_op jit(solution)/shard_map/ppermute | solution.py:97
  67.1 0.9 collective-permute-start.10
  68.1 1.1 %collective-permute-start.13 = (f32[32,2560]{1,0:T(8,128)S(1)}, f32[32,2560]{1,0:T(8,128)S(1)}, u32[]{:S(2)}, u32[]{:S(2)}) collective-permute-start(f32[32,2560]{1,0:T(8,128)S(1)} %get-tuple-element.45.refs_0_), channel_id=1, source_target_pairs={{0,2},{1,5},{2,0},{3,7},{4,6},{5,1},{6,4},{7,3},{8,10},{9,13},{10,... | collective-permute-start | bytes 983048 | tf_op jit(solution)/shard_map/ppermute | solution.py:97
  69.2 1.7 %collective-permute-done.10.refs_1_ = f32[32,128]{1,0:T(8,128)S(1)} collective-permute-done((f32[32,128]{1,0:T(8,128)S(1)}, f32[32,128]{1,0:T(8,128)S(1)}, u32[]{:S(2)}, u32[]{:S(2)}) %collective-permute-start.10) | collective-permute-done | bytes 16416 | tf_op jit(solution)/shard_map/ppermute | solution.py:97
  70.9 5.0 %shard_map.106 = (bf16[256,1792]{1,0:T(8,128)(2,1)S(1)}, bf16[2560,256]{1,0:T(8,128)(2,1)S(1)}) custom-call(f32[32,128]{1,0:T(8,128)S(1)} %get-tuple-element.41.refs_0_, f32[32,128]{1,0:T(8,128)S(1)} %collective-permute-done.10.refs_1_, f32[64,64]{1,0:T(8,128)S(1)} %get-tuple-element.35.refs_2_, f32[64,64]{1,0:T(8,128)S(1)} %collective-permute-done.11.refs_3_, ...), custom_call_target="tpu_custom_call" | custom-call | flops 6899999744 | bytes 1024 | tf_op jit(solution)/shard_map/pallas_call | solution.py:150
  76.0 1.3 %collective-permute-start.14 = (f32[32,2560]{1,0:T(8,128)S(1)}, f32[32,2560]{1,0:T(8,128)S(1)}, u32[]{:S(2)}, u32[]{:S(2)}) collective-permute-start(f32[32,2560]{1,0:T(8,128)S(1)} %shard_map.107.refs_4_.refs_0_), channel_id=1, source_target_pairs={{0,4},{1,3},{2,6},{3,1},{4,0},{5,7},{6,2},{7,5},{8,12},{9,11},{10,... | collective-permute-start | bytes 983048 | tf_op jit(solution)/shard_map/ppermute | solution.py:97
  77.3 9.6 %shard_map.108 = (bf16[2560,1792]{1,0:T(8,128)(2,1)}, bf16[1280,1792]{1,0:T(8,128)(2,1)}, f32[8,128]{1,0:T(8,128)S(1)}) custom-call(bf16[2560,256]{1,0:T(8,128)(2,1)S(1)} %get-tuple-element.44.refs_0_, f32[32,1792]{1,0:T(8,128)S(1)} %shard_map.104.refs_2_.refs_1_, f32[32,1792]{1,0:T(8,128)S(1)} %collective-permute-done.12.refs_2_, ...), custom_call_target="tpu_custom_call" | custom-call | flops 9200000000 | bytes 1024 | tf_op jit(solution)/shard_map/pallas_call | solution.py:150
  86.9 2.0 %collective-permute-start.15 = (f32[32,2560]{1,0:T(8,128)S(1)}, f32[32,2560]{1,0:T(8,128)S(1)}, u32[]{:S(2)}, u32[]{:S(2)}) collective-permute-start(f32[32,2560]{1,0:T(8,128)S(1)} %shard_map.109.refs_1_), channel_id=1, source_target_pairs={{0,1},{1,0},{2,3},{3,2},{4,5},{5,4},{6,7},{7,6},{8,9},{9,8},{10,11... | collective-permute-start | bytes 983048 | tf_op jit(solution)/shard_map/ppermute | solution.py:97
  88.9 1.3 %collective-permute-done.15.refs_2_ = f32[32,2560]{1,0:T(8,128)S(1)} collective-permute-done((f32[32,2560]{1,0:T(8,128)S(1)}, f32[32,2560]{1,0:T(8,128)S(1)}, u32[]{:S(2)}, u32[]{:S(2)}) %collective-permute-start.15) | collective-permute-done | bytes 327712 | tf_op jit(solution)/shard_map/ppermute | solution.py:97
  90.2 10.5 %shard_map.110 = (bf16[2560,1792]{1,0:T(8,128)(2,1)}, bf16[1280,1792]{1,0:T(8,128)(2,1)}, f32[8,128]{1,0:T(8,128)}) custom-call(bf16[256,1792]{1,0:T(8,128)(2,1)S(1)} %get-tuple-element.46.refs_2_.refs_0_, f32[32,2560]{1,0:T(8,128)S(1)} %shard_map.109.refs_1_, f32[32,2560]{1,0:T(8,128)S(1)} %collective-permute-done.15.refs_2_, ...), custom_call_target="tpu_custom_call" | custom-call | flops 9200000000 | bytes 1024 | tf_op jit(solution)/shard_map/pallas_call | solution.py:150
  (28 shorter events, 3.1 us)
Async XLA Ops:
  0.6 0.9 copy-start
  10.5 2.8 %collective-permute-start = (f32[32,2560]{1,0:T(8,128)S(1)}, f32[32,2560]{1,0:T(8,128)S(1)}, u32[]{:S(2)}, u32[]{:S(2)}) collective-permute-start(f32[32,2560]{1,0:T(8,128)S(1)} %get-tuple-element.31), channel_id=1, source_target_pairs={{0,1},{1,0},{2,3},{3,2},{4,5},{5,4},{6,7},{7,6},{8,9},{9,8},{10,11... | collective-permute-start | bytes 983048 | tf_op jit(solution)/shard_map/ppermute | solution.py:97
  13.4 11.7 %collective-permute-start.2 = (f32[32,2560]{1,0:T(8,128)S(1)}, f32[32,2560]{1,0:T(8,128)S(1)}, u32[]{:S(2)}, u32[]{:S(2)}) collective-permute-start(f32[32,2560]{1,0:T(8,128)S(1)} %shard_map.95.refs_5_.refs_0_), channel_id=1, source_target_pairs={{0,2},{1,5},{2,0},{3,7},{4,6},{5,1},{6,4},{7,3},{8,10},{9,13},{10,... | collective-permute-start | bytes 983048 | tf_op jit(solution)/shard_map/ppermute | solution.py:97
  23.4 7.9 %collective-permute-start.1 = (f32[32,1792]{1,0:T(8,128)S(1)}, f32[32,1792]{1,0:T(8,128)S(1)}, u32[]{:S(2)}, u32[]{:S(2)}) collective-permute-start(f32[32,1792]{1,0:T(8,128)S(1)} %get-tuple-element.33), channel_id=1, source_target_pairs={{0,4},{1,5},{2,6},{3,7},{4,0},{5,1},{6,2},{7,3},{8,12},{9,13},{10,... | collective-permute-start | bytes 688136 | tf_op jit(solution)/shard_map/ppermute | solution.py:97
  25.1 9.7 %collective-permute-start.4 = (f32[32,2560]{1,0:T(8,128)S(1)}, f32[32,2560]{1,0:T(8,128)S(1)}, u32[]{:S(2)}, u32[]{:S(2)}) collective-permute-start(f32[32,2560]{1,0:T(8,128)S(1)} %shard_map.97.refs_2_.refs_0_), channel_id=1, source_target_pairs={{0,4},{1,3},{2,6},{3,1},{4,0},{5,7},{6,2},{7,5},{8,12},{9,11},{10,... | collective-permute-start | bytes 983048 | tf_op jit(solution)/shard_map/ppermute | solution.py:97
  34.9 2.7 %collective-permute-start.5 = (f32[32,2560]{1,0:T(8,128)S(1)}, f32[32,2560]{1,0:T(8,128)S(1)}, u32[]{:S(2)}, u32[]{:S(2)}) collective-permute-start(f32[32,2560]{1,0:T(8,128)S(1)} %shard_map.99.refs_0_), channel_id=1, source_target_pairs={{0,1},{1,0},{2,3},{3,2},{4,5},{5,4},{6,7},{7,6},{8,9},{9,8},{10,11... | collective-permute-start | bytes 983048 | tf_op jit(solution)/shard_map/ppermute | solution.py:97
  34.9 13.8 %collective-permute-start.3 = (f32[32,1792]{1,0:T(8,128)S(1)}, f32[32,1792]{1,0:T(8,128)S(1)}, u32[]{:S(2)}, u32[]{:S(2)}) collective-permute-start(f32[32,1792]{1,0:T(8,128)S(1)} %shard_map.98.refs_2_.refs_0_), channel_id=1, source_target_pairs={{0,8},{1,9},{2,10},{3,11},{4,12},{5,13},{6,14},{7,15},{8,0},{9,1},... | collective-permute-start | bytes 688136 | tf_op jit(solution)/shard_map/ppermute | solution.py:97
  40.8 13.4 %collective-permute-start.7 = (f32[32,1792]{1,0:T(8,128)S(1)}, f32[32,1792]{1,0:T(8,128)S(1)}, u32[]{:S(2)}, u32[]{:S(2)}) collective-permute-start(f32[32,1792]{1,0:T(8,128)S(1)} %get-tuple-element.38), channel_id=1, source_target_pairs={{0,4},{1,5},{2,6},{3,7},{4,0},{5,1},{6,2},{7,3},{8,12},{9,13},{10,... | collective-permute-start | bytes 688136 | tf_op jit(solution)/shard_map/ppermute | solution.py:97
  48.7 10.7 %collective-permute-start.6 = (f32[32,1792]{1,0:T(8,128)S(1)}, f32[32,1792]{1,0:T(8,128)S(1)}, u32[]{:S(2)}, u32[]{:S(2)}) collective-permute-start(f32[32,1792]{1,0:T(8,128)S(1)} %shard_map.101.refs_2_.refs_0_), channel_id=1, source_target_pairs={{0,4},{1,5},{2,6},{3,7},{4,0},{5,1},{6,2},{7,3},{8,12},{9,13},{10,... | collective-permute-start | bytes 688136 | tf_op jit(solution)/shard_map/ppermute | solution.py:97
  48.8 20.4 %collective-permute-start.11 = (f32[64,64]{1,0:T(8,128)S(1)}, f32[64,64]{1,0:T(8,128)S(1)}, u32[]{:S(2)}, u32[]{:S(2)}) collective-permute-start(f32[64,64]{1,0:T(8,128)S(1)} %get-tuple-element.35.refs_2_), channel_id=1, source_target_pairs={{0,8},{1,9},{2,10},{3,11},{4,12},{5,13},{6,14},{7,15},{8,0},{9,1},... | collective-permute-start | bytes 49160 | tf_op jit(solution)/shard_map/ppermute | solution.py:97
  54.3 12.7 %collective-permute-start.9 = (f32[32,1792]{1,0:T(8,128)S(1)}, f32[32,1792]{1,0:T(8,128)S(1)}, u32[]{:S(2)}, u32[]{:S(2)}) collective-permute-start(f32[32,1792]{1,0:T(8,128)S(1)} %shard_map.102.refs_3_.refs_0_), channel_id=1, source_target_pairs={{0,8},{1,9},{2,10},{3,11},{4,12},{5,13},{6,14},{7,15},{8,0},{9,1},... | collective-permute-start | bytes 688136 | tf_op jit(solution)/shard_map/ppermute | solution.py:97
  64.7 2.4 %collective-permute-start.8 = (f32[32,2688]{1,0:T(8,128)S(1)}, f32[32,2688]{1,0:T(8,128)S(1)}, u32[]{:S(2)}, u32[]{:S(2)}) collective-permute-start(f32[32,2688]{1,0:T(8,128)S(1)} %get-tuple-element.40), channel_id=1, source_target_pairs={{0,1},{1,0},{2,3},{3,2},{4,5},{5,4},{6,7},{7,6},{8,9},{9,8},{10,11... | collective-permute-start | bytes 1032200 | tf_op jit(solution)/shard_map/ppermute | solution.py:97
  67.1 3.8 %collective-permute-start.10 = (f32[32,128]{1,0:T(8,128)S(1)}, f32[32,128]{1,0:T(8,128)S(1)}, u32[]{:S(2)}, u32[]{:S(2)}) collective-permute-start(f32[32,128]{1,0:T(8,128)S(1)} %get-tuple-element.41.refs_0_), channel_id=1, source_target_pairs={{0,2},{1,3},{2,0},{3,1},{4,6},{5,7},{6,4},{7,5},{8,10},{9,11},{10,... | collective-permute-start | bytes 49160 | tf_op jit(solution)/shard_map/ppermute | solution.py:97
  68.1 9.2 %collective-permute-start.12 = (f32[32,1792]{1,0:T(8,128)S(1)}, f32[32,1792]{1,0:T(8,128)S(1)}, u32[]{:S(2)}, u32[]{:S(2)}) collective-permute-start(f32[32,1792]{1,0:T(8,128)S(1)} %shard_map.104.refs_2_.refs_1_), channel_id=1, source_target_pairs={{0,4},{1,5},{2,6},{3,7},{4,0},{5,1},{6,2},{7,3},{8,12},{9,13},{10,... | collective-permute-start | bytes 688136 | tf_op jit(solution)/shard_map/ppermute | solution.py:97
  68.1 7.9 %collective-permute-start.13 = (f32[32,2560]{1,0:T(8,128)S(1)}, f32[32,2560]{1,0:T(8,128)S(1)}, u32[]{:S(2)}, u32[]{:S(2)}) collective-permute-start(f32[32,2560]{1,0:T(8,128)S(1)} %get-tuple-element.45.refs_0_), channel_id=1, source_target_pairs={{0,2},{1,5},{2,0},{3,7},{4,6},{5,1},{6,4},{7,3},{8,10},{9,13},{10,... | collective-permute-start | bytes 983048 | tf_op jit(solution)/shard_map/ppermute | solution.py:97
  76.0 10.8 %collective-permute-start.14 = (f32[32,2560]{1,0:T(8,128)S(1)}, f32[32,2560]{1,0:T(8,128)S(1)}, u32[]{:S(2)}, u32[]{:S(2)}) collective-permute-start(f32[32,2560]{1,0:T(8,128)S(1)} %shard_map.107.refs_4_.refs_0_), channel_id=1, source_target_pairs={{0,4},{1,3},{2,6},{3,1},{4,0},{5,7},{6,2},{7,5},{8,12},{9,11},{10,... | collective-permute-start | bytes 983048 | tf_op jit(solution)/shard_map/ppermute | solution.py:97
  86.9 3.3 %collective-permute-start.15 = (f32[32,2560]{1,0:T(8,128)S(1)}, f32[32,2560]{1,0:T(8,128)S(1)}, u32[]{:S(2)}, u32[]{:S(2)}) collective-permute-start(f32[32,2560]{1,0:T(8,128)S(1)} %shard_map.109.refs_1_), channel_id=1, source_target_pairs={{0,1},{1,0},{2,3},{3,2},{4,5},{5,4},{6,7},{7,6},{8,9},{9,8},{10,11... | collective-permute-start | bytes 983048 | tf_op jit(solution)/shard_map/ppermute | solution.py:97

commit v6 on v5

--- a/solution.py
+++ b/solution.py
@@ -11,7 +11,7 @@
 RANK = 64
 TILE = 256
 FLOPS = 1.15e9
-WEIGHTS = (8.0, 2.0, 1.0, 7.0, 1.0, 5.0, 1.0, 4.0, 5.0, 1.0, 5.0, 5.0, 1.0, 6.0, 1.0, 8.0, 1.0, 8.0)
+WEIGHTS = (8.0, 4.0, 1.0, 4.0, 0.1, 5.0, 1.0, 5.0, 1.0, 1.0, 4.0, 0.2, 0.5, 1.0, 1.0, 0.3, 1.0, 8.0)
 MIB = 1 << 20
 BF16 = jnp.bfloat16
 F32 = jnp.float32
@@ -127,6 +127,10 @@
     return d ^ 1, t
 
 
+def to_other_core(pieces):
+    return [exchange(x, other_core) for x in pieces]
+
+
 VMEM = pl.BlockSpec(memory_space=pltpu.VMEM)
 HBM = pl.BlockSpec(memory_space=pltpu.HBM)
 ANY = pl.BlockSpec(memory_space=pl.ANY)
@@ -171,28 +175,45 @@
     return hi, lo
 
 
-def add_kernel(x, y, out):
-    out[...] = x[...] + y[...]
-
-
-def add(run, x, y, after=()):
-    return run(add_kernel, [(x, VMEM), (y, VMEM)], [(x.shape, F32, VMEM)], mib=2, after=after)[0]
-
-
-def add_split_kernel(x, y, own, rest):
-    n = own.shape[1]
-    own[...] = x[:, :n] + y[:, :n]
-    rest[...] = x[:, n:] + y[:, n:]
-
-
-def add_split(run, x, y, after=()):
-    outs = [((HALF, x.shape[1] - 2 * RANK), F32, VMEM), ((HALF, 2 * RANK), F32, VMEM)]
-    return run(add_split_kernel, [(x, VMEM), (y, VMEM)], outs, mib=2, after=after)
-
-
-def halve(whole, place, keep, give):
+def spans(*widths):
+    edges = sorted({sum(w[:i]) for w in widths for i in range(len(w) + 1)})
+    for low, high in zip(edges, edges[1:]):
+        places = []
+        for w in widths:
+            k = max(i for i in range(len(w)) if sum(w[:i]) <= low)
+            places.append((k, low - sum(w[:k]), high - sum(w[:k])))
+        yield places
+
+
+def widths_of(refs):
+    return [ref.shape[1] for ref in refs]
+
+
+def add(run, xs, ys, widths=None, after=()):
+    widths = widths or widths_of(xs)
+    n_x, n_y = len(xs), len(ys)
+
+    def kernel(*refs):
+        x, y, out = refs[:n_x], refs[n_x : n_x + n_y], refs[n_x + n_y :]
+        for (i, i0, i1), (j, j0, j1), (k, k0, k1) in spans(widths_of(x), widths_of(y), widths):
+            out[k][:, k0:k1] = x[i][:, i0:i1] + y[j][:, j0:j1]
+
+    outs = [((HALF, n), F32, VMEM) for n in widths]
+    return list(run(kernel, [(x, VMEM) for x in (*xs, *ys)], outs, mib=2, after=after))
+
+
+def in_two(width):
+    cut = width // 256 * 128
+    return [cut, width - cut]
+
+
+def halve(whole, place, keep, gives):
     keep[...] = whole[pl.ds(pl.multiple_of(place * HALF, HALF), HALF), :]
-    give[...] = whole[pl.ds(pl.multiple_of((1 - place) * HALF, HALF), HALF), :]
+    at = 0
+    for give in gives:
+        n = give.shape[1]
+        give[...] = whole[pl.ds(pl.multiple_of((1 - place) * HALF, HALF), HALF), at : at + n]
+        at += n
 
 
 def tile_at(i):
@@ -208,7 +229,7 @@
             refs = refs[2:]
         left, fixed = refs[:2]
 
-        def step(g, e):
+        def step(g, e, start):
             at = tile_at(first + pl.program_id(0))
             term = jnp.zeros((TILE, RANK), F32)
             for j in range(0, cols, TILE):
@@ -219,14 +240,15 @@
             left[:, at] = term.T
 
         spec = pl.BlockSpec((TILE, cols), lambda i: (first + i, 0), pipeline_mode=pl.Buffered(3))
-        pltpu.emit_pipeline(step, grid=(count,), in_specs=[spec, spec])(grad, error)
+        whole = pl.BlockSpec((RANK, cols), lambda i: (0, 0))
+        pltpu.emit_pipeline(step, grid=(count,), in_specs=[spec, spec, whole])(grad, error, start)
         if last:
-            halve(left, core_of(), *refs[2:])
-
-    args = [(grad, HBM), (error, HBM), (start, VMEM)]
+            halve(left, core_of(), refs[2], refs[3:])
+
+    args = [(grad, HBM), (error, HBM), (start, HBM)]
     outs = [((RANK, rows), F32, VMEM), ((rows, cols), BF16, VMEM)]
     if last:
-        outs += [((HALF, rows), F32, VMEM)] * 2
+        outs += [((HALF, n), F32, VMEM) for n in (rows, *in_two(rows))]
     aliases = None
     if before is not None:
         args += [(x, VMEM) for x in before]
@@ -258,7 +280,7 @@
         part = pl.BlockSpec((RANK, TILE), lambda i: (0, block + i))
         pltpu.emit_pipeline(step, grid=(count,), in_specs=[spec, spec, part])(grad, error, start)
         if last:
-            halve(left, replica_of(), *refs[2:])
+            halve(left, replica_of(), refs[2], refs[3:])
 
     args = [(grad, HBM), (error, HBM), (start, HBM)]
     outs = [((RANK, cols), F32, VMEM), ((rows, cols), BF16, VMEM)]
@@ -271,9 +293,13 @@
     return run(kernel, args, outs, mib=8, aliases=aliases, after=after)
 
 
-def load_left(own, other, place, left, stack):
-    left[pl.ds(pl.multiple_of(place * HALF, HALF), HALF), :] = own[...]
-    left[pl.ds(pl.multiple_of((1 - place) * HALF, HALF), HALF), :] = other[...]
+def load_left(owns, others, place, left, stack):
+    for refs, half in ((owns, place), (others, 1 - place)):
+        at = 0
+        for ref in refs:
+            n = ref.shape[1]
+            left[pl.ds(pl.multiple_of(half * HALF, HALF), HALF), at : at + n] = ref[...]
+            at += n
     hi, lo = parts_of(left[...])
     stack[:RANK, :] = hi
     stack[RANK:, :] = lo
@@ -282,11 +308,13 @@
     )
 
 
-def gate_right(run, own, other, fixed, after=()):
+def gate_right(run, owns, others, fixed, after=()):
     rows, cols = fixed.shape
-
-    def kernel(own, other, fixed, keep, give, gram, left, stack, right):
-        gram[...] = load_left(own, other, core_of(), left, stack)
+    n_own, n_both = len(owns), len(owns) + len(others)
+
+    def kernel(*refs):
+        fixed, keep, give, gram, left, stack, right = refs[n_both:]
+        gram[...] = load_left(refs[:n_own], refs[n_own:n_both], core_of(), left, stack)
 
         def step(i, _):
             both = jnp.dot(stack[...], fixed[:, tile_at(i)], preferred_element_type=F32)
@@ -294,11 +322,11 @@
             return 0
 
         lax.fori_loop(0, cols // TILE, step, 0)
-        halve(right, replica_of(), keep, give)
+        halve(right, replica_of(), keep, [give])
 
     return run(
         kernel,
-        [(own, VMEM), (other, VMEM), (fixed, VMEM)],
+        [(x, VMEM) for x in (*owns, *others, fixed)],
         [((HALF, cols), F32, VMEM)] * 2 + [((RANK, RANK), F32, VMEM), ((RANK, rows), F32, VMEM)],
         [pltpu.VMEM((2 * RANK, rows), BF16), pltpu.VMEM((RANK, cols), F32)],
         mib=4,
@@ -306,11 +334,14 @@
     )
 
 
-def down_right(run, own, other, fixed, after=()):
+def down_right(run, owns, others, fixed, after=()):
     rows, cols = fixed.shape
-
-    def kernel(own, other, fixed, keep, give, left, stack, right):
-        gram = load_left(own, other, replica_of(), left, stack)
+    n_own, n_both = len(owns), len(owns) + len(others)
+    cut, rest = in_two(rows)
+
+    def kernel(*refs):
+        fixed, keep, give_1, give_2, left, stack, right = refs[n_both:]
+        gram = load_left(refs[:n_own], refs[n_own:n_both], replica_of(), left, stack)
 
         def step(i, _):
             both = lax.dot_general(stack[...], fixed[tile_at(i), :], NT, preferred_element_type=F32)
@@ -318,15 +349,16 @@
             return 0
 
         lax.fori_loop(0, rows // TILE, step, 0)
-        halve(right, core_of(), keep.at[:, :rows], give.at[:, :rows])
         packed = jnp.concatenate([gram[:HALF], gram[HALF:]], axis=1)
+        halve(right, core_of(), keep.at[:, :rows], [give_1, give_2.at[:, :rest]])
         keep[:, rows:] = packed
-        give[:, rows:] = packed
-
+        give_2[:, rest:] = packed
+
+    widths = (rows + 2 * RANK, cut, rest + 2 * RANK)
     return run(
         kernel,
-        [(own, VMEM), (other, VMEM), (fixed, VMEM)],
-        [((HALF, rows + 2 * RANK), F32, VMEM)] * 2 + [((RANK, cols), F32, VMEM)],
+        [(x, VMEM) for x in (*owns, *others, fixed)],
+        [((HALF, n), F32, VMEM) for n in widths] + [((RANK, cols), F32, VMEM)],
         [pltpu.VMEM((2 * RANK, cols), BF16), pltpu.VMEM((RANK, rows), F32)],
         mib=4,
         after=after,
@@ -420,56 +452,73 @@
     )
 
 
-def rebuild(run, row_turned, col_stack, halves, fixed, after=()):
+def rebuild(run, row_turned, col_stack, owns, others, fixed, after=()):
+    halves = [
+        (x, half, sum(widths_of(xs[:i])))
+        for half, xs in ((0, owns), (HALF, others))
+        for i, x in enumerate(xs)
+    ]
     rows, cols = fixed.shape
-    share, tiles = rows // REPLICAS, cols // TILE
+    height = rows // REPLICAS // 2
+    tiles = rows // REPLICAS // height
     rows_late = row_turned is None
     scratch = [pltpu.VMEM((4 * RANK, rows if rows_late else cols), BF16)]
     if rows_late:
         scratch.append(pltpu.VMEM((rows, 4 * RANK), BF16))
-
-    def kernel(ready, own, other, fixed, new_error, update, done, late, *turned):
+    n_half = len(halves)
+
+    def kernel(ready, *refs):
+        fixed, new_error, update, done, late, *turned = refs[n_half:]
         done[...] = jnp.zeros_like(done)
-        stacked([own, other], ROW_ORDER if rows_late else COL_ORDER, late)
+        order = ROW_ORDER if rows_late else COL_ORDER
+        for (_, at, left), ref in zip(halves, refs):
+            parts = parts_of(ref[...])
+            n, width = ref.shape
+            for k, which in enumerate(order):
+                late[k * RANK + at : k * RANK + at + n, left : left + width] = parts[which]
         row, col = ready, late
         if rows_late:
             row, col = turned[0], ready
             turn(late, row)
         replica = replica_of()
-
-        def share_of(i):
-            return jnp.where(i < tiles, replica, 1 - replica)
+        mine, theirs = replica * tiles, (1 - replica) * tiles
+
+        def tile_of(i):
+            return jnp.where(i < tiles, mine + i, theirs + i - tiles)
 
         def step(e, u):
             i = pl.program_id(0)
-            at = pl.ds(pl.multiple_of(share_of(i) * share, share), share)
-            here = tile_at(lax.rem(i, tiles))
+            at = pl.ds(pl.multiple_of(tile_of(i) * height, height), height)
 
             def tile(with_update):
-                value = jnp.dot(row[at, :], col[:, here], preferred_element_type=F32)
-                e[...] = (fixed[at, here].astype(F32) - value).astype(BF16)
-                if with_update:
-                    u[...] = value.astype(BF16)
+                row_here = row[at, :]
+                for j in range(0, cols, TILE):
+                    here = slice(j, j + TILE)
+                    value = jnp.dot(row_here, col[:, here], preferred_element_type=F32)
+                    e[:, here] = (fixed[at, here].astype(F32) - value).astype(BF16)
+                    if with_update:
+                        u[:, here] = value.astype(BF16)
 
             pl.when(i < tiles)(lambda: tile(True))
             pl.when(i >= tiles)(lambda: tile(False))
 
-        block = (share, TILE)
+        block = (height, cols)
         pltpu.emit_pipeline(
             step,
             grid=(REPLICAS * tiles,),
             out_specs=[
-                pl.BlockSpec(block, lambda i: (share_of(i), lax.rem(i, tiles))),
-                pl.BlockSpec(block, lambda i: (0, jnp.minimum(i, tiles - 1))),
+                pl.BlockSpec(block, lambda i: (tile_of(i), 0)),
+                pl.BlockSpec(block, lambda i: (jnp.minimum(i, tiles - 1), 0)),
             ],
         )(new_error, update)
 
+    pieces = [x for x, _, _ in halves]
     return run(
         kernel,
-        [(x, VMEM) for x in (col_stack if rows_late else row_turned, *halves, fixed)],
-        [((rows, cols), BF16, HBM), ((share, cols), BF16, HBM), ((8, 128), F32, VMEM)],
+        [(x, VMEM) for x in (col_stack if rows_late else row_turned, *pieces, fixed)],
+        [((rows, cols), BF16, HBM), ((rows // REPLICAS, cols), BF16, HBM), ((8, 128), F32, VMEM)],
         scratch,
-        mib=12,
+        mib=18,
         after=after,
     )
 
@@ -481,58 +530,63 @@
     hops, steps = row_steps(), col_steps()
     tiles = slab // TILE
 
-    _, fixed_gate, keep_gate, give = gate_left(run, grad_gate, error_gate, start_gate, 0, tiles)
-    got_gate = exchange(give, other_core)
-    cut = tiles // 5
-    down_args = (run, grad_down, error_down, start_down)
-    first = down_left(*down_args, 0, cut, after=(keep_gate,))
-    gate = add(run, keep_gate, got_gate, after=(first[0],))
+    _, fixed_down, keep, give = down_left(run, grad_down, error_down, start_down, 0, tiles)
+    got = exchange(give, other_replica)
+    gate_args = (run, grad_gate, error_gate, start_gate)
+    first = gate_left(*gate_args, 0, tiles // 2, after=(keep,))
+    (down,) = add(run, [keep], [got], after=(first[0],))
+    got = exchange(down, steps[0])
+    _, fixed_gate, keep_gate, *gives = gate_left(
+        *gate_args, tiles // 2, tiles - tiles // 2, first, after=(down,)
+    )
+    (gate,) = add(run, [keep_gate], to_other_core(gives))
     got_gate = exchange(gate, hops[0])
-    _, fixed_down, keep, give = down_left(*down_args, cut, tiles - cut, first, after=(gate,))
-    got = exchange(give, other_replica)
+    for i in range(len(steps)):
+        (down,) = add(run, [down], [got], after=(gate,))
+        if i + 1 < len(steps):
+            got = exchange(down, steps[i + 1])
+    other_down = exchange(down, other_replica)
     for hop in hops[1:]:
-        gate = add(run, gate, got_gate, after=(keep,))
+        (gate,) = add(run, [gate], [got_gate], after=(down,))
         got_gate = exchange(gate, hop)
-    down = add(run, keep, got, after=(gate,))
-    got = exchange(down, steps[0])
-    gate = add(run, gate, got_gate, after=(down,))
-    other_gate = exchange(gate, other_core)
-
-    keep_gate, give_gate, gram_gate, left_gate = gate_right(run, gate, other_gate, fixed_gate)
+
+    keep, *gives, left_down = down_right(run, [down], [other_down], fixed_down, after=(gate,))
+    gots = to_other_core(gives)
+    gates = add(run, [gate], [got_gate], in_two(slab), after=(keep,))
+    others_gate = to_other_core(gates)
+    down, gram_down = add(run, [keep], gots, [slab, 2 * RANK], after=(gates[0],))
+    grams_down = [gram_down] + [
+        exchange(gram_down, lambda d, t, b=b: (d, t ^ b)) for b in range(2, n_t, 2)
+    ]
+    got = exchange(down, hops[0])
+    keep_gate, give_gate, gram_gate, left_gate = gate_right(
+        run, gates, others_gate, fixed_gate, after=(down,)
+    )
     got_gate = exchange(give_gate, other_replica)
     grams_gate = [gram_gate] + [
         exchange(gram_gate, lambda d, t, b=b: (d ^ b, t)) for b in range(REPLICAS, n_dp, REPLICAS)
     ]
+    for hop in hops[1:]:
+        (down,) = add(run, [down], [got], after=(gram_gate,))
+        got = exchange(down, hop)
+    col_stack, row_turned = solve(
+        run, grams_down, left_down, grams_gate, left_gate, after=(down,)
+    )
+    (gate,) = add(run, [keep_gate], [got_gate], after=(col_stack,))
+    got_gate = exchange(gate, steps[0])
+    downs = add(run, [down], [got], in_two(slab), after=(gate,))
+    others_down = to_other_core(downs)
+    new_error_down, update_down, done = rebuild(
+        run, None, col_stack, downs, others_down, fixed_down
+    )
     for i in range(len(steps)):
-        down = add(run, down, got, after=(gram_gate,))
-        if i + 1 < len(steps):
-            got = exchange(down, steps[i + 1])
-    other_down = exchange(down, other_replica)
-    gate = add(run, keep_gate, got_gate, after=(down,))
-    got_gate = exchange(gate, steps[0])
-
-    keep, give, left_down = down_right(run, down, other_down, fixed_down, after=(gate,))
-    got = exchange(give, other_core)
-    for i in range(len(steps)):
-        gate = add(run, gate, got_gate, after=(keep,))
+        (gate,) = add(run, [gate], [got_gate], after=(done,))
         if i + 1 < len(steps):
             got_gate = exchange(gate, steps[i + 1])
     other_gate = exchange(gate, other_replica)
-    down, gram_down = add_split(run, keep, got, after=(gate,))
-    grams_down = [gram_down] + [
-        exchange(gram_down, lambda d, t, b=b: (d, t ^ b)) for b in range(2, n_t, 2)
-    ]
-    got = exchange(down, hops[0])
-    col_stack, row_turned = solve(run, grams_down, left_down, grams_gate, left_gate)
-    for hop in hops[1:]:
-        down = add(run, down, got, after=(col_stack,))
-        got = exchange(down, hop)
-    new_error_gate, update_gate, done = rebuild(
-        run, row_turned, None, (gate, other_gate), fixed_gate, after=(down,)
-    )
-    down = add(run, down, got, after=(done,))
-    other_down = exchange(down, other_core)
-    new_error_down, update_down, _ = rebuild(run, None, col_stack, (down, other_down), fixed_down)
+    new_error_gate, update_gate, _ = rebuild(
+        run, row_turned, None, [gate], [other_gate], fixed_gate
+    )
     return (update_gate, update_down, new_error_gate, new_error_down)
 
 

time: 101 us -> 95.8 us (0.949)
  waiting for transfers between devices: 29.1 us -> 21.5 us
  starting transfers between devices: 17.2 us -> 24.2 us
  Pallas kernels: 52.7 us -> 49.1 us
    ppermute x16 -> x20, waiting for transfers between devices: 29.1 us -> 21.5 us  [exchange(): return lax.ppermute(x, ('dp', 'tensor'), pairs)]
    ppermute x16 -> x20, starting transfers between devices: 17.2 us -> 24.2 us  [exchange(): return lax.ppermute(x, ('dp', 'tensor'), pairs)]
    pallas_call x18, Pallas kernels: 52.7 us -> 49.1 us  [__call__(): pl.pallas_call(body, out_shape=tuple(((pltpu.VMEM if spec is VMEM else pl...]
  transfers between devices with their start and end apart: 16 -> 20, of which waited for: 8 -> 13; matrix products, arithmetic and copies ran while one was open for 0% -> 0% of each run, Pallas kernels for 33% -> 33%
where the time goes in v6:
time: 95.8 us; the launch traced here: 95.5 us
  Pallas kernels  49.1 us (51%)
  starting transfers between devices  24.2 us (25%)
  waiting for transfers between devices  21.5 us (22%)
    pallas_call x18, Pallas kernels, __call__(): pl.pallas_call(body, out_shape=tuple(((pltpu.VMEM if spec is VMEM else pl...  49.1 us
    ppermute x20, starting transfers between devices, exchange(): return lax.ppermute(x, ('dp', 'tensor'), pairs)  24.2 us
    ppermute x20, waiting for transfers between devices, exchange(): return lax.ppermute(x, ('dp', 'tensor'), pairs)  21.5 us
  transfers between devices with their start and end apart: 20, of which 13 were waited for; matrix products, arithmetic and copies ran while one was open for 0% of the time, Pallas kernels for 33%

profile of v6, /device:TPU:0, one launch (start us, length us, event | category | flops | bytes accessed | tf_op | source)
XLA Modules:
  0.0 95.5 jit_solution(17135358542300471410)
XLA Ops:
  0.6 10.1 %shard_map.93 = (f32[64,1792]{1,0:T(8,128)}, bf16[2560,1792]{1,0:T(8,128)(2,1)S(1)}, f32[32,1792]{1,0:T(8,128)S(1)}, f32[32,1792]{1,0:T(8,128)S(1)}) custom-call(bf16[2560,1792]{1,0:T(8,128)(2,1)} %refs_0_.3, bf16[2560,1792]{1,0:T(8,128)(2,1)} %refs_1_.3, bf16[64,5120]{1,0:T(8,128)(2,1)} %refs_2_.3), custom_call_target="tpu_custom_call" | custom-call | flops 9200000000 | bytes 1024 | tf_op jit(solution)/shard_map/pallas_call | solution.py:154
  10.7 3.0 %collective-permute-start = (f32[32,1792]{1,0:T(8,128)S(1)}, f32[32,1792]{1,0:T(8,128)S(1)}, u32[]{:S(2)}, u32[]{:S(2)}) collective-permute-start(f32[32,1792]{1,0:T(8,128)S(1)} %get-tuple-element.35), channel_id=1, source_target_pairs={{0,4},{1,5},{2,6},{3,7},{4,0},{5,1},{6,2},{7,3},{8,12},{9,13},{10,... | collective-permute-start | bytes 688136 | tf_op jit(solution)/shard_map/ppermute | solution.py:97
  13.7 5.4 %shard_map.94 = (f32[64,2560]{1,0:T(8,128)S(1)}, bf16[2560,1792]{1,0:T(8,128)(2,1)S(1)}) custom-call(bf16[2560,1792]{1,0:T(8,128)(2,1)} %refs_0_.5, bf16[2560,1792]{1,0:T(8,128)(2,1)} %refs_1_.5, bf16[64,1792]{1,0:T(8,128)(2,1)} %refs_2_.5, f32[32,1792]{1,0:T(8,128)S(1)} %get-tuple-element.34.refs_3_.refs_0_), custom_call_target="tpu_custom_call" | custom-call | flops 4600000000 | bytes 1024 | tf_op jit(solution)/shard_map/pallas_call | solution.py:154
  19.3 2.8 %collective-permute-start.1 = (f32[32,1792]{1,0:T(8,128)S(1)}, f32[32,1792]{1,0:T(8,128)S(1)}, u32[]{:S(2)}, u32[]{:S(2)}) collective-permute-start(f32[32,1792]{1,0:T(8,128)S(1)} %shard_map.95.refs_5_.refs_0_), channel_id=1, source_target_pairs={{0,8},{1,9},{2,10},{3,11},{4,12},{5,13},{6,14},{7,15},{8,0},{9,1},... | collective-permute-start | bytes 688136 | tf_op jit(solution)/shard_map/ppermute | solution.py:97
  22.2 5.4 %shard_map.96 = (f32[64,2560]{1,0:T(8,128)S(1)}, bf16[2560,1792]{1,0:T(8,128)(2,1)S(1)}, f32[32,2560]{1,0:T(8,128)S(1)}, f32[32,1280]{1,0:T(8,128)S(1)}, f32[32,1280]{1,0:T(8,128)S(1)}) custom-call(bf16[2560,1792]{1,0:T(8,128)(2,1)} %refs_0_.5, bf16[2560,1792]{1,0:T(8,128)(2,1)} %refs_1_.5, ...), custom_call_target="tpu_custom_call", output_to_operand_aliasing={{0}: (3, {}), {1}: (4, {})} | custom-call | flops 4600000000 | bytes 1024 | tf_op jit(solution)/shard_map/pallas_call | solution.py:154
  29.3 1.6 %collective-permute-start.5 = (f32[32,2560]{1,0:T(8,128)S(1)}, f32[32,2560]{1,0:T(8,128)S(1)}, u32[]{:S(2)}, u32[]{:S(2)}) collective-permute-start(f32[32,2560]{1,0:T(8,128)S(1)} %shard_map.97.refs_2_.refs_0_), channel_id=1, source_target_pairs={{0,2},{1,5},{2,0},{3,7},{4,6},{5,1},{6,4},{7,3},{8,10},{9,13},{10,... | collective-permute-start | bytes 983048 | tf_op jit(solution)/shard_map/ppermute | solution.py:97
  30.9 1.2 %collective-permute-done.1.refs_1_ = f32[32,1792]{1,0:T(8,128)S(1)} collective-permute-done((f32[32,1792]{1,0:T(8,128)S(1)}, f32[32,1792]{1,0:T(8,128)S(1)}, u32[]{:S(2)}, u32[]{:S(2)}) %collective-permute-start.1) | collective-permute-done | bytes 229408 | tf_op jit(solution)/shard_map/ppermute | solution.py:97
  32.8 3.7 %collective-permute-done.5.refs_1_ = f32[32,2560]{1,0:T(8,128)S(1)} collective-permute-done((f32[32,2560]{1,0:T(8,128)S(1)}, f32[32,2560]{1,0:T(8,128)S(1)}, u32[]{:S(2)}, u32[]{:S(2)}) %collective-permute-start.5) | collective-permute-done | bytes 327712 | tf_op jit(solution)/shard_map/ppermute | solution.py:97
  36.5 1.6 %collective-permute-start.8 = (f32[32,2560]{1,0:T(8,128)S(1)}, f32[32,2560]{1,0:T(8,128)S(1)}, u32[]{:S(2)}, u32[]{:S(2)}) collective-permute-start(f32[32,2560]{1,0:T(8,128)S(1)} %shard_map.99.refs_3_.refs_0_), channel_id=1, source_target_pairs={{0,4},{1,3},{2,6},{3,1},{4,0},{5,7},{6,2},{7,5},{8,12},{9,11},{10,... | collective-permute-start | bytes 983048 | tf_op jit(solution)/shard_map/ppermute | solution.py:97
  38.2 2.5 %collective-permute-done.4.refs_1_ = f32[32,1792]{1,0:T(8,128)S(1)} collective-permute-done((f32[32,1792]{1,0:T(8,128)S(1)}, f32[32,1792]{1,0:T(8,128)S(1)}, u32[]{:S(2)}, u32[]{:S(2)}) %collective-permute-start.4) | collective-permute-done | bytes 229408 | tf_op jit(solution)/shard_map/ppermute | solution.py:97
  40.7 5.2 %shard_map.100 = (f32[32,2688]{1,0:T(8,128)S(1)}, f32[32,1280]{1,0:T(8,128)S(1)}, f32[32,1408]{1,0:T(8,128)S(1)}, f32[64,1792]{1,0:T(8,128)S(1)}) custom-call(f32[32,1792]{1,0:T(8,128)S(1)} %shard_map.98.refs_2_.refs_0_, f32[32,1792]{1,0:T(8,128)S(1)} %collective-permute-done.4.refs_1_, bf16[2560,1792]{1,0:T(8,128)(2,1)S(1)} %get-tuple-element.41.refs_2_.refs_5_, ...), custom_call_target="tpu_custom_call" | custom-call | flops 5750000128 | bytes 1024 | tf_op jit(solution)/shard_map/pallas_call | solution.py:154
  47.7 1.5 %collective-permute-start.13 = (f32[32,2560]{1,0:T(8,128)S(1)}, f32[32,2560]{1,0:T(8,128)S(1)}, u32[]{:S(2)}, u32[]{:S(2)}) collective-permute-start(f32[32,2560]{1,0:T(8,128)S(1)} %get-tuple-element.49.refs_5_.refs_0_), channel_id=1, source_target_pairs={{0,2},{1,5},{2,0},{3,7},{4,6},{5,1},{6,4},{7,3},{8,10},{9,13},{10,... | collective-permute-start | bytes 983048 | tf_op jit(solution)/shard_map/ppermute | solution.py:97
  49.3 3.2 %shard_map.103 = (f32[32,1792]{1,0:T(8,128)S(1)}, f32[32,1792]{1,0:T(8,128)S(1)}, f32[64,64]{1,0:T(8,128)S(1)}, f32[64,2560]{1,0:T(8,128)S(1)}) custom-call(f32[32,1280]{1,0:T(8,128)S(1)} %get-tuple-element.45.refs_3_.refs_0_, f32[32,1280]{1,0:T(8,128)S(1)} %get-tuple-element.47.refs_1_, f32[32,1280]{1,0:T(8,128)S(1)} %collective-permute-done.10.refs_2_, ...), custom_call_target="tpu_custom_call" | custom-call | flops 4600000000 | bytes 1024 | tf_op jit(solution)/shard_map/pallas_call | solution.py:154
  52.5 2.0 %collective-permute-start.14 = (f32[32,1792]{1,0:T(8,128)S(1)}, f32[32,1792]{1,0:T(8,128)S(1)}, u32[]{:S(2)}, u32[]{:S(2)}) collective-permute-start(f32[32,1792]{1,0:T(8,128)S(1)} %get-tuple-element.55), channel_id=1, source_target_pairs={{0,4},{1,5},{2,6},{3,7},{4,0},{5,1},{6,2},{7,3},{8,12},{9,13},{10,... | collective-permute-start | bytes 688136 | tf_op jit(solution)/shard_map/ppermute | solution.py:97
  54.9 2.0 %collective-permute-start.16 = (f32[32,2560]{1,0:T(8,128)S(1)}, f32[32,2560]{1,0:T(8,128)S(1)}, u32[]{:S(2)}, u32[]{:S(2)}) collective-permute-start(f32[32,2560]{1,0:T(8,128)S(1)} %shard_map.104.refs_6_.refs_0_), channel_id=1, source_target_pairs={{0,4},{1,3},{2,6},{3,1},{4,0},{5,7},{6,2},{7,5},{8,12},{9,11},{10,... | collective-permute-start | bytes 983048 | tf_op jit(solution)/shard_map/ppermute | solution.py:97
  56.9 1.5 %collective-permute-start.9 = (f32[32,128]{1,0:T(8,128)S(1)}, f32[32,128]{1,0:T(8,128)S(1)}, u32[]{:S(2)}, u32[]{:S(2)}) collective-permute-start(f32[32,128]{1,0:T(8,128)S(1)} %get-tuple-element.46.refs_0_), channel_id=1, source_target_pairs={{0,2},{1,3},{2,0},{3,1},{4,6},{5,7},{6,4},{7,5},{8,10},{9,11},{10,... | collective-permute-start | bytes 49160 | tf_op jit(solution)/shard_map/ppermute | solution.py:97
  58.4 1.8 %collective-permute-start.12 = (f32[64,64]{1,0:T(8,128)S(1)}, f32[64,64]{1,0:T(8,128)S(1)}, u32[]{:S(2)}, u32[]{:S(2)}) collective-permute-start(f32[64,64]{1,0:T(8,128)S(1)} %get-tuple-element.50.refs_2_), channel_id=1, source_target_pairs={{0,8},{1,9},{2,10},{3,11},{4,12},{5,13},{6,14},{7,15},{8,0},{9,1},... | collective-permute-start | bytes 49160 | tf_op jit(solution)/shard_map/ppermute | solution.py:97
  60.8 2.4 %collective-permute-done.12.refs_3_ = f32[64,64]{1,0:T(8,128)S(1)} collective-permute-done((f32[64,64]{1,0:T(8,128)S(1)}, f32[64,64]{1,0:T(8,128)S(1)}, u32[]{:S(2)}, u32[]{:S(2)}) %collective-permute-start.12) | collective-permute-done | bytes 16416 | tf_op jit(solution)/shard_map/ppermute | solution.py:97
  63.3 5.0 %shard_map.105 = (bf16[256,1792]{1,0:T(8,128)(2,1)S(1)}, bf16[2560,256]{1,0:T(8,128)(2,1)S(1)}) custom-call(f32[32,128]{1,0:T(8,128)S(1)} %get-tuple-element.46.refs_0_, f32[32,128]{1,0:T(8,128)S(1)} %collective-permute-done.9.refs_1_, f32[64,64]{1,0:T(8,128)S(1)} %get-tuple-element.50.refs_2_, f32[64,64]{1,0:T(8,128)S(1)} %collective-permute-done.12.refs_3_, ...), custom_call_target="tpu_custom_call" | custom-call | flops 575000000 | bytes 1024 | tf_op jit(solution)/shard_map/pallas_call | solution.py:154
  68.4 3.2 %collective-permute-start.15 = (f32[32,1792]{1,0:T(8,128)S(1)}, f32[32,1792]{1,0:T(8,128)S(1)}, u32[]{:S(2)}, u32[]{:S(2)}) collective-permute-start(f32[32,1792]{1,0:T(8,128)S(1)} %shard_map.106.refs_2_.refs_0_), channel_id=1, source_target_pairs={{0,8},{1,9},{2,10},{3,11},{4,12},{5,13},{6,14},{7,15},{8,0},{9,1},... | collective-permute-start | bytes 688136 | tf_op jit(solution)/shard_map/ppermute | solution.py:97
  72.1 0.9 collective-permute-done.17.refs_3_
  73.3 7.0 %shard_map.108 = (bf16[2560,1792]{1,0:T(8,128)(2,1)}, bf16[1280,1792]{1,0:T(8,128)(2,1)}, f32[8,128]{1,0:T(8,128)S(1)}) custom-call(bf16[256,1792]{1,0:T(8,128)(2,1)S(1)} %get-tuple-element.56.refs_2_.refs_0_, f32[32,1280]{1,0:T(8,128)S(1)} %get-tuple-element.57.refs_1_, f32[32,1280]{1,0:T(8,128)S(1)} %get-tuple-element.58.refs_2_, ...), custom_call_target="tpu_custom_call" | custom-call | flops 345000000 | bytes 1024 | tf_op jit(solution)/shard_map/pallas_call | solution.py:154
  80.6 7.6 %collective-permute-done.19.refs_2_ = f32[32,1792]{1,0:T(8,128)S(1)} collective-permute-done((f32[32,1792]{1,0:T(8,128)S(1)}, f32[32,1792]{1,0:T(8,128)S(1)}, u32[]{:S(2)}, u32[]{:S(2)}) %collective-permute-start.19) | collective-permute-done | bytes 229408 | tf_op jit(solution)/shard_map/ppermute | solution.py:97
  88.2 7.3 %shard_map.110 = (bf16[2560,1792]{1,0:T(8,128)(2,1)}, bf16[1280,1792]{1,0:T(8,128)(2,1)}, f32[8,128]{1,0:T(8,128)}) custom-call(bf16[2560,256]{1,0:T(8,128)(2,1)S(1)} %get-tuple-element.53.refs_0_, f32[32,1792]{1,0:T(8,128)S(1)} %shard_map.109.refs_1_, f32[32,1792]{1,0:T(8,128)S(1)} %collective-permute-done.19.refs_2_, ...), custom_call_target="tpu_custom_call" | custom-call | flops 9200000000 | bytes 1024 | tf_op jit(solution)/shard_map/pallas_call | solution.py:154
  (34 shorter events, 6.6 us)
Async XLA Ops:
  10.7 8.6 %collective-permute-start = (f32[32,1792]{1,0:T(8,128)S(1)}, f32[32,1792]{1,0:T(8,128)S(1)}, u32[]{:S(2)}, u32[]{:S(2)}) collective-permute-start(f32[32,1792]{1,0:T(8,128)S(1)} %get-tuple-element.35), channel_id=1, source_target_pairs={{0,4},{1,5},{2,6},{3,7},{4,0},{5,1},{6,2},{7,3},{8,12},{9,13},{10,... | collective-permute-start | bytes 688136 | tf_op jit(solution)/shard_map/ppermute | solution.py:97
  19.3 12.8 %collective-permute-start.1 = (f32[32,1792]{1,0:T(8,128)S(1)}, f32[32,1792]{1,0:T(8,128)S(1)}, u32[]{:S(2)}, u32[]{:S(2)}) collective-permute-start(f32[32,1792]{1,0:T(8,128)S(1)} %shard_map.95.refs_5_.refs_0_), channel_id=1, source_target_pairs={{0,8},{1,9},{2,10},{3,11},{4,12},{5,13},{6,14},{7,15},{8,0},{9,1},... | collective-permute-start | bytes 688136 | tf_op jit(solution)/shard_map/ppermute | solution.py:97
  27.6 1.5 %collective-permute-start.2 = (f32[32,1280]{1,0:T(8,128)S(1)}, f32[32,1280]{1,0:T(8,128)S(1)}, u32[]{:S(2)}, u32[]{:S(2)}) collective-permute-start(f32[32,1280]{1,0:T(8,128)S(1)} %get-tuple-element.39), channel_id=1, source_target_pairs={{0,1},{1,0},{2,3},{3,2},{4,5},{5,4},{6,7},{7,6},{8,9},{9,8},{10,11... | collective-permute-start | bytes 491528 | tf_op jit(solution)/shard_map/ppermute | solution.py:97
  27.7 1.6 %collective-permute-start.3 = (f32[32,1280]{1,0:T(8,128)S(1)}, f32[32,1280]{1,0:T(8,128)S(1)}, u32[]{:S(2)}, u32[]{:S(2)}) collective-permute-start(f32[32,1280]{1,0:T(8,128)S(1)} %get-tuple-element.40), channel_id=1, source_target_pairs={{0,1},{1,0},{2,3},{3,2},{4,5},{5,4},{6,7},{7,6},{8,9},{9,8},{10,11... | collective-permute-start | bytes 491528 | tf_op jit(solution)/shard_map/ppermute | solution.py:97
  29.3 7.1 %collective-permute-start.5 = (f32[32,2560]{1,0:T(8,128)S(1)}, f32[32,2560]{1,0:T(8,128)S(1)}, u32[]{:S(2)}, u32[]{:S(2)}) collective-permute-start(f32[32,2560]{1,0:T(8,128)S(1)} %shard_map.97.refs_2_.refs_0_), channel_id=1, source_target_pairs={{0,2},{1,5},{2,0},{3,7},{4,6},{5,1},{6,4},{7,3},{8,10},{9,13},{10,... | collective-permute-start | bytes 983048 | tf_op jit(solution)/shard_map/ppermute | solution.py:97
  32.1 8.6 %collective-permute-start.4 = (f32[32,1792]{1,0:T(8,128)S(1)}, f32[32,1792]{1,0:T(8,128)S(1)}, u32[]{:S(2)}, u32[]{:S(2)}) collective-permute-start(f32[32,1792]{1,0:T(8,128)S(1)} %shard_map.98.refs_2_.refs_0_), channel_id=1, source_target_pairs={{0,4},{1,5},{2,6},{3,7},{4,0},{5,1},{6,2},{7,3},{8,12},{9,13},{10,... | collective-permute-start | bytes 688136 | tf_op jit(solution)/shard_map/ppermute | solution.py:97
  36.5 10.0 %collective-permute-start.8 = (f32[32,2560]{1,0:T(8,128)S(1)}, f32[32,2560]{1,0:T(8,128)S(1)}, u32[]{:S(2)}, u32[]{:S(2)}) collective-permute-start(f32[32,2560]{1,0:T(8,128)S(1)} %shard_map.99.refs_3_.refs_0_), channel_id=1, source_target_pairs={{0,4},{1,3},{2,6},{3,1},{4,0},{5,7},{6,2},{7,5},{8,12},{9,11},{10,... | collective-permute-start | bytes 983048 | tf_op jit(solution)/shard_map/ppermute | solution.py:97
  45.9 1.7 %collective-permute-start.7 = (f32[32,1408]{1,0:T(8,128)S(1)}, f32[32,1408]{1,0:T(8,128)S(1)}, u32[]{:S(2)}, u32[]{:S(2)}) collective-permute-start(f32[32,1408]{1,0:T(8,128)S(1)} %get-tuple-element.44), channel_id=1, source_target_pairs={{0,1},{1,0},{2,3},{3,2},{4,5},{5,4},{6,7},{7,6},{8,9},{9,8},{10,11... | collective-permute-start | bytes 540680 | tf_op jit(solution)/shard_map/ppermute | solution.py:97
  46.1 1.6 %collective-permute-start.6 = (f32[32,1280]{1,0:T(8,128)S(1)}, f32[32,1280]{1,0:T(8,128)S(1)}, u32[]{:S(2)}, u32[]{:S(2)}) collective-permute-start(f32[32,1280]{1,0:T(8,128)S(1)} %get-tuple-element.43), channel_id=1, source_target_pairs={{0,1},{1,0},{2,3},{3,2},{4,5},{5,4},{6,7},{7,6},{8,9},{9,8},{10,11... | collective-permute-start | bytes 491528 | tf_op jit(solution)/shard_map/ppermute | solution.py:97
  46.6 2.7 %collective-permute-start.11 = (f32[32,1280]{1,0:T(8,128)S(1)}, f32[32,1280]{1,0:T(8,128)S(1)}, u32[]{:S(2)}, u32[]{:S(2)}) collective-permute-start(f32[32,1280]{1,0:T(8,128)S(1)} %get-tuple-element.47.refs_1_), channel_id=1, source_target_pairs={{0,1},{1,0},{2,3},{3,2},{4,5},{5,4},{6,7},{7,6},{8,9},{9,8},{10,11... | collective-permute-start | bytes 491528 | tf_op jit(solution)/shard_map/ppermute | solution.py:97
  46.7 2.5 %collective-permute-start.10 = (f32[32,1280]{1,0:T(8,128)S(1)}, f32[32,1280]{1,0:T(8,128)S(1)}, u32[]{:S(2)}, u32[]{:S(2)}) collective-permute-start(f32[32,1280]{1,0:T(8,128)S(1)} %get-tuple-element.45.refs_3_.refs_0_), channel_id=1, source_target_pairs={{0,1},{1,0},{2,3},{3,2},{4,5},{5,4},{6,7},{7,6},{8,9},{9,8},{10,11... | collective-permute-start | bytes 491528 | tf_op jit(solution)/shard_map/ppermute | solution.py:97
  47.7 7.1 %collective-permute-start.13 = (f32[32,2560]{1,0:T(8,128)S(1)}, f32[32,2560]{1,0:T(8,128)S(1)}, u32[]{:S(2)}, u32[]{:S(2)}) collective-permute-start(f32[32,2560]{1,0:T(8,128)S(1)} %get-tuple-element.49.refs_5_.refs_0_), channel_id=1, source_target_pairs={{0,2},{1,5},{2,0},{3,7},{4,6},{5,1},{6,4},{7,3},{8,10},{9,13},{10,... | collective-permute-start | bytes 983048 | tf_op jit(solution)/shard_map/ppermute | solution.py:97
  52.5 15.8 %collective-permute-start.14 = (f32[32,1792]{1,0:T(8,128)S(1)}, f32[32,1792]{1,0:T(8,128)S(1)}, u32[]{:S(2)}, u32[]{:S(2)}) collective-permute-start(f32[32,1792]{1,0:T(8,128)S(1)} %get-tuple-element.55), channel_id=1, source_target_pairs={{0,4},{1,5},{2,6},{3,7},{4,0},{5,1},{6,2},{7,3},{8,12},{9,13},{10,... | collective-permute-start | bytes 688136 | tf_op jit(solution)/shard_map/ppermute | solution.py:97
  54.9 16.6 %collective-permute-start.16 = (f32[32,2560]{1,0:T(8,128)S(1)}, f32[32,2560]{1,0:T(8,128)S(1)}, u32[]{:S(2)}, u32[]{:S(2)}) collective-permute-start(f32[32,2560]{1,0:T(8,128)S(1)} %shard_map.104.refs_6_.refs_0_), channel_id=1, source_target_pairs={{0,4},{1,3},{2,6},{3,1},{4,0},{5,7},{6,2},{7,5},{8,12},{9,11},{10,... | collective-permute-start | bytes 983048 | tf_op jit(solution)/shard_map/ppermute | solution.py:97
  56.9 4.0 %collective-permute-start.9 = (f32[32,128]{1,0:T(8,128)S(1)}, f32[32,128]{1,0:T(8,128)S(1)}, u32[]{:S(2)}, u32[]{:S(2)}) collective-permute-start(f32[32,128]{1,0:T(8,128)S(1)} %get-tuple-element.46.refs_0_), channel_id=1, source_target_pairs={{0,2},{1,3},{2,0},{3,1},{4,6},{5,7},{6,4},{7,5},{8,10},{9,11},{10,... | collective-permute-start | bytes 49160 | tf_op jit(solution)/shard_map/ppermute | solution.py:97
  58.4 4.9 %collective-permute-start.12 = (f32[64,64]{1,0:T(8,128)S(1)}, f32[64,64]{1,0:T(8,128)S(1)}, u32[]{:S(2)}, u32[]{:S(2)}) collective-permute-start(f32[64,64]{1,0:T(8,128)S(1)} %get-tuple-element.50.refs_2_), channel_id=1, source_target_pairs={{0,8},{1,9},{2,10},{3,11},{4,12},{5,13},{6,14},{7,15},{8,0},{9,1},... | collective-permute-start | bytes 49160 | tf_op jit(solution)/shard_map/ppermute | solution.py:97
  68.4 11.9 %collective-permute-start.15 = (f32[32,1792]{1,0:T(8,128)S(1)}, f32[32,1792]{1,0:T(8,128)S(1)}, u32[]{:S(2)}, u32[]{:S(2)}) collective-permute-start(f32[32,1792]{1,0:T(8,128)S(1)} %shard_map.106.refs_2_.refs_0_), channel_id=1, source_target_pairs={{0,8},{1,9},{2,10},{3,11},{4,12},{5,13},{6,14},{7,15},{8,0},{9,1},... | collective-permute-start | bytes 688136 | tf_op jit(solution)/shard_map/ppermute | solution.py:97
  71.6 1.5 %collective-permute-start.17 = (f32[32,1280]{1,0:T(8,128)S(1)}, f32[32,1280]{1,0:T(8,128)S(1)}, u32[]{:S(2)}, u32[]{:S(2)}) collective-permute-start(f32[32,1280]{1,0:T(8,128)S(1)} %get-tuple-element.57.refs_1_), channel_id=1, source_target_pairs={{0,1},{1,0},{2,3},{3,2},{4,5},{5,4},{6,7},{7,6},{8,9},{9,8},{10,11... | collective-permute-start | bytes 491528 | tf_op jit(solution)/shard_map/ppermute | solution.py:97
  71.6 1.6 %collective-permute-start.18 = (f32[32,1280]{1,0:T(8,128)S(1)}, f32[32,1280]{1,0:T(8,128)S(1)}, u32[]{:S(2)}, u32[]{:S(2)}) collective-permute-start(f32[32,1280]{1,0:T(8,128)S(1)} %get-tuple-element.58.refs_2_), channel_id=1, source_target_pairs={{0,1},{1,0},{2,3},{3,2},{4,5},{5,4},{6,7},{7,6},{8,9},{9,8},{10,11... | collective-permute-start | bytes 491528 | tf_op jit(solution)/shard_map/ppermute | solution.py:97
  80.3 7.9 %collective-permute-start.19 = (f32[32,1792]{1,0:T(8,128)S(1)}, f32[32,1792]{1,0:T(8,128)S(1)}, u32[]{:S(2)}, u32[]{:S(2)}) collective-permute-start(f32[32,1792]{1,0:T(8,128)S(1)} %shard_map.109.refs_1_), channel_id=1, source_target_pairs={{0,4},{1,5},{2,6},{3,7},{4,0},{5,1},{6,2},{7,3},{8,12},{9,13},{10,... | collective-permute-start | bytes 688136 | tf_op jit(solution)/shard_map/ppermute | solution.py:97

commit v7 on v6

--- a/solution.py
+++ b/solution.py
@@ -10,8 +10,9 @@
 REPLICAS = 2
 RANK = 64
 TILE = 256
+THIN = 128
 FLOPS = 1.15e9
-WEIGHTS = (8.0, 4.0, 1.0, 4.0, 0.1, 5.0, 1.0, 5.0, 1.0, 1.0, 4.0, 0.2, 0.5, 1.0, 1.0, 0.3, 1.0, 8.0)
+WEIGHTS = (8.0, 4.0, 1.0, 4.0, 0.1, 5.0, 1.0, 5.0, 1.0, 1.0, 4.0, 0.1, 0.2, 1.0, 5.0, 1.0, 1.0, 8.0, 8.0)
 MIB = 1 << 20
 BF16 = jnp.bfloat16
 F32 = jnp.float32
@@ -230,8 +231,9 @@
         left, fixed = refs[:2]
 
         def step(g, e, start):
-            at = tile_at(first + pl.program_id(0))
-            term = jnp.zeros((TILE, RANK), F32)
+            i = first * TILE // THIN + pl.program_id(0)
+            at = pl.ds(pl.multiple_of(i * THIN, THIN), THIN)
+            term = jnp.zeros((THIN, RANK), F32)
             for j in range(0, cols, TILE):
                 here = slice(j, j + TILE)
                 c = g[:, here] + e[:, here]
@@ -239,9 +241,11 @@
                 term += lax.dot_general(c, start[:, here], NT, preferred_element_type=F32)
             left[:, at] = term.T
 
-        spec = pl.BlockSpec((TILE, cols), lambda i: (first + i, 0), pipeline_mode=pl.Buffered(3))
+        spec = pl.BlockSpec(
+            (THIN, cols), lambda i: (first * TILE // THIN + i, 0), pipeline_mode=pl.Buffered(4)
+        )
         whole = pl.BlockSpec((RANK, cols), lambda i: (0, 0))
-        pltpu.emit_pipeline(step, grid=(count,), in_specs=[spec, spec, whole])(grad, error, start)
+        pltpu.emit_pipeline(step, grid=(count * TILE // THIN,), in_specs=[spec, spec, whole])(grad, error, start)
         if last:
             halve(left, core_of(), refs[2], refs[3:])
 
@@ -276,7 +280,7 @@
                 fixed[at, here] = c
                 left[:, here] += jnp.dot(s[...], c, preferred_element_type=F32)
 
-        spec = pl.BlockSpec((TILE, cols), lambda i: (first + i, 0), pipeline_mode=pl.Buffered(3))
+        spec = pl.BlockSpec((TILE, cols), lambda i: (first + i, 0), pipeline_mode=pl.Buffered(4))
         part = pl.BlockSpec((RANK, TILE), lambda i: (0, block + i))
         pltpu.emit_pipeline(step, grid=(count,), in_specs=[spec, spec, part])(grad, error, start)
         if last:
@@ -290,7 +294,7 @@
     if before is not None:
         args += [(x, VMEM) for x in before]
         aliases = {3: 0, 4: 1}
-    return run(kernel, args, outs, mib=8, aliases=aliases, after=after)
+    return run(kernel, args, outs, mib=12, aliases=aliases, after=after)
 
 
 def load_left(owns, others, place, left, stack):
@@ -416,18 +420,25 @@
         turned[i : i + TILE, :] = stack[:, i : i + TILE].T
 
 
-def solve(run, grams_down, left_down, grams_gate, left_gate, after=()):
-    n_down, n_gate = len(grams_down), len(grams_gate)
+def gram_sums(run, packed, whole, after=()):
+    n = len(packed)
+
+    def kernel(*refs):
+        a = sum((ref[...] for ref in refs[1:n]), refs[0][...])
+        refs[-2][...] = jnp.concatenate([a[:, :RANK], a[:, RANK:]], axis=0)
+        refs[-1][...] = sum((ref[...] for ref in refs[n + 1 : -2]), refs[n][...])
+
+    outs = [((RANK, RANK), F32, VMEM)] * 2
+    return run(kernel, [(x, VMEM) for x in (*packed, *whole)], outs, mib=2, after=after)
+
+
+def solve(run, gram_down, left_down, gram_gate, left_gate, after=()):
     cols, rows = left_down.shape[1], left_gate.shape[1]
 
-    def kernel(*refs):
-        down, gate = refs[:n_down], refs[n_down : n_down + n_gate]
-        left_down, left_gate, col_stack, row_turned, col, row, row_stack = refs[n_down + n_gate :]
-        a = sum((ref[...] for ref in down[1:]), down[0][...])
-        a = jnp.concatenate([a[:, :RANK], a[:, RANK:]], axis=0)
-        b = sum((ref[...] for ref in gate[1:]), gate[0][...])
+    def kernel(gram_down, left_down, gram_gate, left_gate, col_stack, row_turned, col, row, row_stack):
+        grams = [gram_down[...], gram_gate[...]]
         for place, a, left, out in zip(
-            (core_of(), replica_of()), inverses([a, b]), (left_down, left_gate), (col, row)
+            (core_of(), replica_of()), inverses(grams), (left_down, left_gate), (col, row)
         ):
             other = jnp.concatenate([a[HALF:], a[:HALF]], axis=0)
             a = jnp.where(place == 0, a, other) * (1.0 / REPLICAS)
@@ -440,7 +451,7 @@
 
     return run(
         kernel,
-        [(x, VMEM) for x in (*grams_down, *grams_gate, left_down, left_gate)],
+        [(x, VMEM) for x in (gram_down, left_down, gram_gate, left_gate)],
         [((4 * RANK, cols), BF16, VMEM), ((rows, 4 * RANK), BF16, VMEM)],
         [
             pltpu.VMEM((RANK, cols), F32),
@@ -452,14 +463,13 @@
     )
 
 
-def rebuild(run, row_turned, col_stack, owns, others, fixed, after=()):
+def rebuild(run, row_turned, col_stack, owns, others, fixed, height, after=()):
     halves = [
         (x, half, sum(widths_of(xs[:i])))
         for half, xs in ((0, owns), (HALF, others))
         for i, x in enumerate(xs)
     ]
     rows, cols = fixed.shape
-    height = rows // REPLICAS // 2
     tiles = rows // REPLICAS // height
     rows_late = row_turned is None
     scratch = [pltpu.VMEM((4 * RANK, rows if rows_late else cols), BF16)]
@@ -566,26 +576,25 @@
     grams_gate = [gram_gate] + [
         exchange(gram_gate, lambda d, t, b=b: (d ^ b, t)) for b in range(REPLICAS, n_dp, REPLICAS)
     ]
+    gram_down, gram_gate = gram_sums(run, grams_down, grams_gate)
     for hop in hops[1:]:
         (down,) = add(run, [down], [got], after=(gram_gate,))
         got = exchange(down, hop)
-    col_stack, row_turned = solve(
-        run, grams_down, left_down, grams_gate, left_gate, after=(down,)
-    )
-    (gate,) = add(run, [keep_gate], [got_gate], after=(col_stack,))
+    (gate,) = add(run, [keep_gate], [got_gate], after=(down,))
     got_gate = exchange(gate, steps[0])
-    downs = add(run, [down], [got], in_two(slab), after=(gate,))
+    col_stack, row_turned = solve(run, gram_down, left_down, gram_gate, left_gate, after=(gate,))
+    downs = add(run, [down], [got], in_two(slab), after=(col_stack,))
     others_down = to_other_core(downs)
-    new_error_down, update_down, done = rebuild(
-        run, None, col_stack, downs, others_down, fixed_down
-    )
     for i in range(len(steps)):
-        (gate,) = add(run, [gate], [got_gate], after=(done,))
+        (gate,) = add(run, [gate], [got_gate], after=(downs[0],))
         if i + 1 < len(steps):
             got_gate = exchange(gate, steps[i + 1])
     other_gate = exchange(gate, other_replica)
+    new_error_down, update_down, done = rebuild(
+        run, None, col_stack, downs, others_down, fixed_down, slab // 8, after=(gate,)
+    )
     new_error_gate, update_gate, _ = rebuild(
-        run, row_turned, None, [gate], [other_gate], fixed_gate
+        run, row_turned, None, [gate], [other_gate], fixed_gate, slab // 4, after=(done,)
     )
     return (update_gate, update_down, new_error_gate, new_error_down)
 

time: 95.8 us -> 91.8 us (0.958)
  waiting for transfers between devices: 21.5 us -> 17.6 us
  starting transfers between devices: 24.2 us -> 21.4 us
  Pallas kernels: 49.1 us -> 51.6 us
    ppermute x20, waiting for transfers between devices: 21.5 us -> 17.6 us  [exchange(): return lax.ppermute(x, ('dp', 'tensor'), pairs)]
    ppermute x20, starting transfers between devices: 24.2 us -> 21.4 us  [exchange(): return lax.ppermute(x, ('dp', 'tensor'), pairs)]
    pallas_call x18 -> x19, Pallas kernels: 49.1 us -> 51.6 us  [__call__(): pl.pallas_call(body, out_shape=tuple(((pltpu.VMEM if spec is VMEM else pl...]
  transfers between devices with their start and end apart: 20 -> 20, of which waited for: 13 -> 9; matrix products, arithmetic and copies ran while one was open for 0% -> 0% of each run, Pallas kernels for 33% -> 37%
where the time goes in v7:
time: 91.8 us; the launch traced here: 91.4 us
  Pallas kernels  51.6 us (56%)
  starting transfers between devices  21.4 us (23%)
  waiting for transfers between devices  17.6 us (19%)
    pallas_call x19, Pallas kernels, __call__(): pl.pallas_call(body, out_shape=tuple(((pltpu.VMEM if spec is VMEM else pl...  51.6 us
    ppermute x20, starting transfers between devices, exchange(): return lax.ppermute(x, ('dp', 'tensor'), pairs)  21.4 us
    ppermute x20, waiting for transfers between devices, exchange(): return lax.ppermute(x, ('dp', 'tensor'), pairs)  17.6 us
  transfers between devices with their start and end apart: 20, of which 9 were waited for; matrix products, arithmetic and copies ran while one was open for 0% of the time, Pallas kernels for 37%

profile of v7, /device:TPU:0, one launch (start us, length us, event | category | flops | bytes accessed | tf_op | source)
XLA Modules:
  0.0 91.4 jit_solution(12053126093833658114)
XLA Ops:
  0.6 10.5 %shard_map.93 = (f32[64,1792]{1,0:T(8,128)}, bf16[2560,1792]{1,0:T(8,128)(2,1)S(1)}, f32[32,1792]{1,0:T(8,128)S(1)}, f32[32,1792]{1,0:T(8,128)S(1)}) custom-call(bf16[2560,1792]{1,0:T(8,128)(2,1)} %refs_0_.3, bf16[2560,1792]{1,0:T(8,128)(2,1)} %refs_1_.3, bf16[64,5120]{1,0:T(8,128)(2,1)} %refs_2_.3), custom_call_target="tpu_custom_call" | custom-call | flops 9200000000 | bytes 1024 | tf_op jit(solution)/shard_map/pallas_call | solution.py:155
  11.1 3.0 %collective-permute-start = (f32[32,1792]{1,0:T(8,128)S(1)}, f32[32,1792]{1,0:T(8,128)S(1)}, u32[]{:S(2)}, u32[]{:S(2)}) collective-permute-start(f32[32,1792]{1,0:T(8,128)S(1)} %get-tuple-element.37), channel_id=1, source_target_pairs={{0,4},{1,5},{2,6},{3,7},{4,0},{5,1},{6,2},{7,3},{8,12},{9,13},{10,... | collective-permute-start | bytes 688136 | tf_op jit(solution)/shard_map/ppermute | solution.py:98
  14.1 6.0 %shard_map.94 = (f32[64,2560]{1,0:T(8,128)S(1)}, bf16[2560,1792]{1,0:T(8,128)(2,1)S(1)}) custom-call(bf16[2560,1792]{1,0:T(8,128)(2,1)} %refs_0_.5, bf16[2560,1792]{1,0:T(8,128)(2,1)} %refs_1_.5, bf16[64,1792]{1,0:T(8,128)(2,1)} %refs_2_.5, f32[32,1792]{1,0:T(8,128)S(1)} %get-tuple-element.36.refs_3_.refs_0_), custom_call_target="tpu_custom_call" | custom-call | flops 4600000000 | bytes 1024 | tf_op jit(solution)/shard_map/pallas_call | solution.py:155
  20.1 2.6 %collective-permute-start.1 = (f32[32,1792]{1,0:T(8,128)S(1)}, f32[32,1792]{1,0:T(8,128)S(1)}, u32[]{:S(2)}, u32[]{:S(2)}) collective-permute-start(f32[32,1792]{1,0:T(8,128)S(1)} %shard_map.95.refs_5_.refs_0_), channel_id=1, source_target_pairs={{0,8},{1,9},{2,10},{3,11},{4,12},{5,13},{6,14},{7,15},{8,0},{9,1},... | collective-permute-start | bytes 688136 | tf_op jit(solution)/shard_map/ppermute | solution.py:98
  22.8 6.0 %shard_map.96 = (f32[64,2560]{1,0:T(8,128)S(1)}, bf16[2560,1792]{1,0:T(8,128)(2,1)S(1)}, f32[32,2560]{1,0:T(8,128)S(1)}, f32[32,1280]{1,0:T(8,128)S(1)}, f32[32,1280]{1,0:T(8,128)S(1)}) custom-call(bf16[2560,1792]{1,0:T(8,128)(2,1)} %refs_0_.5, bf16[2560,1792]{1,0:T(8,128)(2,1)} %refs_1_.5, ...), custom_call_target="tpu_custom_call", output_to_operand_aliasing={{0}: (3, {}), {1}: (4, {})} | custom-call | flops 4600000000 | bytes 1024 | tf_op jit(solution)/shard_map/pallas_call | solution.py:155
  29.4 0.9 collective-permute-done.2.refs_1_
  30.5 1.5 %collective-permute-start.5 = (f32[32,2560]{1,0:T(8,128)S(1)}, f32[32,2560]{1,0:T(8,128)S(1)}, u32[]{:S(2)}, u32[]{:S(2)}) collective-permute-start(f32[32,2560]{1,0:T(8,128)S(1)} %shard_map.97.refs_2_.refs_0_), channel_id=1, source_target_pairs={{0,2},{1,5},{2,0},{3,7},{4,6},{5,1},{6,4},{7,3},{8,10},{9,13},{10,... | collective-permute-start | bytes 983048 | tf_op jit(solution)/shard_map/ppermute | solution.py:98
  32.1 1.0 %collective-permute-done.1.refs_1_ = f32[32,1792]{1,0:T(8,128)S(1)} collective-permute-done((f32[32,1792]{1,0:T(8,128)S(1)}, f32[32,1792]{1,0:T(8,128)S(1)}, u32[]{:S(2)}, u32[]{:S(2)}) %collective-permute-start.1) | collective-permute-done | bytes 229408 | tf_op jit(solution)/shard_map/ppermute | solution.py:98
  33.5 4.1 %collective-permute-done.5.refs_1_ = f32[32,2560]{1,0:T(8,128)S(1)} collective-permute-done((f32[32,2560]{1,0:T(8,128)S(1)}, f32[32,2560]{1,0:T(8,128)S(1)}, u32[]{:S(2)}, u32[]{:S(2)}) %collective-permute-start.5) | collective-permute-done | bytes 327712 | tf_op jit(solution)/shard_map/ppermute | solution.py:98
  37.7 1.4 %collective-permute-start.8 = (f32[32,2560]{1,0:T(8,128)S(1)}, f32[32,2560]{1,0:T(8,128)S(1)}, u32[]{:S(2)}, u32[]{:S(2)}) collective-permute-start(f32[32,2560]{1,0:T(8,128)S(1)} %shard_map.99.refs_3_.refs_0_), channel_id=1, source_target_pairs={{0,4},{1,3},{2,6},{3,1},{4,0},{5,7},{6,2},{7,5},{8,12},{9,11},{10,... | collective-permute-start | bytes 983048 | tf_op jit(solution)/shard_map/ppermute | solution.py:98
  39.1 2.6 %collective-permute-done.4.refs_1_ = f32[32,1792]{1,0:T(8,128)S(1)} collective-permute-done((f32[32,1792]{1,0:T(8,128)S(1)}, f32[32,1792]{1,0:T(8,128)S(1)}, u32[]{:S(2)}, u32[]{:S(2)}) %collective-permute-start.4) | collective-permute-done | bytes 229408 | tf_op jit(solution)/shard_map/ppermute | solution.py:98
  41.7 5.2 %shard_map.100 = (f32[32,2688]{1,0:T(8,128)S(1)}, f32[32,1280]{1,0:T(8,128)S(1)}, f32[32,1408]{1,0:T(8,128)S(1)}, f32[64,1792]{1,0:T(8,128)S(1)}) custom-call(f32[32,1792]{1,0:T(8,128)S(1)} %shard_map.98.refs_2_.refs_0_, f32[32,1792]{1,0:T(8,128)S(1)} %collective-permute-done.4.refs_1_, bf16[2560,1792]{1,0:T(8,128)(2,1)S(1)} %get-tuple-element.43.refs_2_.refs_5_, ...), custom_call_target="tpu_custom_call" | custom-call | flops 5750000128 | bytes 1024 | tf_op jit(solution)/shard_map/pallas_call | solution.py:155
  48.9 1.5 %collective-permute-start.14 = (f32[32,2560]{1,0:T(8,128)S(1)}, f32[32,2560]{1,0:T(8,128)S(1)}, u32[]{:S(2)}, u32[]{:S(2)}) collective-permute-start(f32[32,2560]{1,0:T(8,128)S(1)} %get-tuple-element.51.refs_5_.refs_0_), channel_id=1, source_target_pairs={{0,2},{1,5},{2,0},{3,7},{4,6},{5,1},{6,4},{7,3},{8,10},{9,13},{10,... | collective-permute-start | bytes 983048 | tf_op jit(solution)/shard_map/ppermute | solution.py:98
  50.4 3.2 %shard_map.103 = (f32[32,1792]{1,0:T(8,128)S(1)}, f32[32,1792]{1,0:T(8,128)S(1)}, f32[64,64]{1,0:T(8,128)S(1)}, f32[64,2560]{1,0:T(8,128)S(1)}) custom-call(f32[32,1280]{1,0:T(8,128)S(1)} %get-tuple-element.47.refs_3_.refs_0_, f32[32,1280]{1,0:T(8,128)S(1)} %get-tuple-element.49.refs_1_, f32[32,1280]{1,0:T(8,128)S(1)} %collective-permute-done.10.refs_2_, ...), custom_call_target="tpu_custom_call" | custom-call | flops 4600000000 | bytes 1024 | tf_op jit(solution)/shard_map/pallas_call | solution.py:155
  53.7 1.8 %collective-permute-start.13 = (f32[32,1792]{1,0:T(8,128)S(1)}, f32[32,1792]{1,0:T(8,128)S(1)}, u32[]{:S(2)}, u32[]{:S(2)}) collective-permute-start(f32[32,1792]{1,0:T(8,128)S(1)} %get-tuple-element.58), channel_id=1, source_target_pairs={{0,4},{1,5},{2,6},{3,7},{4,0},{5,1},{6,2},{7,3},{8,12},{9,13},{10,... | collective-permute-start | bytes 688136 | tf_op jit(solution)/shard_map/ppermute | solution.py:98
  56.0 1.3 %collective-permute-start.12 = (f32[64,64]{1,0:T(8,128)S(1)}, f32[64,64]{1,0:T(8,128)S(1)}, u32[]{:S(2)}, u32[]{:S(2)}) collective-permute-start(f32[64,64]{1,0:T(8,128)S(1)} %get-tuple-element.52.refs_2_), channel_id=1, source_target_pairs={{0,8},{1,9},{2,10},{3,11},{4,12},{5,13},{6,14},{7,15},{8,0},{9,1},... | collective-permute-start | bytes 49160 | tf_op jit(solution)/shard_map/ppermute | solution.py:98
  57.3 1.9 %collective-permute-done.9.refs_1_ = f32[32,128]{1,0:T(8,128)S(1)} collective-permute-done((f32[32,128]{1,0:T(8,128)S(1)}, f32[32,128]{1,0:T(8,128)S(1)}, u32[]{:S(2)}, u32[]{:S(2)}) %collective-permute-start.9) | collective-permute-done | bytes 16416 | tf_op jit(solution)/shard_map/ppermute | solution.py:98
  59.2 1.7 %collective-permute-done.12.refs_3_ = f32[64,64]{1,0:T(8,128)S(1)} collective-permute-done((f32[64,64]{1,0:T(8,128)S(1)}, f32[64,64]{1,0:T(8,128)S(1)}, u32[]{:S(2)}, u32[]{:S(2)}) %collective-permute-start.12) | collective-permute-done | bytes 16416 | tf_op jit(solution)/shard_map/ppermute | solution.py:98
  61.0 2.6 %collective-permute-start.16 = (f32[32,2560]{1,0:T(8,128)S(1)}, f32[32,2560]{1,0:T(8,128)S(1)}, u32[]{:S(2)}, u32[]{:S(2)}) collective-permute-start(f32[32,2560]{1,0:T(8,128)S(1)} %shard_map.105.refs_2_.refs_0_), channel_id=1, source_target_pairs={{0,4},{1,3},{2,6},{3,1},{4,0},{5,7},{6,2},{7,5},{8,12},{9,11},{10,... | collective-permute-start | bytes 983048 | tf_op jit(solution)/shard_map/ppermute | solution.py:98
  64.1 5.0 %shard_map.107 = (bf16[256,1792]{1,0:T(8,128)(2,1)S(1)}, bf16[2560,256]{1,0:T(8,128)(2,1)S(1)}) custom-call(f32[64,64]{1,0:T(8,128)S(1)} %get-tuple-element.53.refs_0_, f32[64,1792]{1,0:T(8,128)S(1)} %get-tuple-element.54.refs_1_, f32[64,64]{1,0:T(8,128)S(1)} %get-tuple-element.55.refs_2_, f32[64,2560]{1,0:T(8,128)S(1)} %get-tuple-element.56.refs_3_, ...), custom_call_target="tpu_custom_call" | custom-call | flops 5750000128 | bytes 1024 | tf_op jit(solution)/shard_map/pallas_call | solution.py:155
  69.1 4.4 %collective-permute-done.16.refs_1_ = f32[32,2560]{1,0:T(8,128)S(1)} collective-permute-done((f32[32,2560]{1,0:T(8,128)S(1)}, f32[32,2560]{1,0:T(8,128)S(1)}, u32[]{:S(2)}, u32[]{:S(2)}) %collective-permute-start.16) | collective-permute-done | bytes 327712 | tf_op jit(solution)/shard_map/ppermute | solution.py:98
  74.2 1.8 %collective-permute-start.17 = (f32[32,1792]{1,0:T(8,128)S(1)}, f32[32,1792]{1,0:T(8,128)S(1)}, u32[]{:S(2)}, u32[]{:S(2)}) collective-permute-start(f32[32,1792]{1,0:T(8,128)S(1)} %shard_map.109.refs_6_.refs_1_), channel_id=1, source_target_pairs={{0,4},{1,5},{2,6},{3,7},{4,0},{5,1},{6,2},{7,3},{8,12},{9,13},{10,... | collective-permute-start | bytes 688136 | tf_op jit(solution)/shard_map/ppermute | solution.py:98
  76.1 8.0 %shard_map.110 = (bf16[2560,1792]{1,0:T(8,128)(2,1)}, bf16[1280,1792]{1,0:T(8,128)(2,1)}, f32[8,128]{1,0:T(8,128)S(1)}) custom-call(bf16[256,1792]{1,0:T(8,128)(2,1)S(1)} %get-tuple-element.60.refs_2_.refs_0_, f32[32,1280]{1,0:T(8,128)S(1)} %get-tuple-element.61.refs_2_.refs_1_, f32[32,1280]{1,0:T(8,128)S(1)} %get-tuple-element.62.refs_2_, ...), custom_call_target="tpu_custom_call" | custom-call | flops 9200000000 | bytes 1024 | tf_op jit(solution)/shard_map/pallas_call | solution.py:155
  84.1 7.3 %shard_map.111 = (bf16[2560,1792]{1,0:T(8,128)(2,1)}, bf16[1280,1792]{1,0:T(8,128)(2,1)}, f32[8,128]{1,0:T(8,128)}) custom-call(bf16[2560,256]{1,0:T(8,128)(2,1)S(1)} %get-tuple-element.59.refs_0_, f32[32,1792]{1,0:T(8,128)S(1)} %shard_map.109.refs_6_.refs_1_, f32[32,1792]{1,0:T(8,128)S(1)} %collective-permute-done.17.refs_2_, ...), custom_call_target="tpu_custom_call" | custom-call | flops 9200000000 | bytes 1024 | tf_op jit(solution)/shard_map/pallas_call | solution.py:155
  (35 shorter events, 5.1 us)
Async XLA Ops:
  11.1 9.0 %collective-permute-start = (f32[32,1792]{1,0:T(8,128)S(1)}, f32[32,1792]{1,0:T(8,128)S(1)}, u32[]{:S(2)}, u32[]{:S(2)}) collective-permute-start(f32[32,1792]{1,0:T(8,128)S(1)} %get-tuple-element.37), channel_id=1, source_target_pairs={{0,4},{1,5},{2,6},{3,7},{4,0},{5,1},{6,2},{7,3},{8,12},{9,13},{10,... | collective-permute-start | bytes 688136 | tf_op jit(solution)/shard_map/ppermute | solution.py:98
  20.1 12.9 %collective-permute-start.1 = (f32[32,1792]{1,0:T(8,128)S(1)}, f32[32,1792]{1,0:T(8,128)S(1)}, u32[]{:S(2)}, u32[]{:S(2)}) collective-permute-start(f32[32,1792]{1,0:T(8,128)S(1)} %shard_map.95.refs_5_.refs_0_), channel_id=1, source_target_pairs={{0,8},{1,9},{2,10},{3,11},{4,12},{5,13},{6,14},{7,15},{8,0},{9,1},... | collective-permute-start | bytes 688136 | tf_op jit(solution)/shard_map/ppermute | solution.py:98
  28.8 1.5 %collective-permute-start.2 = (f32[32,1280]{1,0:T(8,128)S(1)}, f32[32,1280]{1,0:T(8,128)S(1)}, u32[]{:S(2)}, u32[]{:S(2)}) collective-permute-start(f32[32,1280]{1,0:T(8,128)S(1)} %get-tuple-element.41), channel_id=1, source_target_pairs={{0,1},{1,0},{2,3},{3,2},{4,5},{5,4},{6,7},{7,6},{8,9},{9,8},{10,11... | collective-permute-start | bytes 491528 | tf_op jit(solution)/shard_map/ppermute | solution.py:98
  28.9 1.6 %collective-permute-start.3 = (f32[32,1280]{1,0:T(8,128)S(1)}, f32[32,1280]{1,0:T(8,128)S(1)}, u32[]{:S(2)}, u32[]{:S(2)}) collective-permute-start(f32[32,1280]{1,0:T(8,128)S(1)} %get-tuple-element.42), channel_id=1, source_target_pairs={{0,1},{1,0},{2,3},{3,2},{4,5},{5,4},{6,7},{7,6},{8,9},{9,8},{10,11... | collective-permute-start | bytes 491528 | tf_op jit(solution)/shard_map/ppermute | solution.py:98
  30.5 7.1 %collective-permute-start.5 = (f32[32,2560]{1,0:T(8,128)S(1)}, f32[32,2560]{1,0:T(8,128)S(1)}, u32[]{:S(2)}, u32[]{:S(2)}) collective-permute-start(f32[32,2560]{1,0:T(8,128)S(1)} %shard_map.97.refs_2_.refs_0_), channel_id=1, source_target_pairs={{0,2},{1,5},{2,0},{3,7},{4,6},{5,1},{6,4},{7,3},{8,10},{9,13},{10,... | collective-permute-start | bytes 983048 | tf_op jit(solution)/shard_map/ppermute | solution.py:98
  33.1 8.6 %collective-permute-start.4 = (f32[32,1792]{1,0:T(8,128)S(1)}, f32[32,1792]{1,0:T(8,128)S(1)}, u32[]{:S(2)}, u32[]{:S(2)}) collective-permute-start(f32[32,1792]{1,0:T(8,128)S(1)} %shard_map.98.refs_2_.refs_0_), channel_id=1, source_target_pairs={{0,4},{1,5},{2,6},{3,7},{4,0},{5,1},{6,2},{7,3},{8,12},{9,13},{10,... | collective-permute-start | bytes 688136 | tf_op jit(solution)/shard_map/ppermute | solution.py:98
  37.7 9.9 %collective-permute-start.8 = (f32[32,2560]{1,0:T(8,128)S(1)}, f32[32,2560]{1,0:T(8,128)S(1)}, u32[]{:S(2)}, u32[]{:S(2)}) collective-permute-start(f32[32,2560]{1,0:T(8,128)S(1)} %shard_map.99.refs_3_.refs_0_), channel_id=1, source_target_pairs={{0,4},{1,3},{2,6},{3,1},{4,0},{5,7},{6,2},{7,5},{8,12},{9,11},{10,... | collective-permute-start | bytes 983048 | tf_op jit(solution)/shard_map/ppermute | solution.py:98
  46.9 1.9 %collective-permute-start.7 = (f32[32,1408]{1,0:T(8,128)S(1)}, f32[32,1408]{1,0:T(8,128)S(1)}, u32[]{:S(2)}, u32[]{:S(2)}) collective-permute-start(f32[32,1408]{1,0:T(8,128)S(1)} %get-tuple-element.46), channel_id=1, source_target_pairs={{0,1},{1,0},{2,3},{3,2},{4,5},{5,4},{6,7},{7,6},{8,9},{9,8},{10,11... | collective-permute-start | bytes 540680 | tf_op jit(solution)/shard_map/ppermute | solution.py:98
  47.5 1.4 %collective-permute-start.6 = (f32[32,1280]{1,0:T(8,128)S(1)}, f32[32,1280]{1,0:T(8,128)S(1)}, u32[]{:S(2)}, u32[]{:S(2)}) collective-permute-start(f32[32,1280]{1,0:T(8,128)S(1)} %get-tuple-element.45), channel_id=1, source_target_pairs={{0,1},{1,0},{2,3},{3,2},{4,5},{5,4},{6,7},{7,6},{8,9},{9,8},{10,11... | collective-permute-start | bytes 491528 | tf_op jit(solution)/shard_map/ppermute | solution.py:98
  47.6 2.9 %collective-permute-start.11 = (f32[32,1280]{1,0:T(8,128)S(1)}, f32[32,1280]{1,0:T(8,128)S(1)}, u32[]{:S(2)}, u32[]{:S(2)}) collective-permute-start(f32[32,1280]{1,0:T(8,128)S(1)} %get-tuple-element.49.refs_1_), channel_id=1, source_target_pairs={{0,1},{1,0},{2,3},{3,2},{4,5},{5,4},{6,7},{7,6},{8,9},{9,8},{10,11... | collective-permute-start | bytes 491528 | tf_op jit(solution)/shard_map/ppermute | solution.py:98
  48.1 2.4 %collective-permute-start.10 = (f32[32,1280]{1,0:T(8,128)S(1)}, f32[32,1280]{1,0:T(8,128)S(1)}, u32[]{:S(2)}, u32[]{:S(2)}) collective-permute-start(f32[32,1280]{1,0:T(8,128)S(1)} %get-tuple-element.47.refs_3_.refs_0_), channel_id=1, source_target_pairs={{0,1},{1,0},{2,3},{3,2},{4,5},{5,4},{6,7},{7,6},{8,9},{9,8},{10,11... | collective-permute-start | bytes 491528 | tf_op jit(solution)/shard_map/ppermute | solution.py:98
  48.9 12.1 %collective-permute-start.14 = (f32[32,2560]{1,0:T(8,128)S(1)}, f32[32,2560]{1,0:T(8,128)S(1)}, u32[]{:S(2)}, u32[]{:S(2)}) collective-permute-start(f32[32,2560]{1,0:T(8,128)S(1)} %get-tuple-element.51.refs_5_.refs_0_), channel_id=1, source_target_pairs={{0,2},{1,5},{2,0},{3,7},{4,6},{5,1},{6,4},{7,3},{8,10},{9,13},{10,... | collective-permute-start | bytes 983048 | tf_op jit(solution)/shard_map/ppermute | solution.py:98
  53.7 9.9 %collective-permute-start.13 = (f32[32,1792]{1,0:T(8,128)S(1)}, f32[32,1792]{1,0:T(8,128)S(1)}, u32[]{:S(2)}, u32[]{:S(2)}) collective-permute-start(f32[32,1792]{1,0:T(8,128)S(1)} %get-tuple-element.58), channel_id=1, source_target_pairs={{0,4},{1,5},{2,6},{3,7},{4,0},{5,1},{6,2},{7,3},{8,12},{9,13},{10,... | collective-permute-start | bytes 688136 | tf_op jit(solution)/shard_map/ppermute | solution.py:98
  55.5 3.7 %collective-permute-start.9 = (f32[32,128]{1,0:T(8,128)S(1)}, f32[32,128]{1,0:T(8,128)S(1)}, u32[]{:S(2)}, u32[]{:S(2)}) collective-permute-start(f32[32,128]{1,0:T(8,128)S(1)} %get-tuple-element.48.refs_0_), channel_id=1, source_target_pairs={{0,2},{1,3},{2,0},{3,1},{4,6},{5,7},{6,4},{7,5},{8,10},{9,11},{10,... | collective-permute-start | bytes 49160 | tf_op jit(solution)/shard_map/ppermute | solution.py:98
  56.0 4.9 %collective-permute-start.12 = (f32[64,64]{1,0:T(8,128)S(1)}, f32[64,64]{1,0:T(8,128)S(1)}, u32[]{:S(2)}, u32[]{:S(2)}) collective-permute-start(f32[64,64]{1,0:T(8,128)S(1)} %get-tuple-element.52.refs_2_), channel_id=1, source_target_pairs={{0,8},{1,9},{2,10},{3,11},{4,12},{5,13},{6,14},{7,15},{8,0},{9,1},... | collective-permute-start | bytes 49160 | tf_op jit(solution)/shard_map/ppermute | solution.py:98
  61.0 12.5 %collective-permute-start.16 = (f32[32,2560]{1,0:T(8,128)S(1)}, f32[32,2560]{1,0:T(8,128)S(1)}, u32[]{:S(2)}, u32[]{:S(2)}) collective-permute-start(f32[32,2560]{1,0:T(8,128)S(1)} %shard_map.105.refs_2_.refs_0_), channel_id=1, source_target_pairs={{0,4},{1,3},{2,6},{3,1},{4,0},{5,7},{6,2},{7,5},{8,12},{9,11},{10,... | collective-permute-start | bytes 983048 | tf_op jit(solution)/shard_map/ppermute | solution.py:98
  63.7 10.6 %collective-permute-start.15 = (f32[32,1792]{1,0:T(8,128)S(1)}, f32[32,1792]{1,0:T(8,128)S(1)}, u32[]{:S(2)}, u32[]{:S(2)}) collective-permute-start(f32[32,1792]{1,0:T(8,128)S(1)} %shard_map.106.refs_4_.refs_0_), channel_id=1, source_target_pairs={{0,8},{1,9},{2,10},{3,11},{4,12},{5,13},{6,14},{7,15},{8,0},{9,1},... | collective-permute-start | bytes 688136 | tf_op jit(solution)/shard_map/ppermute | solution.py:98
  73.6 2.5 %collective-permute-start.19 = (f32[32,1280]{1,0:T(8,128)S(1)}, f32[32,1280]{1,0:T(8,128)S(1)}, u32[]{:S(2)}, u32[]{:S(2)}) collective-permute-start(f32[32,1280]{1,0:T(8,128)S(1)} %get-tuple-element.62.refs_2_), channel_id=1, source_target_pairs={{0,1},{1,0},{2,3},{3,2},{4,5},{5,4},{6,7},{7,6},{8,9},{9,8},{10,11... | collective-permute-start | bytes 491528 | tf_op jit(solution)/shard_map/ppermute | solution.py:98
  73.7 2.4 %collective-permute-start.18 = (f32[32,1280]{1,0:T(8,128)S(1)}, f32[32,1280]{1,0:T(8,128)S(1)}, u32[]{:S(2)}, u32[]{:S(2)}) collective-permute-start(f32[32,1280]{1,0:T(8,128)S(1)} %get-tuple-element.61.refs_2_.refs_1_), channel_id=1, source_target_pairs={{0,1},{1,0},{2,3},{3,2},{4,5},{5,4},{6,7},{7,6},{8,9},{9,8},{10,11... | collective-permute-start | bytes 491528 | tf_op jit(solution)/shard_map/ppermute | solution.py:98
  74.2 9.8 %collective-permute-start.17 = (f32[32,1792]{1,0:T(8,128)S(1)}, f32[32,1792]{1,0:T(8,128)S(1)}, u32[]{:S(2)}, u32[]{:S(2)}) collective-permute-start(f32[32,1792]{1,0:T(8,128)S(1)} %shard_map.109.refs_6_.refs_1_), channel_id=1, source_target_pairs={{0,4},{1,5},{2,6},{3,7},{4,0},{5,1},{6,2},{7,3},{8,12},{9,13},{10,... | collective-permute-start | bytes 688136 | tf_op jit(solution)/shard_map/ppermute | solution.py:98

commit v8 on v7

--- a/solution.py
+++ b/solution.py
@@ -10,9 +10,8 @@
 REPLICAS = 2
 RANK = 64
 TILE = 256
-THIN = 128
 FLOPS = 1.15e9
-WEIGHTS = (8.0, 4.0, 1.0, 4.0, 0.1, 5.0, 1.0, 5.0, 1.0, 1.0, 4.0, 0.1, 0.2, 1.0, 5.0, 1.0, 1.0, 8.0, 8.0)
+WEIGHTS = (8.0, 4.0, 1.0, 4.0, 0.1, 5.0, 1.0, 5.0, 1.0, 1.0, 4.0, 0.1, 0.1, 1.0, 5.0, 1.0, 1.0, 8.0, 8.0)
 MIB = 1 << 20
 BF16 = jnp.bfloat16
 F32 = jnp.float32
@@ -230,26 +229,22 @@
             refs = refs[2:]
         left, fixed = refs[:2]
 
-        def step(g, e, start):
-            i = first * TILE // THIN + pl.program_id(0)
-            at = pl.ds(pl.multiple_of(i * THIN, THIN), THIN)
-            term = jnp.zeros((THIN, RANK), F32)
+        def step(g, e):
+            at = tile_at(first + pl.program_id(0))
+            term = jnp.zeros((RANK, TILE), F32)
             for j in range(0, cols, TILE):
                 here = slice(j, j + TILE)
                 c = g[:, here] + e[:, here]
                 fixed[at, here] = c
-                term += lax.dot_general(c, start[:, here], NT, preferred_element_type=F32)
-            left[:, at] = term.T
-
-        spec = pl.BlockSpec(
-            (THIN, cols), lambda i: (first * TILE // THIN + i, 0), pipeline_mode=pl.Buffered(4)
-        )
-        whole = pl.BlockSpec((RANK, cols), lambda i: (0, 0))
-        pltpu.emit_pipeline(step, grid=(count * TILE // THIN,), in_specs=[spec, spec, whole])(grad, error, start)
+                term += lax.dot_general(start[:, here], c, NT, preferred_element_type=F32)
+            left[:, at] = term
+
+        spec = pl.BlockSpec((TILE, cols), lambda i: (first + i, 0), pipeline_mode=pl.Buffered(3))
+        pltpu.emit_pipeline(step, grid=(count,), in_specs=[spec, spec])(grad, error)
         if last:
             halve(left, core_of(), refs[2], refs[3:])
 
-    args = [(grad, HBM), (error, HBM), (start, HBM)]
+    args = [(grad, HBM), (error, HBM), (start, VMEM)]
     outs = [((RANK, rows), F32, VMEM), ((rows, cols), BF16, VMEM)]
     if last:
         outs += [((HALF, n), F32, VMEM) for n in (rows, *in_two(rows))]
@@ -280,7 +275,7 @@
                 fixed[at, here] = c
                 left[:, here] += jnp.dot(s[...], c, preferred_element_type=F32)
 
-        spec = pl.BlockSpec((TILE, cols), lambda i: (first + i, 0), pipeline_mode=pl.Buffered(4))
+        spec = pl.BlockSpec((TILE, cols), lambda i: (first + i, 0), pipeline_mode=pl.Buffered(3))
         part = pl.BlockSpec((RANK, TILE), lambda i: (0, block + i))
         pltpu.emit_pipeline(step, grid=(count,), in_specs=[spec, spec, part])(grad, error, start)
         if last:
@@ -294,7 +289,7 @@
     if before is not None:
         args += [(x, VMEM) for x in before]
         aliases = {3: 0, 4: 1}
-    return run(kernel, args, outs, mib=12, aliases=aliases, after=after)
+    return run(kernel, args, outs, mib=8, aliases=aliases, after=after)
 
 
 def load_left(owns, others, place, left, stack):
@@ -306,7 +301,8 @@
             at += n
     hi, lo = parts_of(left[...])
     stack[:RANK, :] = hi
-    stack[RANK:, :] = lo
+    stack[RANK : 2 * RANK, :] = lo
+    stack[2 * RANK :, :] = hi
     return lax.dot_general(
         left[...], left[...], NT, preferred_element_type=F32, precision=lax.Precision.HIGHEST
     )
@@ -317,11 +313,11 @@
     n_own, n_both = len(owns), len(owns) + len(others)
 
     def kernel(*refs):
-        fixed, keep, give, gram, left, stack, right = refs[n_both:]
+        fixed, keep, give, gram, stack, left, right = refs[n_both:]
         gram[...] = load_left(refs[:n_own], refs[n_own:n_both], core_of(), left, stack)
 
         def step(i, _):
-            both = jnp.dot(stack[...], fixed[:, tile_at(i)], preferred_element_type=F32)
+            both = jnp.dot(stack[: 2 * RANK], fixed[:, tile_at(i)], preferred_element_type=F32)
             right[:, tile_at(i)] = both[:RANK] + both[RANK:]
             return 0
 
@@ -331,8 +327,8 @@
     return run(
         kernel,
         [(x, VMEM) for x in (*owns, *others, fixed)],
-        [((HALF, cols), F32, VMEM)] * 2 + [((RANK, RANK), F32, VMEM), ((RANK, rows), F32, VMEM)],
-        [pltpu.VMEM((2 * RANK, rows), BF16), pltpu.VMEM((RANK, cols), F32)],
+        [((HALF, cols), F32, VMEM)] * 2 + [((RANK, RANK), F32, VMEM), ((3 * RANK, rows), BF16, VMEM)],
+        [pltpu.VMEM((RANK, rows), F32), pltpu.VMEM((RANK, cols), F32)],
         mib=4,
         after=after,
     )
@@ -344,11 +340,11 @@
     cut, rest = in_two(rows)
 
     def kernel(*refs):
-        fixed, keep, give_1, give_2, left, stack, right = refs[n_both:]
+        fixed, keep, give_1, give_2, stack, left, right = refs[n_both:]
         gram = load_left(refs[:n_own], refs[n_own:n_both], replica_of(), left, stack)
 
         def step(i, _):
-            both = lax.dot_general(stack[...], fixed[tile_at(i), :], NT, preferred_element_type=F32)
+            both = lax.dot_general(stack[: 2 * RANK], fixed[tile_at(i), :], NT, preferred_element_type=F32)
             right[:, tile_at(i)] = both[:RANK] + both[RANK:]
             return 0
 
@@ -362,8 +358,8 @@
     return run(
         kernel,
         [(x, VMEM) for x in (*owns, *others, fixed)],
-        [((HALF, n), F32, VMEM) for n in widths] + [((RANK, cols), F32, VMEM)],
-        [pltpu.VMEM((2 * RANK, cols), BF16), pltpu.VMEM((RANK, rows), F32)],
+        [((HALF, n), F32, VMEM) for n in widths] + [((3 * RANK, cols), BF16, VMEM)],
+        [pltpu.VMEM((RANK, cols), F32), pltpu.VMEM((RANK, rows), F32)],
         mib=4,
         after=after,
     )
@@ -442,9 +438,9 @@
         ):
             other = jnp.concatenate([a[HALF:], a[:HALF]], axis=0)
             a = jnp.where(place == 0, a, other) * (1.0 / REPLICAS)
-            out[...] = jnp.dot(
-                a, left[...], preferred_element_type=F32, precision=lax.Precision.HIGHEST
-            )
+            hi, lo = parts_of(a)
+            both = jnp.concatenate([hi, hi, lo], axis=1)
+            out[...] = jnp.dot(both, left[...], preferred_element_type=F32)
         stacked([col], COL_ORDER, col_stack)
         stacked([row], ROW_ORDER, row_stack)
         turn(row_stack, row_turned)
@@ -576,11 +572,11 @@
     grams_gate = [gram_gate] + [
         exchange(gram_gate, lambda d, t, b=b: (d ^ b, t)) for b in range(REPLICAS, n_dp, REPLICAS)
     ]
-    gram_down, gram_gate = gram_sums(run, grams_down, grams_gate)
     for hop in hops[1:]:
         (down,) = add(run, [down], [got], after=(gram_gate,))
         got = exchange(down, hop)
-    (gate,) = add(run, [keep_gate], [got_gate], after=(down,))
+    gram_down, gram_gate = gram_sums(run, grams_down, grams_gate, after=(down,))
+    (gate,) = add(run, [keep_gate], [got_gate], after=(gram_gate,))
     got_gate = exchange(gate, steps[0])
     col_stack, row_turned = solve(run, gram_down, left_down, gram_gate, left_gate, after=(gate,))
     downs = add(run, [down], [got], in_two(slab), after=(col_stack,))
@@ -591,7 +587,7 @@
             got_gate = exchange(gate, steps[i + 1])
     other_gate = exchange(gate, other_replica)
     new_error_down, update_down, done = rebuild(
-        run, None, col_stack, downs, others_down, fixed_down, slab // 8, after=(gate,)
+        run, None, col_stack, downs, others_down, fixed_down, slab // 4, after=(gate,)
     )
     new_error_gate, update_gate, _ = rebuild(
         run, row_turned, None, [gate], [other_gate], fixed_gate, slab // 4, after=(done,)

time: 91.8 us -> 87.6 us (0.954)
  Pallas kernels: 51.6 us -> 46.2 us
  waiting for transfers between devices: 17.6 us -> 19.5 us
    pallas_call x19, Pallas kernels: 51.6 us -> 46.2 us  [__call__(): pl.pallas_call(body, out_shape=tuple(((pltpu.VMEM if spec is VMEM else pl...]
    ppermute x20, waiting for transfers between devices: 17.6 us -> 19.5 us  [exchange(): return lax.ppermute(x, ('dp', 'tensor'), pairs)]
  transfers between devices with their start and end apart: 20 -> 20, of which waited for: 9 -> 11; matrix products, arithmetic and copies ran while one was open for 0% -> 0% of each run, Pallas kernels for 37% -> 33%
where the time goes in v8:
time: 87.6 us; the launch traced here: 87.3 us
  Pallas kernels  46.2 us (53%)
  starting transfers between devices  20.9 us (24%)
  waiting for transfers between devices  19.5 us (22%)
    pallas_call x19, Pallas kernels, __call__(): pl.pallas_call(body, out_shape=tuple(((pltpu.VMEM if spec is VMEM else pl...  46.2 us
    ppermute x20, starting transfers between devices, exchange(): return lax.ppermute(x, ('dp', 'tensor'), pairs)  20.9 us
    ppermute x20, waiting for transfers between devices, exchange(): return lax.ppermute(x, ('dp', 'tensor'), pairs)  19.5 us
  transfers between devices with their start and end apart: 20, of which 11 were waited for; matrix products, arithmetic and copies ran while one was open for 0% of the time, Pallas kernels for 33%

profile of v8, /device:TPU:0, one launch (start us, length us, event | category | flops | bytes accessed | tf_op | source)
XLA Modules:
  0.0 87.3 jit_solution(2045144794520659139)
XLA Ops:
  0.6 10.1 %shard_map.93 = (f32[64,1792]{1,0:T(8,128)}, bf16[2560,1792]{1,0:T(8,128)(2,1)S(1)}, f32[32,1792]{1,0:T(8,128)S(1)}, f32[32,1792]{1,0:T(8,128)S(1)}) custom-call(bf16[2560,1792]{1,0:T(8,128)(2,1)} %refs_0_.3, bf16[2560,1792]{1,0:T(8,128)(2,1)} %refs_1_.3, bf16[64,5120]{1,0:T(8,128)(2,1)} %refs_2_.3), custom_call_target="tpu_custom_call" | custom-call | flops 9200000000 | bytes 1024 | tf_op jit(solution)/shard_map/pallas_call | solution.py:154
  10.8 3.0 %collective-permute-start = (f32[32,1792]{1,0:T(8,128)S(1)}, f32[32,1792]{1,0:T(8,128)S(1)}, u32[]{:S(2)}, u32[]{:S(2)}) collective-permute-start(f32[32,1792]{1,0:T(8,128)S(1)} %get-tuple-element.37), channel_id=1, source_target_pairs={{0,4},{1,5},{2,6},{3,7},{4,0},{5,1},{6,2},{7,3},{8,12},{9,13},{10,... | collective-permute-start | bytes 688136 | tf_op jit(solution)/shard_map/ppermute | solution.py:97
  13.8 4.4 %shard_map.94 = (f32[64,2560]{1,0:T(8,128)S(1)}, bf16[2560,1792]{1,0:T(8,128)(2,1)S(1)}) custom-call(bf16[2560,1792]{1,0:T(8,128)(2,1)} %refs_0_.5, bf16[2560,1792]{1,0:T(8,128)(2,1)} %refs_1_.5, bf16[64,1792]{1,0:T(8,128)(2,1)S(1)} %copy-done, f32[32,1792]{1,0:T(8,128)S(1)} %get-tuple-element.36.refs_3_.refs_0_), custom_call_target="tpu_custom_call" | custom-call | flops 4600000000 | bytes 1024 | tf_op jit(solution)/shard_map/pallas_call | solution.py:154
  18.2 1.2 %collective-permute-done.refs_1_ = f32[32,1792]{1,0:T(8,128)S(1)} collective-permute-done((f32[32,1792]{1,0:T(8,128)S(1)}, f32[32,1792]{1,0:T(8,128)S(1)}, u32[]{:S(2)}, u32[]{:S(2)}) %collective-permute-start) | collective-permute-done | bytes 229408 | tf_op jit(solution)/shard_map/ppermute | solution.py:97
  19.4 2.8 %collective-permute-start.1 = (f32[32,1792]{1,0:T(8,128)S(1)}, f32[32,1792]{1,0:T(8,128)S(1)}, u32[]{:S(2)}, u32[]{:S(2)}) collective-permute-start(f32[32,1792]{1,0:T(8,128)S(1)} %shard_map.95.refs_5_.refs_0_), channel_id=1, source_target_pairs={{0,8},{1,9},{2,10},{3,11},{4,12},{5,13},{6,14},{7,15},{8,0},{9,1},... | collective-permute-start | bytes 688136 | tf_op jit(solution)/shard_map/ppermute | solution.py:97
  22.2 4.5 %shard_map.96 = (f32[64,2560]{1,0:T(8,128)S(1)}, bf16[2560,1792]{1,0:T(8,128)(2,1)S(1)}, f32[32,2560]{1,0:T(8,128)S(1)}, f32[32,1280]{1,0:T(8,128)S(1)}, f32[32,1280]{1,0:T(8,128)S(1)}) custom-call(bf16[2560,1792]{1,0:T(8,128)(2,1)} %refs_0_.5, bf16[2560,1792]{1,0:T(8,128)(2,1)} %refs_1_.5, ...), custom_call_target="tpu_custom_call", output_to_operand_aliasing={{0}: (3, {}), {1}: (4, {})} | custom-call | flops 4600000000 | bytes 1024 | tf_op jit(solution)/shard_map/pallas_call | solution.py:154
  27.3 0.9 %collective-permute-done.2.refs_1_ = f32[32,1280]{1,0:T(8,128)S(1)} collective-permute-done((f32[32,1280]{1,0:T(8,128)S(1)}, f32[32,1280]{1,0:T(8,128)S(1)}, u32[]{:S(2)}, u32[]{:S(2)}) %collective-permute-start.2) | collective-permute-done | bytes 163872 | tf_op jit(solution)/shard_map/ppermute | solution.py:97
  28.5 1.6 %collective-permute-start.5 = (f32[32,2560]{1,0:T(8,128)S(1)}, f32[32,2560]{1,0:T(8,128)S(1)}, u32[]{:S(2)}, u32[]{:S(2)}) collective-permute-start(f32[32,2560]{1,0:T(8,128)S(1)} %shard_map.97.refs_2_.refs_0_), channel_id=1, source_target_pairs={{0,2},{1,5},{2,0},{3,7},{4,6},{5,1},{6,4},{7,3},{8,10},{9,13},{10,... | collective-permute-start | bytes 983048 | tf_op jit(solution)/shard_map/ppermute | solution.py:97
  30.0 2.1 %collective-permute-done.1.refs_1_ = f32[32,1792]{1,0:T(8,128)S(1)} collective-permute-done((f32[32,1792]{1,0:T(8,128)S(1)}, f32[32,1792]{1,0:T(8,128)S(1)}, u32[]{:S(2)}, u32[]{:S(2)}) %collective-permute-start.1) | collective-permute-done | bytes 229408 | tf_op jit(solution)/shard_map/ppermute | solution.py:97
  32.7 2.9 %collective-permute-done.5.refs_1_ = f32[32,2560]{1,0:T(8,128)S(1)} collective-permute-done((f32[32,2560]{1,0:T(8,128)S(1)}, f32[32,2560]{1,0:T(8,128)S(1)}, u32[]{:S(2)}, u32[]{:S(2)}) %collective-permute-start.5) | collective-permute-done | bytes 327712 | tf_op jit(solution)/shard_map/ppermute | solution.py:97
  35.6 1.6 %collective-permute-start.8 = (f32[32,2560]{1,0:T(8,128)S(1)}, f32[32,2560]{1,0:T(8,128)S(1)}, u32[]{:S(2)}, u32[]{:S(2)}) collective-permute-start(f32[32,2560]{1,0:T(8,128)S(1)} %shard_map.99.refs_3_.refs_0_), channel_id=1, source_target_pairs={{0,4},{1,3},{2,6},{3,1},{4,0},{5,7},{6,2},{7,5},{8,12},{9,11},{10,... | collective-permute-start | bytes 983048 | tf_op jit(solution)/shard_map/ppermute | solution.py:97
  37.3 3.2 %collective-permute-done.4.refs_1_ = f32[32,1792]{1,0:T(8,128)S(1)} collective-permute-done((f32[32,1792]{1,0:T(8,128)S(1)}, f32[32,1792]{1,0:T(8,128)S(1)}, u32[]{:S(2)}, u32[]{:S(2)}) %collective-permute-start.4) | collective-permute-done | bytes 229408 | tf_op jit(solution)/shard_map/ppermute | solution.py:97
  40.5 5.3 %shard_map.100 = (f32[32,2688]{1,0:T(8,128)S(1)}, f32[32,1280]{1,0:T(8,128)S(1)}, f32[32,1408]{1,0:T(8,128)S(1)}, bf16[192,1792]{1,0:T(8,128)(2,1)S(1)}) custom-call(f32[32,1792]{1,0:T(8,128)S(1)} %shard_map.98.refs_2_.refs_0_, f32[32,1792]{1,0:T(8,128)S(1)} %collective-permute-done.4.refs_1_, bf16[2560,1792]{1,0:T(8,128)(2,1)S(1)} %get-tuple-element.43.refs_2_.refs_5_, ...), custom_call_target="tpu_custom_call" | custom-call | flops 5750000128 | bytes 1024 | tf_op jit(solution)/shard_map/pallas_call | solution.py:154
  47.5 1.4 %collective-permute-start.13 = (f32[32,2560]{1,0:T(8,128)S(1)}, f32[32,2560]{1,0:T(8,128)S(1)}, u32[]{:S(2)}, u32[]{:S(2)}) collective-permute-start(f32[32,2560]{1,0:T(8,128)S(1)} %get-tuple-element.51.refs_5_.refs_0_), channel_id=1, source_target_pairs={{0,2},{1,5},{2,0},{3,7},{4,6},{5,1},{6,4},{7,3},{8,10},{9,13},{10,... | collective-permute-start | bytes 983048 | tf_op jit(solution)/shard_map/ppermute | solution.py:97
  48.9 3.3 %shard_map.103 = (f32[32,1792]{1,0:T(8,128)S(1)}, f32[32,1792]{1,0:T(8,128)S(1)}, f32[64,64]{1,0:T(8,128)S(1)}, bf16[192,2560]{1,0:T(8,128)(2,1)S(1)}) custom-call(f32[32,1280]{1,0:T(8,128)S(1)} %get-tuple-element.47.refs_3_.refs_0_, f32[32,1280]{1,0:T(8,128)S(1)} %get-tuple-element.49.refs_1_, f32[32,1280]{1,0:T(8,128)S(1)} %collective-permute-done.10.refs_2_, ...), custom_call_target="tpu_custom_call" | custom-call | flops 4600000000 | bytes 1024 | tf_op jit(solution)/shard_map/pallas_call | solution.py:154
  52.2 1.1 %collective-permute-start.14 = (f32[32,1792]{1,0:T(8,128)S(1)}, f32[32,1792]{1,0:T(8,128)S(1)}, u32[]{:S(2)}, u32[]{:S(2)}) collective-permute-start(f32[32,1792]{1,0:T(8,128)S(1)} %get-tuple-element.58), channel_id=1, source_target_pairs={{0,4},{1,5},{2,6},{3,7},{4,0},{5,1},{6,2},{7,3},{8,12},{9,13},{10,... | collective-permute-start | bytes 688136 | tf_op jit(solution)/shard_map/ppermute | solution.py:97
  53.8 3.1 %collective-permute-start.12 = (f32[64,64]{1,0:T(8,128)S(1)}, f32[64,64]{1,0:T(8,128)S(1)}, u32[]{:S(2)}, u32[]{:S(2)}) collective-permute-start(f32[64,64]{1,0:T(8,128)S(1)} %get-tuple-element.52.refs_2_), channel_id=1, source_target_pairs={{0,8},{1,9},{2,10},{3,11},{4,12},{5,13},{6,14},{7,15},{8,0},{9,1},... | collective-permute-start | bytes 49160 | tf_op jit(solution)/shard_map/ppermute | solution.py:97
  57.0 1.8 %collective-permute-done.12.refs_3_ = f32[64,64]{1,0:T(8,128)S(1)} collective-permute-done((f32[64,64]{1,0:T(8,128)S(1)}, f32[64,64]{1,0:T(8,128)S(1)}, u32[]{:S(2)}, u32[]{:S(2)}) %collective-permute-start.12) | collective-permute-done | bytes 16416 | tf_op jit(solution)/shard_map/ppermute | solution.py:97
  58.9 1.0 %collective-permute-done.14.refs_1_ = f32[32,1792]{1,0:T(8,128)S(1)} collective-permute-done((f32[32,1792]{1,0:T(8,128)S(1)}, f32[32,1792]{1,0:T(8,128)S(1)}, u32[]{:S(2)}, u32[]{:S(2)}) %collective-permute-start.14) | collective-permute-done | bytes 229408 | tf_op jit(solution)/shard_map/ppermute | solution.py:97
  60.0 2.8 %collective-permute-start.15 = (f32[32,1792]{1,0:T(8,128)S(1)}, f32[32,1792]{1,0:T(8,128)S(1)}, u32[]{:S(2)}, u32[]{:S(2)}) collective-permute-start(f32[32,1792]{1,0:T(8,128)S(1)} %shard_map.106.refs_4_.refs_0_), channel_id=1, source_target_pairs={{0,8},{1,9},{2,10},{3,11},{4,12},{5,13},{6,14},{7,15},{8,0},{9,1},... | collective-permute-start | bytes 688136 | tf_op jit(solution)/shard_map/ppermute | solution.py:97
  62.8 3.9 %shard_map.107 = (bf16[256,1792]{1,0:T(8,128)(2,1)S(1)}, bf16[2560,256]{1,0:T(8,128)(2,1)S(1)}) custom-call(f32[64,64]{1,0:T(8,128)S(1)} %get-tuple-element.53.refs_0_, bf16[192,1792]{1,0:T(8,128)(2,1)S(1)} %get-tuple-element.54.refs_1_, f32[64,64]{1,0:T(8,128)S(1)} %get-tuple-element.55.refs_2_, bf16[192,2560]{1,0:T(8,128)(2,1)S(1)} %get-tuple-element.56.refs_3_, ...), custom_call_target="tpu_custom_call" | custom-call | flops 5750000128 | bytes 1024 | tf_op jit(solution)/shard_map/pallas_call | solution.py:154
  67.7 5.2 %collective-permute-done.15.refs_1_ = f32[32,1792]{1,0:T(8,128)S(1)} collective-permute-done((f32[32,1792]{1,0:T(8,128)S(1)}, f32[32,1792]{1,0:T(8,128)S(1)}, u32[]{:S(2)}, u32[]{:S(2)}) %collective-permute-start.15) | collective-permute-done | bytes 229408 | tf_op jit(solution)/shard_map/ppermute | solution.py:97
  73.0 7.0 %shard_map.110 = (bf16[2560,1792]{1,0:T(8,128)(2,1)}, bf16[1280,1792]{1,0:T(8,128)(2,1)}, f32[8,128]{1,0:T(8,128)S(1)}) custom-call(bf16[256,1792]{1,0:T(8,128)(2,1)S(1)} %get-tuple-element.60.refs_2_.refs_0_, f32[32,1280]{1,0:T(8,128)S(1)} %get-tuple-element.61.refs_2_.refs_1_, f32[32,1280]{1,0:T(8,128)S(1)} %get-tuple-element.62.refs_2_, ...), custom_call_target="tpu_custom_call" | custom-call | flops 9200000000 | bytes 1024 | tf_op jit(solution)/shard_map/pallas_call | solution.py:154
  80.0 7.3 %shard_map.111 = (bf16[2560,1792]{1,0:T(8,128)(2,1)}, bf16[1280,1792]{1,0:T(8,128)(2,1)}, f32[8,128]{1,0:T(8,128)}) custom-call(bf16[2560,256]{1,0:T(8,128)(2,1)S(1)} %get-tuple-element.59.refs_0_, f32[32,1792]{1,0:T(8,128)S(1)} %shard_map.109.refs_6_.refs_1_, f32[32,1792]{1,0:T(8,128)S(1)} %collective-permute-done.17.refs_2_, ...), custom_call_target="tpu_custom_call" | custom-call | flops 9200000000 | bytes 1024 | tf_op jit(solution)/shard_map/pallas_call | solution.py:154
  (37 shorter events, 5.2 us)
Async XLA Ops:
  0.6 13.2 %copy-start = (bf16[64,1792]{1,0:T(8,128)(2,1)S(1)}, bf16[64,1792]{1,0:T(8,128)(2,1)}, u32[]{:S(2)}) copy-start(bf16[64,1792]{1,0:T(8,128)(2,1)} %refs_2_.5) | copy-start | bytes 688132
  10.8 8.6 %collective-permute-start = (f32[32,1792]{1,0:T(8,128)S(1)}, f32[32,1792]{1,0:T(8,128)S(1)}, u32[]{:S(2)}, u32[]{:S(2)}) collective-permute-start(f32[32,1792]{1,0:T(8,128)S(1)} %get-tuple-element.37), channel_id=1, source_target_pairs={{0,4},{1,5},{2,6},{3,7},{4,0},{5,1},{6,2},{7,3},{8,12},{9,13},{10,... | collective-permute-start | bytes 688136 | tf_op jit(solution)/shard_map/ppermute | solution.py:97
  19.4 12.7 %collective-permute-start.1 = (f32[32,1792]{1,0:T(8,128)S(1)}, f32[32,1792]{1,0:T(8,128)S(1)}, u32[]{:S(2)}, u32[]{:S(2)}) collective-permute-start(f32[32,1792]{1,0:T(8,128)S(1)} %shard_map.95.refs_5_.refs_0_), channel_id=1, source_target_pairs={{0,8},{1,9},{2,10},{3,11},{4,12},{5,13},{6,14},{7,15},{8,0},{9,1},... | collective-permute-start | bytes 688136 | tf_op jit(solution)/shard_map/ppermute | solution.py:97
  26.7 1.5 %collective-permute-start.2 = (f32[32,1280]{1,0:T(8,128)S(1)}, f32[32,1280]{1,0:T(8,128)S(1)}, u32[]{:S(2)}, u32[]{:S(2)}) collective-permute-start(f32[32,1280]{1,0:T(8,128)S(1)} %get-tuple-element.41), channel_id=1, source_target_pairs={{0,1},{1,0},{2,3},{3,2},{4,5},{5,4},{6,7},{7,6},{8,9},{9,8},{10,11... | collective-permute-start | bytes 491528 | tf_op jit(solution)/shard_map/ppermute | solution.py:97
  26.8 1.6 %collective-permute-start.3 = (f32[32,1280]{1,0:T(8,128)S(1)}, f32[32,1280]{1,0:T(8,128)S(1)}, u32[]{:S(2)}, u32[]{:S(2)}) collective-permute-start(f32[32,1280]{1,0:T(8,128)S(1)} %get-tuple-element.42), channel_id=1, source_target_pairs={{0,1},{1,0},{2,3},{3,2},{4,5},{5,4},{6,7},{7,6},{8,9},{9,8},{10,11... | collective-permute-start | bytes 491528 | tf_op jit(solution)/shard_map/ppermute | solution.py:97
  28.5 7.1 %collective-permute-start.5 = (f32[32,2560]{1,0:T(8,128)S(1)}, f32[32,2560]{1,0:T(8,128)S(1)}, u32[]{:S(2)}, u32[]{:S(2)}) collective-permute-start(f32[32,2560]{1,0:T(8,128)S(1)} %shard_map.97.refs_2_.refs_0_), channel_id=1, source_target_pairs={{0,2},{1,5},{2,0},{3,7},{4,6},{5,1},{6,4},{7,3},{8,10},{9,13},{10,... | collective-permute-start | bytes 983048 | tf_op jit(solution)/shard_map/ppermute | solution.py:97
  32.2 8.3 %collective-permute-start.4 = (f32[32,1792]{1,0:T(8,128)S(1)}, f32[32,1792]{1,0:T(8,128)S(1)}, u32[]{:S(2)}, u32[]{:S(2)}) collective-permute-start(f32[32,1792]{1,0:T(8,128)S(1)} %shard_map.98.refs_2_.refs_0_), channel_id=1, source_target_pairs={{0,4},{1,5},{2,6},{3,7},{4,0},{5,1},{6,2},{7,3},{8,12},{9,13},{10,... | collective-permute-start | bytes 688136 | tf_op jit(solution)/shard_map/ppermute | solution.py:97
  35.6 10.7 %collective-permute-start.8 = (f32[32,2560]{1,0:T(8,128)S(1)}, f32[32,2560]{1,0:T(8,128)S(1)}, u32[]{:S(2)}, u32[]{:S(2)}) collective-permute-start(f32[32,2560]{1,0:T(8,128)S(1)} %shard_map.99.refs_3_.refs_0_), channel_id=1, source_target_pairs={{0,4},{1,3},{2,6},{3,1},{4,0},{5,7},{6,2},{7,5},{8,12},{9,11},{10,... | collective-permute-start | bytes 983048 | tf_op jit(solution)/shard_map/ppermute | solution.py:97
  45.8 1.7 %collective-permute-start.7 = (f32[32,1408]{1,0:T(8,128)S(1)}, f32[32,1408]{1,0:T(8,128)S(1)}, u32[]{:S(2)}, u32[]{:S(2)}) collective-permute-start(f32[32,1408]{1,0:T(8,128)S(1)} %get-tuple-element.46), channel_id=1, source_target_pairs={{0,1},{1,0},{2,3},{3,2},{4,5},{5,4},{6,7},{7,6},{8,9},{9,8},{10,11... | collective-permute-start | bytes 540680 | tf_op jit(solution)/shard_map/ppermute | solution.py:97
  45.8 1.6 %collective-permute-start.6 = (f32[32,1280]{1,0:T(8,128)S(1)}, f32[32,1280]{1,0:T(8,128)S(1)}, u32[]{:S(2)}, u32[]{:S(2)}) collective-permute-start(f32[32,1280]{1,0:T(8,128)S(1)} %get-tuple-element.45), channel_id=1, source_target_pairs={{0,1},{1,0},{2,3},{3,2},{4,5},{5,4},{6,7},{7,6},{8,9},{9,8},{10,11... | collective-permute-start | bytes 491528 | tf_op jit(solution)/shard_map/ppermute | solution.py:97
  46.4 2.5 %collective-permute-start.11 = (f32[32,1280]{1,0:T(8,128)S(1)}, f32[32,1280]{1,0:T(8,128)S(1)}, u32[]{:S(2)}, u32[]{:S(2)}) collective-permute-start(f32[32,1280]{1,0:T(8,128)S(1)} %get-tuple-element.49.refs_1_), channel_id=1, source_target_pairs={{0,1},{1,0},{2,3},{3,2},{4,5},{5,4},{6,7},{7,6},{8,9},{9,8},{10,11... | collective-permute-start | bytes 491528 | tf_op jit(solution)/shard_map/ppermute | solution.py:97
  46.5 2.4 %collective-permute-start.10 = (f32[32,1280]{1,0:T(8,128)S(1)}, f32[32,1280]{1,0:T(8,128)S(1)}, u32[]{:S(2)}, u32[]{:S(2)}) collective-permute-start(f32[32,1280]{1,0:T(8,128)S(1)} %get-tuple-element.47.refs_3_.refs_0_), channel_id=1, source_target_pairs={{0,1},{1,0},{2,3},{3,2},{4,5},{5,4},{6,7},{7,6},{8,9},{9,8},{10,11... | collective-permute-start | bytes 491528 | tf_op jit(solution)/shard_map/ppermute | solution.py:97
  47.5 9.3 %collective-permute-start.13 = (f32[32,2560]{1,0:T(8,128)S(1)}, f32[32,2560]{1,0:T(8,128)S(1)}, u32[]{:S(2)}, u32[]{:S(2)}) collective-permute-start(f32[32,2560]{1,0:T(8,128)S(1)} %get-tuple-element.51.refs_5_.refs_0_), channel_id=1, source_target_pairs={{0,2},{1,5},{2,0},{3,7},{4,6},{5,1},{6,4},{7,3},{8,10},{9,13},{10,... | collective-permute-start | bytes 983048 | tf_op jit(solution)/shard_map/ppermute | solution.py:97
  52.2 7.8 %collective-permute-start.14 = (f32[32,1792]{1,0:T(8,128)S(1)}, f32[32,1792]{1,0:T(8,128)S(1)}, u32[]{:S(2)}, u32[]{:S(2)}) collective-permute-start(f32[32,1792]{1,0:T(8,128)S(1)} %get-tuple-element.58), channel_id=1, source_target_pairs={{0,4},{1,5},{2,6},{3,7},{4,0},{5,1},{6,2},{7,3},{8,12},{9,13},{10,... | collective-permute-start | bytes 688136 | tf_op jit(solution)/shard_map/ppermute | solution.py:97
  53.3 3.8 %collective-permute-start.9 = (f32[32,128]{1,0:T(8,128)S(1)}, f32[32,128]{1,0:T(8,128)S(1)}, u32[]{:S(2)}, u32[]{:S(2)}) collective-permute-start(f32[32,128]{1,0:T(8,128)S(1)} %get-tuple-element.48.refs_0_), channel_id=1, source_target_pairs={{0,2},{1,3},{2,0},{3,1},{4,6},{5,7},{6,4},{7,5},{8,10},{9,11},{10,... | collective-permute-start | bytes 49160 | tf_op jit(solution)/shard_map/ppermute | solution.py:97
  53.8 5.0 %collective-permute-start.12 = (f32[64,64]{1,0:T(8,128)S(1)}, f32[64,64]{1,0:T(8,128)S(1)}, u32[]{:S(2)}, u32[]{:S(2)}) collective-permute-start(f32[64,64]{1,0:T(8,128)S(1)} %get-tuple-element.52.refs_2_), channel_id=1, source_target_pairs={{0,8},{1,9},{2,10},{3,11},{4,12},{5,13},{6,14},{7,15},{8,0},{9,1},... | collective-permute-start | bytes 49160 | tf_op jit(solution)/shard_map/ppermute | solution.py:97
  56.9 10.2 %collective-permute-start.16 = (f32[32,2560]{1,0:T(8,128)S(1)}, f32[32,2560]{1,0:T(8,128)S(1)}, u32[]{:S(2)}, u32[]{:S(2)}) collective-permute-start(f32[32,2560]{1,0:T(8,128)S(1)} %shard_map.104.refs_4_.refs_0_), channel_id=1, source_target_pairs={{0,4},{1,3},{2,6},{3,1},{4,0},{5,7},{6,2},{7,5},{8,12},{9,11},{10,... | collective-permute-start | bytes 983048 | tf_op jit(solution)/shard_map/ppermute | solution.py:97
  60.0 12.9 %collective-permute-start.15 = (f32[32,1792]{1,0:T(8,128)S(1)}, f32[32,1792]{1,0:T(8,128)S(1)}, u32[]{:S(2)}, u32[]{:S(2)}) collective-permute-start(f32[32,1792]{1,0:T(8,128)S(1)} %shard_map.106.refs_4_.refs_0_), channel_id=1, source_target_pairs={{0,8},{1,9},{2,10},{3,11},{4,12},{5,13},{6,14},{7,15},{8,0},{9,1},... | collective-permute-start | bytes 688136 | tf_op jit(solution)/shard_map/ppermute | solution.py:97
  67.1 5.8 %collective-permute-start.19 = (f32[32,1280]{1,0:T(8,128)S(1)}, f32[32,1280]{1,0:T(8,128)S(1)}, u32[]{:S(2)}, u32[]{:S(2)}) collective-permute-start(f32[32,1280]{1,0:T(8,128)S(1)} %get-tuple-element.62.refs_2_), channel_id=1, source_target_pairs={{0,1},{1,0},{2,3},{3,2},{4,5},{5,4},{6,7},{7,6},{8,9},{9,8},{10,11... | collective-permute-start | bytes 491528 | tf_op jit(solution)/shard_map/ppermute | solution.py:97
  67.2 5.8 %collective-permute-start.18 = (f32[32,1280]{1,0:T(8,128)S(1)}, f32[32,1280]{1,0:T(8,128)S(1)}, u32[]{:S(2)}, u32[]{:S(2)}) collective-permute-start(f32[32,1280]{1,0:T(8,128)S(1)} %get-tuple-element.61.refs_2_.refs_1_), channel_id=1, source_target_pairs={{0,1},{1,0},{2,3},{3,2},{4,5},{5,4},{6,7},{7,6},{8,9},{9,8},{10,11... | collective-permute-start | bytes 491528 | tf_op jit(solution)/shard_map/ppermute | solution.py:97
  72.9 7.1 %collective-permute-start.17 = (f32[32,1792]{1,0:T(8,128)S(1)}, f32[32,1792]{1,0:T(8,128)S(1)}, u32[]{:S(2)}, u32[]{:S(2)}) collective-permute-start(f32[32,1792]{1,0:T(8,128)S(1)} %shard_map.109.refs_6_.refs_1_), channel_id=1, source_target_pairs={{0,4},{1,5},{2,6},{3,7},{4,0},{5,1},{6,2},{7,3},{8,12},{9,13},{10,... | collective-permute-start | bytes 688136 | tf_op jit(solution)/shard_map/ppermute | solution.py:97

commit v9 on v8

--- a/solution.py
+++ b/solution.py
@@ -11,7 +11,7 @@
 RANK = 64
 TILE = 256
 FLOPS = 1.15e9
-WEIGHTS = (8.0, 4.0, 1.0, 4.0, 0.1, 5.0, 1.0, 5.0, 1.0, 1.0, 4.0, 0.1, 0.1, 1.0, 5.0, 1.0, 1.0, 8.0, 8.0)
+WEIGHTS = (8.0, 4.0, 1.0, 4.0, 0.1, 5.0, 1.0, 1.0, 0.1, 5.0, 0.1, 5.0, 0.1, 0.1, 5.0, 1.0, 1.0, 8.0, 8.0)
 MIB = 1 << 20
 BF16 = jnp.bfloat16
 F32 = jnp.float32
@@ -127,8 +127,8 @@
     return d ^ 1, t
 
 
-def to_other_core(pieces):
-    return [exchange(x, other_core) for x in pieces]
+def each(pieces, partner):
+    return [exchange(x, partner) for x in pieces]
 
 
 VMEM = pl.BlockSpec(memory_space=pltpu.VMEM)
@@ -539,55 +539,55 @@
     _, fixed_down, keep, give = down_left(run, grad_down, error_down, start_down, 0, tiles)
     got = exchange(give, other_replica)
     gate_args = (run, grad_gate, error_gate, start_gate)
-    first = gate_left(*gate_args, 0, tiles // 2, after=(keep,))
+    cut = tiles * 3 // 5
+    first = gate_left(*gate_args, 0, cut, after=(keep,))
     (down,) = add(run, [keep], [got], after=(first[0],))
     got = exchange(down, steps[0])
     _, fixed_gate, keep_gate, *gives = gate_left(
-        *gate_args, tiles // 2, tiles - tiles // 2, first, after=(down,)
-    )
-    (gate,) = add(run, [keep_gate], to_other_core(gives))
-    got_gate = exchange(gate, hops[0])
+        *gate_args, cut, tiles - cut, first, after=(down,)
+    )
+    gate = add(run, [keep_gate], each(gives, other_core), in_two(slab))
+    gots_gate = each(gate, hops[0])
     for i in range(len(steps)):
-        (down,) = add(run, [down], [got], after=(gate,))
+        (down,) = add(run, [down], [got], after=(gate[0],))
         if i + 1 < len(steps):
             got = exchange(down, steps[i + 1])
     other_down = exchange(down, other_replica)
     for hop in hops[1:]:
-        (gate,) = add(run, [gate], [got_gate], after=(down,))
-        got_gate = exchange(gate, hop)
-
-    keep, *gives, left_down = down_right(run, [down], [other_down], fixed_down, after=(gate,))
-    gots = to_other_core(gives)
-    gates = add(run, [gate], [got_gate], in_two(slab), after=(keep,))
-    others_gate = to_other_core(gates)
-    down, gram_down = add(run, [keep], gots, [slab, 2 * RANK], after=(gates[0],))
+        gate = add(run, gate, gots_gate, after=(down,))
+        gots_gate = each(gate, hop)
+    gate = add(run, gate, gots_gate)
+    others_gate = each(gate, other_core)
+
+    keep_gate, give, gram_gate, left_gate = gate_right(run, gate, others_gate, fixed_gate)
+    got_gate = exchange(give, other_replica)
+    grams_gate = [gram_gate] + [
+        exchange(gram_gate, lambda d, t, b=b: (d ^ b, t)) for b in range(REPLICAS, n_dp, REPLICAS)
+    ]
+    keep, *gives, left_down = down_right(
+        run, [down], [other_down], fixed_down, after=(gram_gate,)
+    )
+    *down, gram_down = add(run, [keep], each(gives, other_core), [*in_two(slab), 2 * RANK])
     grams_down = [gram_down] + [
         exchange(gram_down, lambda d, t, b=b: (d, t ^ b)) for b in range(2, n_t, 2)
     ]
-    got = exchange(down, hops[0])
-    keep_gate, give_gate, gram_gate, left_gate = gate_right(
-        run, gates, others_gate, fixed_gate, after=(down,)
-    )
-    got_gate = exchange(give_gate, other_replica)
-    grams_gate = [gram_gate] + [
-        exchange(gram_gate, lambda d, t, b=b: (d ^ b, t)) for b in range(REPLICAS, n_dp, REPLICAS)
-    ]
+    gots = each(down, hops[0])
+    (gate,) = add(run, [keep_gate], [got_gate], after=(gram_down,))
+    got_gate = exchange(gate, steps[0])
     for hop in hops[1:]:
-        (down,) = add(run, [down], [got], after=(gram_gate,))
-        got = exchange(down, hop)
-    gram_down, gram_gate = gram_sums(run, grams_down, grams_gate, after=(down,))
-    (gate,) = add(run, [keep_gate], [got_gate], after=(gram_gate,))
-    got_gate = exchange(gate, steps[0])
-    col_stack, row_turned = solve(run, gram_down, left_down, gram_gate, left_gate, after=(gate,))
-    downs = add(run, [down], [got], in_two(slab), after=(col_stack,))
-    others_down = to_other_core(downs)
+        down = add(run, down, gots, after=(gate,))
+        gots = each(down, hop)
+    gram_down, gram_gate = gram_sums(run, grams_down, grams_gate, after=(down[0],))
+    col_stack, row_turned = solve(run, gram_down, left_down, gram_gate, left_gate)
+    down = add(run, down, gots, after=(col_stack,))
+    others_down = each(down, other_core)
     for i in range(len(steps)):
-        (gate,) = add(run, [gate], [got_gate], after=(downs[0],))
+        (gate,) = add(run, [gate], [got_gate], after=(down[0],))
         if i + 1 < len(steps):
             got_gate = exchange(gate, steps[i + 1])
     other_gate = exchange(gate, other_replica)
     new_error_down, update_down, done = rebuild(
-        run, None, col_stack, downs, others_down, fixed_down, slab // 4, after=(gate,)
+        run, None, col_stack, down, others_down, fixed_down, slab // 4, after=(gate,)
     )
     new_error_gate, update_gate, _ = rebuild(
         run, row_turned, None, [gate], [other_gate], fixed_gate, slab // 4, after=(done,)

time: 87.6 us -> 93.5 us (1.067)
  waiting for transfers between devices: 19.5 us -> 23.1 us
  starting transfers between devices: 20.9 us -> 23 us
    ppermute x20 -> x24, waiting for transfers between devices: 19.5 us -> 23.1 us  [exchange(): return lax.ppermute(x, ('dp', 'tensor'), pairs)]
    ppermute x20 -> x24, starting transfers between devices: 20.9 us -> 23 us  [exchange(): return lax.ppermute(x, ('dp', 'tensor'), pairs)]
  transfers between devices with their start and end apart: 20 -> 24, of which waited for: 11 -> 17; matrix products, arithmetic and copies ran while one was open for 0% -> 0% of each run, Pallas kernels for 33% -> 31%
where the time goes in v9:
time: 93.5 us; the launch traced here: 93.2 us
  Pallas kernels  46.3 us (50%)
  waiting for transfers between devices  23.1 us (25%)
  starting transfers between devices  23 us (25%)
    pallas_call x19, Pallas kernels, __call__(): pl.pallas_call(body, out_shape=tuple(((pltpu.VMEM if spec is VMEM else pl...  46.3 us
    ppermute x24, waiting for transfers between devices, exchange(): return lax.ppermute(x, ('dp', 'tensor'), pairs)  23.1 us
    ppermute x24, starting transfers between devices, exchange(): return lax.ppermute(x, ('dp', 'tensor'), pairs)  23 us
  transfers between devices with their start and end apart: 24, of which 17 were waited for; matrix products, arithmetic and copies ran while one was open for 0% of the time, Pallas kernels for 31%

profile of v9, /device:TPU:0, one launch (start us, length us, event | category | flops | bytes accessed | tf_op | source)
XLA Modules:
  0.0 93.2 jit_solution(17392487309398016359)
XLA Ops:
  0.6 10.1 %shard_map.93 = (f32[64,1792]{1,0:T(8,128)}, bf16[2560,1792]{1,0:T(8,128)(2,1)S(1)}, f32[32,1792]{1,0:T(8,128)S(1)}, f32[32,1792]{1,0:T(8,128)S(1)}) custom-call(bf16[2560,1792]{1,0:T(8,128)(2,1)} %refs_0_.3, bf16[2560,1792]{1,0:T(8,128)(2,1)} %refs_1_.3, bf16[64,5120]{1,0:T(8,128)(2,1)} %refs_2_.3), custom_call_target="tpu_custom_call" | custom-call | flops 9200000000 | bytes 1024 | tf_op jit(solution)/shard_map/pallas_call | solution.py:154
  10.8 3.0 %collective-permute-start = (f32[32,1792]{1,0:T(8,128)S(1)}, f32[32,1792]{1,0:T(8,128)S(1)}, u32[]{:S(2)}, u32[]{:S(2)}) collective-permute-start(f32[32,1792]{1,0:T(8,128)S(1)} %get-tuple-element.44), channel_id=1, source_target_pairs={{0,4},{1,5},{2,6},{3,7},{4,0},{5,1},{6,2},{7,3},{8,12},{9,13},{10,... | collective-permute-start | bytes 688136 | tf_op jit(solution)/shard_map/ppermute | solution.py:97
  13.8 5.1 %shard_map.94 = (f32[64,2560]{1,0:T(8,128)S(1)}, bf16[2560,1792]{1,0:T(8,128)(2,1)S(1)}) custom-call(bf16[2560,1792]{1,0:T(8,128)(2,1)} %refs_0_.5, bf16[2560,1792]{1,0:T(8,128)(2,1)} %refs_1_.5, bf16[64,1792]{1,0:T(8,128)(2,1)S(1)} %copy-done, f32[32,1792]{1,0:T(8,128)S(1)} %get-tuple-element.43.refs_3_.refs_0_), custom_call_target="tpu_custom_call" | custom-call | flops 4600000000 | bytes 1024 | tf_op jit(solution)/shard_map/pallas_call | solution.py:154
  19.4 2.8 %collective-permute-start.1 = (f32[32,1792]{1,0:T(8,128)S(1)}, f32[32,1792]{1,0:T(8,128)S(1)}, u32[]{:S(2)}, u32[]{:S(2)}) collective-permute-start(f32[32,1792]{1,0:T(8,128)S(1)} %shard_map.95.refs_5_.refs_0_), channel_id=1, source_target_pairs={{0,8},{1,9},{2,10},{3,11},{4,12},{5,13},{6,14},{7,15},{8,0},{9,1},... | collective-permute-start | bytes 688136 | tf_op jit(solution)/shard_map/ppermute | solution.py:97
  22.2 4.0 %shard_map.96 = (f32[64,2560]{1,0:T(8,128)S(1)}, bf16[2560,1792]{1,0:T(8,128)(2,1)S(1)}, f32[32,2560]{1,0:T(8,128)S(1)}, f32[32,1280]{1,0:T(8,128)S(1)}, f32[32,1280]{1,0:T(8,128)S(1)}) custom-call(bf16[2560,1792]{1,0:T(8,128)(2,1)} %refs_0_.5, bf16[2560,1792]{1,0:T(8,128)(2,1)} %refs_1_.5, ...), custom_call_target="tpu_custom_call", output_to_operand_aliasing={{0}: (3, {}), {1}: (4, {})} | custom-call | flops 4600000000 | bytes 1024 | tf_op jit(solution)/shard_map/pallas_call | solution.py:154
  27.9 1.6 %collective-permute-start.6 = (f32[32,1280]{1,0:T(8,128)S(1)}, f32[32,1280]{1,0:T(8,128)S(1)}, u32[]{:S(2)}, u32[]{:S(2)}) collective-permute-start(f32[32,1280]{1,0:T(8,128)S(1)} %get-tuple-element.52.refs_1_), channel_id=1, source_target_pairs={{0,2},{1,5},{2,0},{3,7},{4,6},{5,1},{6,4},{7,3},{8,10},{9,13},{10,... | collective-permute-start | bytes 491528 | tf_op jit(solution)/shard_map/ppermute | solution.py:97
  30.0 2.2 %collective-permute-done.1.refs_1_ = f32[32,1792]{1,0:T(8,128)S(1)} collective-permute-done((f32[32,1792]{1,0:T(8,128)S(1)}, f32[32,1792]{1,0:T(8,128)S(1)}, u32[]{:S(2)}, u32[]{:S(2)}) %collective-permute-start.1) | collective-permute-done | bytes 229408 | tf_op jit(solution)/shard_map/ppermute | solution.py:97
  33.3 1.8 %collective-permute-done.5.refs_2_ = f32[32,1280]{1,0:T(8,128)S(1)} collective-permute-done((f32[32,1280]{1,0:T(8,128)S(1)}, f32[32,1280]{1,0:T(8,128)S(1)}, u32[]{:S(2)}, u32[]{:S(2)}) %collective-permute-start.5) | collective-permute-done | bytes 163872 | tf_op jit(solution)/shard_map/ppermute | solution.py:97
  35.1 1.6 %collective-permute-start.7 = (f32[32,1280]{1,0:T(8,128)S(1)}, f32[32,1280]{1,0:T(8,128)S(1)}, u32[]{:S(2)}, u32[]{:S(2)}) collective-permute-start(f32[32,1280]{1,0:T(8,128)S(1)} %get-tuple-element.53.refs_0_), channel_id=1, source_target_pairs={{0,4},{1,3},{2,6},{3,1},{4,0},{5,7},{6,2},{7,5},{8,12},{9,11},{10,... | collective-permute-start | bytes 491528 | tf_op jit(solution)/shard_map/ppermute | solution.py:97
  37.2 1.6 %collective-permute-start.4 = (f32[32,1792]{1,0:T(8,128)S(1)}, f32[32,1792]{1,0:T(8,128)S(1)}, u32[]{:S(2)}, u32[]{:S(2)}) collective-permute-start(f32[32,1792]{1,0:T(8,128)S(1)} %shard_map.98.refs_4_.refs_0_), channel_id=1, source_target_pairs={{0,4},{1,5},{2,6},{3,7},{4,0},{5,1},{6,2},{7,3},{8,12},{9,13},{10,... | collective-permute-start | bytes 688136 | tf_op jit(solution)/shard_map/ppermute | solution.py:97
  38.8 2.7 %collective-permute-done.7.refs_2_ = f32[32,1280]{1,0:T(8,128)S(1)} collective-permute-done((f32[32,1280]{1,0:T(8,128)S(1)}, f32[32,1280]{1,0:T(8,128)S(1)}, u32[]{:S(2)}, u32[]{:S(2)}) %collective-permute-start.7) | collective-permute-done | bytes 163872 | tf_op jit(solution)/shard_map/ppermute | solution.py:97
  41.5 3.3 %collective-permute-done.8.refs_3_ = f32[32,1280]{1,0:T(8,128)S(1)} collective-permute-done((f32[32,1280]{1,0:T(8,128)S(1)}, f32[32,1280]{1,0:T(8,128)S(1)}, u32[]{:S(2)}, u32[]{:S(2)}) %collective-permute-start.8) | collective-permute-done | bytes 163872 | tf_op jit(solution)/shard_map/ppermute | solution.py:97
  46.4 3.2 %shard_map.101 = (f32[32,1792]{1,0:T(8,128)S(1)}, f32[32,1792]{1,0:T(8,128)S(1)}, f32[64,64]{1,0:T(8,128)S(1)}, bf16[192,2560]{1,0:T(8,128)(2,1)S(1)}) custom-call(f32[32,1280]{1,0:T(8,128)S(1)} %get-tuple-element.55.refs_0_, f32[32,1280]{1,0:T(8,128)S(1)} %get-tuple-element.56.refs_1_, f32[32,1280]{1,0:T(8,128)S(1)} %collective-permute-done.9.refs_2_, ...), custom_call_target="tpu_custom_call" | custom-call | flops 115000000 | bytes 1024 | tf_op jit(solution)/shard_map/pallas_call | solution.py:154
  49.7 1.6 %collective-permute-start.17 = (f32[32,1792]{1,0:T(8,128)S(1)}, f32[32,1792]{1,0:T(8,128)S(1)}, u32[]{:S(2)}, u32[]{:S(2)}) collective-permute-start(f32[32,1792]{1,0:T(8,128)S(1)} %get-tuple-element.66), channel_id=1, source_target_pairs={{0,4},{1,5},{2,6},{3,7},{4,0},{5,1},{6,2},{7,3},{8,12},{9,13},{10,... | collective-permute-start | bytes 688136 | tf_op jit(solution)/shard_map/ppermute | solution.py:97
  51.3 5.2 %shard_map.102 = (f32[32,2688]{1,0:T(8,128)S(1)}, f32[32,1280]{1,0:T(8,128)S(1)}, f32[32,1408]{1,0:T(8,128)S(1)}, bf16[192,1792]{1,0:T(8,128)(2,1)S(1)}) custom-call(f32[32,1792]{1,0:T(8,128)S(1)} %shard_map.98.refs_4_.refs_0_, f32[32,1792]{1,0:T(8,128)S(1)} %collective-permute-done.4.refs_1_, bf16[2560,1792]{1,0:T(8,128)(2,1)S(1)} %get-tuple-element.51.refs_2_.refs_5_, ...), custom_call_target="tpu_custom_call" | custom-call | flops 5750000128 | bytes 1024 | tf_op jit(solution)/shard_map/pallas_call | solution.py:154
  58.3 1.6 %collective-permute-start.13 = (f32[32,128]{1,0:T(8,128)S(1)}, f32[32,128]{1,0:T(8,128)S(1)}, u32[]{:S(2)}, u32[]{:S(2)}) collective-permute-start(f32[32,128]{1,0:T(8,128)S(1)} %get-tuple-element.62.refs_2_.refs_0_), channel_id=1, source_target_pairs={{0,2},{1,3},{2,0},{3,1},{4,6},{5,7},{6,4},{7,5},{8,10},{9,11},{10,... | collective-permute-start | bytes 49160 | tf_op jit(solution)/shard_map/ppermute | solution.py:97
  60.4 1.5 %collective-permute-start.16 = (f32[32,1280]{1,0:T(8,128)S(1)}, f32[32,1280]{1,0:T(8,128)S(1)}, u32[]{:S(2)}, u32[]{:S(2)}) collective-permute-start(f32[32,1280]{1,0:T(8,128)S(1)} %get-tuple-element.64.refs_1_), channel_id=1, source_target_pairs={{0,2},{1,5},{2,0},{3,7},{4,6},{5,1},{6,4},{7,3},{8,10},{9,13},{10,... | collective-permute-start | bytes 491528 | tf_op jit(solution)/shard_map/ppermute | solution.py:97
  61.9 1.9 %collective-permute-start.18 = (f32[32,1792]{1,0:T(8,128)S(1)}, f32[32,1792]{1,0:T(8,128)S(1)}, u32[]{:S(2)}, u32[]{:S(2)}) collective-permute-start(f32[32,1792]{1,0:T(8,128)S(1)} %shard_map.104.refs_4_.refs_0_), channel_id=1, source_target_pairs={{0,8},{1,9},{2,10},{3,11},{4,12},{5,13},{6,14},{7,15},{8,0},{9,1},... | collective-permute-start | bytes 688136 | tf_op jit(solution)/shard_map/ppermute | solution.py:97
  65.2 1.8 %collective-permute-done.16.refs_3_ = f32[32,1280]{1,0:T(8,128)S(1)} collective-permute-done((f32[32,1280]{1,0:T(8,128)S(1)}, f32[32,1280]{1,0:T(8,128)S(1)}, u32[]{:S(2)}, u32[]{:S(2)}) %collective-permute-start.16) | collective-permute-done | bytes 163872 | tf_op jit(solution)/shard_map/ppermute | solution.py:97
  69.1 3.9 %shard_map.107 = (bf16[256,1792]{1,0:T(8,128)(2,1)S(1)}, bf16[2560,256]{1,0:T(8,128)(2,1)S(1)}) custom-call(f32[64,64]{1,0:T(8,128)S(1)} %get-tuple-element.68.refs_0_, bf16[192,1792]{1,0:T(8,128)(2,1)S(1)} %get-tuple-element.69.refs_1_, f32[64,64]{1,0:T(8,128)S(1)} %get-tuple-element.70.refs_2_, bf16[192,2560]{1,0:T(8,128)(2,1)S(1)} %get-tuple-element.71.refs_3_), custom_call_target="tpu_custom_call" | custom-call | flops 5750000128 | bytes 1024 | tf_op jit(solution)/shard_map/pallas_call | solution.py:154
  73.0 2.3 %collective-permute-done.20.refs_3_ = f32[32,1280]{1,0:T(8,128)S(1)} collective-permute-done((f32[32,1280]{1,0:T(8,128)S(1)}, f32[32,1280]{1,0:T(8,128)S(1)}, u32[]{:S(2)}, u32[]{:S(2)}) %collective-permute-start.20) | collective-permute-done | bytes 163872 | tf_op jit(solution)/shard_map/ppermute | solution.py:97
  75.4 1.8 %collective-permute-done.19.refs_2_ = f32[32,1280]{1,0:T(8,128)S(1)} collective-permute-done((f32[32,1280]{1,0:T(8,128)S(1)}, f32[32,1280]{1,0:T(8,128)S(1)}, u32[]{:S(2)}, u32[]{:S(2)}) %collective-permute-start.19) | collective-permute-done | bytes 163872 | tf_op jit(solution)/shard_map/ppermute | solution.py:97
  78.9 7.0 %shard_map.110 = (bf16[2560,1792]{1,0:T(8,128)(2,1)}, bf16[1280,1792]{1,0:T(8,128)(2,1)}, f32[8,128]{1,0:T(8,128)S(1)}) custom-call(bf16[256,1792]{1,0:T(8,128)(2,1)S(1)} %get-tuple-element.74.refs_4_.refs_0_, f32[32,1280]{1,0:T(8,128)S(1)} %get-tuple-element.75.refs_2_.refs_1_, f32[32,1280]{1,0:T(8,128)S(1)} %get-tuple-element.76.refs_2_, ...), custom_call_target="tpu_custom_call" | custom-call | flops 9200000000 | bytes 1024 | tf_op jit(solution)/shard_map/pallas_call | solution.py:154
  85.9 7.3 %shard_map.111 = (bf16[2560,1792]{1,0:T(8,128)(2,1)}, bf16[1280,1792]{1,0:T(8,128)(2,1)}, f32[8,128]{1,0:T(8,128)}) custom-call(bf16[2560,256]{1,0:T(8,128)(2,1)S(1)} %get-tuple-element.72.refs_0_, f32[32,1792]{1,0:T(8,128)S(1)} %shard_map.109.refs_6_.refs_1_, f32[32,1792]{1,0:T(8,128)S(1)} %collective-permute-done.21.refs_2_, ...), custom_call_target="tpu_custom_call" | custom-call | flops 9200000000 | bytes 1024 | tf_op jit(solution)/shard_map/pallas_call | solution.py:154
  (45 shorter events, 13.8 us)
Async XLA Ops:
  10.8 8.6 %collective-permute-start = (f32[32,1792]{1,0:T(8,128)S(1)}, f32[32,1792]{1,0:T(8,128)S(1)}, u32[]{:S(2)}, u32[]{:S(2)}) collective-permute-start(f32[32,1792]{1,0:T(8,128)S(1)} %get-tuple-element.44), channel_id=1, source_target_pairs={{0,4},{1,5},{2,6},{3,7},{4,0},{5,1},{6,2},{7,3},{8,12},{9,13},{10,... | collective-permute-start | bytes 688136 | tf_op jit(solution)/shard_map/ppermute | solution.py:97
  19.4 12.8 %collective-permute-start.1 = (f32[32,1792]{1,0:T(8,128)S(1)}, f32[32,1792]{1,0:T(8,128)S(1)}, u32[]{:S(2)}, u32[]{:S(2)}) collective-permute-start(f32[32,1792]{1,0:T(8,128)S(1)} %shard_map.95.refs_5_.refs_0_), channel_id=1, source_target_pairs={{0,8},{1,9},{2,10},{3,11},{4,12},{5,13},{6,14},{7,15},{8,0},{9,1},... | collective-permute-start | bytes 688136 | tf_op jit(solution)/shard_map/ppermute | solution.py:97
  26.2 1.5 %collective-permute-start.2 = (f32[32,1280]{1,0:T(8,128)S(1)}, f32[32,1280]{1,0:T(8,128)S(1)}, u32[]{:S(2)}, u32[]{:S(2)}) collective-permute-start(f32[32,1280]{1,0:T(8,128)S(1)} %get-tuple-element.48), channel_id=1, source_target_pairs={{0,1},{1,0},{2,3},{3,2},{4,5},{5,4},{6,7},{7,6},{8,9},{9,8},{10,11... | collective-permute-start | bytes 491528 | tf_op jit(solution)/shard_map/ppermute | solution.py:97
  26.3 1.6 %collective-permute-start.3 = (f32[32,1280]{1,0:T(8,128)S(1)}, f32[32,1280]{1,0:T(8,128)S(1)}, u32[]{:S(2)}, u32[]{:S(2)}) collective-permute-start(f32[32,1280]{1,0:T(8,128)S(1)} %get-tuple-element.49), channel_id=1, source_target_pairs={{0,1},{1,0},{2,3},{3,2},{4,5},{5,4},{6,7},{7,6},{8,9},{9,8},{10,11... | collective-permute-start | bytes 491528 | tf_op jit(solution)/shard_map/ppermute | solution.py:97
  27.9 5.4 %collective-permute-start.6 = (f32[32,1280]{1,0:T(8,128)S(1)}, f32[32,1280]{1,0:T(8,128)S(1)}, u32[]{:S(2)}, u32[]{:S(2)}) collective-permute-start(f32[32,1280]{1,0:T(8,128)S(1)} %get-tuple-element.52.refs_1_), channel_id=1, source_target_pairs={{0,2},{1,5},{2,0},{3,7},{4,6},{5,1},{6,4},{7,3},{8,10},{9,13},{10,... | collective-permute-start | bytes 491528 | tf_op jit(solution)/shard_map/ppermute | solution.py:97
  29.5 5.6 %collective-permute-start.5 = (f32[32,1280]{1,0:T(8,128)S(1)}, f32[32,1280]{1,0:T(8,128)S(1)}, u32[]{:S(2)}, u32[]{:S(2)}) collective-permute-start(f32[32,1280]{1,0:T(8,128)S(1)} %get-tuple-element.50.refs_2_.refs_0_), channel_id=1, source_target_pairs={{0,2},{1,5},{2,0},{3,7},{4,6},{5,1},{6,4},{7,3},{8,10},{9,13},{10,... | collective-permute-start | bytes 491528 | tf_op jit(solution)/shard_map/ppermute | solution.py:97
  35.1 6.3 %collective-permute-start.7 = (f32[32,1280]{1,0:T(8,128)S(1)}, f32[32,1280]{1,0:T(8,128)S(1)}, u32[]{:S(2)}, u32[]{:S(2)}) collective-permute-start(f32[32,1280]{1,0:T(8,128)S(1)} %get-tuple-element.53.refs_0_), channel_id=1, source_target_pairs={{0,4},{1,3},{2,6},{3,1},{4,0},{5,7},{6,2},{7,5},{8,12},{9,11},{10,... | collective-permute-start | bytes 491528 | tf_op jit(solution)/shard_map/ppermute | solution.py:97
  36.8 8.0 %collective-permute-start.8 = (f32[32,1280]{1,0:T(8,128)S(1)}, f32[32,1280]{1,0:T(8,128)S(1)}, u32[]{:S(2)}, u32[]{:S(2)}) collective-permute-start(f32[32,1280]{1,0:T(8,128)S(1)} %get-tuple-element.54.refs_1_), channel_id=1, source_target_pairs={{0,4},{1,3},{2,6},{3,1},{4,0},{5,7},{6,2},{7,5},{8,12},{9,11},{10,... | collective-permute-start | bytes 491528 | tf_op jit(solution)/shard_map/ppermute | solution.py:97
  37.2 14.1 %collective-permute-start.4 = (f32[32,1792]{1,0:T(8,128)S(1)}, f32[32,1792]{1,0:T(8,128)S(1)}, u32[]{:S(2)}, u32[]{:S(2)}) collective-permute-start(f32[32,1792]{1,0:T(8,128)S(1)} %shard_map.98.refs_4_.refs_0_), channel_id=1, source_target_pairs={{0,4},{1,5},{2,6},{3,7},{4,0},{5,1},{6,2},{7,3},{8,12},{9,13},{10,... | collective-permute-start | bytes 688136 | tf_op jit(solution)/shard_map/ppermute | solution.py:97
  44.8 1.5 %collective-permute-start.9 = (f32[32,1280]{1,0:T(8,128)S(1)}, f32[32,1280]{1,0:T(8,128)S(1)}, u32[]{:S(2)}, u32[]{:S(2)}) collective-permute-start(f32[32,1280]{1,0:T(8,128)S(1)} %get-tuple-element.55.refs_0_), channel_id=1, source_target_pairs={{0,1},{1,0},{2,3},{3,2},{4,5},{5,4},{6,7},{7,6},{8,9},{9,8},{10,11... | collective-permute-start | bytes 491528 | tf_op jit(solution)/shard_map/ppermute | solution.py:97
  44.8 1.6 %collective-permute-start.10 = (f32[32,1280]{1,0:T(8,128)S(1)}, f32[32,1280]{1,0:T(8,128)S(1)}, u32[]{:S(2)}, u32[]{:S(2)}) collective-permute-start(f32[32,1280]{1,0:T(8,128)S(1)} %get-tuple-element.56.refs_1_), channel_id=1, source_target_pairs={{0,1},{1,0},{2,3},{3,2},{4,5},{5,4},{6,7},{7,6},{8,9},{9,8},{10,11... | collective-permute-start | bytes 491528 | tf_op jit(solution)/shard_map/ppermute | solution.py:97
  49.7 12.2 %collective-permute-start.17 = (f32[32,1792]{1,0:T(8,128)S(1)}, f32[32,1792]{1,0:T(8,128)S(1)}, u32[]{:S(2)}, u32[]{:S(2)}) collective-permute-start(f32[32,1792]{1,0:T(8,128)S(1)} %get-tuple-element.66), channel_id=1, source_target_pairs={{0,4},{1,5},{2,6},{3,7},{4,0},{5,1},{6,2},{7,3},{8,12},{9,13},{10,... | collective-permute-start | bytes 688136 | tf_op jit(solution)/shard_map/ppermute | solution.py:97
  56.5 1.7 %collective-permute-start.12 = (f32[32,1408]{1,0:T(8,128)S(1)}, f32[32,1408]{1,0:T(8,128)S(1)}, u32[]{:S(2)}, u32[]{:S(2)}) collective-permute-start(f32[32,1408]{1,0:T(8,128)S(1)} %get-tuple-element.61), channel_id=1, source_target_pairs={{0,1},{1,0},{2,3},{3,2},{4,5},{5,4},{6,7},{7,6},{8,9},{9,8},{10,11... | collective-permute-start | bytes 540680 | tf_op jit(solution)/shard_map/ppermute | solution.py:97
  56.6 1.6 %collective-permute-start.11 = (f32[32,1280]{1,0:T(8,128)S(1)}, f32[32,1280]{1,0:T(8,128)S(1)}, u32[]{:S(2)}, u32[]{:S(2)}) collective-permute-start(f32[32,1280]{1,0:T(8,128)S(1)} %get-tuple-element.60), channel_id=1, source_target_pairs={{0,1},{1,0},{2,3},{3,2},{4,5},{5,4},{6,7},{7,6},{8,9},{9,8},{10,11... | collective-permute-start | bytes 491528 | tf_op jit(solution)/shard_map/ppermute | solution.py:97
  57.1 11.9 %collective-permute-start.14 = (f32[64,64]{1,0:T(8,128)S(1)}, f32[64,64]{1,0:T(8,128)S(1)}, u32[]{:S(2)}, u32[]{:S(2)}) collective-permute-start(f32[64,64]{1,0:T(8,128)S(1)} %get-tuple-element.58.refs_3_.refs_2_), channel_id=1, source_target_pairs={{0,8},{1,9},{2,10},{3,11},{4,12},{5,13},{6,14},{7,15},{8,0},{9,1},... | collective-permute-start | bytes 49160 | tf_op jit(solution)/shard_map/ppermute | solution.py:97
  58.3 10.8 %collective-permute-start.13 = (f32[32,128]{1,0:T(8,128)S(1)}, f32[32,128]{1,0:T(8,128)S(1)}, u32[]{:S(2)}, u32[]{:S(2)}) collective-permute-start(f32[32,128]{1,0:T(8,128)S(1)} %get-tuple-element.62.refs_2_.refs_0_), channel_id=1, source_target_pairs={{0,2},{1,3},{2,0},{3,1},{4,6},{5,7},{6,4},{7,5},{8,10},{9,11},{10,... | collective-permute-start | bytes 49160 | tf_op jit(solution)/shard_map/ppermute | solution.py:97
  59.8 5.3 %collective-permute-start.15 = (f32[32,1280]{1,0:T(8,128)S(1)}, f32[32,1280]{1,0:T(8,128)S(1)}, u32[]{:S(2)}, u32[]{:S(2)}) collective-permute-start(f32[32,1280]{1,0:T(8,128)S(1)} %get-tuple-element.63.refs_0_), channel_id=1, source_target_pairs={{0,2},{1,5},{2,0},{3,7},{4,6},{5,1},{6,4},{7,3},{8,10},{9,13},{10,... | collective-permute-start | bytes 491528 | tf_op jit(solution)/shard_map/ppermute | solution.py:97
  60.4 6.5 %collective-permute-start.16 = (f32[32,1280]{1,0:T(8,128)S(1)}, f32[32,1280]{1,0:T(8,128)S(1)}, u32[]{:S(2)}, u32[]{:S(2)}) collective-permute-start(f32[32,1280]{1,0:T(8,128)S(1)} %get-tuple-element.64.refs_1_), channel_id=1, source_target_pairs={{0,2},{1,5},{2,0},{3,7},{4,6},{5,1},{6,4},{7,3},{8,10},{9,13},{10,... | collective-permute-start | bytes 491528 | tf_op jit(solution)/shard_map/ppermute | solution.py:97
  61.9 15.9 %collective-permute-start.18 = (f32[32,1792]{1,0:T(8,128)S(1)}, f32[32,1792]{1,0:T(8,128)S(1)}, u32[]{:S(2)}, u32[]{:S(2)}) collective-permute-start(f32[32,1792]{1,0:T(8,128)S(1)} %shard_map.104.refs_4_.refs_0_), channel_id=1, source_target_pairs={{0,8},{1,9},{2,10},{3,11},{4,12},{5,13},{6,14},{7,15},{8,0},{9,1},... | collective-permute-start | bytes 688136 | tf_op jit(solution)/shard_map/ppermute | solution.py:97
  67.0 8.4 %collective-permute-start.20 = (f32[32,1280]{1,0:T(8,128)S(1)}, f32[32,1280]{1,0:T(8,128)S(1)}, u32[]{:S(2)}, u32[]{:S(2)}) collective-permute-start(f32[32,1280]{1,0:T(8,128)S(1)} %get-tuple-element.73.refs_1_), channel_id=1, source_target_pairs={{0,4},{1,3},{2,6},{3,1},{4,0},{5,7},{6,2},{7,5},{8,12},{9,11},{10,... | collective-permute-start | bytes 491528 | tf_op jit(solution)/shard_map/ppermute | solution.py:97
  67.6 9.6 %collective-permute-start.19 = (f32[32,1280]{1,0:T(8,128)S(1)}, f32[32,1280]{1,0:T(8,128)S(1)}, u32[]{:S(2)}, u32[]{:S(2)}) collective-permute-start(f32[32,1280]{1,0:T(8,128)S(1)} %get-tuple-element.67.refs_4_.refs_0_), channel_id=1, source_target_pairs={{0,4},{1,3},{2,6},{3,1},{4,0},{5,7},{6,2},{7,5},{8,12},{9,11},{10,... | collective-permute-start | bytes 491528 | tf_op jit(solution)/shard_map/ppermute | solution.py:97
  77.2 1.5 %collective-permute-start.23 = (f32[32,1280]{1,0:T(8,128)S(1)}, f32[32,1280]{1,0:T(8,128)S(1)}, u32[]{:S(2)}, u32[]{:S(2)}) collective-permute-start(f32[32,1280]{1,0:T(8,128)S(1)} %get-tuple-element.76.refs_2_), channel_id=1, source_target_pairs={{0,1},{1,0},{2,3},{3,2},{4,5},{5,4},{6,7},{7,6},{8,9},{9,8},{10,11... | collective-permute-start | bytes 491528 | tf_op jit(solution)/shard_map/ppermute | solution.py:97
  77.3 1.6 %collective-permute-start.22 = (f32[32,1280]{1,0:T(8,128)S(1)}, f32[32,1280]{1,0:T(8,128)S(1)}, u32[]{:S(2)}, u32[]{:S(2)}) collective-permute-start(f32[32,1280]{1,0:T(8,128)S(1)} %get-tuple-element.75.refs_2_.refs_1_), channel_id=1, source_target_pairs={{0,1},{1,0},{2,3},{3,2},{4,5},{5,4},{6,7},{7,6},{8,9},{9,8},{10,11... | collective-permute-start | bytes 491528 | tf_op jit(solution)/shard_map/ppermute | solution.py:97
  77.8 8.1 %collective-permute-start.21 = (f32[32,1792]{1,0:T(8,128)S(1)}, f32[32,1792]{1,0:T(8,128)S(1)}, u32[]{:S(2)}, u32[]{:S(2)}) collective-permute-start(f32[32,1792]{1,0:T(8,128)S(1)} %shard_map.109.refs_6_.refs_1_), channel_id=1, source_target_pairs={{0,4},{1,5},{2,6},{3,7},{4,0},{5,1},{6,2},{7,3},{8,12},{9,13},{10,... | collective-permute-start | bytes 688136 | tf_op jit(solution)/shard_map/ppermute | solution.py:97
  (1 other events, 13.2 us)

commit v10 on v8

--- a/solution.py
+++ b/solution.py
@@ -11,7 +11,7 @@
 RANK = 64
 TILE = 256
 FLOPS = 1.15e9
-WEIGHTS = (8.0, 4.0, 1.0, 4.0, 0.1, 5.0, 1.0, 5.0, 1.0, 1.0, 4.0, 0.1, 0.1, 1.0, 5.0, 1.0, 1.0, 8.0, 8.0)
+WEIGHTS = (8.0, 4.0, 1.0, 4.0, 0.1, 5.0, 1.0, 5.0, 1.0, 1.0, 4.0, 0.1, 0.1, 1.0, 5.0, 1.0, 0.1, 1.0, 4.0, 4.0, 4.0)
 MIB = 1 << 20
 BF16 = jnp.bfloat16
 F32 = jnp.float32
@@ -459,72 +459,83 @@
     )
 
 
-def rebuild(run, row_turned, col_stack, owns, others, fixed, height, after=()):
-    halves = [
-        (x, half, sum(widths_of(xs[:i])))
-        for half, xs in ((0, owns), (HALF, others))
-        for i, x in enumerate(xs)
-    ]
+def rebuild(run, ready, owns, others, fixed, shares, first=0, before=None, after=()):
     rows, cols = fixed.shape
-    tiles = rows // REPLICAS // height
-    rows_late = row_turned is None
-    scratch = [pltpu.VMEM((4 * RANK, rows if rows_late else cols), BF16)]
-    if rows_late:
-        scratch.append(pltpu.VMEM((rows, 4 * RANK), BF16))
-    n_half = len(halves)
-
-    def kernel(ready, *refs):
-        fixed, new_error, update, done, late, *turned = refs[n_half:]
-        done[...] = jnp.zeros_like(done)
-        order = ROW_ORDER if rows_late else COL_ORDER
-        for (_, at, left), ref in zip(halves, refs):
-            parts = parts_of(ref[...])
-            n, width = ref.shape
-            for k, which in enumerate(order):
-                late[k * RANK + at : k * RANK + at + n, left : left + width] = parts[which]
-        row, col = ready, late
+    share = rows // REPLICAS
+    height = share // 2
+    rows_late = ready[0] is None
+    late_width = sum(widths_of(owns))
+    width = ready[1].shape[1] if rows_late or not owns else late_width
+    n_ready = sum(x is not None for x in ready)
+    n_own, n_late = len(owns), len(owns) + len(others)
+    n_before = 0 if before is None else len(before)
+    with_update = 0 in shares
+    spots = [(s, t, j) for s in shares for t in range(2) for j in range(0, width, TILE)]
+
+    def kernel(*refs):
+        given, late = refs[:n_ready], refs[n_ready : n_ready + n_late]
+        fixed = refs[n_ready + n_late]
+        refs = refs[n_ready + n_late + 1 + n_before :]
+        new_error, update, turned = refs[0], refs[1], refs[2]
+        errors, updates, stack, error_sems, update_sems = refs[3:]
+        if late:
+            order = ROW_ORDER if rows_late else COL_ORDER
+            for at, pieces in ((0, late[:n_own]), (HALF, late[n_own:])):
+                left = 0
+                for ref in pieces:
+                    parts = parts_of(ref[...])
+                    n, w = ref.shape
+                    for k, which in enumerate(order):
+                        stack[k * RANK + at : k * RANK + at + n, left : left + w] = parts[which]
+                    left += w
         if rows_late:
-            row, col = turned[0], ready
-            turn(late, row)
+            turn(stack, turned)
+            row, col = turned, given[0]
+        else:
+            turned[...] = jnp.zeros_like(turned)
+            row, col = given[0], given[1] if n_ready == 2 else stack
         replica = replica_of()
-        mine, theirs = replica * tiles, (1 - replica) * tiles
-
-        def tile_of(i):
-            return jnp.where(i < tiles, mine + i, theirs + i - tiles)
-
-        def step(e, u):
-            i = pl.program_id(0)
-            at = pl.ds(pl.multiple_of(tile_of(i) * height, height), height)
-
-            def tile(with_update):
-                row_here = row[at, :]
-                for j in range(0, cols, TILE):
-                    here = slice(j, j + TILE)
-                    value = jnp.dot(row_here, col[:, here], preferred_element_type=F32)
-                    e[:, here] = (fixed[at, here].astype(F32) - value).astype(BF16)
-                    if with_update:
-                        u[:, here] = value.astype(BF16)
-
-            pl.when(i < tiles)(lambda: tile(True))
-            pl.when(i >= tiles)(lambda: tile(False))
-
-        block = (height, cols)
-        pltpu.emit_pipeline(
-            step,
-            grid=(REPLICAS * tiles,),
-            out_specs=[
-                pl.BlockSpec(block, lambda i: (tile_of(i), 0)),
-                pl.BlockSpec(block, lambda i: (jnp.minimum(i, tiles - 1), 0)),
-            ],
-        )(new_error, update)
-
-    pieces = [x for x, _, _ in halves]
+        copies = []
+        for k, (s, t, j) in enumerate(spots):
+            at = pl.multiple_of((replica if s == 0 else 1 - replica) * share, height) + t * height
+            at = pl.ds(pl.multiple_of(at, height), height)
+            here, there = slice(j, j + TILE), pl.ds(first + j, TILE)
+            mine = pl.ds(t * height, height)
+            value = jnp.dot(row[at, :], col[:, here], preferred_element_type=F32)
+            slot = pl.ds((shares.index(s) * 2 + t) * height, height)
+            errors[slot, here] = (fixed[at, there].astype(F32) - value).astype(BF16)
+            copies.append(
+                pltpu.make_async_copy(errors.at[slot, here], new_error.at[at, there], error_sems.at[k])
+            )
+            copies[-1].start()
+            if s == 0:
+                updates[mine, here] = value.astype(BF16)
+                copies.append(
+                    pltpu.make_async_copy(updates.at[mine, here], update.at[mine, there], update_sems.at[k])
+                )
+                copies[-1].start()
+        for copy in copies:
+            copy.wait()
+
+    turned_shape = (rows, 4 * RANK) if rows_late else (16, 128)
+    args = [(x, VMEM) for x in (*(x for x in ready if x is not None), *owns, *others, fixed)]
+    aliases = None
+    if before is not None:
+        aliases = {len(args): 0, len(args) + 1: 1}
+        args += [(x, HBM) for x in before]
     return run(
         kernel,
-        [(x, VMEM) for x in (col_stack if rows_late else row_turned, *pieces, fixed)],
-        [((rows, cols), BF16, HBM), ((rows // REPLICAS, cols), BF16, HBM), ((8, 128), F32, VMEM)],
-        scratch,
+        args,
+        [((rows, cols), BF16, HBM), ((share, cols), BF16, HBM), (turned_shape, BF16, VMEM)],
+        [
+            pltpu.VMEM((len(shares) * share, width), BF16),
+            pltpu.VMEM((share if with_update else 16, width), BF16),
+            pltpu.VMEM((4 * RANK, late_width if n_late else 128), BF16),
+            pltpu.SemaphoreType.DMA((len(spots),)),
+            pltpu.SemaphoreType.DMA((len(spots),)),
+        ],
         mib=18,
+        aliases=aliases,
         after=after,
     )
 
@@ -539,11 +550,12 @@
     _, fixed_down, keep, give = down_left(run, grad_down, error_down, start_down, 0, tiles)
     got = exchange(give, other_replica)
     gate_args = (run, grad_gate, error_gate, start_gate)
-    first = gate_left(*gate_args, 0, tiles // 2, after=(keep,))
+    cut = tiles * 3 // 5
+    first = gate_left(*gate_args, 0, cut, after=(keep,))
     (down,) = add(run, [keep], [got], after=(first[0],))
     got = exchange(down, steps[0])
     _, fixed_gate, keep_gate, *gives = gate_left(
-        *gate_args, tiles // 2, tiles - tiles // 2, first, after=(down,)
+        *gate_args, cut, tiles - cut, first, after=(down,)
     )
     (gate,) = add(run, [keep_gate], to_other_core(gives))
     got_gate = exchange(gate, hops[0])
@@ -581,16 +593,26 @@
     col_stack, row_turned = solve(run, gram_down, left_down, gram_gate, left_gate, after=(gate,))
     downs = add(run, [down], [got], in_two(slab), after=(col_stack,))
     others_down = to_other_core(downs)
+    *outs_down, turned = rebuild(
+        run, (None, col_stack), downs, others_down, fixed_down, (0,), after=(downs[0],)
+    )
+    few = width // TILE * 3 // 7 * TILE
     for i in range(len(steps)):
-        (gate,) = add(run, [gate], [got_gate], after=(downs[0],))
-        if i + 1 < len(steps):
+        last = i + 1 == len(steps)
+        gate = add(run, [gate], [got_gate], [few, width - few] if last else None, after=(turned,))
+        if not last:
+            (gate,) = gate
             got_gate = exchange(gate, steps[i + 1])
-    other_gate = exchange(gate, other_replica)
+    others_gate = [exchange(x, other_replica) for x in gate]
     new_error_down, update_down, done = rebuild(
-        run, None, col_stack, downs, others_down, fixed_down, slab // 4, after=(gate,)
+        run, (turned, col_stack), [], [], fixed_down, (1,), before=outs_down, after=(gate[0],)
+    )
+    *outs_gate, done = rebuild(
+        run, (row_turned, None), gate[:1], others_gate[:1], fixed_gate, (0, 1), after=(done,)
     )
     new_error_gate, update_gate, _ = rebuild(
-        run, row_turned, None, [gate], [other_gate], fixed_gate, slab // 4, after=(done,)
+        run, (row_turned, None), gate[1:], others_gate[1:], fixed_gate, (0, 1), few, outs_gate,
+        after=(done,),
     )
     return (update_gate, update_down, new_error_gate, new_error_down)
 

time: 87.6 us -> 86.7 us (0.990)
  waiting for transfers between devices: 19.5 us -> 16.1 us
  starting transfers between devices: 20.9 us -> 22.9 us
    ppermute x20 -> x21, waiting for transfers between devices: 19.5 us -> 16.1 us  [exchange(): return lax.ppermute(x, ('dp', 'tensor'), pairs)]
    ppermute x20 -> x21, starting transfers between devices: 20.9 us -> 22.9 us  [exchange(): return lax.ppermute(x, ('dp', 'tensor'), pairs)]
    pallas_call x19 -> x21, Pallas kernels: 46.2 us -> 46.5 us  [__call__(): pl.pallas_call(body, out_shape=tuple(((pltpu.VMEM if spec is VMEM else pl...]
  transfers between devices with their start and end apart: 20 -> 21, of which waited for: 11 -> 13; matrix products, arithmetic and copies ran while one was open for 0% -> 0% of each run, Pallas kernels for 33% -> 37%
where the time goes in v10:
time: 86.7 us; the launch traced here: 86.5 us
  Pallas kernels  46.5 us (54%)
  starting transfers between devices  22.9 us (26%)
  waiting for transfers between devices  16.1 us (19%)
  between operations  0.96 us (1%)
    pallas_call x21, Pallas kernels, __call__(): pl.pallas_call(body, out_shape=tuple(((pltpu.VMEM if spec is VMEM else pl...  46.5 us
    ppermute x21, starting transfers between devices, exchange(): return lax.ppermute(x, ('dp', 'tensor'), pairs)  22.9 us
    ppermute x21, waiting for transfers between devices, exchange(): return lax.ppermute(x, ('dp', 'tensor'), pairs)  16.1 us
  transfers between devices with their start and end apart: 21, of which 13 were waited for; matrix products, arithmetic and copies ran while one was open for 0% of the time, Pallas kernels for 37%

profile of v10, /device:TPU:0, one launch (start us, length us, event | category | flops | bytes accessed | tf_op | source)
XLA Modules:
  0.0 86.5 jit_solution(15429862984794351523)
XLA Ops:
  0.6 10.1 %shard_map.93 = (f32[64,1792]{1,0:T(8,128)}, bf16[2560,1792]{1,0:T(8,128)(2,1)S(1)}, f32[32,1792]{1,0:T(8,128)S(1)}, f32[32,1792]{1,0:T(8,128)S(1)}) custom-call(bf16[2560,1792]{1,0:T(8,128)(2,1)} %refs_0_.3, bf16[2560,1792]{1,0:T(8,128)(2,1)} %refs_1_.3, bf16[64,5120]{1,0:T(8,128)(2,1)} %refs_2_.3), custom_call_target="tpu_custom_call" | custom-call | flops 9200000000 | bytes 1024 | tf_op jit(solution)/shard_map/pallas_call | solution.py:154
  10.8 3.0 %collective-permute-start = (f32[32,1792]{1,0:T(8,128)S(1)}, f32[32,1792]{1,0:T(8,128)S(1)}, u32[]{:S(2)}, u32[]{:S(2)}) collective-permute-start(f32[32,1792]{1,0:T(8,128)S(1)} %get-tuple-element.45), channel_id=1, source_target_pairs={{0,4},{1,5},{2,6},{3,7},{4,0},{5,1},{6,2},{7,3},{8,12},{9,13},{10,... | collective-permute-start | bytes 688136 | tf_op jit(solution)/shard_map/ppermute | solution.py:97
  13.8 5.1 %shard_map.94 = (f32[64,2560]{1,0:T(8,128)S(1)}, bf16[2560,1792]{1,0:T(8,128)(2,1)S(1)}) custom-call(bf16[2560,1792]{1,0:T(8,128)(2,1)} %refs_0_.5, bf16[2560,1792]{1,0:T(8,128)(2,1)} %refs_1_.5, bf16[64,1792]{1,0:T(8,128)(2,1)S(1)} %copy-done, f32[32,1792]{1,0:T(8,128)S(1)} %get-tuple-element.44.refs_3_.refs_0_), custom_call_target="tpu_custom_call" | custom-call | flops 4600000000 | bytes 1024 | tf_op jit(solution)/shard_map/pallas_call | solution.py:154
  19.4 2.8 %collective-permute-start.1 = (f32[32,1792]{1,0:T(8,128)S(1)}, f32[32,1792]{1,0:T(8,128)S(1)}, u32[]{:S(2)}, u32[]{:S(2)}) collective-permute-start(f32[32,1792]{1,0:T(8,128)S(1)} %shard_map.95.refs_5_.refs_0_), channel_id=1, source_target_pairs={{0,8},{1,9},{2,10},{3,11},{4,12},{5,13},{6,14},{7,15},{8,0},{9,1},... | collective-permute-start | bytes 688136 | tf_op jit(solution)/shard_map/ppermute | solution.py:97
  22.2 4.0 %shard_map.96 = (f32[64,2560]{1,0:T(8,128)S(1)}, bf16[2560,1792]{1,0:T(8,128)(2,1)S(1)}, f32[32,2560]{1,0:T(8,128)S(1)}, f32[32,1280]{1,0:T(8,128)S(1)}, f32[32,1280]{1,0:T(8,128)S(1)}) custom-call(bf16[2560,1792]{1,0:T(8,128)(2,1)} %refs_0_.5, bf16[2560,1792]{1,0:T(8,128)(2,1)} %refs_1_.5, ...), custom_call_target="tpu_custom_call", output_to_operand_aliasing={{0}: (3, {}), {1}: (4, {})} | custom-call | flops 4600000000 | bytes 1024 | tf_op jit(solution)/shard_map/pallas_call | solution.py:154
  26.8 0.9 %collective-permute-done.2.refs_1_ = f32[32,1280]{1,0:T(8,128)S(1)} collective-permute-done((f32[32,1280]{1,0:T(8,128)S(1)}, f32[32,1280]{1,0:T(8,128)S(1)}, u32[]{:S(2)}, u32[]{:S(2)}) %collective-permute-start.2) | collective-permute-done | bytes 163872 | tf_op jit(solution)/shard_map/ppermute | solution.py:97
  27.9 1.6 %collective-permute-start.5 = (f32[32,2560]{1,0:T(8,128)S(1)}, f32[32,2560]{1,0:T(8,128)S(1)}, u32[]{:S(2)}, u32[]{:S(2)}) collective-permute-start(f32[32,2560]{1,0:T(8,128)S(1)} %shard_map.97.refs_2_.refs_0_), channel_id=1, source_target_pairs={{0,2},{1,5},{2,0},{3,7},{4,6},{5,1},{6,4},{7,3},{8,10},{9,13},{10,... | collective-permute-start | bytes 983048 | tf_op jit(solution)/shard_map/ppermute | solution.py:97
  29.5 2.7 %collective-permute-done.1.refs_1_ = f32[32,1792]{1,0:T(8,128)S(1)} collective-permute-done((f32[32,1792]{1,0:T(8,128)S(1)}, f32[32,1792]{1,0:T(8,128)S(1)}, u32[]{:S(2)}, u32[]{:S(2)}) %collective-permute-start.1) | collective-permute-done | bytes 229408 | tf_op jit(solution)/shard_map/ppermute | solution.py:97
  32.7 2.3 %collective-permute-done.5.refs_1_ = f32[32,2560]{1,0:T(8,128)S(1)} collective-permute-done((f32[32,2560]{1,0:T(8,128)S(1)}, f32[32,2560]{1,0:T(8,128)S(1)}, u32[]{:S(2)}, u32[]{:S(2)}) %collective-permute-start.5) | collective-permute-done | bytes 327712 | tf_op jit(solution)/shard_map/ppermute | solution.py:97
  35.1 1.6 %collective-permute-start.8 = (f32[32,2560]{1,0:T(8,128)S(1)}, f32[32,2560]{1,0:T(8,128)S(1)}, u32[]{:S(2)}, u32[]{:S(2)}) collective-permute-start(f32[32,2560]{1,0:T(8,128)S(1)} %shard_map.99.refs_3_.refs_0_), channel_id=1, source_target_pairs={{0,4},{1,3},{2,6},{3,1},{4,0},{5,7},{6,2},{7,5},{8,12},{9,11},{10,... | collective-permute-start | bytes 983048 | tf_op jit(solution)/shard_map/ppermute | solution.py:97
  36.8 3.7 %collective-permute-done.4.refs_1_ = f32[32,1792]{1,0:T(8,128)S(1)} collective-permute-done((f32[32,1792]{1,0:T(8,128)S(1)}, f32[32,1792]{1,0:T(8,128)S(1)}, u32[]{:S(2)}, u32[]{:S(2)}) %collective-permute-start.4) | collective-permute-done | bytes 229408 | tf_op jit(solution)/shard_map/ppermute | solution.py:97
  40.5 5.2 %shard_map.100 = (f32[32,2688]{1,0:T(8,128)S(1)}, f32[32,1280]{1,0:T(8,128)S(1)}, f32[32,1408]{1,0:T(8,128)S(1)}, bf16[192,1792]{1,0:T(8,128)(2,1)S(1)}) custom-call(f32[32,1792]{1,0:T(8,128)S(1)} %shard_map.98.refs_2_.refs_0_, f32[32,1792]{1,0:T(8,128)S(1)} %collective-permute-done.4.refs_1_, bf16[2560,1792]{1,0:T(8,128)(2,1)S(1)} %get-tuple-element.51.refs_2_.refs_5_, ...), custom_call_target="tpu_custom_call" | custom-call | flops 5750000128 | bytes 1024 | tf_op jit(solution)/shard_map/pallas_call | solution.py:154
  47.5 1.4 %collective-permute-start.13 = (f32[32,2560]{1,0:T(8,128)S(1)}, f32[32,2560]{1,0:T(8,128)S(1)}, u32[]{:S(2)}, u32[]{:S(2)}) collective-permute-start(f32[32,2560]{1,0:T(8,128)S(1)} %get-tuple-element.59.refs_5_.refs_0_), channel_id=1, source_target_pairs={{0,2},{1,5},{2,0},{3,7},{4,6},{5,1},{6,4},{7,3},{8,10},{9,13},{10,... | collective-permute-start | bytes 983048 | tf_op jit(solution)/shard_map/ppermute | solution.py:97
  48.9 3.4 %shard_map.103 = (f32[32,1792]{1,0:T(8,128)S(1)}, f32[32,1792]{1,0:T(8,128)S(1)}, f32[64,64]{1,0:T(8,128)S(1)}, bf16[192,2560]{1,0:T(8,128)(2,1)S(1)}) custom-call(f32[32,1280]{1,0:T(8,128)S(1)} %get-tuple-element.55.refs_3_.refs_0_, f32[32,1280]{1,0:T(8,128)S(1)} %get-tuple-element.57.refs_1_, f32[32,1280]{1,0:T(8,128)S(1)} %collective-permute-done.10.refs_2_, ...), custom_call_target="tpu_custom_call" | custom-call | flops 4600000000 | bytes 1024 | tf_op jit(solution)/shard_map/pallas_call | solution.py:154
  53.5 3.5 %collective-permute-start.12 = (f32[64,64]{1,0:T(8,128)S(1)}, f32[64,64]{1,0:T(8,128)S(1)}, u32[]{:S(2)}, u32[]{:S(2)}) collective-permute-start(f32[64,64]{1,0:T(8,128)S(1)} %get-tuple-element.60.refs_2_), channel_id=1, source_target_pairs={{0,8},{1,9},{2,10},{3,11},{4,12},{5,13},{6,14},{7,15},{8,0},{9,1},... | collective-permute-start | bytes 49160 | tf_op jit(solution)/shard_map/ppermute | solution.py:97
  57.2 1.8 %collective-permute-done.12.refs_3_ = f32[64,64]{1,0:T(8,128)S(1)} collective-permute-done((f32[64,64]{1,0:T(8,128)S(1)}, f32[64,64]{1,0:T(8,128)S(1)}, u32[]{:S(2)}, u32[]{:S(2)}) %collective-permute-start.12) | collective-permute-done | bytes 16416 | tf_op jit(solution)/shard_map/ppermute | solution.py:97
  59.1 1.0 %collective-permute-done.14.refs_1_ = f32[32,1792]{1,0:T(8,128)S(1)} collective-permute-done((f32[32,1792]{1,0:T(8,128)S(1)}, f32[32,1792]{1,0:T(8,128)S(1)}, u32[]{:S(2)}, u32[]{:S(2)}) %collective-permute-start.14) | collective-permute-done | bytes 229408 | tf_op jit(solution)/shard_map/ppermute | solution.py:97
  60.1 2.8 %collective-permute-start.15 = (f32[32,1792]{1,0:T(8,128)S(1)}, f32[32,1792]{1,0:T(8,128)S(1)}, u32[]{:S(2)}, u32[]{:S(2)}) collective-permute-start(f32[32,1792]{1,0:T(8,128)S(1)} %shard_map.106.refs_4_.refs_0_), channel_id=1, source_target_pairs={{0,8},{1,9},{2,10},{3,11},{4,12},{5,13},{6,14},{7,15},{8,0},{9,1},... | collective-permute-start | bytes 688136 | tf_op jit(solution)/shard_map/ppermute | solution.py:97
  62.9 3.9 %shard_map.107 = (bf16[256,1792]{1,0:T(8,128)(2,1)S(1)}, bf16[2560,256]{1,0:T(8,128)(2,1)S(1)}) custom-call(f32[64,64]{1,0:T(8,128)S(1)} %get-tuple-element.61.refs_0_, bf16[192,1792]{1,0:T(8,128)(2,1)S(1)} %get-tuple-element.62.refs_1_, f32[64,64]{1,0:T(8,128)S(1)} %get-tuple-element.63.refs_2_, bf16[192,2560]{1,0:T(8,128)(2,1)S(1)} %get-tuple-element.64.refs_3_, ...), custom_call_target="tpu_custom_call" | custom-call | flops 5750000128 | bytes 1024 | tf_op jit(solution)/shard_map/pallas_call | solution.py:154
  69.0 4.2 %shard_map.109 = (bf16[2560,1792]{1,0:T(8,128)(2,1)}, bf16[1280,1792]{1,0:T(8,128)(2,1)}, bf16[2560,256]{1,0:T(8,128)(2,1)S(1)}) custom-call(bf16[256,1792]{1,0:T(8,128)(2,1)S(1)} %get-tuple-element.68.refs_2_.refs_0_.refs_1_, f32[32,1280]{1,0:T(8,128)S(1)} %get-tuple-element.69.refs_1_.refs_6_, f32[32,1280]{1,0:T(8,128)S(1)} %get-tuple-element.70.refs_2_, ...), custom_call_target="tpu_custom_call" | custom-call | flops 115000000 | bytes 1024 | tf_op jit(solution)/shard_map/pallas_call | solution.py:154
  74.0 1.3 %collective-permute-start.19 = (f32[32,1024]{1,0:T(8,128)S(1)}, f32[32,1024]{1,0:T(8,128)S(1)}, u32[]{:S(2)}, u32[]{:S(2)}) collective-permute-start(f32[32,1024]{1,0:T(8,128)S(1)} %get-tuple-element.72.refs_1_), channel_id=1, source_target_pairs={{0,4},{1,5},{2,6},{3,7},{4,0},{5,1},{6,2},{7,3},{8,12},{9,13},{10,... | collective-permute-start | bytes 393224 | tf_op jit(solution)/shard_map/ppermute | solution.py:97
  75.3 2.7 %shard_map.111 = (bf16[2560,1792]{1,0:T(8,128)(2,1)}, bf16[1280,1792]{1,0:T(8,128)(2,1)}, bf16[16,128]{1,0:T(8,128)(2,1)S(1)}) custom-call(bf16[2560,256]{1,0:T(8,128)(2,1)S(1)} %get-tuple-element.71.refs_2_.refs_0_, bf16[256,1792]{1,0:T(8,128)(2,1)S(1)} %get-tuple-element.68.refs_2_.refs_0_.refs_1_, ...), custom_call_target="tpu_custom_call", output_to_operand_aliasing={{0}: (3, {}), {1}: (4, {})} | custom-call | flops 4600000000 | bytes 1024 | tf_op jit(solution)/shard_map/pallas_call | solution.py:154
  78.9 3.1 %shard_map.112 = (bf16[2560,1792]{1,0:T(8,128)(2,1)}, bf16[1280,1792]{1,0:T(8,128)(2,1)}, bf16[16,128]{1,0:T(8,128)(2,1)S(1)}) custom-call(bf16[2560,256]{1,0:T(8,128)(2,1)S(1)} %get-tuple-element.67.refs_0_, f32[32,768]{1,0:T(8,128)S(1)} %get-tuple-element.73.refs_5_.refs_1_, f32[32,768]{1,0:T(8,128)S(1)} %collective-permute-done.20.refs_2_, ...), custom_call_target="tpu_custom_call" | custom-call | flops 4600000000 | bytes 1024 | tf_op jit(solution)/shard_map/pallas_call | solution.py:154
  82.0 4.3 %shard_map.113 = (bf16[2560,1792]{1,0:T(8,128)(2,1)}, bf16[1280,1792]{1,0:T(8,128)(2,1)}, bf16[16,128]{1,0:T(8,128)(2,1)}) custom-call(bf16[2560,256]{1,0:T(8,128)(2,1)S(1)} %get-tuple-element.67.refs_0_, f32[32,1024]{1,0:T(8,128)S(1)} %get-tuple-element.72.refs_1_, ...), custom_call_target="tpu_custom_call", output_to_operand_aliasing={{0}: (4, {}), {1}: (5, {})} | custom-call | flops 4600000000 | bytes 1024 | tf_op jit(solution)/shard_map/pallas_call | solution.py:154
  (41 shorter events, 8.9 us)
Async XLA Ops:
  0.6 13.2 %copy-start = (bf16[64,1792]{1,0:T(8,128)(2,1)S(1)}, bf16[64,1792]{1,0:T(8,128)(2,1)}, u32[]{:S(2)}) copy-start(bf16[64,1792]{1,0:T(8,128)(2,1)} %refs_2_.5) | copy-start | bytes 688132
  10.8 8.6 %collective-permute-start = (f32[32,1792]{1,0:T(8,128)S(1)}, f32[32,1792]{1,0:T(8,128)S(1)}, u32[]{:S(2)}, u32[]{:S(2)}) collective-permute-start(f32[32,1792]{1,0:T(8,128)S(1)} %get-tuple-element.45), channel_id=1, source_target_pairs={{0,4},{1,5},{2,6},{3,7},{4,0},{5,1},{6,2},{7,3},{8,12},{9,13},{10,... | collective-permute-start | bytes 688136 | tf_op jit(solution)/shard_map/ppermute | solution.py:97
  19.4 12.8 %collective-permute-start.1 = (f32[32,1792]{1,0:T(8,128)S(1)}, f32[32,1792]{1,0:T(8,128)S(1)}, u32[]{:S(2)}, u32[]{:S(2)}) collective-permute-start(f32[32,1792]{1,0:T(8,128)S(1)} %shard_map.95.refs_5_.refs_0_), channel_id=1, source_target_pairs={{0,8},{1,9},{2,10},{3,11},{4,12},{5,13},{6,14},{7,15},{8,0},{9,1},... | collective-permute-start | bytes 688136 | tf_op jit(solution)/shard_map/ppermute | solution.py:97
  26.2 1.5 %collective-permute-start.2 = (f32[32,1280]{1,0:T(8,128)S(1)}, f32[32,1280]{1,0:T(8,128)S(1)}, u32[]{:S(2)}, u32[]{:S(2)}) collective-permute-start(f32[32,1280]{1,0:T(8,128)S(1)} %get-tuple-element.49), channel_id=1, source_target_pairs={{0,1},{1,0},{2,3},{3,2},{4,5},{5,4},{6,7},{7,6},{8,9},{9,8},{10,11... | collective-permute-start | bytes 491528 | tf_op jit(solution)/shard_map/ppermute | solution.py:97
  26.3 1.6 %collective-permute-start.3 = (f32[32,1280]{1,0:T(8,128)S(1)}, f32[32,1280]{1,0:T(8,128)S(1)}, u32[]{:S(2)}, u32[]{:S(2)}) collective-permute-start(f32[32,1280]{1,0:T(8,128)S(1)} %get-tuple-element.50), channel_id=1, source_target_pairs={{0,1},{1,0},{2,3},{3,2},{4,5},{5,4},{6,7},{7,6},{8,9},{9,8},{10,11... | collective-permute-start | bytes 491528 | tf_op jit(solution)/shard_map/ppermute | solution.py:97
  27.9 7.1 %collective-permute-start.5 = (f32[32,2560]{1,0:T(8,128)S(1)}, f32[32,2560]{1,0:T(8,128)S(1)}, u32[]{:S(2)}, u32[]{:S(2)}) collective-permute-start(f32[32,2560]{1,0:T(8,128)S(1)} %shard_map.97.refs_2_.refs_0_), channel_id=1, source_target_pairs={{0,2},{1,5},{2,0},{3,7},{4,6},{5,1},{6,4},{7,3},{8,10},{9,13},{10,... | collective-permute-start | bytes 983048 | tf_op jit(solution)/shard_map/ppermute | solution.py:97
  32.2 8.3 %collective-permute-start.4 = (f32[32,1792]{1,0:T(8,128)S(1)}, f32[32,1792]{1,0:T(8,128)S(1)}, u32[]{:S(2)}, u32[]{:S(2)}) collective-permute-start(f32[32,1792]{1,0:T(8,128)S(1)} %shard_map.98.refs_2_.refs_0_), channel_id=1, source_target_pairs={{0,4},{1,5},{2,6},{3,7},{4,0},{5,1},{6,2},{7,3},{8,12},{9,13},{10,... | collective-permute-start | bytes 688136 | tf_op jit(solution)/shard_map/ppermute | solution.py:97
  35.1 11.2 %collective-permute-start.8 = (f32[32,2560]{1,0:T(8,128)S(1)}, f32[32,2560]{1,0:T(8,128)S(1)}, u32[]{:S(2)}, u32[]{:S(2)}) collective-permute-start(f32[32,2560]{1,0:T(8,128)S(1)} %shard_map.99.refs_3_.refs_0_), channel_id=1, source_target_pairs={{0,4},{1,3},{2,6},{3,1},{4,0},{5,7},{6,2},{7,5},{8,12},{9,11},{10,... | collective-permute-start | bytes 983048 | tf_op jit(solution)/shard_map/ppermute | solution.py:97
  45.8 1.7 %collective-permute-start.7 = (f32[32,1408]{1,0:T(8,128)S(1)}, f32[32,1408]{1,0:T(8,128)S(1)}, u32[]{:S(2)}, u32[]{:S(2)}) collective-permute-start(f32[32,1408]{1,0:T(8,128)S(1)} %get-tuple-element.54), channel_id=1, source_target_pairs={{0,1},{1,0},{2,3},{3,2},{4,5},{5,4},{6,7},{7,6},{8,9},{9,8},{10,11... | collective-permute-start | bytes 540680 | tf_op jit(solution)/shard_map/ppermute | solution.py:97
  45.8 1.6 %collective-permute-start.6 = (f32[32,1280]{1,0:T(8,128)S(1)}, f32[32,1280]{1,0:T(8,128)S(1)}, u32[]{:S(2)}, u32[]{:S(2)}) collective-permute-start(f32[32,1280]{1,0:T(8,128)S(1)} %get-tuple-element.53), channel_id=1, source_target_pairs={{0,1},{1,0},{2,3},{3,2},{4,5},{5,4},{6,7},{7,6},{8,9},{9,8},{10,11... | collective-permute-start | bytes 491528 | tf_op jit(solution)/shard_map/ppermute | solution.py:97
  46.4 2.5 %collective-permute-start.11 = (f32[32,1280]{1,0:T(8,128)S(1)}, f32[32,1280]{1,0:T(8,128)S(1)}, u32[]{:S(2)}, u32[]{:S(2)}) collective-permute-start(f32[32,1280]{1,0:T(8,128)S(1)} %get-tuple-element.57.refs_1_), channel_id=1, source_target_pairs={{0,1},{1,0},{2,3},{3,2},{4,5},{5,4},{6,7},{7,6},{8,9},{9,8},{10,11... | collective-permute-start | bytes 491528 | tf_op jit(solution)/shard_map/ppermute | solution.py:97
  46.5 2.4 %collective-permute-start.10 = (f32[32,1280]{1,0:T(8,128)S(1)}, f32[32,1280]{1,0:T(8,128)S(1)}, u32[]{:S(2)}, u32[]{:S(2)}) collective-permute-start(f32[32,1280]{1,0:T(8,128)S(1)} %get-tuple-element.55.refs_3_.refs_0_), channel_id=1, source_target_pairs={{0,1},{1,0},{2,3},{3,2},{4,5},{5,4},{6,7},{7,6},{8,9},{9,8},{10,11... | collective-permute-start | bytes 491528 | tf_op jit(solution)/shard_map/ppermute | solution.py:97
  47.5 9.5 %collective-permute-start.13 = (f32[32,2560]{1,0:T(8,128)S(1)}, f32[32,2560]{1,0:T(8,128)S(1)}, u32[]{:S(2)}, u32[]{:S(2)}) collective-permute-start(f32[32,2560]{1,0:T(8,128)S(1)} %get-tuple-element.59.refs_5_.refs_0_), channel_id=1, source_target_pairs={{0,2},{1,5},{2,0},{3,7},{4,6},{5,1},{6,4},{7,3},{8,10},{9,13},{10,... | collective-permute-start | bytes 983048 | tf_op jit(solution)/shard_map/ppermute | solution.py:97
  52.4 7.7 %collective-permute-start.14 = (f32[32,1792]{1,0:T(8,128)S(1)}, f32[32,1792]{1,0:T(8,128)S(1)}, u32[]{:S(2)}, u32[]{:S(2)}) collective-permute-start(f32[32,1792]{1,0:T(8,128)S(1)} %get-tuple-element.66), channel_id=1, source_target_pairs={{0,4},{1,5},{2,6},{3,7},{4,0},{5,1},{6,2},{7,3},{8,12},{9,13},{10,... | collective-permute-start | bytes 688136 | tf_op jit(solution)/shard_map/ppermute | solution.py:97
  53.0 4.2 %collective-permute-start.9 = (f32[32,128]{1,0:T(8,128)S(1)}, f32[32,128]{1,0:T(8,128)S(1)}, u32[]{:S(2)}, u32[]{:S(2)}) collective-permute-start(f32[32,128]{1,0:T(8,128)S(1)} %get-tuple-element.56.refs_0_), channel_id=1, source_target_pairs={{0,2},{1,3},{2,0},{3,1},{4,6},{5,7},{6,4},{7,5},{8,10},{9,11},{10,... | collective-permute-start | bytes 49160 | tf_op jit(solution)/shard_map/ppermute | solution.py:97
  53.5 5.5 %collective-permute-start.12 = (f32[64,64]{1,0:T(8,128)S(1)}, f32[64,64]{1,0:T(8,128)S(1)}, u32[]{:S(2)}, u32[]{:S(2)}) collective-permute-start(f32[64,64]{1,0:T(8,128)S(1)} %get-tuple-element.60.refs_2_), channel_id=1, source_target_pairs={{0,8},{1,9},{2,10},{3,11},{4,12},{5,13},{6,14},{7,15},{8,0},{9,1},... | collective-permute-start | bytes 49160 | tf_op jit(solution)/shard_map/ppermute | solution.py:97
  57.1 10.2 %collective-permute-start.16 = (f32[32,2560]{1,0:T(8,128)S(1)}, f32[32,2560]{1,0:T(8,128)S(1)}, u32[]{:S(2)}, u32[]{:S(2)}) collective-permute-start(f32[32,2560]{1,0:T(8,128)S(1)} %shard_map.104.refs_4_.refs_0_), channel_id=1, source_target_pairs={{0,4},{1,3},{2,6},{3,1},{4,0},{5,7},{6,2},{7,5},{8,12},{9,11},{10,... | collective-permute-start | bytes 983048 | tf_op jit(solution)/shard_map/ppermute | solution.py:97
  60.1 13.1 %collective-permute-start.15 = (f32[32,1792]{1,0:T(8,128)S(1)}, f32[32,1792]{1,0:T(8,128)S(1)}, u32[]{:S(2)}, u32[]{:S(2)}) collective-permute-start(f32[32,1792]{1,0:T(8,128)S(1)} %shard_map.106.refs_4_.refs_0_), channel_id=1, source_target_pairs={{0,8},{1,9},{2,10},{3,11},{4,12},{5,13},{6,14},{7,15},{8,0},{9,1},... | collective-permute-start | bytes 688136 | tf_op jit(solution)/shard_map/ppermute | solution.py:97
  67.3 1.5 %collective-permute-start.17 = (f32[32,1280]{1,0:T(8,128)S(1)}, f32[32,1280]{1,0:T(8,128)S(1)}, u32[]{:S(2)}, u32[]{:S(2)}) collective-permute-start(f32[32,1280]{1,0:T(8,128)S(1)} %get-tuple-element.69.refs_1_.refs_6_), channel_id=1, source_target_pairs={{0,1},{1,0},{2,3},{3,2},{4,5},{5,4},{6,7},{7,6},{8,9},{9,8},{10,11... | collective-permute-start | bytes 491528 | tf_op jit(solution)/shard_map/ppermute | solution.py:97
  67.3 1.6 %collective-permute-start.18 = (f32[32,1280]{1,0:T(8,128)S(1)}, f32[32,1280]{1,0:T(8,128)S(1)}, u32[]{:S(2)}, u32[]{:S(2)}) collective-permute-start(f32[32,1280]{1,0:T(8,128)S(1)} %get-tuple-element.70.refs_2_), channel_id=1, source_target_pairs={{0,1},{1,0},{2,3},{3,2},{4,5},{5,4},{6,7},{7,6},{8,9},{9,8},{10,11... | collective-permute-start | bytes 491528 | tf_op jit(solution)/shard_map/ppermute | solution.py:97
  73.2 5.7 %collective-permute-start.20 = (f32[32,768]{1,0:T(8,128)S(1)}, f32[32,768]{1,0:T(8,128)S(1)}, u32[]{:S(2)}, u32[]{:S(2)}) collective-permute-start(f32[32,768]{1,0:T(8,128)S(1)} %get-tuple-element.73.refs_5_.refs_1_), channel_id=1, source_target_pairs={{0,4},{1,5},{2,6},{3,7},{4,0},{5,1},{6,2},{7,3},{8,12},{9,13},{10,... | collective-permute-start | bytes 294920 | tf_op jit(solution)/shard_map/ppermute | solution.py:97
  74.0 7.9 %collective-permute-start.19 = (f32[32,1024]{1,0:T(8,128)S(1)}, f32[32,1024]{1,0:T(8,128)S(1)}, u32[]{:S(2)}, u32[]{:S(2)}) collective-permute-start(f32[32,1024]{1,0:T(8,128)S(1)} %get-tuple-element.72.refs_1_), channel_id=1, source_target_pairs={{0,4},{1,5},{2,6},{3,7},{4,0},{5,1},{6,2},{7,3},{8,12},{9,13},{10,... | collective-permute-start | bytes 393224 | tf_op jit(solution)/shard_map/ppermute | solution.py:97

commit v11 on v10

--- a/solution.py
+++ b/solution.py
@@ -11,7 +11,7 @@
 RANK = 64
 TILE = 256
 FLOPS = 1.15e9
-WEIGHTS = (8.0, 4.0, 1.0, 4.0, 0.1, 5.0, 1.0, 5.0, 1.0, 1.0, 4.0, 0.1, 0.1, 1.0, 5.0, 1.0, 0.1, 1.0, 4.0, 4.0, 4.0)
+WEIGHTS = (8.0, 4.0, 1.0, 4.0, 0.1, 5.0, 1.0, 5.0, 1.0, 1.0, 2.0, 2.0, 0.1, 5.0, 5.0, 1.0, 0.1, 0.5, 1.0, 8.0, 8.0)
 MIB = 1 << 20
 BF16 = jnp.bfloat16
 F32 = jnp.float32
@@ -189,17 +189,23 @@
     return [ref.shape[1] for ref in refs]
 
 
-def add(run, xs, ys, widths=None, after=()):
-    widths = widths or widths_of(xs)
+def add(run, xs, ys, widths=None, beside=None, after=()):
+    widths = list(widths or widths_of(xs))
+    more = 0 if beside is None else beside.shape[1]
     n_x, n_y = len(xs), len(ys)
 
     def kernel(*refs):
-        x, y, out = refs[:n_x], refs[n_x : n_x + n_y], refs[n_x + n_y :]
+        x, y, out = refs[:n_x], refs[n_x : n_x + n_y], refs[-len(widths) :]
         for (i, i0, i1), (j, j0, j1), (k, k0, k1) in spans(widths_of(x), widths_of(y), widths):
             out[k][:, k0:k1] = x[i][:, i0:i1] + y[j][:, j0:j1]
-
-    outs = [((HALF, n), F32, VMEM) for n in widths]
-    return list(run(kernel, [(x, VMEM) for x in (*xs, *ys)], outs, mib=2, after=after))
+        if more:
+            out[-1][:, widths[-1] :] = refs[n_x + n_y][...]
+
+    outs = [((HALF, n), F32, VMEM) for n in (*widths[:-1], widths[-1] + more)]
+    args = [(x, VMEM) for x in (*xs, *ys)]
+    if more:
+        args.append((beside, VMEM))
+    return list(run(kernel, args, outs, mib=2, after=after))
 
 
 def in_two(width):
@@ -263,20 +269,27 @@
         if before is not None:
             refs = refs[2:]
         left, fixed = refs[:2]
-        block = lax.div(lax.axis_index("dp"), REPLICAS) * (rows // TILE) + first
+        pair = 2 * TILE
+        block = lax.div(lax.axis_index("dp"), REPLICAS) * (rows // pair) + first // 2
         if before is None:
             left[...] = jnp.zeros_like(left)
 
         def step(g, e, s):
-            at = tile_at(first + pl.program_id(0))
+            i = pl.program_id(0)
+            at = tile_at(first + i)
             for j in range(0, cols, TILE):
                 here = slice(j, j + TILE)
-                c = g[:, here] + e[:, here]
-                fixed[at, here] = c
-                left[:, here] += jnp.dot(s[...], c, preferred_element_type=F32)
+                fixed[at, here] = g[:, here] + e[:, here]
+
+            @pl.when(lax.rem(i, 2) == 1)
+            def _():
+                both = pl.ds(pl.multiple_of((first + i - 1) * TILE, pair), pair)
+                for j in range(0, cols, TILE):
+                    here = slice(j, j + TILE)
+                    left[:, here] += jnp.dot(s[...], fixed[both, here], preferred_element_type=F32)
 
         spec = pl.BlockSpec((TILE, cols), lambda i: (first + i, 0), pipeline_mode=pl.Buffered(3))
-        part = pl.BlockSpec((RANK, TILE), lambda i: (0, block + i))
+        part = pl.BlockSpec((RANK, pair), lambda i: (0, block + lax.div(i, 2)))
         pltpu.emit_pipeline(step, grid=(count,), in_specs=[spec, spec, part])(grad, error, start)
         if last:
             halve(left, replica_of(), refs[2], refs[3:])
@@ -308,27 +321,57 @@
     )
 
 
-def gate_right(run, owns, others, fixed, after=()):
-    rows, cols = fixed.shape
+def packed(gram):
+    return jnp.concatenate([gram[:HALF], gram[HALF:]], axis=1)
+
+
+def gate_right(run, owns, others, fixed, count, after=()):
+    rows = fixed.shape[0]
+    width = count * TILE
     n_own, n_both = len(owns), len(owns) + len(others)
 
     def kernel(*refs):
         fixed, keep, give, gram, stack, left, right = refs[n_both:]
-        gram[...] = load_left(refs[:n_own], refs[n_own:n_both], core_of(), left, stack)
+        gram[...] = packed(load_left(refs[:n_own], refs[n_own:n_both], core_of(), left, stack))
 
         def step(i, _):
             both = jnp.dot(stack[: 2 * RANK], fixed[:, tile_at(i)], preferred_element_type=F32)
             right[:, tile_at(i)] = both[:RANK] + both[RANK:]
             return 0
 
-        lax.fori_loop(0, cols // TILE, step, 0)
+        lax.fori_loop(0, count, step, 0)
         halve(right, replica_of(), keep, [give])
 
     return run(
         kernel,
         [(x, VMEM) for x in (*owns, *others, fixed)],
-        [((HALF, cols), F32, VMEM)] * 2 + [((RANK, RANK), F32, VMEM), ((3 * RANK, rows), BF16, VMEM)],
-        [pltpu.VMEM((RANK, rows), F32), pltpu.VMEM((RANK, cols), F32)],
+        [((HALF, width), F32, VMEM)] * 2
+        + [((HALF, 2 * RANK), F32, VMEM), ((3 * RANK, rows), BF16, VMEM)],
+        [pltpu.VMEM((RANK, rows), F32), pltpu.VMEM((RANK, width), F32)],
+        mib=4,
+        after=after,
+    )
+
+
+def gate_right_rest(run, stack, fixed, first, after=()):
+    width = fixed.shape[1] - first * TILE
+
+    def kernel(stack, fixed, keep, give, right):
+        def step(i, _):
+            both = jnp.dot(
+                stack[: 2 * RANK], fixed[:, tile_at(first + i)], preferred_element_type=F32
+            )
+            right[:, tile_at(i)] = both[:RANK] + both[RANK:]
+            return 0
+
+        lax.fori_loop(0, width // TILE, step, 0)
+        halve(right, replica_of(), keep, [give])
+
+    return run(
+        kernel,
+        [(stack, VMEM), (fixed, VMEM)],
+        [((HALF, width), F32, VMEM)] * 2,
+        [pltpu.VMEM((RANK, width), F32)],
         mib=4,
         after=after,
     )
@@ -349,10 +392,9 @@
             return 0
 
         lax.fori_loop(0, rows // TILE, step, 0)
-        packed = jnp.concatenate([gram[:HALF], gram[HALF:]], axis=1)
         halve(right, core_of(), keep.at[:, :rows], [give_1, give_2.at[:, :rest]])
-        keep[:, rows:] = packed
-        give_2[:, rest:] = packed
+        keep[:, rows:] = packed(gram)
+        give_2[:, rest:] = packed(gram)
 
     widths = (rows + 2 * RANK, cut, rest + 2 * RANK)
     return run(
@@ -416,23 +458,17 @@
         turned[i : i + TILE, :] = stack[:, i : i + TILE].T
 
 
-def gram_sums(run, packed, whole, after=()):
-    n = len(packed)
+def solve(run, grams_down, left_down, gram_gate, left_gate, after=()):
+    cols, rows = left_down.shape[1], left_gate.shape[1]
+
+    n = len(grams_down)
 
     def kernel(*refs):
-        a = sum((ref[...] for ref in refs[1:n]), refs[0][...])
-        refs[-2][...] = jnp.concatenate([a[:, :RANK], a[:, RANK:]], axis=0)
-        refs[-1][...] = sum((ref[...] for ref in refs[n + 1 : -2]), refs[n][...])
-
-    outs = [((RANK, RANK), F32, VMEM)] * 2
-    return run(kernel, [(x, VMEM) for x in (*packed, *whole)], outs, mib=2, after=after)
-
-
-def solve(run, gram_down, left_down, gram_gate, left_gate, after=()):
-    cols, rows = left_down.shape[1], left_gate.shape[1]
-
-    def kernel(gram_down, left_down, gram_gate, left_gate, col_stack, row_turned, col, row, row_stack):
-        grams = [gram_down[...], gram_gate[...]]
+        gram_gate, left_down, left_gate, col_stack, row_turned, col, row, row_stack = refs[n:]
+        gram_down = sum((ref[...] for ref in refs[1:n]), refs[0][...])
+        grams = [
+            jnp.concatenate([a[:, :RANK], a[:, RANK:]], axis=0) for a in (gram_down, gram_gate[...])
+        ]
         for place, a, left, out in zip(
             (core_of(), replica_of()), inverses(grams), (left_down, left_gate), (col, row)
         ):
@@ -447,7 +483,7 @@
 
     return run(
         kernel,
-        [(x, VMEM) for x in (gram_down, left_down, gram_gate, left_gate)],
+        [(x, VMEM) for x in (*grams_down, gram_gate, left_down, left_gate)],
         [((4 * RANK, cols), BF16, VMEM), ((rows, 4 * RANK), BF16, VMEM)],
         [
             pltpu.VMEM((RANK, cols), F32),
@@ -459,10 +495,10 @@
     )
 
 
-def rebuild(run, ready, owns, others, fixed, shares, first=0, before=None, after=()):
+def rebuild(run, ready, owns, others, fixed, shares, height, first=0, before=None, after=()):
     rows, cols = fixed.shape
     share = rows // REPLICAS
-    height = share // 2
+    parts = share // height
     rows_late = ready[0] is None
     late_width = sum(widths_of(owns))
     width = ready[1].shape[1] if rows_late or not owns else late_width
@@ -470,7 +506,7 @@
     n_own, n_late = len(owns), len(owns) + len(others)
     n_before = 0 if before is None else len(before)
     with_update = 0 in shares
-    spots = [(s, t, j) for s in shares for t in range(2) for j in range(0, width, TILE)]
+    spots = [(s, t, j) for s in shares for t in range(parts) for j in range(0, width, TILE)]
 
     def kernel(*refs):
         given, late = refs[:n_ready], refs[n_ready : n_ready + n_late]
@@ -483,10 +519,10 @@
             for at, pieces in ((0, late[:n_own]), (HALF, late[n_own:])):
                 left = 0
                 for ref in pieces:
-                    parts = parts_of(ref[...])
+                    split = parts_of(ref[...])
                     n, w = ref.shape
                     for k, which in enumerate(order):
-                        stack[k * RANK + at : k * RANK + at + n, left : left + w] = parts[which]
+                        stack[k * RANK + at : k * RANK + at + n, left : left + w] = split[which]
                     left += w
         if rows_late:
             turn(stack, turned)
@@ -502,7 +538,7 @@
             here, there = slice(j, j + TILE), pl.ds(first + j, TILE)
             mine = pl.ds(t * height, height)
             value = jnp.dot(row[at, :], col[:, here], preferred_element_type=F32)
-            slot = pl.ds((shares.index(s) * 2 + t) * height, height)
+            slot = pl.ds((shares.index(s) * parts + t) * height, height)
             errors[slot, here] = (fixed[at, there].astype(F32) - value).astype(BF16)
             copies.append(
                 pltpu.make_async_copy(errors.at[slot, here], new_error.at[at, there], error_sems.at[k])
@@ -577,42 +613,38 @@
         exchange(gram_down, lambda d, t, b=b: (d, t ^ b)) for b in range(2, n_t, 2)
     ]
     got = exchange(down, hops[0])
-    keep_gate, give_gate, gram_gate, left_gate = gate_right(
-        run, gates, others_gate, fixed_gate, after=(down,)
-    )
-    got_gate = exchange(give_gate, other_replica)
-    grams_gate = [gram_gate] + [
-        exchange(gram_gate, lambda d, t, b=b: (d ^ b, t)) for b in range(REPLICAS, n_dp, REPLICAS)
-    ]
+    few = width // TILE * 3 // 7
+    keep_a, give_a, gram_gate, left_gate = gate_right(
+        run, gates, others_gate, fixed_gate, few, after=(down,)
+    )
+    got_a = exchange(give_a, other_replica)
+    keep_b, give_b = gate_right_rest(run, left_gate, fixed_gate, few)
+    got_b = exchange(give_b, other_replica)
     for hop in hops[1:]:
-        (down,) = add(run, [down], [got], after=(gram_gate,))
+        (down,) = add(run, [down], [got], after=(give_b,))
         got = exchange(down, hop)
-    gram_down, gram_gate = gram_sums(run, grams_down, grams_gate, after=(down,))
-    (gate,) = add(run, [keep_gate], [got_gate], after=(gram_gate,))
-    got_gate = exchange(gate, steps[0])
-    col_stack, row_turned = solve(run, gram_down, left_down, gram_gate, left_gate, after=(gate,))
-    downs = add(run, [down], [got], in_two(slab), after=(col_stack,))
+    (gate_a,) = add(run, [keep_a], [got_a], beside=gram_gate, after=(down,))
+    got_a = exchange(gate_a, steps[0])
+    (gate_b,) = add(run, [keep_b], [got_b], after=(gate_a,))
+    got_b = exchange(gate_b, steps[0])
+    downs = add(run, [down], [got], in_two(slab), after=(gate_b,))
     others_down = to_other_core(downs)
-    *outs_down, turned = rebuild(
-        run, (None, col_stack), downs, others_down, fixed_down, (0,), after=(downs[0],)
-    )
-    few = width // TILE * 3 // 7 * TILE
-    for i in range(len(steps)):
-        last = i + 1 == len(steps)
-        gate = add(run, [gate], [got_gate], [few, width - few] if last else None, after=(turned,))
-        if not last:
-            (gate,) = gate
-            got_gate = exchange(gate, steps[i + 1])
-    others_gate = [exchange(x, other_replica) for x in gate]
-    new_error_down, update_down, done = rebuild(
-        run, (turned, col_stack), [], [], fixed_down, (1,), before=outs_down, after=(gate[0],)
-    )
-    *outs_gate, done = rebuild(
-        run, (row_turned, None), gate[:1], others_gate[:1], fixed_gate, (0, 1), after=(done,)
+    for step in steps[1:]:
+        (gate_a,) = add(run, [gate_a], [got_a])
+        got_a = exchange(gate_a, step)
+        (gate_b,) = add(run, [gate_b], [got_b])
+        got_b = exchange(gate_b, step)
+    gate_a, gram_gate = add(run, [gate_a], [got_a], [few * TILE, 2 * RANK], after=(downs[0],))
+    other_a = exchange(gate_a, other_replica)
+    col_stack, row_turned = solve(run, grams_down, left_down, gram_gate, left_gate)
+    (gate_b,) = add(run, [gate_b], [got_b], after=(col_stack,))
+    other_b = exchange(gate_b, other_replica)
+    new_error_down, update_down, turned = rebuild(
+        run, (None, col_stack), downs, others_down, fixed_down, (0, 1), slab // 8, after=(gate_b,)
     )
     new_error_gate, update_gate, _ = rebuild(
-        run, (row_turned, None), gate[1:], others_gate[1:], fixed_gate, (0, 1), few, outs_gate,
-        after=(done,),
+        run, (row_turned, None), [gate_a, gate_b], [other_a, other_b], fixed_gate, (0, 1), slab // 2,
+        after=(turned,),
     )
     return (update_gate, update_down, new_error_gate, new_error_down)
 

time: 86.7 us -> 87.5 us (level)
  Pallas kernels: 46.5 us -> 44.3 us
  waiting for transfers between devices: 16.1 us -> 18.1 us
  starting transfers between devices: 22.9 us -> 23.8 us
    pallas_call x21, Pallas kernels: 46.5 us -> 44.3 us  [__call__(): pl.pallas_call(body, out_shape=tuple(((pltpu.VMEM if spec is VMEM else pl...]
    ppermute x21 -> x22, waiting for transfers between devices: 16.1 us -> 18.1 us  [exchange(): return lax.ppermute(x, ('dp', 'tensor'), pairs)]
    ppermute x21 -> x22, starting transfers between devices: 22.9 us -> 23.8 us  [exchange(): return lax.ppermute(x, ('dp', 'tensor'), pairs)]
  transfers between devices with their start and end apart: 21 -> 22, of which waited for: 13 -> 10; matrix products, arithmetic and copies ran while one was open for 0% -> 0% of each run, Pallas kernels for 37% -> 32%
where the time goes in v11:
time: 87.5 us; the launch traced here: 87.2 us
  Pallas kernels  44.3 us (51%)
  starting transfers between devices  23.8 us (27%)
  waiting for transfers between devices  18.1 us (21%)
  between operations  0.97 us (1%)
    pallas_call x21, Pallas kernels, __call__(): pl.pallas_call(body, out_shape=tuple(((pltpu.VMEM if spec is VMEM else pl...  44.3 us
    ppermute x22, starting transfers between devices, exchange(): return lax.ppermute(x, ('dp', 'tensor'), pairs)  23.8 us
    ppermute x22, waiting for transfers between devices, exchange(): return lax.ppermute(x, ('dp', 'tensor'), pairs)  18.1 us
  transfers between devices with their start and end apart: 22, of which 10 were waited for; matrix products, arithmetic and copies ran while one was open for 0% of the time, Pallas kernels for 32%

profile of v11, /device:TPU:0, one launch (start us, length us, event | category | flops | bytes accessed | tf_op | source)
XLA Modules:
  0.0 87.2 jit_solution(14896189193534202136)
XLA Ops:
  0.6 9.8 %shard_map.93 = (f32[64,1792]{1,0:T(8,128)}, bf16[2560,1792]{1,0:T(8,128)(2,1)S(1)}, f32[32,1792]{1,0:T(8,128)S(1)}, f32[32,1792]{1,0:T(8,128)S(1)}) custom-call(bf16[2560,1792]{1,0:T(8,128)(2,1)} %refs_0_.3, bf16[2560,1792]{1,0:T(8,128)(2,1)} %refs_1_.3, bf16[64,5120]{1,0:T(8,128)(2,1)} %refs_2_.3), custom_call_target="tpu_custom_call" | custom-call | flops 9200000000 | bytes 1024 | tf_op jit(solution)/shard_map/pallas_call | solution.py:154
  10.4 3.0 %collective-permute-start = (f32[32,1792]{1,0:T(8,128)S(1)}, f32[32,1792]{1,0:T(8,128)S(1)}, u32[]{:S(2)}, u32[]{:S(2)}) collective-permute-start(f32[32,1792]{1,0:T(8,128)S(1)} %get-tuple-element.39), channel_id=1, source_target_pairs={{0,4},{1,5},{2,6},{3,7},{4,0},{5,1},{6,2},{7,3},{8,12},{9,13},{10,... | collective-permute-start | bytes 688136 | tf_op jit(solution)/shard_map/ppermute | solution.py:97
  13.5 5.1 %shard_map.94 = (f32[64,2560]{1,0:T(8,128)S(1)}, bf16[2560,1792]{1,0:T(8,128)(2,1)S(1)}) custom-call(bf16[2560,1792]{1,0:T(8,128)(2,1)} %refs_0_.5, bf16[2560,1792]{1,0:T(8,128)(2,1)} %refs_1_.5, bf16[64,1792]{1,0:T(8,128)(2,1)S(1)} %copy-done, f32[32,1792]{1,0:T(8,128)S(1)} %get-tuple-element.38.refs_3_.refs_0_), custom_call_target="tpu_custom_call" | custom-call | flops 4600000000 | bytes 1024 | tf_op jit(solution)/shard_map/pallas_call | solution.py:154
  19.1 2.8 %collective-permute-start.1 = (f32[32,1792]{1,0:T(8,128)S(1)}, f32[32,1792]{1,0:T(8,128)S(1)}, u32[]{:S(2)}, u32[]{:S(2)}) collective-permute-start(f32[32,1792]{1,0:T(8,128)S(1)} %shard_map.95.refs_5_.refs_0_), channel_id=1, source_target_pairs={{0,8},{1,9},{2,10},{3,11},{4,12},{5,13},{6,14},{7,15},{8,0},{9,1},... | collective-permute-start | bytes 688136 | tf_op jit(solution)/shard_map/ppermute | solution.py:97
  21.9 4.0 %shard_map.96 = (f32[64,2560]{1,0:T(8,128)S(1)}, bf16[2560,1792]{1,0:T(8,128)(2,1)S(1)}, f32[32,2560]{1,0:T(8,128)S(1)}, f32[32,1280]{1,0:T(8,128)S(1)}, f32[32,1280]{1,0:T(8,128)S(1)}) custom-call(bf16[2560,1792]{1,0:T(8,128)(2,1)} %refs_0_.5, bf16[2560,1792]{1,0:T(8,128)(2,1)} %refs_1_.5, ...), custom_call_target="tpu_custom_call", output_to_operand_aliasing={{0}: (3, {}), {1}: (4, {})} | custom-call | flops 4600000000 | bytes 1024 | tf_op jit(solution)/shard_map/pallas_call | solution.py:154
  26.5 0.9 %collective-permute-done.2.refs_1_ = f32[32,1280]{1,0:T(8,128)S(1)} collective-permute-done((f32[32,1280]{1,0:T(8,128)S(1)}, f32[32,1280]{1,0:T(8,128)S(1)}, u32[]{:S(2)}, u32[]{:S(2)}) %collective-permute-start.2) | collective-permute-done | bytes 163872 | tf_op jit(solution)/shard_map/ppermute | solution.py:97
  27.6 1.6 %collective-permute-start.5 = (f32[32,2560]{1,0:T(8,128)S(1)}, f32[32,2560]{1,0:T(8,128)S(1)}, u32[]{:S(2)}, u32[]{:S(2)}) collective-permute-start(f32[32,2560]{1,0:T(8,128)S(1)} %shard_map.97.refs_2_.refs_0_), channel_id=1, source_target_pairs={{0,2},{1,5},{2,0},{3,7},{4,6},{5,1},{6,4},{7,3},{8,10},{9,13},{10,... | collective-permute-start | bytes 983048 | tf_op jit(solution)/shard_map/ppermute | solution.py:97
  29.2 2.7 %collective-permute-done.1.refs_1_ = f32[32,1792]{1,0:T(8,128)S(1)} collective-permute-done((f32[32,1792]{1,0:T(8,128)S(1)}, f32[32,1792]{1,0:T(8,128)S(1)}, u32[]{:S(2)}, u32[]{:S(2)}) %collective-permute-start.1) | collective-permute-done | bytes 229408 | tf_op jit(solution)/shard_map/ppermute | solution.py:97
  32.4 2.3 %collective-permute-done.5.refs_1_ = f32[32,2560]{1,0:T(8,128)S(1)} collective-permute-done((f32[32,2560]{1,0:T(8,128)S(1)}, f32[32,2560]{1,0:T(8,128)S(1)}, u32[]{:S(2)}, u32[]{:S(2)}) %collective-permute-start.5) | collective-permute-done | bytes 327712 | tf_op jit(solution)/shard_map/ppermute | solution.py:97
  34.8 1.6 %collective-permute-start.8 = (f32[32,2560]{1,0:T(8,128)S(1)}, f32[32,2560]{1,0:T(8,128)S(1)}, u32[]{:S(2)}, u32[]{:S(2)}) collective-permute-start(f32[32,2560]{1,0:T(8,128)S(1)} %shard_map.99.refs_3_.refs_0_), channel_id=1, source_target_pairs={{0,4},{1,3},{2,6},{3,1},{4,0},{5,7},{6,2},{7,5},{8,12},{9,11},{10,... | collective-permute-start | bytes 983048 | tf_op jit(solution)/shard_map/ppermute | solution.py:97
  36.4 3.7 %collective-permute-done.4.refs_1_ = f32[32,1792]{1,0:T(8,128)S(1)} collective-permute-done((f32[32,1792]{1,0:T(8,128)S(1)}, f32[32,1792]{1,0:T(8,128)S(1)}, u32[]{:S(2)}, u32[]{:S(2)}) %collective-permute-start.4) | collective-permute-done | bytes 229408 | tf_op jit(solution)/shard_map/ppermute | solution.py:97
  40.2 5.2 %shard_map.100 = (f32[32,2688]{1,0:T(8,128)S(1)}, f32[32,1280]{1,0:T(8,128)S(1)}, f32[32,1408]{1,0:T(8,128)S(1)}, bf16[192,1792]{1,0:T(8,128)(2,1)S(1)}) custom-call(f32[32,1792]{1,0:T(8,128)S(1)} %shard_map.98.refs_2_.refs_0_, f32[32,1792]{1,0:T(8,128)S(1)} %collective-permute-done.4.refs_1_, bf16[2560,1792]{1,0:T(8,128)(2,1)S(1)} %get-tuple-element.45.refs_2_.refs_5_, ...), custom_call_target="tpu_custom_call" | custom-call | flops 5750000128 | bytes 1024 | tf_op jit(solution)/shard_map/pallas_call | solution.py:154
  47.2 1.4 %collective-permute-start.9 = (f32[32,128]{1,0:T(8,128)S(1)}, f32[32,128]{1,0:T(8,128)S(1)}, u32[]{:S(2)}, u32[]{:S(2)}) collective-permute-start(f32[32,128]{1,0:T(8,128)S(1)} %get-tuple-element.50.refs_0_), channel_id=1, source_target_pairs={{0,2},{1,3},{2,0},{3,1},{4,6},{5,7},{6,4},{7,5},{8,10},{9,11},{10,... | collective-permute-start | bytes 49160 | tf_op jit(solution)/shard_map/ppermute | solution.py:97
  49.3 1.9 %shard_map.103 = (f32[32,768]{1,0:T(8,128)S(1)}, f32[32,768]{1,0:T(8,128)S(1)}, f32[32,128]{1,0:T(8,128)S(1)}, bf16[192,2560]{1,0:T(8,128)(2,1)S(1)}) custom-call(f32[32,1280]{1,0:T(8,128)S(1)} %get-tuple-element.49.refs_3_.refs_0_, f32[32,1280]{1,0:T(8,128)S(1)} %get-tuple-element.51.refs_1_, f32[32,1280]{1,0:T(8,128)S(1)} %collective-permute-done.10.refs_2_, ...), custom_call_target="tpu_custom_call" | custom-call | flops 2300000000 | bytes 1024 | tf_op jit(solution)/shard_map/pallas_call | solution.py:154
  51.7 1.6 %shard_map.104 = (f32[32,1024]{1,0:T(8,128)S(1)}, f32[32,1024]{1,0:T(8,128)S(1)}) custom-call(bf16[192,2560]{1,0:T(8,128)(2,1)S(1)} %get-tuple-element.57.refs_0_.refs_4_, bf16[2560,1792]{1,0:T(8,128)(2,1)S(1)} %get-tuple-element.52.refs_4_.refs_1_.refs_5_), custom_call_target="tpu_custom_call" | custom-call | flops 2300000000 | bytes 1024 | tf_op jit(solution)/shard_map/pallas_call | solution.py:154
  53.3 1.7 %collective-permute-start.16 = (f32[32,1024]{1,0:T(8,128)S(1)}, f32[32,1024]{1,0:T(8,128)S(1)}, u32[]{:S(2)}, u32[]{:S(2)}) collective-permute-start(f32[32,1024]{1,0:T(8,128)S(1)} %get-tuple-element.58.refs_2_), channel_id=1, source_target_pairs={{0,4},{1,5},{2,6},{3,7},{4,0},{5,1},{6,2},{7,3},{8,12},{9,13},{10,... | collective-permute-start | bytes 393224 | tf_op jit(solution)/shard_map/ppermute | solution.py:97
  57.0 2.9 %collective-permute-start.14 = (f32[32,896]{1,0:T(8,128)S(1)}, f32[32,896]{1,0:T(8,128)S(1)}, u32[]{:S(2)}, u32[]{:S(2)}) collective-permute-start(f32[32,896]{1,0:T(8,128)S(1)} %shard_map.106.refs_2_.refs_0_), channel_id=1, source_target_pairs={{0,8},{1,9},{2,10},{3,11},{4,12},{5,13},{6,14},{7,15},{8,0},{9,1},... | collective-permute-start | bytes 344072 | tf_op jit(solution)/shard_map/ppermute | solution.py:97
  59.9 2.1 %collective-permute-start.17 = (f32[32,1024]{1,0:T(8,128)S(1)}, f32[32,1024]{1,0:T(8,128)S(1)}, u32[]{:S(2)}, u32[]{:S(2)}) collective-permute-start(f32[32,1024]{1,0:T(8,128)S(1)} %shard_map.107.refs_2_.refs_0_), channel_id=1, source_target_pairs={{0,8},{1,9},{2,10},{3,11},{4,12},{5,13},{6,14},{7,15},{8,0},{9,1},... | collective-permute-start | bytes 393224 | tf_op jit(solution)/shard_map/ppermute | solution.py:97
  62.0 5.7 %collective-permute-done.15.refs_1_ = f32[32,2560]{1,0:T(8,128)S(1)} collective-permute-done((f32[32,2560]{1,0:T(8,128)S(1)}, f32[32,2560]{1,0:T(8,128)S(1)}, u32[]{:S(2)}, u32[]{:S(2)}) %collective-permute-start.15) | collective-permute-done | bytes 327712 | tf_op jit(solution)/shard_map/ppermute | solution.py:97
  68.4 1.1 %collective-permute-start.18 = (f32[32,768]{1,0:T(8,128)S(1)}, f32[32,768]{1,0:T(8,128)S(1)}, u32[]{:S(2)}, u32[]{:S(2)}) collective-permute-start(f32[32,768]{1,0:T(8,128)S(1)} %get-tuple-element.64.refs_1_), channel_id=1, source_target_pairs={{0,4},{1,5},{2,6},{3,7},{4,0},{5,1},{6,2},{7,3},{8,12},{9,13},{10,... | collective-permute-start | bytes 294920 | tf_op jit(solution)/shard_map/ppermute | solution.py:97
  69.5 4.0 %shard_map.110 = (bf16[256,1792]{1,0:T(8,128)(2,1)S(1)}, bf16[2560,256]{1,0:T(8,128)(2,1)S(1)}) custom-call(f32[32,128]{1,0:T(8,128)S(1)} %get-tuple-element.50.refs_0_, f32[32,128]{1,0:T(8,128)S(1)} %collective-permute-done.9.refs_1_, f32[32,128]{1,0:T(8,128)S(1)} %get-tuple-element.61.refs_2_, bf16[192,1792]{1,0:T(8,128)(2,1)S(1)} %get-tuple-element.62.refs_3_, ...), custom_call_target="tpu_custom_call" | custom-call | flops 575000000 | bytes 1024 | tf_op jit(solution)/shard_map/pallas_call | solution.py:154
  73.5 1.1 %collective-permute-start.19 = (f32[32,1024]{1,0:T(8,128)S(1)}, f32[32,1024]{1,0:T(8,128)S(1)}, u32[]{:S(2)}, u32[]{:S(2)}) collective-permute-start(f32[32,1024]{1,0:T(8,128)S(1)} %shard_map.111.refs_6_.refs_2_), channel_id=1, source_target_pairs={{0,4},{1,5},{2,6},{3,7},{4,0},{5,1},{6,2},{7,3},{8,12},{9,13},{10,... | collective-permute-start | bytes 393224 | tf_op jit(solution)/shard_map/ppermute | solution.py:97
  74.6 6.2 %shard_map.112 = (bf16[2560,1792]{1,0:T(8,128)(2,1)}, bf16[1280,1792]{1,0:T(8,128)(2,1)}, bf16[2560,256]{1,0:T(8,128)(2,1)S(1)}) custom-call(bf16[256,1792]{1,0:T(8,128)(2,1)S(1)} %get-tuple-element.65.refs_2_.refs_0_, f32[32,1280]{1,0:T(8,128)S(1)} %get-tuple-element.60.refs_2_.refs_1_, f32[32,1280]{1,0:T(8,128)S(1)} %get-tuple-element.66.refs_2_, ...), custom_call_target="tpu_custom_call" | custom-call | flops 9200000000 | bytes 1024 | tf_op jit(solution)/shard_map/pallas_call | solution.py:154
  80.8 6.3 %shard_map.113 = (bf16[2560,1792]{1,0:T(8,128)(2,1)}, bf16[1280,1792]{1,0:T(8,128)(2,1)}, bf16[16,128]{1,0:T(8,128)(2,1)}) custom-call(bf16[2560,256]{1,0:T(8,128)(2,1)S(1)} %get-tuple-element.63.refs_0_, f32[32,768]{1,0:T(8,128)S(1)} %get-tuple-element.64.refs_1_, f32[32,1024]{1,0:T(8,128)S(1)} %shard_map.111.refs_6_.refs_2_, ...), custom_call_target="tpu_custom_call" | custom-call | flops 9200000000 | bytes 1024 | tf_op jit(solution)/shard_map/pallas_call | solution.py:154
  (43 shorter events, 7.6 us)
Async XLA Ops:
  0.6 12.8 %copy-start = (bf16[64,1792]{1,0:T(8,128)(2,1)S(1)}, bf16[64,1792]{1,0:T(8,128)(2,1)}, u32[]{:S(2)}) copy-start(bf16[64,1792]{1,0:T(8,128)(2,1)} %refs_2_.5) | copy-start | bytes 688132
  10.4 8.6 %collective-permute-start = (f32[32,1792]{1,0:T(8,128)S(1)}, f32[32,1792]{1,0:T(8,128)S(1)}, u32[]{:S(2)}, u32[]{:S(2)}) collective-permute-start(f32[32,1792]{1,0:T(8,128)S(1)} %get-tuple-element.39), channel_id=1, source_target_pairs={{0,4},{1,5},{2,6},{3,7},{4,0},{5,1},{6,2},{7,3},{8,12},{9,13},{10,... | collective-permute-start | bytes 688136 | tf_op jit(solution)/shard_map/ppermute | solution.py:97
  19.1 12.8 %collective-permute-start.1 = (f32[32,1792]{1,0:T(8,128)S(1)}, f32[32,1792]{1,0:T(8,128)S(1)}, u32[]{:S(2)}, u32[]{:S(2)}) collective-permute-start(f32[32,1792]{1,0:T(8,128)S(1)} %shard_map.95.refs_5_.refs_0_), channel_id=1, source_target_pairs={{0,8},{1,9},{2,10},{3,11},{4,12},{5,13},{6,14},{7,15},{8,0},{9,1},... | collective-permute-start | bytes 688136 | tf_op jit(solution)/shard_map/ppermute | solution.py:97
  25.9 1.5 %collective-permute-start.2 = (f32[32,1280]{1,0:T(8,128)S(1)}, f32[32,1280]{1,0:T(8,128)S(1)}, u32[]{:S(2)}, u32[]{:S(2)}) collective-permute-start(f32[32,1280]{1,0:T(8,128)S(1)} %get-tuple-element.43), channel_id=1, source_target_pairs={{0,1},{1,0},{2,3},{3,2},{4,5},{5,4},{6,7},{7,6},{8,9},{9,8},{10,11... | collective-permute-start | bytes 491528 | tf_op jit(solution)/shard_map/ppermute | solution.py:97
  26.0 1.6 %collective-permute-start.3 = (f32[32,1280]{1,0:T(8,128)S(1)}, f32[32,1280]{1,0:T(8,128)S(1)}, u32[]{:S(2)}, u32[]{:S(2)}) collective-permute-start(f32[32,1280]{1,0:T(8,128)S(1)} %get-tuple-element.44), channel_id=1, source_target_pairs={{0,1},{1,0},{2,3},{3,2},{4,5},{5,4},{6,7},{7,6},{8,9},{9,8},{10,11... | collective-permute-start | bytes 491528 | tf_op jit(solution)/shard_map/ppermute | solution.py:97
  27.6 7.1 %collective-permute-start.5 = (f32[32,2560]{1,0:T(8,128)S(1)}, f32[32,2560]{1,0:T(8,128)S(1)}, u32[]{:S(2)}, u32[]{:S(2)}) collective-permute-start(f32[32,2560]{1,0:T(8,128)S(1)} %shard_map.97.refs_2_.refs_0_), channel_id=1, source_target_pairs={{0,2},{1,5},{2,0},{3,7},{4,6},{5,1},{6,4},{7,3},{8,10},{9,13},{10,... | collective-permute-start | bytes 983048 | tf_op jit(solution)/shard_map/ppermute | solution.py:97
  31.9 8.3 %collective-permute-start.4 = (f32[32,1792]{1,0:T(8,128)S(1)}, f32[32,1792]{1,0:T(8,128)S(1)}, u32[]{:S(2)}, u32[]{:S(2)}) collective-permute-start(f32[32,1792]{1,0:T(8,128)S(1)} %shard_map.98.refs_2_.refs_0_), channel_id=1, source_target_pairs={{0,4},{1,5},{2,6},{3,7},{4,0},{5,1},{6,2},{7,3},{8,12},{9,13},{10,... | collective-permute-start | bytes 688136 | tf_op jit(solution)/shard_map/ppermute | solution.py:97
  34.8 11.2 %collective-permute-start.8 = (f32[32,2560]{1,0:T(8,128)S(1)}, f32[32,2560]{1,0:T(8,128)S(1)}, u32[]{:S(2)}, u32[]{:S(2)}) collective-permute-start(f32[32,2560]{1,0:T(8,128)S(1)} %shard_map.99.refs_3_.refs_0_), channel_id=1, source_target_pairs={{0,4},{1,3},{2,6},{3,1},{4,0},{5,7},{6,2},{7,5},{8,12},{9,11},{10,... | collective-permute-start | bytes 983048 | tf_op jit(solution)/shard_map/ppermute | solution.py:97
  45.4 1.7 %collective-permute-start.7 = (f32[32,1408]{1,0:T(8,128)S(1)}, f32[32,1408]{1,0:T(8,128)S(1)}, u32[]{:S(2)}, u32[]{:S(2)}) collective-permute-start(f32[32,1408]{1,0:T(8,128)S(1)} %get-tuple-element.48), channel_id=1, source_target_pairs={{0,1},{1,0},{2,3},{3,2},{4,5},{5,4},{6,7},{7,6},{8,9},{9,8},{10,11... | collective-permute-start | bytes 540680 | tf_op jit(solution)/shard_map/ppermute | solution.py:97
  45.5 1.6 %collective-permute-start.6 = (f32[32,1280]{1,0:T(8,128)S(1)}, f32[32,1280]{1,0:T(8,128)S(1)}, u32[]{:S(2)}, u32[]{:S(2)}) collective-permute-start(f32[32,1280]{1,0:T(8,128)S(1)} %get-tuple-element.47), channel_id=1, source_target_pairs={{0,1},{1,0},{2,3},{3,2},{4,5},{5,4},{6,7},{7,6},{8,9},{9,8},{10,11... | collective-permute-start | bytes 491528 | tf_op jit(solution)/shard_map/ppermute | solution.py:97
  46.0 3.2 %collective-permute-start.11 = (f32[32,1280]{1,0:T(8,128)S(1)}, f32[32,1280]{1,0:T(8,128)S(1)}, u32[]{:S(2)}, u32[]{:S(2)}) collective-permute-start(f32[32,1280]{1,0:T(8,128)S(1)} %get-tuple-element.51.refs_1_), channel_id=1, source_target_pairs={{0,1},{1,0},{2,3},{3,2},{4,5},{5,4},{6,7},{7,6},{8,9},{9,8},{10,11... | collective-permute-start | bytes 491528 | tf_op jit(solution)/shard_map/ppermute | solution.py:97
  46.2 3.1 %collective-permute-start.10 = (f32[32,1280]{1,0:T(8,128)S(1)}, f32[32,1280]{1,0:T(8,128)S(1)}, u32[]{:S(2)}, u32[]{:S(2)}) collective-permute-start(f32[32,1280]{1,0:T(8,128)S(1)} %get-tuple-element.49.refs_3_.refs_0_), channel_id=1, source_target_pairs={{0,1},{1,0},{2,3},{3,2},{4,5},{5,4},{6,7},{7,6},{8,9},{9,8},{10,11... | collective-permute-start | bytes 491528 | tf_op jit(solution)/shard_map/ppermute | solution.py:97
  47.2 22.3 %collective-permute-start.9 = (f32[32,128]{1,0:T(8,128)S(1)}, f32[32,128]{1,0:T(8,128)S(1)}, u32[]{:S(2)}, u32[]{:S(2)}) collective-permute-start(f32[32,128]{1,0:T(8,128)S(1)} %get-tuple-element.50.refs_0_), channel_id=1, source_target_pairs={{0,2},{1,3},{2,0},{3,1},{4,6},{5,7},{6,4},{7,5},{8,10},{9,11},{10,... | collective-permute-start | bytes 49160 | tf_op jit(solution)/shard_map/ppermute | solution.py:97
  48.6 7.1 %collective-permute-start.13 = (f32[32,2560]{1,0:T(8,128)S(1)}, f32[32,2560]{1,0:T(8,128)S(1)}, u32[]{:S(2)}, u32[]{:S(2)}) collective-permute-start(f32[32,2560]{1,0:T(8,128)S(1)} %get-tuple-element.53.refs_5_.refs_0_), channel_id=1, source_target_pairs={{0,2},{1,5},{2,0},{3,7},{4,6},{5,1},{6,4},{7,3},{8,10},{9,13},{10,... | collective-permute-start | bytes 983048 | tf_op jit(solution)/shard_map/ppermute | solution.py:97
  51.2 5.8 %collective-permute-start.12 = (f32[32,768]{1,0:T(8,128)S(1)}, f32[32,768]{1,0:T(8,128)S(1)}, u32[]{:S(2)}, u32[]{:S(2)}) collective-permute-start(f32[32,768]{1,0:T(8,128)S(1)} %get-tuple-element.55), channel_id=1, source_target_pairs={{0,4},{1,5},{2,6},{3,7},{4,0},{5,1},{6,2},{7,3},{8,12},{9,13},{10,... | collective-permute-start | bytes 294920 | tf_op jit(solution)/shard_map/ppermute | solution.py:97
  53.3 6.7 %collective-permute-start.16 = (f32[32,1024]{1,0:T(8,128)S(1)}, f32[32,1024]{1,0:T(8,128)S(1)}, u32[]{:S(2)}, u32[]{:S(2)}) collective-permute-start(f32[32,1024]{1,0:T(8,128)S(1)} %get-tuple-element.58.refs_2_), channel_id=1, source_target_pairs={{0,4},{1,5},{2,6},{3,7},{4,0},{5,1},{6,2},{7,3},{8,12},{9,13},{10,... | collective-permute-start | bytes 393224 | tf_op jit(solution)/shard_map/ppermute | solution.py:97
  55.7 12.1 %collective-permute-start.15 = (f32[32,2560]{1,0:T(8,128)S(1)}, f32[32,2560]{1,0:T(8,128)S(1)}, u32[]{:S(2)}, u32[]{:S(2)}) collective-permute-start(f32[32,2560]{1,0:T(8,128)S(1)} %shard_map.105.refs_3_.refs_0_), channel_id=1, source_target_pairs={{0,4},{1,3},{2,6},{3,1},{4,0},{5,7},{6,2},{7,5},{8,12},{9,11},{10,... | collective-permute-start | bytes 983048 | tf_op jit(solution)/shard_map/ppermute | solution.py:97
  57.0 11.4 %collective-permute-start.14 = (f32[32,896]{1,0:T(8,128)S(1)}, f32[32,896]{1,0:T(8,128)S(1)}, u32[]{:S(2)}, u32[]{:S(2)}) collective-permute-start(f32[32,896]{1,0:T(8,128)S(1)} %shard_map.106.refs_2_.refs_0_), channel_id=1, source_target_pairs={{0,8},{1,9},{2,10},{3,11},{4,12},{5,13},{6,14},{7,15},{8,0},{9,1},... | collective-permute-start | bytes 344072 | tf_op jit(solution)/shard_map/ppermute | solution.py:97
  59.9 13.5 %collective-permute-start.17 = (f32[32,1024]{1,0:T(8,128)S(1)}, f32[32,1024]{1,0:T(8,128)S(1)}, u32[]{:S(2)}, u32[]{:S(2)}) collective-permute-start(f32[32,1024]{1,0:T(8,128)S(1)} %shard_map.107.refs_2_.refs_0_), channel_id=1, source_target_pairs={{0,8},{1,9},{2,10},{3,11},{4,12},{5,13},{6,14},{7,15},{8,0},{9,1},... | collective-permute-start | bytes 393224 | tf_op jit(solution)/shard_map/ppermute | solution.py:97
  67.8 6.8 %collective-permute-start.21 = (f32[32,1280]{1,0:T(8,128)S(1)}, f32[32,1280]{1,0:T(8,128)S(1)}, u32[]{:S(2)}, u32[]{:S(2)}) collective-permute-start(f32[32,1280]{1,0:T(8,128)S(1)} %get-tuple-element.66.refs_2_), channel_id=1, source_target_pairs={{0,1},{1,0},{2,3},{3,2},{4,5},{5,4},{6,7},{7,6},{8,9},{9,8},{10,11... | collective-permute-start | bytes 491528 | tf_op jit(solution)/shard_map/ppermute | solution.py:97
  67.9 6.7 %collective-permute-start.20 = (f32[32,1280]{1,0:T(8,128)S(1)}, f32[32,1280]{1,0:T(8,128)S(1)}, u32[]{:S(2)}, u32[]{:S(2)}) collective-permute-start(f32[32,1280]{1,0:T(8,128)S(1)} %get-tuple-element.60.refs_2_.refs_1_), channel_id=1, source_target_pairs={{0,1},{1,0},{2,3},{3,2},{4,5},{5,4},{6,7},{7,6},{8,9},{9,8},{10,11... | collective-permute-start | bytes 491528 | tf_op jit(solution)/shard_map/ppermute | solution.py:97
  68.4 12.4 %collective-permute-start.18 = (f32[32,768]{1,0:T(8,128)S(1)}, f32[32,768]{1,0:T(8,128)S(1)}, u32[]{:S(2)}, u32[]{:S(2)}) collective-permute-start(f32[32,768]{1,0:T(8,128)S(1)} %get-tuple-element.64.refs_1_), channel_id=1, source_target_pairs={{0,4},{1,5},{2,6},{3,7},{4,0},{5,1},{6,2},{7,3},{8,12},{9,13},{10,... | collective-permute-start | bytes 294920 | tf_op jit(solution)/shard_map/ppermute | solution.py:97
  73.5 7.3 %collective-permute-start.19 = (f32[32,1024]{1,0:T(8,128)S(1)}, f32[32,1024]{1,0:T(8,128)S(1)}, u32[]{:S(2)}, u32[]{:S(2)}) collective-permute-start(f32[32,1024]{1,0:T(8,128)S(1)} %shard_map.111.refs_6_.refs_2_), channel_id=1, source_target_pairs={{0,4},{1,5},{2,6},{3,7},{4,0},{5,1},{6,2},{7,3},{8,12},{9,13},{10,... | collective-permute-start | bytes 393224 | tf_op jit(solution)/shard_map/ppermute | solution.py:97

commit v12 on v10

--- a/solution.py
+++ b/solution.py
@@ -263,20 +263,27 @@
         if before is not None:
             refs = refs[2:]
         left, fixed = refs[:2]
-        block = lax.div(lax.axis_index("dp"), REPLICAS) * (rows // TILE) + first
+        pair = 2 * TILE
+        block = lax.div(lax.axis_index("dp"), REPLICAS) * (rows // pair) + first // 2
         if before is None:
             left[...] = jnp.zeros_like(left)
 
         def step(g, e, s):
-            at = tile_at(first + pl.program_id(0))
+            i = pl.program_id(0)
+            at = tile_at(first + i)
             for j in range(0, cols, TILE):
                 here = slice(j, j + TILE)
-                c = g[:, here] + e[:, here]
-                fixed[at, here] = c
-                left[:, here] += jnp.dot(s[...], c, preferred_element_type=F32)
+                fixed[at, here] = g[:, here] + e[:, here]
+
+            @pl.when(lax.rem(i, 2) == 1)
+            def _():
+                both = pl.ds(pl.multiple_of((first + i - 1) * TILE, pair), pair)
+                for j in range(0, cols, TILE):
+                    here = slice(j, j + TILE)
+                    left[:, here] += jnp.dot(s[...], fixed[both, here], preferred_element_type=F32)
 
         spec = pl.BlockSpec((TILE, cols), lambda i: (first + i, 0), pipeline_mode=pl.Buffered(3))
-        part = pl.BlockSpec((RANK, TILE), lambda i: (0, block + i))
+        part = pl.BlockSpec((RANK, pair), lambda i: (0, block + lax.div(i, 2)))
         pltpu.emit_pipeline(step, grid=(count,), in_specs=[spec, spec, part])(grad, error, start)
         if last:
             halve(left, replica_of(), refs[2], refs[3:])
@@ -303,9 +310,10 @@
     stack[:RANK, :] = hi
     stack[RANK : 2 * RANK, :] = lo
     stack[2 * RANK :, :] = hi
-    return lax.dot_general(
-        left[...], left[...], NT, preferred_element_type=F32, precision=lax.Precision.HIGHEST
-    )
+    parts = stack[: 2 * RANK]
+    gram = lax.dot_general(parts, parts, NT, preferred_element_type=F32)
+    mixed = gram[:RANK, RANK:] + gram[RANK:, :RANK]
+    return gram[:RANK, :RANK] + (mixed + gram[RANK:, RANK:])
 
 
 def gate_right(run, owns, others, fixed, after=()):
@@ -459,10 +467,10 @@
     )
 
 
-def rebuild(run, ready, owns, others, fixed, shares, first=0, before=None, after=()):
+def rebuild(run, ready, owns, others, fixed, shares, height, first=0, before=None, after=()):
     rows, cols = fixed.shape
     share = rows // REPLICAS
-    height = share // 2
+    parts = share // height
     rows_late = ready[0] is None
     late_width = sum(widths_of(owns))
     width = ready[1].shape[1] if rows_late or not owns else late_width
@@ -470,7 +478,7 @@
     n_own, n_late = len(owns), len(owns) + len(others)
     n_before = 0 if before is None else len(before)
     with_update = 0 in shares
-    spots = [(s, t, j) for s in shares for t in range(2) for j in range(0, width, TILE)]
+    spots = [(s, t, j) for s in shares for t in range(parts) for j in range(0, width, TILE)]
 
     def kernel(*refs):
         given, late = refs[:n_ready], refs[n_ready : n_ready + n_late]
@@ -483,10 +491,10 @@
             for at, pieces in ((0, late[:n_own]), (HALF, late[n_own:])):
                 left = 0
                 for ref in pieces:
-                    parts = parts_of(ref[...])
+                    split = parts_of(ref[...])
                     n, w = ref.shape
                     for k, which in enumerate(order):
-                        stack[k * RANK + at : k * RANK + at + n, left : left + w] = parts[which]
+                        stack[k * RANK + at : k * RANK + at + n, left : left + w] = split[which]
                     left += w
         if rows_late:
             turn(stack, turned)
@@ -502,7 +510,7 @@
             here, there = slice(j, j + TILE), pl.ds(first + j, TILE)
             mine = pl.ds(t * height, height)
             value = jnp.dot(row[at, :], col[:, here], preferred_element_type=F32)
-            slot = pl.ds((shares.index(s) * 2 + t) * height, height)
+            slot = pl.ds((shares.index(s) * parts + t) * height, height)
             errors[slot, here] = (fixed[at, there].astype(F32) - value).astype(BF16)
             copies.append(
                 pltpu.make_async_copy(errors.at[slot, here], new_error.at[at, there], error_sems.at[k])
@@ -570,7 +578,7 @@
 
     keep, *gives, left_down = down_right(run, [down], [other_down], fixed_down, after=(gate,))
     gots = to_other_core(gives)
-    gates = add(run, [gate], [got_gate], in_two(slab), after=(keep,))
+    gates = add(run, [gate], [got_gate], after=(keep,))
     others_gate = to_other_core(gates)
     down, gram_down = add(run, [keep], gots, [slab, 2 * RANK], after=(gates[0],))
     grams_down = [gram_down] + [
@@ -594,7 +602,7 @@
     downs = add(run, [down], [got], in_two(slab), after=(col_stack,))
     others_down = to_other_core(downs)
     *outs_down, turned = rebuild(
-        run, (None, col_stack), downs, others_down, fixed_down, (0,), after=(downs[0],)
+        run, (None, col_stack), downs, others_down, fixed_down, (0,), slab // 8, after=(downs[0],)
     )
     few = width // TILE * 3 // 7 * TILE
     for i in range(len(steps)):
@@ -605,13 +613,13 @@
             got_gate = exchange(gate, steps[i + 1])
     others_gate = [exchange(x, other_replica) for x in gate]
     new_error_down, update_down, done = rebuild(
-        run, (turned, col_stack), [], [], fixed_down, (1,), before=outs_down, after=(gate[0],)
+        run, (turned, col_stack), [], [], fixed_down, (1,), slab // 8, before=outs_down, after=(gate[0],)
     )
     *outs_gate, done = rebuild(
-        run, (row_turned, None), gate[:1], others_gate[:1], fixed_gate, (0, 1), after=(done,)
+        run, (row_turned, None), gate[:1], others_gate[:1], fixed_gate, (0, 1), slab // 8, after=(done,)
     )
     new_error_gate, update_gate, _ = rebuild(
-        run, (row_turned, None), gate[1:], others_gate[1:], fixed_gate, (0, 1), few, outs_gate,
+        run, (row_turned, None), gate[1:], others_gate[1:], fixed_gate, (0, 1), slab // 8, few, outs_gate,
         after=(done,),
     )
     return (update_gate, update_down, new_error_gate, new_error_down)

time: 86.7 us -> 87.1 us (level)
    ppermute x21 -> x20, waiting for transfers between devices: 16.1 us -> 16.9 us  [exchange(): return lax.ppermute(x, ('dp', 'tensor'), pairs)]
    ppermute x21 -> x20, starting transfers between devices: 22.9 us -> 22.7 us  [exchange(): return lax.ppermute(x, ('dp', 'tensor'), pairs)]
  transfers between devices with their start and end apart: 21 -> 20, of which waited for: 13 -> 13; matrix products, arithmetic and copies ran while one was open for 0% -> 0% of each run, Pallas kernels for 37% -> 37%
where the time goes in v12:
time: 87.1 us; the launch traced here: 86.8 us
  Pallas kernels  46.3 us (53%)
  starting transfers between devices  22.7 us (26%)
  waiting for transfers between devices  16.9 us (19%)
  between operations  0.97 us (1%)
    pallas_call x21, Pallas kernels, __call__(): pl.pallas_call(body, out_shape=tuple(((pltpu.VMEM if spec is VMEM else pl...  46.3 us
    ppermute x20, starting transfers between devices, exchange(): return lax.ppermute(x, ('dp', 'tensor'), pairs)  22.7 us
    ppermute x20, waiting for transfers between devices, exchange(): return lax.ppermute(x, ('dp', 'tensor'), pairs)  16.9 us
  transfers between devices with their start and end apart: 20, of which 13 were waited for; matrix products, arithmetic and copies ran while one was open for 0% of the time, Pallas kernels for 37%

profile of v12, /device:TPU:0, one launch (start us, length us, event | category | flops | bytes accessed | tf_op | source)
XLA Modules:
  0.0 86.8 jit_solution(612290138009873931)
XLA Ops:
  0.6 9.8 %shard_map.93 = (f32[64,1792]{1,0:T(8,128)}, bf16[2560,1792]{1,0:T(8,128)(2,1)S(1)}, f32[32,1792]{1,0:T(8,128)S(1)}, f32[32,1792]{1,0:T(8,128)S(1)}) custom-call(bf16[2560,1792]{1,0:T(8,128)(2,1)} %refs_0_.3, bf16[2560,1792]{1,0:T(8,128)(2,1)} %refs_1_.3, bf16[64,5120]{1,0:T(8,128)(2,1)} %refs_2_.3), custom_call_target="tpu_custom_call" | custom-call | flops 9200000000 | bytes 1024 | tf_op jit(solution)/shard_map/pallas_call | solution.py:154
  10.4 3.0 %collective-permute-start = (f32[32,1792]{1,0:T(8,128)S(1)}, f32[32,1792]{1,0:T(8,128)S(1)}, u32[]{:S(2)}, u32[]{:S(2)}) collective-permute-start(f32[32,1792]{1,0:T(8,128)S(1)} %get-tuple-element.43), channel_id=1, source_target_pairs={{0,4},{1,5},{2,6},{3,7},{4,0},{5,1},{6,2},{7,3},{8,12},{9,13},{10,... | collective-permute-start | bytes 688136 | tf_op jit(solution)/shard_map/ppermute | solution.py:97
  13.4 5.1 %shard_map.94 = (f32[64,2560]{1,0:T(8,128)S(1)}, bf16[2560,1792]{1,0:T(8,128)(2,1)S(1)}) custom-call(bf16[2560,1792]{1,0:T(8,128)(2,1)} %refs_0_.5, bf16[2560,1792]{1,0:T(8,128)(2,1)} %refs_1_.5, bf16[64,1792]{1,0:T(8,128)(2,1)S(1)} %copy-done, f32[32,1792]{1,0:T(8,128)S(1)} %get-tuple-element.42.refs_3_.refs_0_), custom_call_target="tpu_custom_call" | custom-call | flops 4600000000 | bytes 1024 | tf_op jit(solution)/shard_map/pallas_call | solution.py:154
  19.1 2.8 %collective-permute-start.1 = (f32[32,1792]{1,0:T(8,128)S(1)}, f32[32,1792]{1,0:T(8,128)S(1)}, u32[]{:S(2)}, u32[]{:S(2)}) collective-permute-start(f32[32,1792]{1,0:T(8,128)S(1)} %shard_map.95.refs_5_.refs_0_), channel_id=1, source_target_pairs={{0,8},{1,9},{2,10},{3,11},{4,12},{5,13},{6,14},{7,15},{8,0},{9,1},... | collective-permute-start | bytes 688136 | tf_op jit(solution)/shard_map/ppermute | solution.py:97
  21.9 4.0 %shard_map.96 = (f32[64,2560]{1,0:T(8,128)S(1)}, bf16[2560,1792]{1,0:T(8,128)(2,1)S(1)}, f32[32,2560]{1,0:T(8,128)S(1)}, f32[32,1280]{1,0:T(8,128)S(1)}, f32[32,1280]{1,0:T(8,128)S(1)}) custom-call(bf16[2560,1792]{1,0:T(8,128)(2,1)} %refs_0_.5, bf16[2560,1792]{1,0:T(8,128)(2,1)} %refs_1_.5, ...), custom_call_target="tpu_custom_call", output_to_operand_aliasing={{0}: (3, {}), {1}: (4, {})} | custom-call | flops 4600000000 | bytes 1024 | tf_op jit(solution)/shard_map/pallas_call | solution.py:154
  26.4 0.9 %collective-permute-done.2.refs_1_ = f32[32,1280]{1,0:T(8,128)S(1)} collective-permute-done((f32[32,1280]{1,0:T(8,128)S(1)}, f32[32,1280]{1,0:T(8,128)S(1)}, u32[]{:S(2)}, u32[]{:S(2)}) %collective-permute-start.2) | collective-permute-done | bytes 163872 | tf_op jit(solution)/shard_map/ppermute | solution.py:97
  27.6 1.6 %collective-permute-start.5 = (f32[32,2560]{1,0:T(8,128)S(1)}, f32[32,2560]{1,0:T(8,128)S(1)}, u32[]{:S(2)}, u32[]{:S(2)}) collective-permute-start(f32[32,2560]{1,0:T(8,128)S(1)} %shard_map.97.refs_2_.refs_0_), channel_id=1, source_target_pairs={{0,2},{1,5},{2,0},{3,7},{4,6},{5,1},{6,4},{7,3},{8,10},{9,13},{10,... | collective-permute-start | bytes 983048 | tf_op jit(solution)/shard_map/ppermute | solution.py:97
  29.2 2.7 %collective-permute-done.1.refs_1_ = f32[32,1792]{1,0:T(8,128)S(1)} collective-permute-done((f32[32,1792]{1,0:T(8,128)S(1)}, f32[32,1792]{1,0:T(8,128)S(1)}, u32[]{:S(2)}, u32[]{:S(2)}) %collective-permute-start.1) | collective-permute-done | bytes 229408 | tf_op jit(solution)/shard_map/ppermute | solution.py:97
  32.4 2.3 %collective-permute-done.5.refs_1_ = f32[32,2560]{1,0:T(8,128)S(1)} collective-permute-done((f32[32,2560]{1,0:T(8,128)S(1)}, f32[32,2560]{1,0:T(8,128)S(1)}, u32[]{:S(2)}, u32[]{:S(2)}) %collective-permute-start.5) | collective-permute-done | bytes 327712 | tf_op jit(solution)/shard_map/ppermute | solution.py:97
  34.8 1.6 %collective-permute-start.8 = (f32[32,2560]{1,0:T(8,128)S(1)}, f32[32,2560]{1,0:T(8,128)S(1)}, u32[]{:S(2)}, u32[]{:S(2)}) collective-permute-start(f32[32,2560]{1,0:T(8,128)S(1)} %shard_map.99.refs_3_.refs_0_), channel_id=1, source_target_pairs={{0,4},{1,3},{2,6},{3,1},{4,0},{5,7},{6,2},{7,5},{8,12},{9,11},{10,... | collective-permute-start | bytes 983048 | tf_op jit(solution)/shard_map/ppermute | solution.py:97
  36.4 3.7 %collective-permute-done.4.refs_1_ = f32[32,1792]{1,0:T(8,128)S(1)} collective-permute-done((f32[32,1792]{1,0:T(8,128)S(1)}, f32[32,1792]{1,0:T(8,128)S(1)}, u32[]{:S(2)}, u32[]{:S(2)}) %collective-permute-start.4) | collective-permute-done | bytes 229408 | tf_op jit(solution)/shard_map/ppermute | solution.py:97
  40.2 5.1 %shard_map.100 = (f32[32,2688]{1,0:T(8,128)S(1)}, f32[32,1280]{1,0:T(8,128)S(1)}, f32[32,1408]{1,0:T(8,128)S(1)}, bf16[192,1792]{1,0:T(8,128)(2,1)S(1)}) custom-call(f32[32,1792]{1,0:T(8,128)S(1)} %shard_map.98.refs_2_.refs_0_, f32[32,1792]{1,0:T(8,128)S(1)} %collective-permute-done.4.refs_1_, bf16[2560,1792]{1,0:T(8,128)(2,1)S(1)} %get-tuple-element.49.refs_2_.refs_5_, ...), custom_call_target="tpu_custom_call" | custom-call | flops 5750000128 | bytes 1024 | tf_op jit(solution)/shard_map/pallas_call | solution.py:154
  46.0 1.5 %collective-permute-done.6.refs_1_ = f32[32,1280]{1,0:T(8,128)S(1)} collective-permute-done((f32[32,1280]{1,0:T(8,128)S(1)}, f32[32,1280]{1,0:T(8,128)S(1)}, u32[]{:S(2)}, u32[]{:S(2)}) %collective-permute-start.6) | collective-permute-done | bytes 163872 | tf_op jit(solution)/shard_map/ppermute | solution.py:97
  47.6 1.4 %collective-permute-start.12 = (f32[32,2560]{1,0:T(8,128)S(1)}, f32[32,2560]{1,0:T(8,128)S(1)}, u32[]{:S(2)}, u32[]{:S(2)}) collective-permute-start(f32[32,2560]{1,0:T(8,128)S(1)} %get-tuple-element.55.refs_3_.refs_0_), channel_id=1, source_target_pairs={{0,2},{1,5},{2,0},{3,7},{4,6},{5,1},{6,4},{7,3},{8,10},{9,13},{10,... | collective-permute-start | bytes 983048 | tf_op jit(solution)/shard_map/ppermute | solution.py:97
  49.0 3.2 %shard_map.103 = (f32[32,1792]{1,0:T(8,128)S(1)}, f32[32,1792]{1,0:T(8,128)S(1)}, f32[64,64]{1,0:T(8,128)S(1)}, bf16[192,2560]{1,0:T(8,128)(2,1)S(1)}) custom-call(f32[32,2560]{1,0:T(8,128)S(1)} %shard_map.101.refs_3_.refs_0_, f32[32,2560]{1,0:T(8,128)S(1)} %collective-permute-done.10.refs_1_, bf16[2560,1792]{1,0:T(8,128)(2,1)S(1)} %get-tuple-element.54.refs_2_.refs_3_, ...), custom_call_target="tpu_custom_call" | custom-call | flops 4600000000 | bytes 1024 | tf_op jit(solution)/shard_map/pallas_call | solution.py:154
  53.3 3.5 %collective-permute-start.11 = (f32[64,64]{1,0:T(8,128)S(1)}, f32[64,64]{1,0:T(8,128)S(1)}, u32[]{:S(2)}, u32[]{:S(2)}) collective-permute-start(f32[64,64]{1,0:T(8,128)S(1)} %get-tuple-element.56.refs_2_), channel_id=1, source_target_pairs={{0,8},{1,9},{2,10},{3,11},{4,12},{5,13},{6,14},{7,15},{8,0},{9,1},... | collective-permute-start | bytes 49160 | tf_op jit(solution)/shard_map/ppermute | solution.py:97
  57.0 1.8 %collective-permute-done.11.refs_3_ = f32[64,64]{1,0:T(8,128)S(1)} collective-permute-done((f32[64,64]{1,0:T(8,128)S(1)}, f32[64,64]{1,0:T(8,128)S(1)}, u32[]{:S(2)}, u32[]{:S(2)}) %collective-permute-start.11) | collective-permute-done | bytes 16416 | tf_op jit(solution)/shard_map/ppermute | solution.py:97
  59.5 3.1 %collective-permute-start.14 = (f32[32,1792]{1,0:T(8,128)S(1)}, f32[32,1792]{1,0:T(8,128)S(1)}, u32[]{:S(2)}, u32[]{:S(2)}) collective-permute-start(f32[32,1792]{1,0:T(8,128)S(1)} %shard_map.106.refs_4_.refs_0_), channel_id=1, source_target_pairs={{0,8},{1,9},{2,10},{3,11},{4,12},{5,13},{6,14},{7,15},{8,0},{9,1},... | collective-permute-start | bytes 688136 | tf_op jit(solution)/shard_map/ppermute | solution.py:97
  62.6 3.9 %shard_map.107 = (bf16[256,1792]{1,0:T(8,128)(2,1)S(1)}, bf16[2560,256]{1,0:T(8,128)(2,1)S(1)}) custom-call(f32[64,64]{1,0:T(8,128)S(1)} %get-tuple-element.57.refs_0_, bf16[192,1792]{1,0:T(8,128)(2,1)S(1)} %get-tuple-element.58.refs_1_, f32[64,64]{1,0:T(8,128)S(1)} %get-tuple-element.59.refs_2_, bf16[192,2560]{1,0:T(8,128)(2,1)S(1)} %get-tuple-element.60.refs_3_, ...), custom_call_target="tpu_custom_call" | custom-call | flops 5750000128 | bytes 1024 | tf_op jit(solution)/shard_map/pallas_call | solution.py:154
  68.9 4.3 %shard_map.109 = (bf16[2560,1792]{1,0:T(8,128)(2,1)}, bf16[1280,1792]{1,0:T(8,128)(2,1)}, bf16[2560,256]{1,0:T(8,128)(2,1)S(1)}) custom-call(bf16[256,1792]{1,0:T(8,128)(2,1)S(1)} %get-tuple-element.64.refs_2_.refs_0_.refs_1_, f32[32,1280]{1,0:T(8,128)S(1)} %get-tuple-element.65.refs_1_.refs_6_, f32[32,1280]{1,0:T(8,128)S(1)} %get-tuple-element.66.refs_2_, ...), custom_call_target="tpu_custom_call" | custom-call | flops 115000000 | bytes 1024 | tf_op jit(solution)/shard_map/pallas_call | solution.py:154
  73.6 1.8 %collective-permute-start.18 = (f32[32,1024]{1,0:T(8,128)S(1)}, f32[32,1024]{1,0:T(8,128)S(1)}, u32[]{:S(2)}, u32[]{:S(2)}) collective-permute-start(f32[32,1024]{1,0:T(8,128)S(1)} %get-tuple-element.68.refs_1_), channel_id=1, source_target_pairs={{0,4},{1,5},{2,6},{3,7},{4,0},{5,1},{6,2},{7,3},{8,12},{9,13},{10,... | collective-permute-start | bytes 393224 | tf_op jit(solution)/shard_map/ppermute | solution.py:97
  75.4 2.9 %shard_map.111 = (bf16[2560,1792]{1,0:T(8,128)(2,1)}, bf16[1280,1792]{1,0:T(8,128)(2,1)}, bf16[16,128]{1,0:T(8,128)(2,1)S(1)}) custom-call(bf16[2560,256]{1,0:T(8,128)(2,1)S(1)} %get-tuple-element.67.refs_2_.refs_0_, bf16[256,1792]{1,0:T(8,128)(2,1)S(1)} %get-tuple-element.64.refs_2_.refs_0_.refs_1_, ...), custom_call_target="tpu_custom_call", output_to_operand_aliasing={{0}: (3, {}), {1}: (4, {})} | custom-call | flops 4600000000 | bytes 1024 | tf_op jit(solution)/shard_map/pallas_call | solution.py:154
  79.0 3.2 %shard_map.112 = (bf16[2560,1792]{1,0:T(8,128)(2,1)}, bf16[1280,1792]{1,0:T(8,128)(2,1)}, bf16[16,128]{1,0:T(8,128)(2,1)S(1)}) custom-call(bf16[2560,256]{1,0:T(8,128)(2,1)S(1)} %get-tuple-element.63.refs_0_, f32[32,768]{1,0:T(8,128)S(1)} %get-tuple-element.69.refs_5_.refs_1_, f32[32,768]{1,0:T(8,128)S(1)} %collective-permute-done.19.refs_2_, ...), custom_call_target="tpu_custom_call" | custom-call | flops 4600000000 | bytes 1024 | tf_op jit(solution)/shard_map/pallas_call | solution.py:154
  82.2 4.5 %shard_map.113 = (bf16[2560,1792]{1,0:T(8,128)(2,1)}, bf16[1280,1792]{1,0:T(8,128)(2,1)}, bf16[16,128]{1,0:T(8,128)(2,1)}) custom-call(bf16[2560,256]{1,0:T(8,128)(2,1)S(1)} %get-tuple-element.63.refs_0_, f32[32,1024]{1,0:T(8,128)S(1)} %get-tuple-element.68.refs_1_, ...), custom_call_target="tpu_custom_call", output_to_operand_aliasing={{0}: (4, {}), {1}: (5, {})} | custom-call | flops 4600000000 | bytes 1024 | tf_op jit(solution)/shard_map/pallas_call | solution.py:154
  (39 shorter events, 8.1 us)
Async XLA Ops:
  0.6 12.8 %copy-start = (bf16[64,1792]{1,0:T(8,128)(2,1)S(1)}, bf16[64,1792]{1,0:T(8,128)(2,1)}, u32[]{:S(2)}) copy-start(bf16[64,1792]{1,0:T(8,128)(2,1)} %refs_2_.5) | copy-start | bytes 688132
  10.4 8.6 %collective-permute-start = (f32[32,1792]{1,0:T(8,128)S(1)}, f32[32,1792]{1,0:T(8,128)S(1)}, u32[]{:S(2)}, u32[]{:S(2)}) collective-permute-start(f32[32,1792]{1,0:T(8,128)S(1)} %get-tuple-element.43), channel_id=1, source_target_pairs={{0,4},{1,5},{2,6},{3,7},{4,0},{5,1},{6,2},{7,3},{8,12},{9,13},{10,... | collective-permute-start | bytes 688136 | tf_op jit(solution)/shard_map/ppermute | solution.py:97
  19.1 12.8 %collective-permute-start.1 = (f32[32,1792]{1,0:T(8,128)S(1)}, f32[32,1792]{1,0:T(8,128)S(1)}, u32[]{:S(2)}, u32[]{:S(2)}) collective-permute-start(f32[32,1792]{1,0:T(8,128)S(1)} %shard_map.95.refs_5_.refs_0_), channel_id=1, source_target_pairs={{0,8},{1,9},{2,10},{3,11},{4,12},{5,13},{6,14},{7,15},{8,0},{9,1},... | collective-permute-start | bytes 688136 | tf_op jit(solution)/shard_map/ppermute | solution.py:97
  25.9 1.5 %collective-permute-start.2 = (f32[32,1280]{1,0:T(8,128)S(1)}, f32[32,1280]{1,0:T(8,128)S(1)}, u32[]{:S(2)}, u32[]{:S(2)}) collective-permute-start(f32[32,1280]{1,0:T(8,128)S(1)} %get-tuple-element.47), channel_id=1, source_target_pairs={{0,1},{1,0},{2,3},{3,2},{4,5},{5,4},{6,7},{7,6},{8,9},{9,8},{10,11... | collective-permute-start | bytes 491528 | tf_op jit(solution)/shard_map/ppermute | solution.py:97
  25.9 1.6 %collective-permute-start.3 = (f32[32,1280]{1,0:T(8,128)S(1)}, f32[32,1280]{1,0:T(8,128)S(1)}, u32[]{:S(2)}, u32[]{:S(2)}) collective-permute-start(f32[32,1280]{1,0:T(8,128)S(1)} %get-tuple-element.48), channel_id=1, source_target_pairs={{0,1},{1,0},{2,3},{3,2},{4,5},{5,4},{6,7},{7,6},{8,9},{9,8},{10,11... | collective-permute-start | bytes 491528 | tf_op jit(solution)/shard_map/ppermute | solution.py:97
  27.6 7.1 %collective-permute-start.5 = (f32[32,2560]{1,0:T(8,128)S(1)}, f32[32,2560]{1,0:T(8,128)S(1)}, u32[]{:S(2)}, u32[]{:S(2)}) collective-permute-start(f32[32,2560]{1,0:T(8,128)S(1)} %shard_map.97.refs_2_.refs_0_), channel_id=1, source_target_pairs={{0,2},{1,5},{2,0},{3,7},{4,6},{5,1},{6,4},{7,3},{8,10},{9,13},{10,... | collective-permute-start | bytes 983048 | tf_op jit(solution)/shard_map/ppermute | solution.py:97
  31.9 8.3 %collective-permute-start.4 = (f32[32,1792]{1,0:T(8,128)S(1)}, f32[32,1792]{1,0:T(8,128)S(1)}, u32[]{:S(2)}, u32[]{:S(2)}) collective-permute-start(f32[32,1792]{1,0:T(8,128)S(1)} %shard_map.98.refs_2_.refs_0_), channel_id=1, source_target_pairs={{0,4},{1,5},{2,6},{3,7},{4,0},{5,1},{6,2},{7,3},{8,12},{9,13},{10,... | collective-permute-start | bytes 688136 | tf_op jit(solution)/shard_map/ppermute | solution.py:97
  34.8 10.5 %collective-permute-start.8 = (f32[32,2560]{1,0:T(8,128)S(1)}, f32[32,2560]{1,0:T(8,128)S(1)}, u32[]{:S(2)}, u32[]{:S(2)}) collective-permute-start(f32[32,2560]{1,0:T(8,128)S(1)} %shard_map.99.refs_3_.refs_0_), channel_id=1, source_target_pairs={{0,4},{1,3},{2,6},{3,1},{4,0},{5,7},{6,2},{7,5},{8,12},{9,11},{10,... | collective-permute-start | bytes 983048 | tf_op jit(solution)/shard_map/ppermute | solution.py:97
  45.3 3.6 %collective-permute-start.10 = (f32[32,2560]{1,0:T(8,128)S(1)}, f32[32,2560]{1,0:T(8,128)S(1)}, u32[]{:S(2)}, u32[]{:S(2)}) collective-permute-start(f32[32,2560]{1,0:T(8,128)S(1)} %shard_map.101.refs_3_.refs_0_), channel_id=1, source_target_pairs={{0,1},{1,0},{2,3},{3,2},{4,5},{5,4},{6,7},{7,6},{8,9},{9,8},{10,11... | collective-permute-start | bytes 983048 | tf_op jit(solution)/shard_map/ppermute | solution.py:97
  45.4 2.1 %collective-permute-start.7 = (f32[32,1408]{1,0:T(8,128)S(1)}, f32[32,1408]{1,0:T(8,128)S(1)}, u32[]{:S(2)}, u32[]{:S(2)}) collective-permute-start(f32[32,1408]{1,0:T(8,128)S(1)} %get-tuple-element.52), channel_id=1, source_target_pairs={{0,1},{1,0},{2,3},{3,2},{4,5},{5,4},{6,7},{7,6},{8,9},{9,8},{10,11... | collective-permute-start | bytes 540680 | tf_op jit(solution)/shard_map/ppermute | solution.py:97
  45.9 1.6 %collective-permute-start.6 = (f32[32,1280]{1,0:T(8,128)S(1)}, f32[32,1280]{1,0:T(8,128)S(1)}, u32[]{:S(2)}, u32[]{:S(2)}) collective-permute-start(f32[32,1280]{1,0:T(8,128)S(1)} %get-tuple-element.51), channel_id=1, source_target_pairs={{0,1},{1,0},{2,3},{3,2},{4,5},{5,4},{6,7},{7,6},{8,9},{9,8},{10,11... | collective-permute-start | bytes 491528 | tf_op jit(solution)/shard_map/ppermute | solution.py:97
  47.6 9.3 %collective-permute-start.12 = (f32[32,2560]{1,0:T(8,128)S(1)}, f32[32,2560]{1,0:T(8,128)S(1)}, u32[]{:S(2)}, u32[]{:S(2)}) collective-permute-start(f32[32,2560]{1,0:T(8,128)S(1)} %get-tuple-element.55.refs_3_.refs_0_), channel_id=1, source_target_pairs={{0,2},{1,5},{2,0},{3,7},{4,6},{5,1},{6,4},{7,3},{8,10},{9,13},{10,... | collective-permute-start | bytes 983048 | tf_op jit(solution)/shard_map/ppermute | solution.py:97
  52.2 7.3 %collective-permute-start.13 = (f32[32,1792]{1,0:T(8,128)S(1)}, f32[32,1792]{1,0:T(8,128)S(1)}, u32[]{:S(2)}, u32[]{:S(2)}) collective-permute-start(f32[32,1792]{1,0:T(8,128)S(1)} %get-tuple-element.62), channel_id=1, source_target_pairs={{0,4},{1,5},{2,6},{3,7},{4,0},{5,1},{6,2},{7,3},{8,12},{9,13},{10,... | collective-permute-start | bytes 688136 | tf_op jit(solution)/shard_map/ppermute | solution.py:97
  52.8 4.2 %collective-permute-start.9 = (f32[32,128]{1,0:T(8,128)S(1)}, f32[32,128]{1,0:T(8,128)S(1)}, u32[]{:S(2)}, u32[]{:S(2)}) collective-permute-start(f32[32,128]{1,0:T(8,128)S(1)} %get-tuple-element.53.refs_0_), channel_id=1, source_target_pairs={{0,2},{1,3},{2,0},{3,1},{4,6},{5,7},{6,4},{7,5},{8,10},{9,11},{10,... | collective-permute-start | bytes 49160 | tf_op jit(solution)/shard_map/ppermute | solution.py:97
  53.3 5.5 %collective-permute-start.11 = (f32[64,64]{1,0:T(8,128)S(1)}, f32[64,64]{1,0:T(8,128)S(1)}, u32[]{:S(2)}, u32[]{:S(2)}) collective-permute-start(f32[64,64]{1,0:T(8,128)S(1)} %get-tuple-element.56.refs_2_), channel_id=1, source_target_pairs={{0,8},{1,9},{2,10},{3,11},{4,12},{5,13},{6,14},{7,15},{8,0},{9,1},... | collective-permute-start | bytes 49160 | tf_op jit(solution)/shard_map/ppermute | solution.py:97
  56.9 10.3 %collective-permute-start.15 = (f32[32,2560]{1,0:T(8,128)S(1)}, f32[32,2560]{1,0:T(8,128)S(1)}, u32[]{:S(2)}, u32[]{:S(2)}) collective-permute-start(f32[32,2560]{1,0:T(8,128)S(1)} %shard_map.104.refs_4_.refs_0_), channel_id=1, source_target_pairs={{0,4},{1,3},{2,6},{3,1},{4,0},{5,7},{6,2},{7,5},{8,12},{9,11},{10,... | collective-permute-start | bytes 983048 | tf_op jit(solution)/shard_map/ppermute | solution.py:97
  59.5 13.7 %collective-permute-start.14 = (f32[32,1792]{1,0:T(8,128)S(1)}, f32[32,1792]{1,0:T(8,128)S(1)}, u32[]{:S(2)}, u32[]{:S(2)}) collective-permute-start(f32[32,1792]{1,0:T(8,128)S(1)} %shard_map.106.refs_4_.refs_0_), channel_id=1, source_target_pairs={{0,8},{1,9},{2,10},{3,11},{4,12},{5,13},{6,14},{7,15},{8,0},{9,1},... | collective-permute-start | bytes 688136 | tf_op jit(solution)/shard_map/ppermute | solution.py:97
  67.2 1.5 %collective-permute-start.16 = (f32[32,1280]{1,0:T(8,128)S(1)}, f32[32,1280]{1,0:T(8,128)S(1)}, u32[]{:S(2)}, u32[]{:S(2)}) collective-permute-start(f32[32,1280]{1,0:T(8,128)S(1)} %get-tuple-element.65.refs_1_.refs_6_), channel_id=1, source_target_pairs={{0,1},{1,0},{2,3},{3,2},{4,5},{5,4},{6,7},{7,6},{8,9},{9,8},{10,11... | collective-permute-start | bytes 491528 | tf_op jit(solution)/shard_map/ppermute | solution.py:97
  67.3 1.6 %collective-permute-start.17 = (f32[32,1280]{1,0:T(8,128)S(1)}, f32[32,1280]{1,0:T(8,128)S(1)}, u32[]{:S(2)}, u32[]{:S(2)}) collective-permute-start(f32[32,1280]{1,0:T(8,128)S(1)} %get-tuple-element.66.refs_2_), channel_id=1, source_target_pairs={{0,1},{1,0},{2,3},{3,2},{4,5},{5,4},{6,7},{7,6},{8,9},{9,8},{10,11... | collective-permute-start | bytes 491528 | tf_op jit(solution)/shard_map/ppermute | solution.py:97
  73.3 5.7 %collective-permute-start.19 = (f32[32,768]{1,0:T(8,128)S(1)}, f32[32,768]{1,0:T(8,128)S(1)}, u32[]{:S(2)}, u32[]{:S(2)}) collective-permute-start(f32[32,768]{1,0:T(8,128)S(1)} %get-tuple-element.69.refs_5_.refs_1_), channel_id=1, source_target_pairs={{0,4},{1,5},{2,6},{3,7},{4,0},{5,1},{6,2},{7,3},{8,12},{9,13},{10,... | collective-permute-start | bytes 294920 | tf_op jit(solution)/shard_map/ppermute | solution.py:97
  73.6 8.6 %collective-permute-start.18 = (f32[32,1024]{1,0:T(8,128)S(1)}, f32[32,1024]{1,0:T(8,128)S(1)}, u32[]{:S(2)}, u32[]{:S(2)}) collective-permute-start(f32[32,1024]{1,0:T(8,128)S(1)} %get-tuple-element.68.refs_1_), channel_id=1, source_target_pairs={{0,4},{1,5},{2,6},{3,7},{4,0},{5,1},{6,2},{7,3},{8,12},{9,13},{10,... | collective-permute-start | bytes 393224 | tf_op jit(solution)/shard_map/ppermute | solution.py:97

commit v13 on v12

--- a/solution.py
+++ b/solution.py
@@ -11,7 +11,7 @@
 RANK = 64
 TILE = 256
 FLOPS = 1.15e9
-WEIGHTS = (8.0, 4.0, 1.0, 4.0, 0.1, 5.0, 1.0, 5.0, 1.0, 1.0, 4.0, 0.1, 0.1, 1.0, 5.0, 1.0, 0.1, 1.0, 4.0, 4.0, 4.0)
+WEIGHTS = (8.0, 4.0, 1.0, 4.0, 0.1, 5.0, 1.0, 5.0, 1.0, 4.0, 1.0, 0.1, 1.0, 0.1, 5.0, 1.0, 1.0, 8.0, 8.0)
 MIB = 1 << 20
 BF16 = jnp.bfloat16
 F32 = jnp.float32
@@ -580,47 +580,37 @@
     gots = to_other_core(gives)
     gates = add(run, [gate], [got_gate], after=(keep,))
     others_gate = to_other_core(gates)
-    down, gram_down = add(run, [keep], gots, [slab, 2 * RANK], after=(gates[0],))
+    keep_gate, give_gate, gram_gate, left_gate = gate_right(run, gates, others_gate, fixed_gate)
+    got_gate = exchange(give_gate, other_replica)
+    grams_gate = [gram_gate] + [
+        exchange(gram_gate, lambda d, t, b=b: (d ^ b, t)) for b in range(REPLICAS, n_dp, REPLICAS)
+    ]
+    down, gram_down = add(run, [keep], gots, [slab, 2 * RANK], after=(gram_gate,))
     grams_down = [gram_down] + [
         exchange(gram_down, lambda d, t, b=b: (d, t ^ b)) for b in range(2, n_t, 2)
     ]
     got = exchange(down, hops[0])
-    keep_gate, give_gate, gram_gate, left_gate = gate_right(
-        run, gates, others_gate, fixed_gate, after=(down,)
-    )
-    got_gate = exchange(give_gate, other_replica)
-    grams_gate = [gram_gate] + [
-        exchange(gram_gate, lambda d, t, b=b: (d ^ b, t)) for b in range(REPLICAS, n_dp, REPLICAS)
-    ]
-    for hop in hops[1:]:
-        (down,) = add(run, [down], [got], after=(gram_gate,))
-        got = exchange(down, hop)
-    gram_down, gram_gate = gram_sums(run, grams_down, grams_gate, after=(down,))
+    gram_down, gram_gate = gram_sums(run, grams_down, grams_gate)
     (gate,) = add(run, [keep_gate], [got_gate], after=(gram_gate,))
     got_gate = exchange(gate, steps[0])
-    col_stack, row_turned = solve(run, gram_down, left_down, gram_gate, left_gate, after=(gate,))
+    for hop in hops[1:]:
+        (down,) = add(run, [down], [got], after=(gate,))
+        got = exchange(down, hop)
+    col_stack, row_turned = solve(
+        run, gram_down, left_down, gram_gate, left_gate, after=(down,)
+    )
     downs = add(run, [down], [got], in_two(slab), after=(col_stack,))
     others_down = to_other_core(downs)
-    *outs_down, turned = rebuild(
-        run, (None, col_stack), downs, others_down, fixed_down, (0,), slab // 8, after=(downs[0],)
-    )
-    few = width // TILE * 3 // 7 * TILE
     for i in range(len(steps)):
-        last = i + 1 == len(steps)
-        gate = add(run, [gate], [got_gate], [few, width - few] if last else None, after=(turned,))
-        if not last:
-            (gate,) = gate
+        (gate,) = add(run, [gate], [got_gate], after=(downs[0],))
+        if i + 1 < len(steps):
             got_gate = exchange(gate, steps[i + 1])
-    others_gate = [exchange(x, other_replica) for x in gate]
+    other_gate = exchange(gate, other_replica)
     new_error_down, update_down, done = rebuild(
-        run, (turned, col_stack), [], [], fixed_down, (1,), slab // 8, before=outs_down, after=(gate[0],)
-    )
-    *outs_gate, done = rebuild(
-        run, (row_turned, None), gate[:1], others_gate[:1], fixed_gate, (0, 1), slab // 8, after=(done,)
+        run, (None, col_stack), downs, others_down, fixed_down, (0, 1), slab // 8, after=(gate,)
     )
     new_error_gate, update_gate, _ = rebuild(
-        run, (row_turned, None), gate[1:], others_gate[1:], fixed_gate, (0, 1), slab // 8, few, outs_gate,
-        after=(done,),
+        run, (row_turned, None), [gate], [other_gate], fixed_gate, (0, 1), slab // 8, after=(done,)
     )
     return (update_gate, update_down, new_error_gate, new_error_down)
 

time: 87.1 us -> 88.4 us (1.015)
  waiting for transfers between devices: 16.9 us -> 20.6 us
  Pallas kernels: 46.3 us -> 44.3 us
    ppermute x20 -> x19, waiting for transfers between devices: 16.9 us -> 20.6 us  [exchange(): return lax.ppermute(x, ('dp', 'tensor'), pairs)]
    pallas_call x21 -> x19, Pallas kernels: 46.3 us -> 44.3 us  [__call__(): pl.pallas_call(body, out_shape=tuple(((pltpu.VMEM if spec is VMEM else pl...]
    ppermute x20 -> x19, starting transfers between devices: 22.7 us -> 22.3 us  [exchange(): return lax.ppermute(x, ('dp', 'tensor'), pairs)]
  transfers between devices with their start and end apart: 20 -> 19, of which waited for: 13 -> 13; matrix products, arithmetic and copies ran while one was open for 0% -> 0% of each run, Pallas kernels for 37% -> 32%
where the time goes in v13:
time: 88.4 us; the launch traced here: 88.1 us
  Pallas kernels  44.3 us (50%)
  starting transfers between devices  22.3 us (25%)
  waiting for transfers between devices  20.6 us (23%)
  between operations  0.93 us (1%)
    pallas_call x19, Pallas kernels, __call__(): pl.pallas_call(body, out_shape=tuple(((pltpu.VMEM if spec is VMEM else pl...  44.3 us
    ppermute x19, starting transfers between devices, exchange(): return lax.ppermute(x, ('dp', 'tensor'), pairs)  22.3 us
    ppermute x19, waiting for transfers between devices, exchange(): return lax.ppermute(x, ('dp', 'tensor'), pairs)  20.6 us
  transfers between devices with their start and end apart: 19, of which 13 were waited for; matrix products, arithmetic and copies ran while one was open for 0% of the time, Pallas kernels for 32%

profile of v13, /device:TPU:0, one launch (start us, length us, event | category | flops | bytes accessed | tf_op | source)
XLA Modules:
  0.0 88.1 jit_solution(12538546835728203743)
XLA Ops:
  0.6 9.8 %shard_map.93 = (f32[64,1792]{1,0:T(8,128)}, bf16[2560,1792]{1,0:T(8,128)(2,1)S(1)}, f32[32,1792]{1,0:T(8,128)S(1)}, f32[32,1792]{1,0:T(8,128)S(1)}) custom-call(bf16[2560,1792]{1,0:T(8,128)(2,1)} %refs_0_.3, bf16[2560,1792]{1,0:T(8,128)(2,1)} %refs_1_.3, bf16[64,5120]{1,0:T(8,128)(2,1)} %refs_2_.3), custom_call_target="tpu_custom_call" | custom-call | flops 9200000000 | bytes 1024 | tf_op jit(solution)/shard_map/pallas_call | solution.py:154
  10.4 3.0 %collective-permute-start = (f32[32,1792]{1,0:T(8,128)S(1)}, f32[32,1792]{1,0:T(8,128)S(1)}, u32[]{:S(2)}, u32[]{:S(2)}) collective-permute-start(f32[32,1792]{1,0:T(8,128)S(1)} %get-tuple-element.35), channel_id=1, source_target_pairs={{0,4},{1,5},{2,6},{3,7},{4,0},{5,1},{6,2},{7,3},{8,12},{9,13},{10,... | collective-permute-start | bytes 688136 | tf_op jit(solution)/shard_map/ppermute | solution.py:97
  13.4 5.1 %shard_map.94 = (f32[64,2560]{1,0:T(8,128)S(1)}, bf16[2560,1792]{1,0:T(8,128)(2,1)S(1)}) custom-call(bf16[2560,1792]{1,0:T(8,128)(2,1)} %refs_0_.5, bf16[2560,1792]{1,0:T(8,128)(2,1)} %refs_1_.5, bf16[64,1792]{1,0:T(8,128)(2,1)S(1)} %copy-done, f32[32,1792]{1,0:T(8,128)S(1)} %get-tuple-element.34.refs_3_.refs_0_), custom_call_target="tpu_custom_call" | custom-call | flops 4600000000 | bytes 1024 | tf_op jit(solution)/shard_map/pallas_call | solution.py:154
  19.1 2.8 %collective-permute-start.1 = (f32[32,1792]{1,0:T(8,128)S(1)}, f32[32,1792]{1,0:T(8,128)S(1)}, u32[]{:S(2)}, u32[]{:S(2)}) collective-permute-start(f32[32,1792]{1,0:T(8,128)S(1)} %shard_map.95.refs_5_.refs_0_), channel_id=1, source_target_pairs={{0,8},{1,9},{2,10},{3,11},{4,12},{5,13},{6,14},{7,15},{8,0},{9,1},... | collective-permute-start | bytes 688136 | tf_op jit(solution)/shard_map/ppermute | solution.py:97
  21.9 4.0 %shard_map.96 = (f32[64,2560]{1,0:T(8,128)S(1)}, bf16[2560,1792]{1,0:T(8,128)(2,1)S(1)}, f32[32,2560]{1,0:T(8,128)S(1)}, f32[32,1280]{1,0:T(8,128)S(1)}, f32[32,1280]{1,0:T(8,128)S(1)}) custom-call(bf16[2560,1792]{1,0:T(8,128)(2,1)} %refs_0_.5, bf16[2560,1792]{1,0:T(8,128)(2,1)} %refs_1_.5, ...), custom_call_target="tpu_custom_call", output_to_operand_aliasing={{0}: (3, {}), {1}: (4, {})} | custom-call | flops 4600000000 | bytes 1024 | tf_op jit(solution)/shard_map/pallas_call | solution.py:154
  27.6 1.6 %collective-permute-start.5 = (f32[32,2560]{1,0:T(8,128)S(1)}, f32[32,2560]{1,0:T(8,128)S(1)}, u32[]{:S(2)}, u32[]{:S(2)}) collective-permute-start(f32[32,2560]{1,0:T(8,128)S(1)} %shard_map.97.refs_2_.refs_0_), channel_id=1, source_target_pairs={{0,2},{1,5},{2,0},{3,7},{4,6},{5,1},{6,4},{7,3},{8,10},{9,13},{10,... | collective-permute-start | bytes 983048 | tf_op jit(solution)/shard_map/ppermute | solution.py:97
  29.2 2.7 %collective-permute-done.1.refs_1_ = f32[32,1792]{1,0:T(8,128)S(1)} collective-permute-done((f32[32,1792]{1,0:T(8,128)S(1)}, f32[32,1792]{1,0:T(8,128)S(1)}, u32[]{:S(2)}, u32[]{:S(2)}) %collective-permute-start.1) | collective-permute-done | bytes 229408 | tf_op jit(solution)/shard_map/ppermute | solution.py:97
  32.4 2.3 %collective-permute-done.5.refs_1_ = f32[32,2560]{1,0:T(8,128)S(1)} collective-permute-done((f32[32,2560]{1,0:T(8,128)S(1)}, f32[32,2560]{1,0:T(8,128)S(1)}, u32[]{:S(2)}, u32[]{:S(2)}) %collective-permute-start.5) | collective-permute-done | bytes 327712 | tf_op jit(solution)/shard_map/ppermute | solution.py:97
  34.8 1.6 %collective-permute-start.8 = (f32[32,2560]{1,0:T(8,128)S(1)}, f32[32,2560]{1,0:T(8,128)S(1)}, u32[]{:S(2)}, u32[]{:S(2)}) collective-permute-start(f32[32,2560]{1,0:T(8,128)S(1)} %shard_map.99.refs_3_.refs_0_), channel_id=1, source_target_pairs={{0,4},{1,3},{2,6},{3,1},{4,0},{5,7},{6,2},{7,5},{8,12},{9,11},{10,... | collective-permute-start | bytes 983048 | tf_op jit(solution)/shard_map/ppermute | solution.py:97
  36.4 3.7 %collective-permute-done.4.refs_1_ = f32[32,1792]{1,0:T(8,128)S(1)} collective-permute-done((f32[32,1792]{1,0:T(8,128)S(1)}, f32[32,1792]{1,0:T(8,128)S(1)}, u32[]{:S(2)}, u32[]{:S(2)}) %collective-permute-start.4) | collective-permute-done | bytes 229408 | tf_op jit(solution)/shard_map/ppermute | solution.py:97
  40.2 5.1 %shard_map.100 = (f32[32,2688]{1,0:T(8,128)S(1)}, f32[32,1280]{1,0:T(8,128)S(1)}, f32[32,1408]{1,0:T(8,128)S(1)}, bf16[192,1792]{1,0:T(8,128)(2,1)S(1)}) custom-call(f32[32,1792]{1,0:T(8,128)S(1)} %shard_map.98.refs_2_.refs_0_, f32[32,1792]{1,0:T(8,128)S(1)} %collective-permute-done.4.refs_1_, bf16[2560,1792]{1,0:T(8,128)(2,1)S(1)} %get-tuple-element.41.refs_2_.refs_5_, ...), custom_call_target="tpu_custom_call" | custom-call | flops 5750000128 | bytes 1024 | tf_op jit(solution)/shard_map/pallas_call | solution.py:154
  46.0 1.0 %collective-permute-done.9.refs_1_ = f32[32,2560]{1,0:T(8,128)S(1)} collective-permute-done((f32[32,2560]{1,0:T(8,128)S(1)}, f32[32,2560]{1,0:T(8,128)S(1)}, u32[]{:S(2)}, u32[]{:S(2)}) %collective-permute-start.9) | collective-permute-done | bytes 327712 | tf_op jit(solution)/shard_map/ppermute | solution.py:97
  47.0 3.2 %shard_map.102 = (f32[32,1792]{1,0:T(8,128)S(1)}, f32[32,1792]{1,0:T(8,128)S(1)}, f32[64,64]{1,0:T(8,128)S(1)}, bf16[192,2560]{1,0:T(8,128)(2,1)S(1)}) custom-call(f32[32,2560]{1,0:T(8,128)S(1)} %shard_map.101.refs_0_, f32[32,2560]{1,0:T(8,128)S(1)} %collective-permute-done.9.refs_1_, bf16[2560,1792]{1,0:T(8,128)(2,1)S(1)} %get-tuple-element.45.refs_2_.refs_3_), custom_call_target="tpu_custom_call" | custom-call | flops 4600000000 | bytes 1024 | tf_op jit(solution)/shard_map/pallas_call | solution.py:154
  50.7 1.6 %collective-permute-start.12 = (f32[32,2560]{1,0:T(8,128)S(1)}, f32[32,2560]{1,0:T(8,128)S(1)}, u32[]{:S(2)}, u32[]{:S(2)}) collective-permute-start(f32[32,2560]{1,0:T(8,128)S(1)} %get-tuple-element.52.refs_0_), channel_id=1, source_target_pairs={{0,2},{1,5},{2,0},{3,7},{4,6},{5,1},{6,4},{7,3},{8,10},{9,13},{10,... | collective-permute-start | bytes 983048 | tf_op jit(solution)/shard_map/ppermute | solution.py:97
  52.8 3.5 %collective-permute-start.11 = (f32[64,64]{1,0:T(8,128)S(1)}, f32[64,64]{1,0:T(8,128)S(1)}, u32[]{:S(2)}, u32[]{:S(2)}) collective-permute-start(f32[64,64]{1,0:T(8,128)S(1)} %get-tuple-element.46.refs_3_.refs_2_), channel_id=1, source_target_pairs={{0,8},{1,9},{2,10},{3,11},{4,12},{5,13},{6,14},{7,15},{8,0},{9,1},... | collective-permute-start | bytes 49160 | tf_op jit(solution)/shard_map/ppermute | solution.py:97
  56.3 1.9 %collective-permute-done.10.refs_1_ = f32[32,128]{1,0:T(8,128)S(1)} collective-permute-done((f32[32,128]{1,0:T(8,128)S(1)}, f32[32,128]{1,0:T(8,128)S(1)}, u32[]{:S(2)}, u32[]{:S(2)}) %collective-permute-start.10) | collective-permute-done | bytes 16416 | tf_op jit(solution)/shard_map/ppermute | solution.py:97
  58.4 1.0 %collective-permute-done.13.refs_1_ = f32[32,1792]{1,0:T(8,128)S(1)} collective-permute-done((f32[32,1792]{1,0:T(8,128)S(1)}, f32[32,1792]{1,0:T(8,128)S(1)}, u32[]{:S(2)}, u32[]{:S(2)}) %collective-permute-start.13) | collective-permute-done | bytes 229408 | tf_op jit(solution)/shard_map/ppermute | solution.py:97
  59.5 2.3 %collective-permute-start.14 = (f32[32,1792]{1,0:T(8,128)S(1)}, f32[32,1792]{1,0:T(8,128)S(1)}, u32[]{:S(2)}, u32[]{:S(2)}) collective-permute-start(f32[32,1792]{1,0:T(8,128)S(1)} %shard_map.105.refs_2_.refs_0_), channel_id=1, source_target_pairs={{0,8},{1,9},{2,10},{3,11},{4,12},{5,13},{6,14},{7,15},{8,0},{9,1},... | collective-permute-start | bytes 688136 | tf_op jit(solution)/shard_map/ppermute | solution.py:97
  61.8 1.8 %collective-permute-start.15 = (f32[32,2560]{1,0:T(8,128)S(1)}, f32[32,2560]{1,0:T(8,128)S(1)}, u32[]{:S(2)}, u32[]{:S(2)}) collective-permute-start(f32[32,2560]{1,0:T(8,128)S(1)} %shard_map.106.refs_4_.refs_0_), channel_id=1, source_target_pairs={{0,4},{1,3},{2,6},{3,1},{4,0},{5,7},{6,2},{7,5},{8,12},{9,11},{10,... | collective-permute-start | bytes 983048 | tf_op jit(solution)/shard_map/ppermute | solution.py:97
  63.6 3.9 %shard_map.107 = (bf16[256,1792]{1,0:T(8,128)(2,1)S(1)}, bf16[2560,256]{1,0:T(8,128)(2,1)S(1)}) custom-call(f32[64,64]{1,0:T(8,128)S(1)} %get-tuple-element.48.refs_0_, bf16[192,1792]{1,0:T(8,128)(2,1)S(1)} %get-tuple-element.49.refs_1_, f32[64,64]{1,0:T(8,128)S(1)} %get-tuple-element.50.refs_2_, bf16[192,2560]{1,0:T(8,128)(2,1)S(1)} %get-tuple-element.51.refs_3_, ...), custom_call_target="tpu_custom_call" | custom-call | flops 5750000128 | bytes 1024 | tf_op jit(solution)/shard_map/pallas_call | solution.py:154
  67.5 3.8 %collective-permute-done.15.refs_1_ = f32[32,2560]{1,0:T(8,128)S(1)} collective-permute-done((f32[32,2560]{1,0:T(8,128)S(1)}, f32[32,2560]{1,0:T(8,128)S(1)}, u32[]{:S(2)}, u32[]{:S(2)}) %collective-permute-start.15) | collective-permute-done | bytes 327712 | tf_op jit(solution)/shard_map/ppermute | solution.py:97
  71.9 1.7 %collective-permute-done.14.refs_1_ = f32[32,1792]{1,0:T(8,128)S(1)} collective-permute-done((f32[32,1792]{1,0:T(8,128)S(1)}, f32[32,1792]{1,0:T(8,128)S(1)}, u32[]{:S(2)}, u32[]{:S(2)}) %collective-permute-start.14) | collective-permute-done | bytes 229408 | tf_op jit(solution)/shard_map/ppermute | solution.py:97
  74.5 6.2 %shard_map.110 = (bf16[2560,1792]{1,0:T(8,128)(2,1)}, bf16[1280,1792]{1,0:T(8,128)(2,1)}, bf16[2560,256]{1,0:T(8,128)(2,1)S(1)}) custom-call(bf16[256,1792]{1,0:T(8,128)(2,1)S(1)} %get-tuple-element.56.refs_2_.refs_0_, f32[32,1280]{1,0:T(8,128)S(1)} %get-tuple-element.57.refs_2_.refs_1_, f32[32,1280]{1,0:T(8,128)S(1)} %get-tuple-element.58.refs_2_, ...), custom_call_target="tpu_custom_call" | custom-call | flops 9200000000 | bytes 1024 | tf_op jit(solution)/shard_map/pallas_call | solution.py:154
  81.3 6.7 %shard_map.111 = (bf16[2560,1792]{1,0:T(8,128)(2,1)}, bf16[1280,1792]{1,0:T(8,128)(2,1)}, bf16[16,128]{1,0:T(8,128)(2,1)}) custom-call(bf16[2560,256]{1,0:T(8,128)(2,1)S(1)} %get-tuple-element.55.refs_0_, f32[32,1792]{1,0:T(8,128)S(1)} %shard_map.109.refs_6_.refs_1_, f32[32,1792]{1,0:T(8,128)S(1)} %collective-permute-done.16.refs_2_, ...), custom_call_target="tpu_custom_call" | custom-call | flops 9200000000 | bytes 1024 | tf_op jit(solution)/shard_map/pallas_call | solution.py:154
  (35 shorter events, 6.9 us)
Async XLA Ops:
  0.6 12.8 %copy-start = (bf16[64,1792]{1,0:T(8,128)(2,1)S(1)}, bf16[64,1792]{1,0:T(8,128)(2,1)}, u32[]{:S(2)}) copy-start(bf16[64,1792]{1,0:T(8,128)(2,1)} %refs_2_.5) | copy-start | bytes 688132
  10.4 8.6 %collective-permute-start = (f32[32,1792]{1,0:T(8,128)S(1)}, f32[32,1792]{1,0:T(8,128)S(1)}, u32[]{:S(2)}, u32[]{:S(2)}) collective-permute-start(f32[32,1792]{1,0:T(8,128)S(1)} %get-tuple-element.35), channel_id=1, source_target_pairs={{0,4},{1,5},{2,6},{3,7},{4,0},{5,1},{6,2},{7,3},{8,12},{9,13},{10,... | collective-permute-start | bytes 688136 | tf_op jit(solution)/shard_map/ppermute | solution.py:97
  19.1 12.8 %collective-permute-start.1 = (f32[32,1792]{1,0:T(8,128)S(1)}, f32[32,1792]{1,0:T(8,128)S(1)}, u32[]{:S(2)}, u32[]{:S(2)}) collective-permute-start(f32[32,1792]{1,0:T(8,128)S(1)} %shard_map.95.refs_5_.refs_0_), channel_id=1, source_target_pairs={{0,8},{1,9},{2,10},{3,11},{4,12},{5,13},{6,14},{7,15},{8,0},{9,1},... | collective-permute-start | bytes 688136 | tf_op jit(solution)/shard_map/ppermute | solution.py:97
  25.9 1.5 %collective-permute-start.2 = (f32[32,1280]{1,0:T(8,128)S(1)}, f32[32,1280]{1,0:T(8,128)S(1)}, u32[]{:S(2)}, u32[]{:S(2)}) collective-permute-start(f32[32,1280]{1,0:T(8,128)S(1)} %get-tuple-element.39), channel_id=1, source_target_pairs={{0,1},{1,0},{2,3},{3,2},{4,5},{5,4},{6,7},{7,6},{8,9},{9,8},{10,11... | collective-permute-start | bytes 491528 | tf_op jit(solution)/shard_map/ppermute | solution.py:97
  25.9 1.6 %collective-permute-start.3 = (f32[32,1280]{1,0:T(8,128)S(1)}, f32[32,1280]{1,0:T(8,128)S(1)}, u32[]{:S(2)}, u32[]{:S(2)}) collective-permute-start(f32[32,1280]{1,0:T(8,128)S(1)} %get-tuple-element.40), channel_id=1, source_target_pairs={{0,1},{1,0},{2,3},{3,2},{4,5},{5,4},{6,7},{7,6},{8,9},{9,8},{10,11... | collective-permute-start | bytes 491528 | tf_op jit(solution)/shard_map/ppermute | solution.py:97
  27.6 7.1 %collective-permute-start.5 = (f32[32,2560]{1,0:T(8,128)S(1)}, f32[32,2560]{1,0:T(8,128)S(1)}, u32[]{:S(2)}, u32[]{:S(2)}) collective-permute-start(f32[32,2560]{1,0:T(8,128)S(1)} %shard_map.97.refs_2_.refs_0_), channel_id=1, source_target_pairs={{0,2},{1,5},{2,0},{3,7},{4,6},{5,1},{6,4},{7,3},{8,10},{9,13},{10,... | collective-permute-start | bytes 983048 | tf_op jit(solution)/shard_map/ppermute | solution.py:97
  31.9 8.3 %collective-permute-start.4 = (f32[32,1792]{1,0:T(8,128)S(1)}, f32[32,1792]{1,0:T(8,128)S(1)}, u32[]{:S(2)}, u32[]{:S(2)}) collective-permute-start(f32[32,1792]{1,0:T(8,128)S(1)} %shard_map.98.refs_2_.refs_0_), channel_id=1, source_target_pairs={{0,4},{1,5},{2,6},{3,7},{4,0},{5,1},{6,2},{7,3},{8,12},{9,13},{10,... | collective-permute-start | bytes 688136 | tf_op jit(solution)/shard_map/ppermute | solution.py:97
  34.8 10.5 %collective-permute-start.8 = (f32[32,2560]{1,0:T(8,128)S(1)}, f32[32,2560]{1,0:T(8,128)S(1)}, u32[]{:S(2)}, u32[]{:S(2)}) collective-permute-start(f32[32,2560]{1,0:T(8,128)S(1)} %shard_map.99.refs_3_.refs_0_), channel_id=1, source_target_pairs={{0,4},{1,3},{2,6},{3,1},{4,0},{5,7},{6,2},{7,5},{8,12},{9,11},{10,... | collective-permute-start | bytes 983048 | tf_op jit(solution)/shard_map/ppermute | solution.py:97
  45.3 1.7 %collective-permute-start.9 = (f32[32,2560]{1,0:T(8,128)S(1)}, f32[32,2560]{1,0:T(8,128)S(1)}, u32[]{:S(2)}, u32[]{:S(2)}) collective-permute-start(f32[32,2560]{1,0:T(8,128)S(1)} %shard_map.101.refs_0_), channel_id=1, source_target_pairs={{0,1},{1,0},{2,3},{3,2},{4,5},{5,4},{6,7},{7,6},{8,9},{9,8},{10,11... | collective-permute-start | bytes 983048 | tf_op jit(solution)/shard_map/ppermute | solution.py:97
  45.4 5.3 %collective-permute-start.6 = (f32[32,1280]{1,0:T(8,128)S(1)}, f32[32,1280]{1,0:T(8,128)S(1)}, u32[]{:S(2)}, u32[]{:S(2)}) collective-permute-start(f32[32,1280]{1,0:T(8,128)S(1)} %get-tuple-element.43), channel_id=1, source_target_pairs={{0,1},{1,0},{2,3},{3,2},{4,5},{5,4},{6,7},{7,6},{8,9},{9,8},{10,11... | collective-permute-start | bytes 491528 | tf_op jit(solution)/shard_map/ppermute | solution.py:97
  45.9 4.8 %collective-permute-start.7 = (f32[32,1408]{1,0:T(8,128)S(1)}, f32[32,1408]{1,0:T(8,128)S(1)}, u32[]{:S(2)}, u32[]{:S(2)}) collective-permute-start(f32[32,1408]{1,0:T(8,128)S(1)} %get-tuple-element.44), channel_id=1, source_target_pairs={{0,1},{1,0},{2,3},{3,2},{4,5},{5,4},{6,7},{7,6},{8,9},{9,8},{10,11... | collective-permute-start | bytes 540680 | tf_op jit(solution)/shard_map/ppermute | solution.py:97
  50.2 9.2 %collective-permute-start.13 = (f32[32,1792]{1,0:T(8,128)S(1)}, f32[32,1792]{1,0:T(8,128)S(1)}, u32[]{:S(2)}, u32[]{:S(2)}) collective-permute-start(f32[32,1792]{1,0:T(8,128)S(1)} %get-tuple-element.54), channel_id=1, source_target_pairs={{0,4},{1,5},{2,6},{3,7},{4,0},{5,1},{6,2},{7,3},{8,12},{9,13},{10,... | collective-permute-start | bytes 688136 | tf_op jit(solution)/shard_map/ppermute | solution.py:97
  50.7 11.0 %collective-permute-start.12 = (f32[32,2560]{1,0:T(8,128)S(1)}, f32[32,2560]{1,0:T(8,128)S(1)}, u32[]{:S(2)}, u32[]{:S(2)}) collective-permute-start(f32[32,2560]{1,0:T(8,128)S(1)} %get-tuple-element.52.refs_0_), channel_id=1, source_target_pairs={{0,2},{1,5},{2,0},{3,7},{4,6},{5,1},{6,4},{7,3},{8,10},{9,13},{10,... | collective-permute-start | bytes 983048 | tf_op jit(solution)/shard_map/ppermute | solution.py:97
  52.3 5.9 %collective-permute-start.10 = (f32[32,128]{1,0:T(8,128)S(1)}, f32[32,128]{1,0:T(8,128)S(1)}, u32[]{:S(2)}, u32[]{:S(2)}) collective-permute-start(f32[32,128]{1,0:T(8,128)S(1)} %get-tuple-element.47.refs_0_), channel_id=1, source_target_pairs={{0,2},{1,3},{2,0},{3,1},{4,6},{5,7},{6,4},{7,5},{8,10},{9,11},{10,... | collective-permute-start | bytes 49160 | tf_op jit(solution)/shard_map/ppermute | solution.py:97
  52.8 5.5 %collective-permute-start.11 = (f32[64,64]{1,0:T(8,128)S(1)}, f32[64,64]{1,0:T(8,128)S(1)}, u32[]{:S(2)}, u32[]{:S(2)}) collective-permute-start(f32[64,64]{1,0:T(8,128)S(1)} %get-tuple-element.46.refs_3_.refs_2_), channel_id=1, source_target_pairs={{0,8},{1,9},{2,10},{3,11},{4,12},{5,13},{6,14},{7,15},{8,0},{9,1},... | collective-permute-start | bytes 49160 | tf_op jit(solution)/shard_map/ppermute | solution.py:97
  59.5 14.1 %collective-permute-start.14 = (f32[32,1792]{1,0:T(8,128)S(1)}, f32[32,1792]{1,0:T(8,128)S(1)}, u32[]{:S(2)}, u32[]{:S(2)}) collective-permute-start(f32[32,1792]{1,0:T(8,128)S(1)} %shard_map.105.refs_2_.refs_0_), channel_id=1, source_target_pairs={{0,8},{1,9},{2,10},{3,11},{4,12},{5,13},{6,14},{7,15},{8,0},{9,1},... | collective-permute-start | bytes 688136 | tf_op jit(solution)/shard_map/ppermute | solution.py:97
  61.8 9.5 %collective-permute-start.15 = (f32[32,2560]{1,0:T(8,128)S(1)}, f32[32,2560]{1,0:T(8,128)S(1)}, u32[]{:S(2)}, u32[]{:S(2)}) collective-permute-start(f32[32,2560]{1,0:T(8,128)S(1)} %shard_map.106.refs_4_.refs_0_), channel_id=1, source_target_pairs={{0,4},{1,3},{2,6},{3,1},{4,0},{5,7},{6,2},{7,5},{8,12},{9,11},{10,... | collective-permute-start | bytes 983048 | tf_op jit(solution)/shard_map/ppermute | solution.py:97
  71.3 3.2 %collective-permute-start.18 = (f32[32,1280]{1,0:T(8,128)S(1)}, f32[32,1280]{1,0:T(8,128)S(1)}, u32[]{:S(2)}, u32[]{:S(2)}) collective-permute-start(f32[32,1280]{1,0:T(8,128)S(1)} %get-tuple-element.58.refs_2_), channel_id=1, source_target_pairs={{0,1},{1,0},{2,3},{3,2},{4,5},{5,4},{6,7},{7,6},{8,9},{9,8},{10,11... | collective-permute-start | bytes 491528 | tf_op jit(solution)/shard_map/ppermute | solution.py:97
  71.4 3.1 %collective-permute-start.17 = (f32[32,1280]{1,0:T(8,128)S(1)}, f32[32,1280]{1,0:T(8,128)S(1)}, u32[]{:S(2)}, u32[]{:S(2)}) collective-permute-start(f32[32,1280]{1,0:T(8,128)S(1)} %get-tuple-element.57.refs_2_.refs_1_), channel_id=1, source_target_pairs={{0,1},{1,0},{2,3},{3,2},{4,5},{5,4},{6,7},{7,6},{8,9},{9,8},{10,11... | collective-permute-start | bytes 491528 | tf_op jit(solution)/shard_map/ppermute | solution.py:97
  73.6 7.7 %collective-permute-start.16 = (f32[32,1792]{1,0:T(8,128)S(1)}, f32[32,1792]{1,0:T(8,128)S(1)}, u32[]{:S(2)}, u32[]{:S(2)}) collective-permute-start(f32[32,1792]{1,0:T(8,128)S(1)} %shard_map.109.refs_6_.refs_1_), channel_id=1, source_target_pairs={{0,4},{1,5},{2,6},{3,7},{4,0},{5,1},{6,2},{7,3},{8,12},{9,13},{10,... | collective-permute-start | bytes 688136 | tf_op jit(solution)/shard_map/ppermute | solution.py:97

commit v14 on v13

--- a/solution.py
+++ b/solution.py
@@ -11,7 +11,7 @@
 RANK = 64
 TILE = 256
 FLOPS = 1.15e9
-WEIGHTS = (8.0, 4.0, 1.0, 4.0, 0.1, 5.0, 1.0, 5.0, 1.0, 4.0, 1.0, 0.1, 1.0, 0.1, 5.0, 1.0, 1.0, 8.0, 8.0)
+WEIGHTS = (8.0, 4.0, 1.0, 4.0, 0.1, 5.0, 1.0, 5.0, 1.0, 1.0, 4.0, 1.0, 1.0, 1.0, 0.1, 5.0, 0.1, 1.0, 8.0, 8.0)
 MIB = 1 << 20
 BF16 = jnp.bfloat16
 F32 = jnp.float32
@@ -83,6 +83,10 @@
     return lax.rem(lax.axis_index("tensor"), 2)
 
 
+def pair_of():
+    return lax.rem(lax.div(lax.axis_index("tensor"), 2), 2)
+
+
 def replica_of():
     return lax.rem(lax.axis_index("dp"), REPLICAS)
 
@@ -125,6 +129,10 @@
 
 def other_replica(d, t):
     return d ^ 1, t
+
+
+def other_pair(d, t):
+    return d, t ^ 2
 
 
 def to_other_core(pieces):
@@ -198,8 +206,34 @@
         for (i, i0, i1), (j, j0, j1), (k, k0, k1) in spans(widths_of(x), widths_of(y), widths):
             out[k][:, k0:k1] = x[i][:, i0:i1] + y[j][:, j0:j1]
 
-    outs = [((HALF, n), F32, VMEM) for n in widths]
+    outs = [((xs[0].shape[0], n), F32, VMEM) for n in widths]
     return list(run(kernel, [(x, VMEM) for x in (*xs, *ys)], outs, mib=2, after=after))
+
+
+def add_halved(run, xs, ys, width, place_of, after=()):
+    rest = sum(widths_of(xs)) - width
+    n_x, n_y = len(xs), len(ys)
+    high = xs[0].shape[0] // 2
+
+    def kernel(*refs):
+        x, y = refs[:n_x], refs[n_x : n_x + n_y]
+        keep, give, left_over, total = refs[n_x + n_y :]
+        for (i, i0, i1), (j, j0, j1), (k, k0, k1) in spans(widths_of(x), widths_of(y), [width, rest]):
+            (total, left_over)[k][:, k0:k1] = x[i][:, i0:i1] + y[j][:, j0:j1]
+        place = place_of()
+        keep[...] = total[pl.ds(pl.multiple_of(place * high, high), high), :]
+        give[...] = total[pl.ds(pl.multiple_of((1 - place) * high, high), high), :]
+
+    outs = [((high, width), F32, VMEM)] * 2 + [((2 * high, rest), F32, VMEM)]
+    scratch = [pltpu.VMEM((2 * high, width), F32)]
+    return run(kernel, [(x, VMEM) for x in (*xs, *ys)], outs, scratch, mib=3, after=after)
+
+
+def pass_on(run, x, after):
+    def kernel(x, out):
+        out[...] = x[...]
+
+    return run(kernel, [(x, VMEM)], [(x.shape, F32, VMEM)], mib=2, after=after)[0]
 
 
 def in_two(width):
@@ -436,6 +470,12 @@
     return run(kernel, [(x, VMEM) for x in (*packed, *whole)], outs, mib=2, after=after)
 
 
+def swapped(a, size, place):
+    groups = [a[i : i + size] for i in range(0, RANK, size)]
+    other = jnp.concatenate([groups[i ^ 1] for i in range(len(groups))], axis=0)
+    return jnp.where(place == 0, a, other)
+
+
 def solve(run, gram_down, left_down, gram_gate, left_gate, after=()):
     cols, rows = left_down.shape[1], left_gate.shape[1]
 
@@ -444,8 +484,9 @@
         for place, a, left, out in zip(
             (core_of(), replica_of()), inverses(grams), (left_down, left_gate), (col, row)
         ):
-            other = jnp.concatenate([a[HALF:], a[:HALF]], axis=0)
-            a = jnp.where(place == 0, a, other) * (1.0 / REPLICAS)
+            a = swapped(a, HALF, place) * (1.0 / REPLICAS)
+            if out is col:
+                a = swapped(a, HALF // 2, pair_of())
             hi, lo = parts_of(a)
             both = jnp.concatenate([hi, hi, lo], axis=1)
             out[...] = jnp.dot(both, left[...], preferred_element_type=F32)
@@ -472,10 +513,10 @@
     share = rows // REPLICAS
     parts = share // height
     rows_late = ready[0] is None
-    late_width = sum(widths_of(owns))
+    late_width = rows if rows_late else sum(widths_of(owns))
     width = ready[1].shape[1] if rows_late or not owns else late_width
     n_ready = sum(x is not None for x in ready)
-    n_own, n_late = len(owns), len(owns) + len(others)
+    n_late = len(owns) + len(others)
     n_before = 0 if before is None else len(before)
     with_update = 0 in shares
     spots = [(s, t, j) for s in shares for t in range(parts) for j in range(0, width, TILE)]
@@ -488,14 +529,15 @@
         errors, updates, stack, error_sems, update_sems = refs[3:]
         if late:
             order = ROW_ORDER if rows_late else COL_ORDER
-            for at, pieces in ((0, late[:n_own]), (HALF, late[n_own:])):
-                left = 0
-                for ref in pieces:
-                    split = parts_of(ref[...])
-                    n, w = ref.shape
-                    for k, which in enumerate(order):
-                        stack[k * RANK + at : k * RANK + at + n, left : left + w] = split[which]
-                    left += w
+            at = left = 0
+            for ref in late:
+                split = parts_of(ref[...])
+                n, w = ref.shape
+                for k, which in enumerate(order):
+                    stack[k * RANK + at : k * RANK + at + n, left : left + w] = split[which]
+                left += w
+                if left == late_width:
+                    at, left = at + n, 0
         if rows_late:
             turn(stack, turned)
             row, col = turned, given[0]
@@ -580,29 +622,34 @@
     gots = to_other_core(gives)
     gates = add(run, [gate], [got_gate], after=(keep,))
     others_gate = to_other_core(gates)
-    keep_gate, give_gate, gram_gate, left_gate = gate_right(run, gates, others_gate, fixed_gate)
+    keep, give, gram_down = add_halved(run, [keep], gots, slab, pair_of, after=(gates[0],))
+    got = exchange(give, other_pair)
+    grams_down = [gram_down] + [
+        exchange(gram_down, lambda d, t, b=b: (d, t ^ b)) for b in range(2, n_t, 2)
+    ]
+    keep_gate, give_gate, gram_gate, left_gate = gate_right(
+        run, gates, others_gate, fixed_gate, after=(keep,)
+    )
     got_gate = exchange(give_gate, other_replica)
     grams_gate = [gram_gate] + [
         exchange(gram_gate, lambda d, t, b=b: (d ^ b, t)) for b in range(REPLICAS, n_dp, REPLICAS)
     ]
-    down, gram_down = add(run, [keep], gots, [slab, 2 * RANK], after=(gram_gate,))
-    grams_down = [gram_down] + [
-        exchange(gram_down, lambda d, t, b=b: (d, t ^ b)) for b in range(2, n_t, 2)
-    ]
-    got = exchange(down, hops[0])
-    gram_down, gram_gate = gram_sums(run, grams_down, grams_gate)
+    (down,) = add(run, [keep], [got], after=(gram_gate,))
+    for b in bits(n_t, 4):
+        (down,) = add(run, [down], [exchange(down, lambda d, t, b=b: (d, t ^ b))])
+    got = exchange(down, other_replica)
+    gram_down, gram_gate = gram_sums(run, grams_down, grams_gate, after=(down,))
     (gate,) = add(run, [keep_gate], [got_gate], after=(gram_gate,))
     got_gate = exchange(gate, steps[0])
-    for hop in hops[1:]:
-        (down,) = add(run, [down], [got], after=(gate,))
-        got = exchange(down, hop)
+    (down,) = add(run, [down], [got], after=(gate,))
+    down_pair = exchange(down, other_pair)
     col_stack, row_turned = solve(
         run, gram_down, left_down, gram_gate, left_gate, after=(down,)
     )
-    downs = add(run, [down], [got], in_two(slab), after=(col_stack,))
+    downs = [down, pass_on(run, down_pair, after=(col_stack,))]
     others_down = to_other_core(downs)
     for i in range(len(steps)):
-        (gate,) = add(run, [gate], [got_gate], after=(downs[0],))
+        (gate,) = add(run, [gate], [got_gate], after=(col_stack, others_down[1]))
         if i + 1 < len(steps):
             got_gate = exchange(gate, steps[i + 1])
     other_gate = exchange(gate, other_replica)
@@ -624,7 +671,7 @@
         groups = mesh.shape["mix"] * mesh.shape["dp"]
         slab = grad_gate.shape[0] // groups
         width = grad_gate.shape[1] // mesh.shape["tensor"]
-        fits = slab % (REPLICAS * TILE) == 0 and width % TILE == 0
+        fits = slab % (REPLICAS * TILE) == 0 and width % TILE == 0 and mesh.shape["tensor"] % 4 == 0
         body = local if fits else local_plain
         return jax.shard_map(
             body, mesh=mesh, in_specs=in_specs, out_specs=out_specs, check_vma=False

time: 88.4 us -> 88.3 us (level)
  starting transfers between devices: 22.3 us -> 20.1 us
  waiting for transfers between devices: 20.6 us -> 22.6 us
    ppermute x19 -> x20, starting transfers between devices: 22.3 us -> 20.1 us  [exchange(): return lax.ppermute(x, ('dp', 'tensor'), pairs)]
    ppermute x19 -> x20, waiting for transfers between devices: 20.6 us -> 22.6 us  [exchange(): return lax.ppermute(x, ('dp', 'tensor'), pairs)]
    pallas_call x19 -> x20, Pallas kernels: 44.3 us -> 44.4 us  [__call__(): pl.pallas_call(body, out_shape=tuple(((pltpu.VMEM if spec is VMEM else pl...]
  transfers between devices with their start and end apart: 19 -> 20, of which waited for: 13 -> 15; matrix products, arithmetic and copies ran while one was open for 0% -> 0% of each run, Pallas kernels for 32% -> 32%
where the time goes in v14:
time: 88.3 us; the launch traced here: 88.1 us
  Pallas kernels  44.4 us (50%)
  waiting for transfers between devices  22.6 us (26%)
  starting transfers between devices  20.1 us (23%)
  between operations  0.95 us (1%)
    pallas_call x20, Pallas kernels, __call__(): pl.pallas_call(body, out_shape=tuple(((pltpu.VMEM if spec is VMEM else pl...  44.4 us
    ppermute x20, waiting for transfers between devices, exchange(): return lax.ppermute(x, ('dp', 'tensor'), pairs)  22.6 us
    ppermute x20, starting transfers between devices, exchange(): return lax.ppermute(x, ('dp', 'tensor'), pairs)  20.1 us
  transfers between devices with their start and end apart: 20, of which 15 were waited for; matrix products, arithmetic and copies ran while one was open for 0% of the time, Pallas kernels for 32%

profile of v14, /device:TPU:0, one launch (start us, length us, event | category | flops | bytes accessed | tf_op | source)
XLA Modules:
  0.0 88.1 jit_solution(16644981284979868832)
XLA Ops:
  0.6 9.8 %shard_map.93 = (f32[64,1792]{1,0:T(8,128)}, bf16[2560,1792]{1,0:T(8,128)(2,1)S(1)}, f32[32,1792]{1,0:T(8,128)S(1)}, f32[32,1792]{1,0:T(8,128)S(1)}) custom-call(bf16[2560,1792]{1,0:T(8,128)(2,1)} %refs_0_.3, bf16[2560,1792]{1,0:T(8,128)(2,1)} %refs_1_.3, bf16[64,5120]{1,0:T(8,128)(2,1)} %refs_2_.3), custom_call_target="tpu_custom_call" | custom-call | flops 9200000000 | bytes 1024 | tf_op jit(solution)/shard_map/pallas_call | solution.py:162
  10.4 3.0 %collective-permute-start = (f32[32,1792]{1,0:T(8,128)S(1)}, f32[32,1792]{1,0:T(8,128)S(1)}, u32[]{:S(2)}, u32[]{:S(2)}) collective-permute-start(f32[32,1792]{1,0:T(8,128)S(1)} %get-tuple-element.34), channel_id=1, source_target_pairs={{0,4},{1,5},{2,6},{3,7},{4,0},{5,1},{6,2},{7,3},{8,12},{9,13},{10,... | collective-permute-start | bytes 688136 | tf_op jit(solution)/shard_map/ppermute | solution.py:101
  13.4 5.1 %shard_map.94 = (f32[64,2560]{1,0:T(8,128)S(1)}, bf16[2560,1792]{1,0:T(8,128)(2,1)S(1)}) custom-call(bf16[2560,1792]{1,0:T(8,128)(2,1)} %refs_0_.5, bf16[2560,1792]{1,0:T(8,128)(2,1)} %refs_1_.5, bf16[64,1792]{1,0:T(8,128)(2,1)S(1)} %copy-done, f32[32,1792]{1,0:T(8,128)S(1)} %get-tuple-element.33.refs_3_.refs_0_), custom_call_target="tpu_custom_call" | custom-call | flops 4600000000 | bytes 1024 | tf_op jit(solution)/shard_map/pallas_call | solution.py:162
  19.1 2.8 %collective-permute-start.1 = (f32[32,1792]{1,0:T(8,128)S(1)}, f32[32,1792]{1,0:T(8,128)S(1)}, u32[]{:S(2)}, u32[]{:S(2)}) collective-permute-start(f32[32,1792]{1,0:T(8,128)S(1)} %shard_map.95.refs_5_.refs_0_), channel_id=1, source_target_pairs={{0,8},{1,9},{2,10},{3,11},{4,12},{5,13},{6,14},{7,15},{8,0},{9,1},... | collective-permute-start | bytes 688136 | tf_op jit(solution)/shard_map/ppermute | solution.py:101
  21.9 4.0 %shard_map.96 = (f32[64,2560]{1,0:T(8,128)S(1)}, bf16[2560,1792]{1,0:T(8,128)(2,1)S(1)}, f32[32,2560]{1,0:T(8,128)S(1)}, f32[32,1280]{1,0:T(8,128)S(1)}, f32[32,1280]{1,0:T(8,128)S(1)}) custom-call(bf16[2560,1792]{1,0:T(8,128)(2,1)} %refs_0_.5, bf16[2560,1792]{1,0:T(8,128)(2,1)} %refs_1_.5, ...), custom_call_target="tpu_custom_call", output_to_operand_aliasing={{0}: (3, {}), {1}: (4, {})} | custom-call | flops 4600000000 | bytes 1024 | tf_op jit(solution)/shard_map/pallas_call | solution.py:162
  26.4 0.9 %collective-permute-done.2.refs_1_ = f32[32,1280]{1,0:T(8,128)S(1)} collective-permute-done((f32[32,1280]{1,0:T(8,128)S(1)}, f32[32,1280]{1,0:T(8,128)S(1)}, u32[]{:S(2)}, u32[]{:S(2)}) %collective-permute-start.2) | collective-permute-done | bytes 163872 | tf_op jit(solution)/shard_map/ppermute | solution.py:101
  27.6 1.6 %collective-permute-start.5 = (f32[32,2560]{1,0:T(8,128)S(1)}, f32[32,2560]{1,0:T(8,128)S(1)}, u32[]{:S(2)}, u32[]{:S(2)}) collective-permute-start(f32[32,2560]{1,0:T(8,128)S(1)} %shard_map.97.refs_2_.refs_0_), channel_id=1, source_target_pairs={{0,2},{1,5},{2,0},{3,7},{4,6},{5,1},{6,4},{7,3},{8,10},{9,13},{10,... | collective-permute-start | bytes 983048 | tf_op jit(solution)/shard_map/ppermute | solution.py:101
  29.2 2.7 %collective-permute-done.1.refs_1_ = f32[32,1792]{1,0:T(8,128)S(1)} collective-permute-done((f32[32,1792]{1,0:T(8,128)S(1)}, f32[32,1792]{1,0:T(8,128)S(1)}, u32[]{:S(2)}, u32[]{:S(2)}) %collective-permute-start.1) | collective-permute-done | bytes 229408 | tf_op jit(solution)/shard_map/ppermute | solution.py:101
  32.4 2.3 %collective-permute-done.5.refs_1_ = f32[32,2560]{1,0:T(8,128)S(1)} collective-permute-done((f32[32,2560]{1,0:T(8,128)S(1)}, f32[32,2560]{1,0:T(8,128)S(1)}, u32[]{:S(2)}, u32[]{:S(2)}) %collective-permute-start.5) | collective-permute-done | bytes 327712 | tf_op jit(solution)/shard_map/ppermute | solution.py:101
  34.8 1.6 %collective-permute-start.8 = (f32[32,2560]{1,0:T(8,128)S(1)}, f32[32,2560]{1,0:T(8,128)S(1)}, u32[]{:S(2)}, u32[]{:S(2)}) collective-permute-start(f32[32,2560]{1,0:T(8,128)S(1)} %shard_map.99.refs_3_.refs_0_), channel_id=1, source_target_pairs={{0,4},{1,3},{2,6},{3,1},{4,0},{5,7},{6,2},{7,5},{8,12},{9,11},{10,... | collective-permute-start | bytes 983048 | tf_op jit(solution)/shard_map/ppermute | solution.py:101
  36.4 3.7 %collective-permute-done.4.refs_1_ = f32[32,1792]{1,0:T(8,128)S(1)} collective-permute-done((f32[32,1792]{1,0:T(8,128)S(1)}, f32[32,1792]{1,0:T(8,128)S(1)}, u32[]{:S(2)}, u32[]{:S(2)}) %collective-permute-start.4) | collective-permute-done | bytes 229408 | tf_op jit(solution)/shard_map/ppermute | solution.py:101
  40.2 5.1 %shard_map.100 = (f32[32,2688]{1,0:T(8,128)S(1)}, f32[32,1280]{1,0:T(8,128)S(1)}, f32[32,1408]{1,0:T(8,128)S(1)}, bf16[192,1792]{1,0:T(8,128)(2,1)S(1)}) custom-call(f32[32,1792]{1,0:T(8,128)S(1)} %shard_map.98.refs_2_.refs_0_, f32[32,1792]{1,0:T(8,128)S(1)} %collective-permute-done.4.refs_1_, bf16[2560,1792]{1,0:T(8,128)(2,1)S(1)} %get-tuple-element.40.refs_2_.refs_5_, ...), custom_call_target="tpu_custom_call" | custom-call | flops 5750000128 | bytes 1024 | tf_op jit(solution)/shard_map/pallas_call | solution.py:162
  46.0 1.5 %collective-permute-done.6.refs_1_ = f32[32,1280]{1,0:T(8,128)S(1)} collective-permute-done((f32[32,1280]{1,0:T(8,128)S(1)}, f32[32,1280]{1,0:T(8,128)S(1)}, u32[]{:S(2)}, u32[]{:S(2)}) %collective-permute-start.6) | collective-permute-done | bytes 163872 | tf_op jit(solution)/shard_map/ppermute | solution.py:101
  47.6 1.4 %collective-permute-start.12 = (f32[16,2560]{1,0:T(8,128)S(1)}, f32[16,2560]{1,0:T(8,128)S(1)}, u32[]{:S(2)}, u32[]{:S(2)}) collective-permute-start(f32[16,2560]{1,0:T(8,128)S(1)} %get-tuple-element.48), channel_id=1, source_target_pairs={{0,2},{1,3},{2,0},{3,1},{4,6},{5,7},{6,4},{7,5},{8,10},{9,11},{10,... | collective-permute-start | bytes 491528 | tf_op jit(solution)/shard_map/ppermute | solution.py:101
  49.0 3.2 %shard_map.103 = (f32[32,1792]{1,0:T(8,128)S(1)}, f32[32,1792]{1,0:T(8,128)S(1)}, f32[64,64]{1,0:T(8,128)S(1)}, bf16[192,2560]{1,0:T(8,128)(2,1)S(1)}) custom-call(f32[32,2560]{1,0:T(8,128)S(1)} %shard_map.101.refs_3_.refs_0_, f32[32,2560]{1,0:T(8,128)S(1)} %collective-permute-done.10.refs_1_, bf16[2560,1792]{1,0:T(8,128)(2,1)S(1)} %get-tuple-element.45.refs_2_.refs_3_, ...), custom_call_target="tpu_custom_call" | custom-call | flops 4600000000 | bytes 1024 | tf_op jit(solution)/shard_map/pallas_call | solution.py:162
  53.3 3.5 %collective-permute-start.11 = (f32[64,64]{1,0:T(8,128)S(1)}, f32[64,64]{1,0:T(8,128)S(1)}, u32[]{:S(2)}, u32[]{:S(2)}) collective-permute-start(f32[64,64]{1,0:T(8,128)S(1)} %get-tuple-element.47.refs_2_), channel_id=1, source_target_pairs={{0,8},{1,9},{2,10},{3,11},{4,12},{5,13},{6,14},{7,15},{8,0},{9,1},... | collective-permute-start | bytes 49160 | tf_op jit(solution)/shard_map/ppermute | solution.py:101
  57.0 2.5 %collective-permute-done.11.refs_3_ = f32[64,64]{1,0:T(8,128)S(1)} collective-permute-done((f32[64,64]{1,0:T(8,128)S(1)}, f32[64,64]{1,0:T(8,128)S(1)}, u32[]{:S(2)}, u32[]{:S(2)}) %collective-permute-start.11) | collective-permute-done | bytes 16416 | tf_op jit(solution)/shard_map/ppermute | solution.py:101
  59.6 1.9 %collective-permute-done.14.refs_1_ = f32[32,1792]{1,0:T(8,128)S(1)} collective-permute-done((f32[32,1792]{1,0:T(8,128)S(1)}, f32[32,1792]{1,0:T(8,128)S(1)}, u32[]{:S(2)}, u32[]{:S(2)}) %collective-permute-start.14) | collective-permute-done | bytes 229408 | tf_op jit(solution)/shard_map/ppermute | solution.py:101
  61.5 1.6 %collective-permute-start.15 = (f32[32,1792]{1,0:T(8,128)S(1)}, f32[32,1792]{1,0:T(8,128)S(1)}, u32[]{:S(2)}, u32[]{:S(2)}) collective-permute-start(f32[32,1792]{1,0:T(8,128)S(1)} %shard_map.106.refs_2_.refs_0_), channel_id=1, source_target_pairs={{0,8},{1,9},{2,10},{3,11},{4,12},{5,13},{6,14},{7,15},{8,0},{9,1},... | collective-permute-start | bytes 688136 | tf_op jit(solution)/shard_map/ppermute | solution.py:101
  63.1 3.5 %collective-permute-done.13.refs_1_ = f32[16,2560]{1,0:T(8,128)S(1)} collective-permute-done((f32[16,2560]{1,0:T(8,128)S(1)}, f32[16,2560]{1,0:T(8,128)S(1)}, u32[]{:S(2)}, u32[]{:S(2)}) %collective-permute-start.13) | collective-permute-done | bytes 163872 | tf_op jit(solution)/shard_map/ppermute | solution.py:101
  67.5 4.0 %shard_map.108 = (bf16[256,1792]{1,0:T(8,128)(2,1)S(1)}, bf16[2560,256]{1,0:T(8,128)(2,1)S(1)}) custom-call(f32[64,64]{1,0:T(8,128)S(1)} %get-tuple-element.49.refs_0_, bf16[192,1792]{1,0:T(8,128)(2,1)S(1)} %get-tuple-element.50.refs_1_, f32[64,64]{1,0:T(8,128)S(1)} %get-tuple-element.51.refs_2_, bf16[192,2560]{1,0:T(8,128)(2,1)S(1)} %get-tuple-element.52.refs_3_, ...), custom_call_target="tpu_custom_call" | custom-call | flops 5750000128 | bytes 1024 | tf_op jit(solution)/shard_map/pallas_call | solution.py:162
  73.7 6.2 %shard_map.111 = (bf16[2560,1792]{1,0:T(8,128)(2,1)}, bf16[1280,1792]{1,0:T(8,128)(2,1)}, bf16[2560,256]{1,0:T(8,128)(2,1)S(1)}) custom-call(bf16[256,1792]{1,0:T(8,128)(2,1)S(1)} %get-tuple-element.56.refs_1_.refs_2_.refs_0_, f32[16,2560]{1,0:T(8,128)S(1)} %shard_map.107.refs_4_.refs_1_, f32[16,2560]{1,0:T(8,128)S(1)} %shard_map.109.refs_2_, ...), custom_call_target="tpu_custom_call" | custom-call | flops 9200000000 | bytes 1024 | tf_op jit(solution)/shard_map/pallas_call | solution.py:162
  79.9 1.3 %collective-permute-done.18.refs_2_ = f32[32,1792]{1,0:T(8,128)S(1)} collective-permute-done((f32[32,1792]{1,0:T(8,128)S(1)}, f32[32,1792]{1,0:T(8,128)S(1)}, u32[]{:S(2)}, u32[]{:S(2)}) %collective-permute-start.18) | collective-permute-done | bytes 229408 | tf_op jit(solution)/shard_map/ppermute | solution.py:101
  81.2 6.7 %shard_map.112 = (bf16[2560,1792]{1,0:T(8,128)(2,1)}, bf16[1280,1792]{1,0:T(8,128)(2,1)}, bf16[16,128]{1,0:T(8,128)(2,1)}) custom-call(bf16[2560,256]{1,0:T(8,128)(2,1)S(1)} %get-tuple-element.55.refs_0_, f32[32,1792]{1,0:T(8,128)S(1)} %shard_map.110.refs_6_.refs_1_, f32[32,1792]{1,0:T(8,128)S(1)} %collective-permute-done.18.refs_2_, ...), custom_call_target="tpu_custom_call" | custom-call | flops 9200000000 | bytes 1024 | tf_op jit(solution)/shard_map/pallas_call | solution.py:162
  (38 shorter events, 7.2 us)
Async XLA Ops:
  0.6 12.8 %copy-start = (bf16[64,1792]{1,0:T(8,128)(2,1)S(1)}, bf16[64,1792]{1,0:T(8,128)(2,1)}, u32[]{:S(2)}) copy-start(bf16[64,1792]{1,0:T(8,128)(2,1)} %refs_2_.5) | copy-start | bytes 688132
  10.4 8.6 %collective-permute-start = (f32[32,1792]{1,0:T(8,128)S(1)}, f32[32,1792]{1,0:T(8,128)S(1)}, u32[]{:S(2)}, u32[]{:S(2)}) collective-permute-start(f32[32,1792]{1,0:T(8,128)S(1)} %get-tuple-element.34), channel_id=1, source_target_pairs={{0,4},{1,5},{2,6},{3,7},{4,0},{5,1},{6,2},{7,3},{8,12},{9,13},{10,... | collective-permute-start | bytes 688136 | tf_op jit(solution)/shard_map/ppermute | solution.py:101
  19.1 12.8 %collective-permute-start.1 = (f32[32,1792]{1,0:T(8,128)S(1)}, f32[32,1792]{1,0:T(8,128)S(1)}, u32[]{:S(2)}, u32[]{:S(2)}) collective-permute-start(f32[32,1792]{1,0:T(8,128)S(1)} %shard_map.95.refs_5_.refs_0_), channel_id=1, source_target_pairs={{0,8},{1,9},{2,10},{3,11},{4,12},{5,13},{6,14},{7,15},{8,0},{9,1},... | collective-permute-start | bytes 688136 | tf_op jit(solution)/shard_map/ppermute | solution.py:101
  25.9 1.5 %collective-permute-start.2 = (f32[32,1280]{1,0:T(8,128)S(1)}, f32[32,1280]{1,0:T(8,128)S(1)}, u32[]{:S(2)}, u32[]{:S(2)}) collective-permute-start(f32[32,1280]{1,0:T(8,128)S(1)} %get-tuple-element.38), channel_id=1, source_target_pairs={{0,1},{1,0},{2,3},{3,2},{4,5},{5,4},{6,7},{7,6},{8,9},{9,8},{10,11... | collective-permute-start | bytes 491528 | tf_op jit(solution)/shard_map/ppermute | solution.py:101
  25.9 1.6 %collective-permute-start.3 = (f32[32,1280]{1,0:T(8,128)S(1)}, f32[32,1280]{1,0:T(8,128)S(1)}, u32[]{:S(2)}, u32[]{:S(2)}) collective-permute-start(f32[32,1280]{1,0:T(8,128)S(1)} %get-tuple-element.39), channel_id=1, source_target_pairs={{0,1},{1,0},{2,3},{3,2},{4,5},{5,4},{6,7},{7,6},{8,9},{9,8},{10,11... | collective-permute-start | bytes 491528 | tf_op jit(solution)/shard_map/ppermute | solution.py:101
  27.6 7.1 %collective-permute-start.5 = (f32[32,2560]{1,0:T(8,128)S(1)}, f32[32,2560]{1,0:T(8,128)S(1)}, u32[]{:S(2)}, u32[]{:S(2)}) collective-permute-start(f32[32,2560]{1,0:T(8,128)S(1)} %shard_map.97.refs_2_.refs_0_), channel_id=1, source_target_pairs={{0,2},{1,5},{2,0},{3,7},{4,6},{5,1},{6,4},{7,3},{8,10},{9,13},{10,... | collective-permute-start | bytes 983048 | tf_op jit(solution)/shard_map/ppermute | solution.py:101
  31.9 8.3 %collective-permute-start.4 = (f32[32,1792]{1,0:T(8,128)S(1)}, f32[32,1792]{1,0:T(8,128)S(1)}, u32[]{:S(2)}, u32[]{:S(2)}) collective-permute-start(f32[32,1792]{1,0:T(8,128)S(1)} %shard_map.98.refs_2_.refs_0_), channel_id=1, source_target_pairs={{0,4},{1,5},{2,6},{3,7},{4,0},{5,1},{6,2},{7,3},{8,12},{9,13},{10,... | collective-permute-start | bytes 688136 | tf_op jit(solution)/shard_map/ppermute | solution.py:101
  34.8 10.5 %collective-permute-start.8 = (f32[32,2560]{1,0:T(8,128)S(1)}, f32[32,2560]{1,0:T(8,128)S(1)}, u32[]{:S(2)}, u32[]{:S(2)}) collective-permute-start(f32[32,2560]{1,0:T(8,128)S(1)} %shard_map.99.refs_3_.refs_0_), channel_id=1, source_target_pairs={{0,4},{1,3},{2,6},{3,1},{4,0},{5,7},{6,2},{7,5},{8,12},{9,11},{10,... | collective-permute-start | bytes 983048 | tf_op jit(solution)/shard_map/ppermute | solution.py:101
  45.3 3.7 %collective-permute-start.10 = (f32[32,2560]{1,0:T(8,128)S(1)}, f32[32,2560]{1,0:T(8,128)S(1)}, u32[]{:S(2)}, u32[]{:S(2)}) collective-permute-start(f32[32,2560]{1,0:T(8,128)S(1)} %shard_map.101.refs_3_.refs_0_), channel_id=1, source_target_pairs={{0,1},{1,0},{2,3},{3,2},{4,5},{5,4},{6,7},{7,6},{8,9},{9,8},{10,11... | collective-permute-start | bytes 983048 | tf_op jit(solution)/shard_map/ppermute | solution.py:101
  45.4 2.1 %collective-permute-start.7 = (f32[32,1408]{1,0:T(8,128)S(1)}, f32[32,1408]{1,0:T(8,128)S(1)}, u32[]{:S(2)}, u32[]{:S(2)}) collective-permute-start(f32[32,1408]{1,0:T(8,128)S(1)} %get-tuple-element.43), channel_id=1, source_target_pairs={{0,1},{1,0},{2,3},{3,2},{4,5},{5,4},{6,7},{7,6},{8,9},{9,8},{10,11... | collective-permute-start | bytes 540680 | tf_op jit(solution)/shard_map/ppermute | solution.py:101
  45.9 1.6 %collective-permute-start.6 = (f32[32,1280]{1,0:T(8,128)S(1)}, f32[32,1280]{1,0:T(8,128)S(1)}, u32[]{:S(2)}, u32[]{:S(2)}) collective-permute-start(f32[32,1280]{1,0:T(8,128)S(1)} %get-tuple-element.42), channel_id=1, source_target_pairs={{0,1},{1,0},{2,3},{3,2},{4,5},{5,4},{6,7},{7,6},{8,9},{9,8},{10,11... | collective-permute-start | bytes 491528 | tf_op jit(solution)/shard_map/ppermute | solution.py:101
  47.6 9.3 %collective-permute-start.12 = (f32[16,2560]{1,0:T(8,128)S(1)}, f32[16,2560]{1,0:T(8,128)S(1)}, u32[]{:S(2)}, u32[]{:S(2)}) collective-permute-start(f32[16,2560]{1,0:T(8,128)S(1)} %get-tuple-element.48), channel_id=1, source_target_pairs={{0,2},{1,3},{2,0},{3,1},{4,6},{5,7},{6,4},{7,5},{8,10},{9,11},{10,... | collective-permute-start | bytes 491528 | tf_op jit(solution)/shard_map/ppermute | solution.py:101
  52.2 9.3 %collective-permute-start.14 = (f32[32,1792]{1,0:T(8,128)S(1)}, f32[32,1792]{1,0:T(8,128)S(1)}, u32[]{:S(2)}, u32[]{:S(2)}) collective-permute-start(f32[32,1792]{1,0:T(8,128)S(1)} %get-tuple-element.54), channel_id=1, source_target_pairs={{0,4},{1,5},{2,6},{3,7},{4,0},{5,1},{6,2},{7,3},{8,12},{9,13},{10,... | collective-permute-start | bytes 688136 | tf_op jit(solution)/shard_map/ppermute | solution.py:101
  52.8 4.2 %collective-permute-start.9 = (f32[32,128]{1,0:T(8,128)S(1)}, f32[32,128]{1,0:T(8,128)S(1)}, u32[]{:S(2)}, u32[]{:S(2)}) collective-permute-start(f32[32,128]{1,0:T(8,128)S(1)} %get-tuple-element.44.refs_0_), channel_id=1, source_target_pairs={{0,2},{1,3},{2,0},{3,1},{4,6},{5,7},{6,4},{7,5},{8,10},{9,11},{10,... | collective-permute-start | bytes 49160 | tf_op jit(solution)/shard_map/ppermute | solution.py:101
  53.3 6.2 %collective-permute-start.11 = (f32[64,64]{1,0:T(8,128)S(1)}, f32[64,64]{1,0:T(8,128)S(1)}, u32[]{:S(2)}, u32[]{:S(2)}) collective-permute-start(f32[64,64]{1,0:T(8,128)S(1)} %get-tuple-element.47.refs_2_), channel_id=1, source_target_pairs={{0,8},{1,9},{2,10},{3,11},{4,12},{5,13},{6,14},{7,15},{8,0},{9,1},... | collective-permute-start | bytes 49160 | tf_op jit(solution)/shard_map/ppermute | solution.py:101
  56.9 9.7 %collective-permute-start.13 = (f32[16,2560]{1,0:T(8,128)S(1)}, f32[16,2560]{1,0:T(8,128)S(1)}, u32[]{:S(2)}, u32[]{:S(2)}) collective-permute-start(f32[16,2560]{1,0:T(8,128)S(1)} %shard_map.104.refs_4_.refs_0_), channel_id=1, source_target_pairs={{0,4},{1,5},{2,6},{3,7},{4,0},{5,1},{6,2},{7,3},{8,12},{9,13},{10,... | collective-permute-start | bytes 491528 | tf_op jit(solution)/shard_map/ppermute | solution.py:101
  61.5 11.3 %collective-permute-start.15 = (f32[32,1792]{1,0:T(8,128)S(1)}, f32[32,1792]{1,0:T(8,128)S(1)}, u32[]{:S(2)}, u32[]{:S(2)}) collective-permute-start(f32[32,1792]{1,0:T(8,128)S(1)} %shard_map.106.refs_2_.refs_0_), channel_id=1, source_target_pairs={{0,8},{1,9},{2,10},{3,11},{4,12},{5,13},{6,14},{7,15},{8,0},{9,1},... | collective-permute-start | bytes 688136 | tf_op jit(solution)/shard_map/ppermute | solution.py:101
  66.6 5.4 %collective-permute-start.16 = (f32[16,2560]{1,0:T(8,128)S(1)}, f32[16,2560]{1,0:T(8,128)S(1)}, u32[]{:S(2)}, u32[]{:S(2)}) collective-permute-start(f32[16,2560]{1,0:T(8,128)S(1)} %shard_map.107.refs_4_.refs_1_), channel_id=1, source_target_pairs={{0,2},{1,3},{2,0},{3,1},{4,6},{5,7},{6,4},{7,5},{8,10},{9,11},{10,... | collective-permute-start | bytes 491528 | tf_op jit(solution)/shard_map/ppermute | solution.py:101
  72.0 1.5 %collective-permute-start.17 = (f32[16,2560]{1,0:T(8,128)S(1)}, f32[16,2560]{1,0:T(8,128)S(1)}, u32[]{:S(2)}, u32[]{:S(2)}) collective-permute-start(f32[16,2560]{1,0:T(8,128)S(1)} %shard_map.109.refs_2_), channel_id=1, source_target_pairs={{0,1},{1,0},{2,3},{3,2},{4,5},{5,4},{6,7},{7,6},{8,9},{9,8},{10,11... | collective-permute-start | bytes 491528 | tf_op jit(solution)/shard_map/ppermute | solution.py:101
  72.1 1.6 %collective-permute-start.19 = (f32[16,2560]{1,0:T(8,128)S(1)}, f32[16,2560]{1,0:T(8,128)S(1)}, u32[]{:S(2)}, u32[]{:S(2)}) collective-permute-start(f32[16,2560]{1,0:T(8,128)S(1)} %shard_map.107.refs_4_.refs_1_), channel_id=1, source_target_pairs={{0,1},{1,0},{2,3},{3,2},{4,5},{5,4},{6,7},{7,6},{8,9},{9,8},{10,11... | collective-permute-start | bytes 491528 | tf_op jit(solution)/shard_map/ppermute | solution.py:101
  73.5 7.7 %collective-permute-start.18 = (f32[32,1792]{1,0:T(8,128)S(1)}, f32[32,1792]{1,0:T(8,128)S(1)}, u32[]{:S(2)}, u32[]{:S(2)}) collective-permute-start(f32[32,1792]{1,0:T(8,128)S(1)} %shard_map.110.refs_6_.refs_1_), channel_id=1, source_target_pairs={{0,4},{1,5},{2,6},{3,7},{4,0},{5,1},{6,2},{7,3},{8,12},{9,13},{10,... | collective-permute-start | bytes 688136 | tf_op jit(solution)/shard_map/ppermute | solution.py:101

commit v15 on v11

--- a/solution.py
+++ b/solution.py
@@ -11,7 +11,7 @@
 RANK = 64
 TILE = 256
 FLOPS = 1.15e9
-WEIGHTS = (8.0, 4.0, 1.0, 4.0, 0.1, 5.0, 1.0, 5.0, 1.0, 1.0, 2.0, 2.0, 0.1, 5.0, 5.0, 1.0, 0.1, 0.5, 1.0, 8.0, 8.0)
+WEIGHTS = (8.0, 4.0, 1.0, 4.0, 0.1, 5.0, 1.0, 5.0, 1.0, 1.0, 2.0, 2.0, 0.1, 1.0, 5.0, 0.1, 0.5, 1.0, 1.0, 8.0, 8.0)
 MIB = 1 << 20
 BF16 = jnp.bfloat16
 F32 = jnp.float32
@@ -316,9 +316,10 @@
     stack[:RANK, :] = hi
     stack[RANK : 2 * RANK, :] = lo
     stack[2 * RANK :, :] = hi
-    return lax.dot_general(
-        left[...], left[...], NT, preferred_element_type=F32, precision=lax.Precision.HIGHEST
-    )
+    parts = stack[: 2 * RANK]
+    gram = lax.dot_general(parts, parts, NT, preferred_element_type=F32)
+    mixed = gram[:RANK, RANK:] + gram[RANK:, :RANK]
+    return gram[:RANK, :RANK] + (mixed + gram[RANK:, RANK:])
 
 
 def packed(gram):
@@ -606,7 +607,7 @@
 
     keep, *gives, left_down = down_right(run, [down], [other_down], fixed_down, after=(gate,))
     gots = to_other_core(gives)
-    gates = add(run, [gate], [got_gate], in_two(slab), after=(keep,))
+    gates = add(run, [gate], [got_gate], after=(keep,))
     others_gate = to_other_core(gates)
     down, gram_down = add(run, [keep], gots, [slab, 2 * RANK], after=(gates[0],))
     grams_down = [gram_down] + [
@@ -627,17 +628,17 @@
     got_a = exchange(gate_a, steps[0])
     (gate_b,) = add(run, [keep_b], [got_b], after=(gate_a,))
     got_b = exchange(gate_b, steps[0])
-    downs = add(run, [down], [got], in_two(slab), after=(gate_b,))
-    others_down = to_other_core(downs)
     for step in steps[1:]:
         (gate_a,) = add(run, [gate_a], [got_a])
         got_a = exchange(gate_a, step)
         (gate_b,) = add(run, [gate_b], [got_b])
         got_b = exchange(gate_b, step)
-    gate_a, gram_gate = add(run, [gate_a], [got_a], [few * TILE, 2 * RANK], after=(downs[0],))
+    gate_a, gram_gate = add(run, [gate_a], [got_a], [few * TILE, 2 * RANK], after=(gate_b,))
     other_a = exchange(gate_a, other_replica)
     col_stack, row_turned = solve(run, grams_down, left_down, gram_gate, left_gate)
-    (gate_b,) = add(run, [gate_b], [got_b], after=(col_stack,))
+    downs = add(run, [down], [got], in_two(slab), after=(col_stack,))
+    others_down = to_other_core(downs)
+    (gate_b,) = add(run, [gate_b], [got_b], after=(downs[0],))
     other_b = exchange(gate_b, other_replica)
     new_error_down, update_down, turned = rebuild(
         run, (None, col_stack), downs, others_down, fixed_down, (0, 1), slab // 8, after=(gate_b,)

time: 87.5 us -> 86.5 us (0.989)
  waiting for transfers between devices: 18.1 us -> 15 us
  starting transfers between devices: 23.8 us -> 26.3 us
    ppermute x22 -> x21, waiting for transfers between devices: 18.1 us -> 15 us  [exchange(): return lax.ppermute(x, ('dp', 'tensor'), pairs)]
    ppermute x22 -> x21, starting transfers between devices: 23.8 us -> 26.3 us  [exchange(): return lax.ppermute(x, ('dp', 'tensor'), pairs)]
  transfers between devices with their start and end apart: 22 -> 21, of which waited for: 10 -> 9; matrix products, arithmetic and copies ran while one was open for 0% -> 0% of each run, Pallas kernels for 32% -> 32%
where the time goes in v15:
time: 86.5 us; the launch traced here: 86.3 us
  Pallas kernels  44 us (51%)
  starting transfers between devices  26.3 us (30%)
  waiting for transfers between devices  15 us (17%)
  between operations  1.01 us (1%)
    pallas_call x21, Pallas kernels, __call__(): pl.pallas_call(body, out_shape=tuple(((pltpu.VMEM if spec is VMEM else pl...  44 us
    ppermute x21, starting transfers between devices, exchange(): return lax.ppermute(x, ('dp', 'tensor'), pairs)  26.3 us
    ppermute x21, waiting for transfers between devices, exchange(): return lax.ppermute(x, ('dp', 'tensor'), pairs)  15 us
  transfers between devices with their start and end apart: 21, of which 9 were waited for; matrix products, arithmetic and copies ran while one was open for 0% of the time, Pallas kernels for 32%

profile of v15, /device:TPU:0, one launch (start us, length us, event | category | flops | bytes accessed | tf_op | source)
XLA Modules:
  0.0 86.3 jit_solution(2262399983086950163)
XLA Ops:
  0.6 9.8 %shard_map.93 = (f32[64,1792]{1,0:T(8,128)}, bf16[2560,1792]{1,0:T(8,128)(2,1)S(1)}, f32[32,1792]{1,0:T(8,128)S(1)}, f32[32,1792]{1,0:T(8,128)S(1)}) custom-call(bf16[2560,1792]{1,0:T(8,128)(2,1)} %refs_0_.3, bf16[2560,1792]{1,0:T(8,128)(2,1)} %refs_1_.3, bf16[64,5120]{1,0:T(8,128)(2,1)} %refs_2_.3), custom_call_target="tpu_custom_call" | custom-call | flops 9200000000 | bytes 1024 | tf_op jit(solution)/shard_map/pallas_call | solution.py:154
  10.4 3.0 %collective-permute-start = (f32[32,1792]{1,0:T(8,128)S(1)}, f32[32,1792]{1,0:T(8,128)S(1)}, u32[]{:S(2)}, u32[]{:S(2)}) collective-permute-start(f32[32,1792]{1,0:T(8,128)S(1)} %get-tuple-element.37), channel_id=1, source_target_pairs={{0,4},{1,5},{2,6},{3,7},{4,0},{5,1},{6,2},{7,3},{8,12},{9,13},{10,... | collective-permute-start | bytes 688136 | tf_op jit(solution)/shard_map/ppermute | solution.py:97
  13.5 5.1 %shard_map.94 = (f32[64,2560]{1,0:T(8,128)S(1)}, bf16[2560,1792]{1,0:T(8,128)(2,1)S(1)}) custom-call(bf16[2560,1792]{1,0:T(8,128)(2,1)} %refs_0_.5, bf16[2560,1792]{1,0:T(8,128)(2,1)} %refs_1_.5, bf16[64,1792]{1,0:T(8,128)(2,1)S(1)} %copy-done, f32[32,1792]{1,0:T(8,128)S(1)} %get-tuple-element.36.refs_3_.refs_0_), custom_call_target="tpu_custom_call" | custom-call | flops 4600000000 | bytes 1024 | tf_op jit(solution)/shard_map/pallas_call | solution.py:154
  19.1 2.8 %collective-permute-start.1 = (f32[32,1792]{1,0:T(8,128)S(1)}, f32[32,1792]{1,0:T(8,128)S(1)}, u32[]{:S(2)}, u32[]{:S(2)}) collective-permute-start(f32[32,1792]{1,0:T(8,128)S(1)} %shard_map.95.refs_5_.refs_0_), channel_id=1, source_target_pairs={{0,8},{1,9},{2,10},{3,11},{4,12},{5,13},{6,14},{7,15},{8,0},{9,1},... | collective-permute-start | bytes 688136 | tf_op jit(solution)/shard_map/ppermute | solution.py:97
  21.9 4.0 %shard_map.96 = (f32[64,2560]{1,0:T(8,128)S(1)}, bf16[2560,1792]{1,0:T(8,128)(2,1)S(1)}, f32[32,2560]{1,0:T(8,128)S(1)}, f32[32,1280]{1,0:T(8,128)S(1)}, f32[32,1280]{1,0:T(8,128)S(1)}) custom-call(bf16[2560,1792]{1,0:T(8,128)(2,1)} %refs_0_.5, bf16[2560,1792]{1,0:T(8,128)(2,1)} %refs_1_.5, ...), custom_call_target="tpu_custom_call", output_to_operand_aliasing={{0}: (3, {}), {1}: (4, {})} | custom-call | flops 4600000000 | bytes 1024 | tf_op jit(solution)/shard_map/pallas_call | solution.py:154
  26.5 0.9 %collective-permute-done.2.refs_1_ = f32[32,1280]{1,0:T(8,128)S(1)} collective-permute-done((f32[32,1280]{1,0:T(8,128)S(1)}, f32[32,1280]{1,0:T(8,128)S(1)}, u32[]{:S(2)}, u32[]{:S(2)}) %collective-permute-start.2) | collective-permute-done | bytes 163872 | tf_op jit(solution)/shard_map/ppermute | solution.py:97
  27.6 1.6 %collective-permute-start.5 = (f32[32,2560]{1,0:T(8,128)S(1)}, f32[32,2560]{1,0:T(8,128)S(1)}, u32[]{:S(2)}, u32[]{:S(2)}) collective-permute-start(f32[32,2560]{1,0:T(8,128)S(1)} %shard_map.97.refs_2_.refs_0_), channel_id=1, source_target_pairs={{0,2},{1,5},{2,0},{3,7},{4,6},{5,1},{6,4},{7,3},{8,10},{9,13},{10,... | collective-permute-start | bytes 983048 | tf_op jit(solution)/shard_map/ppermute | solution.py:97
  29.2 2.7 %collective-permute-done.1.refs_1_ = f32[32,1792]{1,0:T(8,128)S(1)} collective-permute-done((f32[32,1792]{1,0:T(8,128)S(1)}, f32[32,1792]{1,0:T(8,128)S(1)}, u32[]{:S(2)}, u32[]{:S(2)}) %collective-permute-start.1) | collective-permute-done | bytes 229408 | tf_op jit(solution)/shard_map/ppermute | solution.py:97
  32.4 2.3 %collective-permute-done.5.refs_1_ = f32[32,2560]{1,0:T(8,128)S(1)} collective-permute-done((f32[32,2560]{1,0:T(8,128)S(1)}, f32[32,2560]{1,0:T(8,128)S(1)}, u32[]{:S(2)}, u32[]{:S(2)}) %collective-permute-start.5) | collective-permute-done | bytes 327712 | tf_op jit(solution)/shard_map/ppermute | solution.py:97
  34.8 1.6 %collective-permute-start.8 = (f32[32,2560]{1,0:T(8,128)S(1)}, f32[32,2560]{1,0:T(8,128)S(1)}, u32[]{:S(2)}, u32[]{:S(2)}) collective-permute-start(f32[32,2560]{1,0:T(8,128)S(1)} %shard_map.99.refs_3_.refs_0_), channel_id=1, source_target_pairs={{0,4},{1,3},{2,6},{3,1},{4,0},{5,7},{6,2},{7,5},{8,12},{9,11},{10,... | collective-permute-start | bytes 983048 | tf_op jit(solution)/shard_map/ppermute | solution.py:97
  36.4 3.7 %collective-permute-done.4.refs_1_ = f32[32,1792]{1,0:T(8,128)S(1)} collective-permute-done((f32[32,1792]{1,0:T(8,128)S(1)}, f32[32,1792]{1,0:T(8,128)S(1)}, u32[]{:S(2)}, u32[]{:S(2)}) %collective-permute-start.4) | collective-permute-done | bytes 229408 | tf_op jit(solution)/shard_map/ppermute | solution.py:97
  40.2 5.1 %shard_map.100 = (f32[32,2688]{1,0:T(8,128)S(1)}, f32[32,1280]{1,0:T(8,128)S(1)}, f32[32,1408]{1,0:T(8,128)S(1)}, bf16[192,1792]{1,0:T(8,128)(2,1)S(1)}) custom-call(f32[32,1792]{1,0:T(8,128)S(1)} %shard_map.98.refs_2_.refs_0_, f32[32,1792]{1,0:T(8,128)S(1)} %collective-permute-done.4.refs_1_, bf16[2560,1792]{1,0:T(8,128)(2,1)S(1)} %get-tuple-element.43.refs_2_.refs_5_, ...), custom_call_target="tpu_custom_call" | custom-call | flops 5750000128 | bytes 1024 | tf_op jit(solution)/shard_map/pallas_call | solution.py:154
  46.0 1.5 %collective-permute-done.6.refs_1_ = f32[32,1280]{1,0:T(8,128)S(1)} collective-permute-done((f32[32,1280]{1,0:T(8,128)S(1)}, f32[32,1280]{1,0:T(8,128)S(1)}, u32[]{:S(2)}, u32[]{:S(2)}) %collective-permute-start.6) | collective-permute-done | bytes 163872 | tf_op jit(solution)/shard_map/ppermute | solution.py:97
  47.6 1.4 %collective-permute-start.12 = (f32[32,2560]{1,0:T(8,128)S(1)}, f32[32,2560]{1,0:T(8,128)S(1)}, u32[]{:S(2)}, u32[]{:S(2)}) collective-permute-start(f32[32,2560]{1,0:T(8,128)S(1)} %get-tuple-element.49.refs_3_.refs_0_), channel_id=1, source_target_pairs={{0,2},{1,5},{2,0},{3,7},{4,6},{5,1},{6,4},{7,3},{8,10},{9,13},{10,... | collective-permute-start | bytes 983048 | tf_op jit(solution)/shard_map/ppermute | solution.py:97
  49.0 1.7 %shard_map.103 = (f32[32,768]{1,0:T(8,128)S(1)}, f32[32,768]{1,0:T(8,128)S(1)}, f32[32,128]{1,0:T(8,128)S(1)}, bf16[192,2560]{1,0:T(8,128)(2,1)S(1)}) custom-call(f32[32,2560]{1,0:T(8,128)S(1)} %shard_map.101.refs_3_.refs_0_, f32[32,2560]{1,0:T(8,128)S(1)} %collective-permute-done.10.refs_1_, ...), custom_call_target="tpu_custom_call" | custom-call | flops 2300000000 | bytes 1024 | tf_op jit(solution)/shard_map/pallas_call | solution.py:154
  51.3 1.6 %shard_map.104 = (f32[32,1024]{1,0:T(8,128)S(1)}, f32[32,1024]{1,0:T(8,128)S(1)}) custom-call(bf16[192,2560]{1,0:T(8,128)(2,1)S(1)} %get-tuple-element.53.refs_0_.refs_4_, bf16[2560,1792]{1,0:T(8,128)(2,1)S(1)} %get-tuple-element.48.refs_2_.refs_1_.refs_5_), custom_call_target="tpu_custom_call" | custom-call | flops 2300000000 | bytes 1024 | tf_op jit(solution)/shard_map/pallas_call | solution.py:154
  52.9 1.6 %collective-permute-start.14 = (f32[32,1024]{1,0:T(8,128)S(1)}, f32[32,1024]{1,0:T(8,128)S(1)}, u32[]{:S(2)}, u32[]{:S(2)}) collective-permute-start(f32[32,1024]{1,0:T(8,128)S(1)} %get-tuple-element.54.refs_2_), channel_id=1, source_target_pairs={{0,4},{1,5},{2,6},{3,7},{4,0},{5,1},{6,2},{7,3},{8,12},{9,13},{10,... | collective-permute-start | bytes 393224 | tf_op jit(solution)/shard_map/ppermute | solution.py:97
  56.5 2.7 %collective-permute-start.13 = (f32[32,896]{1,0:T(8,128)S(1)}, f32[32,896]{1,0:T(8,128)S(1)}, u32[]{:S(2)}, u32[]{:S(2)}) collective-permute-start(f32[32,896]{1,0:T(8,128)S(1)} %shard_map.106.refs_2_.refs_0_), channel_id=1, source_target_pairs={{0,8},{1,9},{2,10},{3,11},{4,12},{5,13},{6,14},{7,15},{8,0},{9,1},... | collective-permute-start | bytes 344072 | tf_op jit(solution)/shard_map/ppermute | solution.py:97
  59.2 3.3 %collective-permute-start.15 = (f32[32,1024]{1,0:T(8,128)S(1)}, f32[32,1024]{1,0:T(8,128)S(1)}, u32[]{:S(2)}, u32[]{:S(2)}) collective-permute-start(f32[32,1024]{1,0:T(8,128)S(1)} %shard_map.107.refs_2_.refs_0_), channel_id=1, source_target_pairs={{0,8},{1,9},{2,10},{3,11},{4,12},{5,13},{6,14},{7,15},{8,0},{9,1},... | collective-permute-start | bytes 393224 | tf_op jit(solution)/shard_map/ppermute | solution.py:97
  62.5 2.2 %collective-permute-done.13.refs_1_ = f32[32,896]{1,0:T(8,128)S(1)} collective-permute-done((f32[32,896]{1,0:T(8,128)S(1)}, f32[32,896]{1,0:T(8,128)S(1)}, u32[]{:S(2)}, u32[]{:S(2)}) %collective-permute-start.13) | collective-permute-done | bytes 114720 | tf_op jit(solution)/shard_map/ppermute | solution.py:97
  64.8 4.0 %shard_map.109 = (bf16[256,1792]{1,0:T(8,128)(2,1)S(1)}, bf16[2560,256]{1,0:T(8,128)(2,1)S(1)}) custom-call(f32[32,128]{1,0:T(8,128)S(1)} %get-tuple-element.47.refs_0_, f32[32,128]{1,0:T(8,128)S(1)} %collective-permute-done.9.refs_1_, f32[32,128]{1,0:T(8,128)S(1)} %get-tuple-element.56.refs_2_, bf16[192,1792]{1,0:T(8,128)(2,1)S(1)} %get-tuple-element.57.refs_3_, ...), custom_call_target="tpu_custom_call" | custom-call | flops 575000000 | bytes 1024 | tf_op jit(solution)/shard_map/pallas_call | solution.py:154
  69.4 4.1 %collective-permute-start.17 = (f32[32,768]{1,0:T(8,128)S(1)}, f32[32,768]{1,0:T(8,128)S(1)}, u32[]{:S(2)}, u32[]{:S(2)}) collective-permute-start(f32[32,768]{1,0:T(8,128)S(1)} %get-tuple-element.59.refs_1_), channel_id=1, source_target_pairs={{0,4},{1,5},{2,6},{3,7},{4,0},{5,1},{6,2},{7,3},{8,12},{9,13},{10,... | collective-permute-start | bytes 294920 | tf_op jit(solution)/shard_map/ppermute | solution.py:97
  73.7 6.2 %shard_map.112 = (bf16[2560,1792]{1,0:T(8,128)(2,1)}, bf16[1280,1792]{1,0:T(8,128)(2,1)}, bf16[2560,256]{1,0:T(8,128)(2,1)S(1)}) custom-call(bf16[256,1792]{1,0:T(8,128)(2,1)S(1)} %get-tuple-element.60.refs_2_.refs_0_, f32[32,1280]{1,0:T(8,128)S(1)} %get-tuple-element.61.refs_2_.refs_1_, f32[32,1280]{1,0:T(8,128)S(1)} %get-tuple-element.62.refs_2_, ...), custom_call_target="tpu_custom_call" | custom-call | flops 9200000000 | bytes 1024 | tf_op jit(solution)/shard_map/pallas_call | solution.py:154
  79.9 6.3 %shard_map.113 = (bf16[2560,1792]{1,0:T(8,128)(2,1)}, bf16[1280,1792]{1,0:T(8,128)(2,1)}, bf16[16,128]{1,0:T(8,128)(2,1)}) custom-call(bf16[2560,256]{1,0:T(8,128)(2,1)S(1)} %get-tuple-element.58.refs_0_, f32[32,768]{1,0:T(8,128)S(1)} %get-tuple-element.59.refs_1_, f32[32,1024]{1,0:T(8,128)S(1)} %shard_map.111.refs_6_.refs_2_, ...), custom_call_target="tpu_custom_call" | custom-call | flops 9200000000 | bytes 1024 | tf_op jit(solution)/shard_map/pallas_call | solution.py:154
  (41 shorter events, 6.1 us)
Async XLA Ops:
  0.6 12.8 %copy-start = (bf16[64,1792]{1,0:T(8,128)(2,1)S(1)}, bf16[64,1792]{1,0:T(8,128)(2,1)}, u32[]{:S(2)}) copy-start(bf16[64,1792]{1,0:T(8,128)(2,1)} %refs_2_.5) | copy-start | bytes 688132
  10.4 8.6 %collective-permute-start = (f32[32,1792]{1,0:T(8,128)S(1)}, f32[32,1792]{1,0:T(8,128)S(1)}, u32[]{:S(2)}, u32[]{:S(2)}) collective-permute-start(f32[32,1792]{1,0:T(8,128)S(1)} %get-tuple-element.37), channel_id=1, source_target_pairs={{0,4},{1,5},{2,6},{3,7},{4,0},{5,1},{6,2},{7,3},{8,12},{9,13},{10,... | collective-permute-start | bytes 688136 | tf_op jit(solution)/shard_map/ppermute | solution.py:97
  19.1 12.8 %collective-permute-start.1 = (f32[32,1792]{1,0:T(8,128)S(1)}, f32[32,1792]{1,0:T(8,128)S(1)}, u32[]{:S(2)}, u32[]{:S(2)}) collective-permute-start(f32[32,1792]{1,0:T(8,128)S(1)} %shard_map.95.refs_5_.refs_0_), channel_id=1, source_target_pairs={{0,8},{1,9},{2,10},{3,11},{4,12},{5,13},{6,14},{7,15},{8,0},{9,1},... | collective-permute-start | bytes 688136 | tf_op jit(solution)/shard_map/ppermute | solution.py:97
  25.9 1.5 %collective-permute-start.2 = (f32[32,1280]{1,0:T(8,128)S(1)}, f32[32,1280]{1,0:T(8,128)S(1)}, u32[]{:S(2)}, u32[]{:S(2)}) collective-permute-start(f32[32,1280]{1,0:T(8,128)S(1)} %get-tuple-element.41), channel_id=1, source_target_pairs={{0,1},{1,0},{2,3},{3,2},{4,5},{5,4},{6,7},{7,6},{8,9},{9,8},{10,11... | collective-permute-start | bytes 491528 | tf_op jit(solution)/shard_map/ppermute | solution.py:97
  26.0 1.6 %collective-permute-start.3 = (f32[32,1280]{1,0:T(8,128)S(1)}, f32[32,1280]{1,0:T(8,128)S(1)}, u32[]{:S(2)}, u32[]{:S(2)}) collective-permute-start(f32[32,1280]{1,0:T(8,128)S(1)} %get-tuple-element.42), channel_id=1, source_target_pairs={{0,1},{1,0},{2,3},{3,2},{4,5},{5,4},{6,7},{7,6},{8,9},{9,8},{10,11... | collective-permute-start | bytes 491528 | tf_op jit(solution)/shard_map/ppermute | solution.py:97
  27.6 7.1 %collective-permute-start.5 = (f32[32,2560]{1,0:T(8,128)S(1)}, f32[32,2560]{1,0:T(8,128)S(1)}, u32[]{:S(2)}, u32[]{:S(2)}) collective-permute-start(f32[32,2560]{1,0:T(8,128)S(1)} %shard_map.97.refs_2_.refs_0_), channel_id=1, source_target_pairs={{0,2},{1,5},{2,0},{3,7},{4,6},{5,1},{6,4},{7,3},{8,10},{9,13},{10,... | collective-permute-start | bytes 983048 | tf_op jit(solution)/shard_map/ppermute | solution.py:97
  31.9 8.3 %collective-permute-start.4 = (f32[32,1792]{1,0:T(8,128)S(1)}, f32[32,1792]{1,0:T(8,128)S(1)}, u32[]{:S(2)}, u32[]{:S(2)}) collective-permute-start(f32[32,1792]{1,0:T(8,128)S(1)} %shard_map.98.refs_2_.refs_0_), channel_id=1, source_target_pairs={{0,4},{1,5},{2,6},{3,7},{4,0},{5,1},{6,2},{7,3},{8,12},{9,13},{10,... | collective-permute-start | bytes 688136 | tf_op jit(solution)/shard_map/ppermute | solution.py:97
  34.8 10.5 %collective-permute-start.8 = (f32[32,2560]{1,0:T(8,128)S(1)}, f32[32,2560]{1,0:T(8,128)S(1)}, u32[]{:S(2)}, u32[]{:S(2)}) collective-permute-start(f32[32,2560]{1,0:T(8,128)S(1)} %shard_map.99.refs_3_.refs_0_), channel_id=1, source_target_pairs={{0,4},{1,3},{2,6},{3,1},{4,0},{5,7},{6,2},{7,5},{8,12},{9,11},{10,... | collective-permute-start | bytes 983048 | tf_op jit(solution)/shard_map/ppermute | solution.py:97
  45.3 3.6 %collective-permute-start.10 = (f32[32,2560]{1,0:T(8,128)S(1)}, f32[32,2560]{1,0:T(8,128)S(1)}, u32[]{:S(2)}, u32[]{:S(2)}) collective-permute-start(f32[32,2560]{1,0:T(8,128)S(1)} %shard_map.101.refs_3_.refs_0_), channel_id=1, source_target_pairs={{0,1},{1,0},{2,3},{3,2},{4,5},{5,4},{6,7},{7,6},{8,9},{9,8},{10,11... | collective-permute-start | bytes 983048 | tf_op jit(solution)/shard_map/ppermute | solution.py:97
  45.4 2.1 %collective-permute-start.7 = (f32[32,1408]{1,0:T(8,128)S(1)}, f32[32,1408]{1,0:T(8,128)S(1)}, u32[]{:S(2)}, u32[]{:S(2)}) collective-permute-start(f32[32,1408]{1,0:T(8,128)S(1)} %get-tuple-element.46), channel_id=1, source_target_pairs={{0,1},{1,0},{2,3},{3,2},{4,5},{5,4},{6,7},{7,6},{8,9},{9,8},{10,11... | collective-permute-start | bytes 540680 | tf_op jit(solution)/shard_map/ppermute | solution.py:97
  45.9 1.6 %collective-permute-start.6 = (f32[32,1280]{1,0:T(8,128)S(1)}, f32[32,1280]{1,0:T(8,128)S(1)}, u32[]{:S(2)}, u32[]{:S(2)}) collective-permute-start(f32[32,1280]{1,0:T(8,128)S(1)} %get-tuple-element.45), channel_id=1, source_target_pairs={{0,1},{1,0},{2,3},{3,2},{4,5},{5,4},{6,7},{7,6},{8,9},{9,8},{10,11... | collective-permute-start | bytes 491528 | tf_op jit(solution)/shard_map/ppermute | solution.py:97
  47.6 7.5 %collective-permute-start.12 = (f32[32,2560]{1,0:T(8,128)S(1)}, f32[32,2560]{1,0:T(8,128)S(1)}, u32[]{:S(2)}, u32[]{:S(2)}) collective-permute-start(f32[32,2560]{1,0:T(8,128)S(1)} %get-tuple-element.49.refs_3_.refs_0_), channel_id=1, source_target_pairs={{0,2},{1,5},{2,0},{3,7},{4,6},{5,1},{6,4},{7,3},{8,10},{9,13},{10,... | collective-permute-start | bytes 983048 | tf_op jit(solution)/shard_map/ppermute | solution.py:97
  50.7 5.8 %collective-permute-start.11 = (f32[32,768]{1,0:T(8,128)S(1)}, f32[32,768]{1,0:T(8,128)S(1)}, u32[]{:S(2)}, u32[]{:S(2)}) collective-permute-start(f32[32,768]{1,0:T(8,128)S(1)} %get-tuple-element.51), channel_id=1, source_target_pairs={{0,4},{1,5},{2,6},{3,7},{4,0},{5,1},{6,2},{7,3},{8,12},{9,13},{10,... | collective-permute-start | bytes 294920 | tf_op jit(solution)/shard_map/ppermute | solution.py:97
  52.9 6.4 %collective-permute-start.14 = (f32[32,1024]{1,0:T(8,128)S(1)}, f32[32,1024]{1,0:T(8,128)S(1)}, u32[]{:S(2)}, u32[]{:S(2)}) collective-permute-start(f32[32,1024]{1,0:T(8,128)S(1)} %get-tuple-element.54.refs_2_), channel_id=1, source_target_pairs={{0,4},{1,5},{2,6},{3,7},{4,0},{5,1},{6,2},{7,3},{8,12},{9,13},{10,... | collective-permute-start | bytes 393224 | tf_op jit(solution)/shard_map/ppermute | solution.py:97
  54.4 10.3 %collective-permute-start.9 = (f32[32,128]{1,0:T(8,128)S(1)}, f32[32,128]{1,0:T(8,128)S(1)}, u32[]{:S(2)}, u32[]{:S(2)}) collective-permute-start(f32[32,128]{1,0:T(8,128)S(1)} %get-tuple-element.47.refs_0_), channel_id=1, source_target_pairs={{0,2},{1,3},{2,0},{3,1},{4,6},{5,7},{6,4},{7,5},{8,10},{9,11},{10,... | collective-permute-start | bytes 49160 | tf_op jit(solution)/shard_map/ppermute | solution.py:97
  55.2 13.6 %collective-permute-start.16 = (f32[32,2560]{1,0:T(8,128)S(1)}, f32[32,2560]{1,0:T(8,128)S(1)}, u32[]{:S(2)}, u32[]{:S(2)}) collective-permute-start(f32[32,2560]{1,0:T(8,128)S(1)} %shard_map.105.refs_3_.refs_0_), channel_id=1, source_target_pairs={{0,4},{1,3},{2,6},{3,1},{4,0},{5,7},{6,2},{7,5},{8,12},{9,11},{10,... | collective-permute-start | bytes 983048 | tf_op jit(solution)/shard_map/ppermute | solution.py:97
  56.5 8.2 %collective-permute-start.13 = (f32[32,896]{1,0:T(8,128)S(1)}, f32[32,896]{1,0:T(8,128)S(1)}, u32[]{:S(2)}, u32[]{:S(2)}) collective-permute-start(f32[32,896]{1,0:T(8,128)S(1)} %shard_map.106.refs_2_.refs_0_), channel_id=1, source_target_pairs={{0,8},{1,9},{2,10},{3,11},{4,12},{5,13},{6,14},{7,15},{8,0},{9,1},... | collective-permute-start | bytes 344072 | tf_op jit(solution)/shard_map/ppermute | solution.py:97
  59.2 14.3 %collective-permute-start.15 = (f32[32,1024]{1,0:T(8,128)S(1)}, f32[32,1024]{1,0:T(8,128)S(1)}, u32[]{:S(2)}, u32[]{:S(2)}) collective-permute-start(f32[32,1024]{1,0:T(8,128)S(1)} %shard_map.107.refs_2_.refs_0_), channel_id=1, source_target_pairs={{0,8},{1,9},{2,10},{3,11},{4,12},{5,13},{6,14},{7,15},{8,0},{9,1},... | collective-permute-start | bytes 393224 | tf_op jit(solution)/shard_map/ppermute | solution.py:97
  68.8 4.8 %collective-permute-start.20 = (f32[32,1280]{1,0:T(8,128)S(1)}, f32[32,1280]{1,0:T(8,128)S(1)}, u32[]{:S(2)}, u32[]{:S(2)}) collective-permute-start(f32[32,1280]{1,0:T(8,128)S(1)} %get-tuple-element.62.refs_2_), channel_id=1, source_target_pairs={{0,1},{1,0},{2,3},{3,2},{4,5},{5,4},{6,7},{7,6},{8,9},{9,8},{10,11... | collective-permute-start | bytes 491528 | tf_op jit(solution)/shard_map/ppermute | solution.py:97
  68.9 4.8 %collective-permute-start.19 = (f32[32,1280]{1,0:T(8,128)S(1)}, f32[32,1280]{1,0:T(8,128)S(1)}, u32[]{:S(2)}, u32[]{:S(2)}) collective-permute-start(f32[32,1280]{1,0:T(8,128)S(1)} %get-tuple-element.61.refs_2_.refs_1_), channel_id=1, source_target_pairs={{0,1},{1,0},{2,3},{3,2},{4,5},{5,4},{6,7},{7,6},{8,9},{9,8},{10,11... | collective-permute-start | bytes 491528 | tf_op jit(solution)/shard_map/ppermute | solution.py:97
  69.4 10.5 %collective-permute-start.17 = (f32[32,768]{1,0:T(8,128)S(1)}, f32[32,768]{1,0:T(8,128)S(1)}, u32[]{:S(2)}, u32[]{:S(2)}) collective-permute-start(f32[32,768]{1,0:T(8,128)S(1)} %get-tuple-element.59.refs_1_), channel_id=1, source_target_pairs={{0,4},{1,5},{2,6},{3,7},{4,0},{5,1},{6,2},{7,3},{8,12},{9,13},{10,... | collective-permute-start | bytes 294920 | tf_op jit(solution)/shard_map/ppermute | solution.py:97
  73.6 6.3 %collective-permute-start.18 = (f32[32,1024]{1,0:T(8,128)S(1)}, f32[32,1024]{1,0:T(8,128)S(1)}, u32[]{:S(2)}, u32[]{:S(2)}) collective-permute-start(f32[32,1024]{1,0:T(8,128)S(1)} %shard_map.111.refs_6_.refs_2_), channel_id=1, source_target_pairs={{0,4},{1,5},{2,6},{3,7},{4,0},{5,1},{6,2},{7,3},{8,12},{9,13},{10,... | collective-permute-start | bytes 393224 | tf_op jit(solution)/shard_map/ppermute | solution.py:97

commit v16 on v15

--- a/solution.py
+++ b/solution.py
@@ -11,7 +11,7 @@
 RANK = 64
 TILE = 256
 FLOPS = 1.15e9
-WEIGHTS = (8.0, 4.0, 1.0, 4.0, 0.1, 5.0, 1.0, 5.0, 1.0, 1.0, 2.0, 2.0, 0.1, 1.0, 5.0, 0.1, 0.5, 1.0, 1.0, 8.0, 8.0)
+WEIGHTS = (8.0, 4.0, 1.0, 4.0, 0.1, 5.0, 1.0, 5.0, 1.0, 1.0, 2.0, 2.0, 5.0, 5.0, 1.0, 0.1, 5.0, 1.0, 1.0, 8.0, 8.0)
 MIB = 1 << 20
 BF16 = jnp.bfloat16
 F32 = jnp.float32
@@ -614,26 +614,26 @@
         exchange(gram_down, lambda d, t, b=b: (d, t ^ b)) for b in range(2, n_t, 2)
     ]
     got = exchange(down, hops[0])
-    few = width // TILE * 3 // 7
+    few = width // TILE * 2 // 7
     keep_a, give_a, gram_gate, left_gate = gate_right(
         run, gates, others_gate, fixed_gate, few, after=(down,)
     )
     got_a = exchange(give_a, other_replica)
     keep_b, give_b = gate_right_rest(run, left_gate, fixed_gate, few)
     got_b = exchange(give_b, other_replica)
-    for hop in hops[1:]:
-        (down,) = add(run, [down], [got], after=(give_b,))
-        got = exchange(down, hop)
-    (gate_a,) = add(run, [keep_a], [got_a], beside=gram_gate, after=(down,))
+    (gate_a,) = add(run, [keep_a], [got_a], beside=gram_gate, after=(give_b,))
     got_a = exchange(gate_a, steps[0])
     (gate_b,) = add(run, [keep_b], [got_b], after=(gate_a,))
     got_b = exchange(gate_b, steps[0])
+    for hop in hops[1:]:
+        (down,) = add(run, [down], [got], after=(gate_b,))
+        got = exchange(down, hop)
     for step in steps[1:]:
         (gate_a,) = add(run, [gate_a], [got_a])
         got_a = exchange(gate_a, step)
         (gate_b,) = add(run, [gate_b], [got_b])
         got_b = exchange(gate_b, step)
-    gate_a, gram_gate = add(run, [gate_a], [got_a], [few * TILE, 2 * RANK], after=(gate_b,))
+    gate_a, gram_gate = add(run, [gate_a], [got_a], [few * TILE, 2 * RANK], after=(down,))
     other_a = exchange(gate_a, other_replica)
     col_stack, row_turned = solve(run, grams_down, left_down, gram_gate, left_gate)
     downs = add(run, [down], [got], in_two(slab), after=(col_stack,))

time: 86.5 us -> 88.8 us (1.027)
  waiting for transfers between devices: 15 us -> 19.8 us
  starting transfers between devices: 26.3 us -> 23.8 us
    ppermute x21, waiting for transfers between devices: 15 us -> 19.8 us  [exchange(): return lax.ppermute(x, ('dp', 'tensor'), pairs)]
    ppermute x21, starting transfers between devices: 26.3 us -> 23.8 us  [exchange(): return lax.ppermute(x, ('dp', 'tensor'), pairs)]
  transfers between devices with their start and end apart: 21 -> 21, of which waited for: 9 -> 10; matrix products, arithmetic and copies ran while one was open for 0% -> 0% of each run, Pallas kernels for 32% -> 31%
where the time goes in v16:
time: 88.8 us; the launch traced here: 88.6 us
  Pallas kernels  44 us (50%)
  starting transfers between devices  23.8 us (27%)
  waiting for transfers between devices  19.8 us (22%)
  between operations  0.97 us (1%)
    pallas_call x21, Pallas kernels, __call__(): pl.pallas_call(body, out_shape=tuple(((pltpu.VMEM if spec is VMEM else pl...  44 us
    ppermute x21, starting transfers between devices, exchange(): return lax.ppermute(x, ('dp', 'tensor'), pairs)  23.8 us
    ppermute x21, waiting for transfers between devices, exchange(): return lax.ppermute(x, ('dp', 'tensor'), pairs)  19.8 us
  transfers between devices with their start and end apart: 21, of which 10 were waited for; matrix products, arithmetic and copies ran while one was open for 0% of the time, Pallas kernels for 31%

profile of v16, /device:TPU:0, one launch (start us, length us, event | category | flops | bytes accessed | tf_op | source)
XLA Modules:
  0.0 88.6 jit_solution(136723227470099594)
XLA Ops:
  0.6 9.8 %shard_map.93 = (f32[64,1792]{1,0:T(8,128)}, bf16[2560,1792]{1,0:T(8,128)(2,1)S(1)}, f32[32,1792]{1,0:T(8,128)S(1)}, f32[32,1792]{1,0:T(8,128)S(1)}) custom-call(bf16[2560,1792]{1,0:T(8,128)(2,1)} %refs_0_.3, bf16[2560,1792]{1,0:T(8,128)(2,1)} %refs_1_.3, bf16[64,5120]{1,0:T(8,128)(2,1)} %refs_2_.3), custom_call_target="tpu_custom_call" | custom-call | flops 9200000000 | bytes 1024 | tf_op jit(solution)/shard_map/pallas_call | solution.py:154
  10.4 3.0 %collective-permute-start = (f32[32,1792]{1,0:T(8,128)S(1)}, f32[32,1792]{1,0:T(8,128)S(1)}, u32[]{:S(2)}, u32[]{:S(2)}) collective-permute-start(f32[32,1792]{1,0:T(8,128)S(1)} %get-tuple-element.37), channel_id=1, source_target_pairs={{0,4},{1,5},{2,6},{3,7},{4,0},{5,1},{6,2},{7,3},{8,12},{9,13},{10,... | collective-permute-start | bytes 688136 | tf_op jit(solution)/shard_map/ppermute | solution.py:97
  13.5 5.1 %shard_map.94 = (f32[64,2560]{1,0:T(8,128)S(1)}, bf16[2560,1792]{1,0:T(8,128)(2,1)S(1)}) custom-call(bf16[2560,1792]{1,0:T(8,128)(2,1)} %refs_0_.5, bf16[2560,1792]{1,0:T(8,128)(2,1)} %refs_1_.5, bf16[64,1792]{1,0:T(8,128)(2,1)S(1)} %copy-done, f32[32,1792]{1,0:T(8,128)S(1)} %get-tuple-element.36.refs_3_.refs_0_), custom_call_target="tpu_custom_call" | custom-call | flops 4600000000 | bytes 1024 | tf_op jit(solution)/shard_map/pallas_call | solution.py:154
  19.1 2.8 %collective-permute-start.1 = (f32[32,1792]{1,0:T(8,128)S(1)}, f32[32,1792]{1,0:T(8,128)S(1)}, u32[]{:S(2)}, u32[]{:S(2)}) collective-permute-start(f32[32,1792]{1,0:T(8,128)S(1)} %shard_map.95.refs_5_.refs_0_), channel_id=1, source_target_pairs={{0,8},{1,9},{2,10},{3,11},{4,12},{5,13},{6,14},{7,15},{8,0},{9,1},... | collective-permute-start | bytes 688136 | tf_op jit(solution)/shard_map/ppermute | solution.py:97
  21.9 4.0 %shard_map.96 = (f32[64,2560]{1,0:T(8,128)S(1)}, bf16[2560,1792]{1,0:T(8,128)(2,1)S(1)}, f32[32,2560]{1,0:T(8,128)S(1)}, f32[32,1280]{1,0:T(8,128)S(1)}, f32[32,1280]{1,0:T(8,128)S(1)}) custom-call(bf16[2560,1792]{1,0:T(8,128)(2,1)} %refs_0_.5, bf16[2560,1792]{1,0:T(8,128)(2,1)} %refs_1_.5, ...), custom_call_target="tpu_custom_call", output_to_operand_aliasing={{0}: (3, {}), {1}: (4, {})} | custom-call | flops 4600000000 | bytes 1024 | tf_op jit(solution)/shard_map/pallas_call | solution.py:154
  27.6 1.6 %collective-permute-start.5 = (f32[32,2560]{1,0:T(8,128)S(1)}, f32[32,2560]{1,0:T(8,128)S(1)}, u32[]{:S(2)}, u32[]{:S(2)}) collective-permute-start(f32[32,2560]{1,0:T(8,128)S(1)} %shard_map.97.refs_2_.refs_0_), channel_id=1, source_target_pairs={{0,2},{1,5},{2,0},{3,7},{4,6},{5,1},{6,4},{7,3},{8,10},{9,13},{10,... | collective-permute-start | bytes 983048 | tf_op jit(solution)/shard_map/ppermute | solution.py:97
  29.2 2.7 %collective-permute-done.1.refs_1_ = f32[32,1792]{1,0:T(8,128)S(1)} collective-permute-done((f32[32,1792]{1,0:T(8,128)S(1)}, f32[32,1792]{1,0:T(8,128)S(1)}, u32[]{:S(2)}, u32[]{:S(2)}) %collective-permute-start.1) | collective-permute-done | bytes 229408 | tf_op jit(solution)/shard_map/ppermute | solution.py:97
  32.4 2.3 %collective-permute-done.5.refs_1_ = f32[32,2560]{1,0:T(8,128)S(1)} collective-permute-done((f32[32,2560]{1,0:T(8,128)S(1)}, f32[32,2560]{1,0:T(8,128)S(1)}, u32[]{:S(2)}, u32[]{:S(2)}) %collective-permute-start.5) | collective-permute-done | bytes 327712 | tf_op jit(solution)/shard_map/ppermute | solution.py:97
  34.8 1.6 %collective-permute-start.8 = (f32[32,2560]{1,0:T(8,128)S(1)}, f32[32,2560]{1,0:T(8,128)S(1)}, u32[]{:S(2)}, u32[]{:S(2)}) collective-permute-start(f32[32,2560]{1,0:T(8,128)S(1)} %shard_map.99.refs_3_.refs_0_), channel_id=1, source_target_pairs={{0,4},{1,3},{2,6},{3,1},{4,0},{5,7},{6,2},{7,5},{8,12},{9,11},{10,... | collective-permute-start | bytes 983048 | tf_op jit(solution)/shard_map/ppermute | solution.py:97
  36.4 3.7 %collective-permute-done.4.refs_1_ = f32[32,1792]{1,0:T(8,128)S(1)} collective-permute-done((f32[32,1792]{1,0:T(8,128)S(1)}, f32[32,1792]{1,0:T(8,128)S(1)}, u32[]{:S(2)}, u32[]{:S(2)}) %collective-permute-start.4) | collective-permute-done | bytes 229408 | tf_op jit(solution)/shard_map/ppermute | solution.py:97
  40.2 5.1 %shard_map.100 = (f32[32,2688]{1,0:T(8,128)S(1)}, f32[32,1280]{1,0:T(8,128)S(1)}, f32[32,1408]{1,0:T(8,128)S(1)}, bf16[192,1792]{1,0:T(8,128)(2,1)S(1)}) custom-call(f32[32,1792]{1,0:T(8,128)S(1)} %shard_map.98.refs_2_.refs_0_, f32[32,1792]{1,0:T(8,128)S(1)} %collective-permute-done.4.refs_1_, bf16[2560,1792]{1,0:T(8,128)(2,1)S(1)} %get-tuple-element.43.refs_2_.refs_5_, ...), custom_call_target="tpu_custom_call" | custom-call | flops 5750000128 | bytes 1024 | tf_op jit(solution)/shard_map/pallas_call | solution.py:154
  46.0 1.5 %collective-permute-done.6.refs_1_ = f32[32,1280]{1,0:T(8,128)S(1)} collective-permute-done((f32[32,1280]{1,0:T(8,128)S(1)}, f32[32,1280]{1,0:T(8,128)S(1)}, u32[]{:S(2)}, u32[]{:S(2)}) %collective-permute-start.6) | collective-permute-done | bytes 163872 | tf_op jit(solution)/shard_map/ppermute | solution.py:97
  47.6 1.4 %collective-permute-start.9 = (f32[32,128]{1,0:T(8,128)S(1)}, f32[32,128]{1,0:T(8,128)S(1)}, u32[]{:S(2)}, u32[]{:S(2)}) collective-permute-start(f32[32,128]{1,0:T(8,128)S(1)} %get-tuple-element.47.refs_0_), channel_id=1, source_target_pairs={{0,2},{1,3},{2,0},{3,1},{4,6},{5,7},{6,4},{7,5},{8,10},{9,11},{10,... | collective-permute-start | bytes 49160 | tf_op jit(solution)/shard_map/ppermute | solution.py:97
  49.7 1.3 %shard_map.103 = (f32[32,512]{1,0:T(8,128)S(1)}, f32[32,512]{1,0:T(8,128)S(1)}, f32[32,128]{1,0:T(8,128)S(1)}, bf16[192,2560]{1,0:T(8,128)(2,1)S(1)}) custom-call(f32[32,2560]{1,0:T(8,128)S(1)} %shard_map.101.refs_3_.refs_0_, f32[32,2560]{1,0:T(8,128)S(1)} %collective-permute-done.10.refs_1_, ...), custom_call_target="tpu_custom_call" | custom-call | flops 2300000000 | bytes 1024 | tf_op jit(solution)/shard_map/pallas_call | solution.py:154
  51.5 1.9 %shard_map.104 = (f32[32,1280]{1,0:T(8,128)S(1)}, f32[32,1280]{1,0:T(8,128)S(1)}) custom-call(bf16[192,2560]{1,0:T(8,128)(2,1)S(1)} %get-tuple-element.53.refs_0_.refs_4_, bf16[2560,1792]{1,0:T(8,128)(2,1)S(1)} %get-tuple-element.48.refs_2_.refs_1_.refs_5_), custom_call_target="tpu_custom_call" | custom-call | flops 2300000000 | bytes 1024 | tf_op jit(solution)/shard_map/pallas_call | solution.py:154
  53.4 1.7 %collective-permute-start.14 = (f32[32,1280]{1,0:T(8,128)S(1)}, f32[32,1280]{1,0:T(8,128)S(1)}, u32[]{:S(2)}, u32[]{:S(2)}) collective-permute-start(f32[32,1280]{1,0:T(8,128)S(1)} %get-tuple-element.54.refs_3_), channel_id=1, source_target_pairs={{0,4},{1,5},{2,6},{3,7},{4,0},{5,1},{6,2},{7,3},{8,12},{9,13},{10,... | collective-permute-start | bytes 491528 | tf_op jit(solution)/shard_map/ppermute | solution.py:97
  56.1 2.0 %collective-permute-start.12 = (f32[32,640]{1,0:T(8,128)S(1)}, f32[32,640]{1,0:T(8,128)S(1)}, u32[]{:S(2)}, u32[]{:S(2)}) collective-permute-start(f32[32,640]{1,0:T(8,128)S(1)} %shard_map.105.refs_2_.refs_0_), channel_id=1, source_target_pairs={{0,8},{1,9},{2,10},{3,11},{4,12},{5,13},{6,14},{7,15},{8,0},{9,1},... | collective-permute-start | bytes 245768 | tf_op jit(solution)/shard_map/ppermute | solution.py:97
  58.1 1.8 %collective-permute-done.14.refs_1_ = f32[32,1280]{1,0:T(8,128)S(1)} collective-permute-done((f32[32,1280]{1,0:T(8,128)S(1)}, f32[32,1280]{1,0:T(8,128)S(1)}, u32[]{:S(2)}, u32[]{:S(2)}) %collective-permute-start.14) | collective-permute-done | bytes 163872 | tf_op jit(solution)/shard_map/ppermute | solution.py:97
  59.9 3.4 %collective-permute-start.15 = (f32[32,1280]{1,0:T(8,128)S(1)}, f32[32,1280]{1,0:T(8,128)S(1)}, u32[]{:S(2)}, u32[]{:S(2)}) collective-permute-start(f32[32,1280]{1,0:T(8,128)S(1)} %shard_map.106.refs_2_.refs_0_), channel_id=1, source_target_pairs={{0,8},{1,9},{2,10},{3,11},{4,12},{5,13},{6,14},{7,15},{8,0},{9,1},... | collective-permute-start | bytes 491528 | tf_op jit(solution)/shard_map/ppermute | solution.py:97
  64.2 4.0 %shard_map.109 = (bf16[256,1792]{1,0:T(8,128)(2,1)S(1)}, bf16[2560,256]{1,0:T(8,128)(2,1)S(1)}) custom-call(f32[32,128]{1,0:T(8,128)S(1)} %get-tuple-element.47.refs_0_, f32[32,128]{1,0:T(8,128)S(1)} %collective-permute-done.9.refs_1_, f32[32,128]{1,0:T(8,128)S(1)} %get-tuple-element.56.refs_2_, bf16[192,1792]{1,0:T(8,128)(2,1)S(1)} %get-tuple-element.57.refs_3_, ...), custom_call_target="tpu_custom_call" | custom-call | flops 5750000128 | bytes 1024 | tf_op jit(solution)/shard_map/pallas_call | solution.py:154
  68.2 5.0 %collective-permute-done.16.refs_1_ = f32[32,2560]{1,0:T(8,128)S(1)} collective-permute-done((f32[32,2560]{1,0:T(8,128)S(1)}, f32[32,2560]{1,0:T(8,128)S(1)}, u32[]{:S(2)}, u32[]{:S(2)}) %collective-permute-start.16) | collective-permute-done | bytes 327712 | tf_op jit(solution)/shard_map/ppermute | solution.py:97
  73.9 2.1 %collective-permute-start.18 = (f32[32,1280]{1,0:T(8,128)S(1)}, f32[32,1280]{1,0:T(8,128)S(1)}, u32[]{:S(2)}, u32[]{:S(2)}) collective-permute-start(f32[32,1280]{1,0:T(8,128)S(1)} %shard_map.111.refs_6_.refs_2_), channel_id=1, source_target_pairs={{0,4},{1,5},{2,6},{3,7},{4,0},{5,1},{6,2},{7,3},{8,12},{9,13},{10,... | collective-permute-start | bytes 491528 | tf_op jit(solution)/shard_map/ppermute | solution.py:97
  76.0 6.2 %shard_map.112 = (bf16[2560,1792]{1,0:T(8,128)(2,1)}, bf16[1280,1792]{1,0:T(8,128)(2,1)}, bf16[2560,256]{1,0:T(8,128)(2,1)S(1)}) custom-call(bf16[256,1792]{1,0:T(8,128)(2,1)S(1)} %get-tuple-element.60.refs_2_.refs_0_, f32[32,1280]{1,0:T(8,128)S(1)} %get-tuple-element.61.refs_2_.refs_1_, f32[32,1280]{1,0:T(8,128)S(1)} %get-tuple-element.62.refs_2_, ...), custom_call_target="tpu_custom_call" | custom-call | flops 9200000000 | bytes 1024 | tf_op jit(solution)/shard_map/pallas_call | solution.py:154
  82.2 6.3 %shard_map.113 = (bf16[2560,1792]{1,0:T(8,128)(2,1)}, bf16[1280,1792]{1,0:T(8,128)(2,1)}, bf16[16,128]{1,0:T(8,128)(2,1)}) custom-call(bf16[2560,256]{1,0:T(8,128)(2,1)S(1)} %get-tuple-element.58.refs_0_, f32[32,512]{1,0:T(8,128)S(1)} %get-tuple-element.59.refs_1_, f32[32,1280]{1,0:T(8,128)S(1)} %shard_map.111.refs_6_.refs_2_, ...), custom_call_target="tpu_custom_call" | custom-call | flops 9200000000 | bytes 1024 | tf_op jit(solution)/shard_map/pallas_call | solution.py:154
  (41 shorter events, 7.2 us)
Async XLA Ops:
  0.6 12.8 %copy-start = (bf16[64,1792]{1,0:T(8,128)(2,1)S(1)}, bf16[64,1792]{1,0:T(8,128)(2,1)}, u32[]{:S(2)}) copy-start(bf16[64,1792]{1,0:T(8,128)(2,1)} %refs_2_.5) | copy-start | bytes 688132
  10.4 8.6 %collective-permute-start = (f32[32,1792]{1,0:T(8,128)S(1)}, f32[32,1792]{1,0:T(8,128)S(1)}, u32[]{:S(2)}, u32[]{:S(2)}) collective-permute-start(f32[32,1792]{1,0:T(8,128)S(1)} %get-tuple-element.37), channel_id=1, source_target_pairs={{0,4},{1,5},{2,6},{3,7},{4,0},{5,1},{6,2},{7,3},{8,12},{9,13},{10,... | collective-permute-start | bytes 688136 | tf_op jit(solution)/shard_map/ppermute | solution.py:97
  19.1 12.8 %collective-permute-start.1 = (f32[32,1792]{1,0:T(8,128)S(1)}, f32[32,1792]{1,0:T(8,128)S(1)}, u32[]{:S(2)}, u32[]{:S(2)}) collective-permute-start(f32[32,1792]{1,0:T(8,128)S(1)} %shard_map.95.refs_5_.refs_0_), channel_id=1, source_target_pairs={{0,8},{1,9},{2,10},{3,11},{4,12},{5,13},{6,14},{7,15},{8,0},{9,1},... | collective-permute-start | bytes 688136 | tf_op jit(solution)/shard_map/ppermute | solution.py:97
  25.9 1.5 %collective-permute-start.2 = (f32[32,1280]{1,0:T(8,128)S(1)}, f32[32,1280]{1,0:T(8,128)S(1)}, u32[]{:S(2)}, u32[]{:S(2)}) collective-permute-start(f32[32,1280]{1,0:T(8,128)S(1)} %get-tuple-element.41), channel_id=1, source_target_pairs={{0,1},{1,0},{2,3},{3,2},{4,5},{5,4},{6,7},{7,6},{8,9},{9,8},{10,11... | collective-permute-start | bytes 491528 | tf_op jit(solution)/shard_map/ppermute | solution.py:97
  26.0 1.6 %collective-permute-start.3 = (f32[32,1280]{1,0:T(8,128)S(1)}, f32[32,1280]{1,0:T(8,128)S(1)}, u32[]{:S(2)}, u32[]{:S(2)}) collective-permute-start(f32[32,1280]{1,0:T(8,128)S(1)} %get-tuple-element.42), channel_id=1, source_target_pairs={{0,1},{1,0},{2,3},{3,2},{4,5},{5,4},{6,7},{7,6},{8,9},{9,8},{10,11... | collective-permute-start | bytes 491528 | tf_op jit(solution)/shard_map/ppermute | solution.py:97
  27.6 7.1 %collective-permute-start.5 = (f32[32,2560]{1,0:T(8,128)S(1)}, f32[32,2560]{1,0:T(8,128)S(1)}, u32[]{:S(2)}, u32[]{:S(2)}) collective-permute-start(f32[32,2560]{1,0:T(8,128)S(1)} %shard_map.97.refs_2_.refs_0_), channel_id=1, source_target_pairs={{0,2},{1,5},{2,0},{3,7},{4,6},{5,1},{6,4},{7,3},{8,10},{9,13},{10,... | collective-permute-start | bytes 983048 | tf_op jit(solution)/shard_map/ppermute | solution.py:97
  31.9 8.3 %collective-permute-start.4 = (f32[32,1792]{1,0:T(8,128)S(1)}, f32[32,1792]{1,0:T(8,128)S(1)}, u32[]{:S(2)}, u32[]{:S(2)}) collective-permute-start(f32[32,1792]{1,0:T(8,128)S(1)} %shard_map.98.refs_2_.refs_0_), channel_id=1, source_target_pairs={{0,4},{1,5},{2,6},{3,7},{4,0},{5,1},{6,2},{7,3},{8,12},{9,13},{10,... | collective-permute-start | bytes 688136 | tf_op jit(solution)/shard_map/ppermute | solution.py:97
  34.8 10.5 %collective-permute-start.8 = (f32[32,2560]{1,0:T(8,128)S(1)}, f32[32,2560]{1,0:T(8,128)S(1)}, u32[]{:S(2)}, u32[]{:S(2)}) collective-permute-start(f32[32,2560]{1,0:T(8,128)S(1)} %shard_map.99.refs_3_.refs_0_), channel_id=1, source_target_pairs={{0,4},{1,3},{2,6},{3,1},{4,0},{5,7},{6,2},{7,5},{8,12},{9,11},{10,... | collective-permute-start | bytes 983048 | tf_op jit(solution)/shard_map/ppermute | solution.py:97
  45.3 4.3 %collective-permute-start.10 = (f32[32,2560]{1,0:T(8,128)S(1)}, f32[32,2560]{1,0:T(8,128)S(1)}, u32[]{:S(2)}, u32[]{:S(2)}) collective-permute-start(f32[32,2560]{1,0:T(8,128)S(1)} %shard_map.101.refs_3_.refs_0_), channel_id=1, source_target_pairs={{0,1},{1,0},{2,3},{3,2},{4,5},{5,4},{6,7},{7,6},{8,9},{9,8},{10,11... | collective-permute-start | bytes 983048 | tf_op jit(solution)/shard_map/ppermute | solution.py:97
  45.4 2.1 %collective-permute-start.7 = (f32[32,1408]{1,0:T(8,128)S(1)}, f32[32,1408]{1,0:T(8,128)S(1)}, u32[]{:S(2)}, u32[]{:S(2)}) collective-permute-start(f32[32,1408]{1,0:T(8,128)S(1)} %get-tuple-element.46), channel_id=1, source_target_pairs={{0,1},{1,0},{2,3},{3,2},{4,5},{5,4},{6,7},{7,6},{8,9},{9,8},{10,11... | collective-permute-start | bytes 540680 | tf_op jit(solution)/shard_map/ppermute | solution.py:97
  45.9 1.6 %collective-permute-start.6 = (f32[32,1280]{1,0:T(8,128)S(1)}, f32[32,1280]{1,0:T(8,128)S(1)}, u32[]{:S(2)}, u32[]{:S(2)}) collective-permute-start(f32[32,1280]{1,0:T(8,128)S(1)} %get-tuple-element.45), channel_id=1, source_target_pairs={{0,1},{1,0},{2,3},{3,2},{4,5},{5,4},{6,7},{7,6},{8,9},{9,8},{10,11... | collective-permute-start | bytes 491528 | tf_op jit(solution)/shard_map/ppermute | solution.py:97
  47.6 16.6 %collective-permute-start.9 = (f32[32,128]{1,0:T(8,128)S(1)}, f32[32,128]{1,0:T(8,128)S(1)}, u32[]{:S(2)}, u32[]{:S(2)}) collective-permute-start(f32[32,128]{1,0:T(8,128)S(1)} %get-tuple-element.47.refs_0_), channel_id=1, source_target_pairs={{0,2},{1,3},{2,0},{3,1},{4,6},{5,7},{6,4},{7,5},{8,10},{9,11},{10,... | collective-permute-start | bytes 49160 | tf_op jit(solution)/shard_map/ppermute | solution.py:97
  49.0 14.3 %collective-permute-start.13 = (f32[32,2560]{1,0:T(8,128)S(1)}, f32[32,2560]{1,0:T(8,128)S(1)}, u32[]{:S(2)}, u32[]{:S(2)}) collective-permute-start(f32[32,2560]{1,0:T(8,128)S(1)} %get-tuple-element.49.refs_3_.refs_0_), channel_id=1, source_target_pairs={{0,2},{1,5},{2,0},{3,7},{4,6},{5,1},{6,4},{7,3},{8,10},{9,13},{10,... | collective-permute-start | bytes 983048 | tf_op jit(solution)/shard_map/ppermute | solution.py:97
  51.0 5.1 %collective-permute-start.11 = (f32[32,512]{1,0:T(8,128)S(1)}, f32[32,512]{1,0:T(8,128)S(1)}, u32[]{:S(2)}, u32[]{:S(2)}) collective-permute-start(f32[32,512]{1,0:T(8,128)S(1)} %get-tuple-element.51), channel_id=1, source_target_pairs={{0,4},{1,5},{2,6},{3,7},{4,0},{5,1},{6,2},{7,3},{8,12},{9,13},{10,... | collective-permute-start | bytes 196616 | tf_op jit(solution)/shard_map/ppermute | solution.py:97
  53.4 6.5 %collective-permute-start.14 = (f32[32,1280]{1,0:T(8,128)S(1)}, f32[32,1280]{1,0:T(8,128)S(1)}, u32[]{:S(2)}, u32[]{:S(2)}) collective-permute-start(f32[32,1280]{1,0:T(8,128)S(1)} %get-tuple-element.54.refs_3_), channel_id=1, source_target_pairs={{0,4},{1,5},{2,6},{3,7},{4,0},{5,1},{6,2},{7,3},{8,12},{9,13},{10,... | collective-permute-start | bytes 491528 | tf_op jit(solution)/shard_map/ppermute | solution.py:97
  56.1 8.0 %collective-permute-start.12 = (f32[32,640]{1,0:T(8,128)S(1)}, f32[32,640]{1,0:T(8,128)S(1)}, u32[]{:S(2)}, u32[]{:S(2)}) collective-permute-start(f32[32,640]{1,0:T(8,128)S(1)} %shard_map.105.refs_2_.refs_0_), channel_id=1, source_target_pairs={{0,8},{1,9},{2,10},{3,11},{4,12},{5,13},{6,14},{7,15},{8,0},{9,1},... | collective-permute-start | bytes 245768 | tf_op jit(solution)/shard_map/ppermute | solution.py:97
  59.9 13.9 %collective-permute-start.15 = (f32[32,1280]{1,0:T(8,128)S(1)}, f32[32,1280]{1,0:T(8,128)S(1)}, u32[]{:S(2)}, u32[]{:S(2)}) collective-permute-start(f32[32,1280]{1,0:T(8,128)S(1)} %shard_map.106.refs_2_.refs_0_), channel_id=1, source_target_pairs={{0,8},{1,9},{2,10},{3,11},{4,12},{5,13},{6,14},{7,15},{8,0},{9,1},... | collective-permute-start | bytes 491528 | tf_op jit(solution)/shard_map/ppermute | solution.py:97
  63.3 9.9 %collective-permute-start.16 = (f32[32,2560]{1,0:T(8,128)S(1)}, f32[32,2560]{1,0:T(8,128)S(1)}, u32[]{:S(2)}, u32[]{:S(2)}) collective-permute-start(f32[32,2560]{1,0:T(8,128)S(1)} %shard_map.107.refs_2_.refs_0_), channel_id=1, source_target_pairs={{0,4},{1,3},{2,6},{3,1},{4,0},{5,7},{6,2},{7,5},{8,12},{9,11},{10,... | collective-permute-start | bytes 983048 | tf_op jit(solution)/shard_map/ppermute | solution.py:97
  73.3 2.7 %collective-permute-start.20 = (f32[32,1280]{1,0:T(8,128)S(1)}, f32[32,1280]{1,0:T(8,128)S(1)}, u32[]{:S(2)}, u32[]{:S(2)}) collective-permute-start(f32[32,1280]{1,0:T(8,128)S(1)} %get-tuple-element.62.refs_2_), channel_id=1, source_target_pairs={{0,1},{1,0},{2,3},{3,2},{4,5},{5,4},{6,7},{7,6},{8,9},{9,8},{10,11... | collective-permute-start | bytes 491528 | tf_op jit(solution)/shard_map/ppermute | solution.py:97
  73.3 2.6 %collective-permute-start.19 = (f32[32,1280]{1,0:T(8,128)S(1)}, f32[32,1280]{1,0:T(8,128)S(1)}, u32[]{:S(2)}, u32[]{:S(2)}) collective-permute-start(f32[32,1280]{1,0:T(8,128)S(1)} %get-tuple-element.61.refs_2_.refs_1_), channel_id=1, source_target_pairs={{0,1},{1,0},{2,3},{3,2},{4,5},{5,4},{6,7},{7,6},{8,9},{9,8},{10,11... | collective-permute-start | bytes 491528 | tf_op jit(solution)/shard_map/ppermute | solution.py:97
  73.8 8.3 %collective-permute-start.17 = (f32[32,512]{1,0:T(8,128)S(1)}, f32[32,512]{1,0:T(8,128)S(1)}, u32[]{:S(2)}, u32[]{:S(2)}) collective-permute-start(f32[32,512]{1,0:T(8,128)S(1)} %get-tuple-element.59.refs_1_), channel_id=1, source_target_pairs={{0,4},{1,5},{2,6},{3,7},{4,0},{5,1},{6,2},{7,3},{8,12},{9,13},{10,... | collective-permute-start | bytes 196616 | tf_op jit(solution)/shard_map/ppermute | solution.py:97
  73.9 8.3 %collective-permute-start.18 = (f32[32,1280]{1,0:T(8,128)S(1)}, f32[32,1280]{1,0:T(8,128)S(1)}, u32[]{:S(2)}, u32[]{:S(2)}) collective-permute-start(f32[32,1280]{1,0:T(8,128)S(1)} %shard_map.111.refs_6_.refs_2_), channel_id=1, source_target_pairs={{0,4},{1,5},{2,6},{3,7},{4,0},{5,1},{6,2},{7,3},{8,12},{9,13},{10,... | collective-permute-start | bytes 491528 | tf_op jit(solution)/shard_map/ppermute | solution.py:97

commit v17 on v15

--- a/solution.py
+++ b/solution.py
@@ -614,7 +614,7 @@
         exchange(gram_down, lambda d, t, b=b: (d, t ^ b)) for b in range(2, n_t, 2)
     ]
     got = exchange(down, hops[0])
-    few = width // TILE * 3 // 7
+    few = width // TILE * 2 // 7
     keep_a, give_a, gram_gate, left_gate = gate_right(
         run, gates, others_gate, fixed_gate, few, after=(down,)
     )

time: 86.5 us -> 86.6 us (level)
  starting transfers between devices: 26.3 us -> 27.8 us
  waiting for transfers between devices: 15 us -> 13.5 us
    ppermute x21, starting transfers between devices: 26.3 us -> 27.8 us  [exchange(): return lax.ppermute(x, ('dp', 'tensor'), pairs)]
    ppermute x21, waiting for transfers between devices: 15 us -> 13.5 us  [exchange(): return lax.ppermute(x, ('dp', 'tensor'), pairs)]
  transfers between devices with their start and end apart: 21 -> 21, of which waited for: 9 -> 8; matrix products, arithmetic and copies ran while one was open for 0% -> 0% of each run, Pallas kernels for 32% -> 32%
where the time goes in v17:
time: 86.6 us; the launch traced here: 86.3 us
  Pallas kernels  44 us (51%)
  starting transfers between devices  27.8 us (32%)
  waiting for transfers between devices  13.5 us (16%)
  between operations  1.01 us (1%)
    pallas_call x21, Pallas kernels, __call__(): pl.pallas_call(body, out_shape=tuple(((pltpu.VMEM if spec is VMEM else pl...  44 us
    ppermute x21, starting transfers between devices, exchange(): return lax.ppermute(x, ('dp', 'tensor'), pairs)  27.8 us
    ppermute x21, waiting for transfers between devices, exchange(): return lax.ppermute(x, ('dp', 'tensor'), pairs)  13.5 us
  transfers between devices with their start and end apart: 21, of which 8 were waited for; matrix products, arithmetic and copies ran while one was open for 0% of the time, Pallas kernels for 32%

profile of v17, /device:TPU:0, one launch (start us, length us, event | category | flops | bytes accessed | tf_op | source)
XLA Modules:
  0.0 86.3 jit_solution(9411420888319428171)
XLA Ops:
  0.6 9.8 %shard_map.93 = (f32[64,1792]{1,0:T(8,128)}, bf16[2560,1792]{1,0:T(8,128)(2,1)S(1)}, f32[32,1792]{1,0:T(8,128)S(1)}, f32[32,1792]{1,0:T(8,128)S(1)}) custom-call(bf16[2560,1792]{1,0:T(8,128)(2,1)} %refs_0_.3, bf16[2560,1792]{1,0:T(8,128)(2,1)} %refs_1_.3, bf16[64,5120]{1,0:T(8,128)(2,1)} %refs_2_.3), custom_call_target="tpu_custom_call" | custom-call | flops 9200000000 | bytes 1024 | tf_op jit(solution)/shard_map/pallas_call | solution.py:154
  10.4 3.0 %collective-permute-start = (f32[32,1792]{1,0:T(8,128)S(1)}, f32[32,1792]{1,0:T(8,128)S(1)}, u32[]{:S(2)}, u32[]{:S(2)}) collective-permute-start(f32[32,1792]{1,0:T(8,128)S(1)} %get-tuple-element.37), channel_id=1, source_target_pairs={{0,4},{1,5},{2,6},{3,7},{4,0},{5,1},{6,2},{7,3},{8,12},{9,13},{10,... | collective-permute-start | bytes 688136 | tf_op jit(solution)/shard_map/ppermute | solution.py:97
  13.5 5.1 %shard_map.94 = (f32[64,2560]{1,0:T(8,128)S(1)}, bf16[2560,1792]{1,0:T(8,128)(2,1)S(1)}) custom-call(bf16[2560,1792]{1,0:T(8,128)(2,1)} %refs_0_.5, bf16[2560,1792]{1,0:T(8,128)(2,1)} %refs_1_.5, bf16[64,1792]{1,0:T(8,128)(2,1)S(1)} %copy-done, f32[32,1792]{1,0:T(8,128)S(1)} %get-tuple-element.36.refs_3_.refs_0_), custom_call_target="tpu_custom_call" | custom-call | flops 4600000000 | bytes 1024 | tf_op jit(solution)/shard_map/pallas_call | solution.py:154
  19.1 2.8 %collective-permute-start.1 = (f32[32,1792]{1,0:T(8,128)S(1)}, f32[32,1792]{1,0:T(8,128)S(1)}, u32[]{:S(2)}, u32[]{:S(2)}) collective-permute-start(f32[32,1792]{1,0:T(8,128)S(1)} %shard_map.95.refs_5_.refs_0_), channel_id=1, source_target_pairs={{0,8},{1,9},{2,10},{3,11},{4,12},{5,13},{6,14},{7,15},{8,0},{9,1},... | collective-permute-start | bytes 688136 | tf_op jit(solution)/shard_map/ppermute | solution.py:97
  21.9 4.0 %shard_map.96 = (f32[64,2560]{1,0:T(8,128)S(1)}, bf16[2560,1792]{1,0:T(8,128)(2,1)S(1)}, f32[32,2560]{1,0:T(8,128)S(1)}, f32[32,1280]{1,0:T(8,128)S(1)}, f32[32,1280]{1,0:T(8,128)S(1)}) custom-call(bf16[2560,1792]{1,0:T(8,128)(2,1)} %refs_0_.5, bf16[2560,1792]{1,0:T(8,128)(2,1)} %refs_1_.5, ...), custom_call_target="tpu_custom_call", output_to_operand_aliasing={{0}: (3, {}), {1}: (4, {})} | custom-call | flops 4600000000 | bytes 1024 | tf_op jit(solution)/shard_map/pallas_call | solution.py:154
  26.5 0.9 %collective-permute-done.2.refs_1_ = f32[32,1280]{1,0:T(8,128)S(1)} collective-permute-done((f32[32,1280]{1,0:T(8,128)S(1)}, f32[32,1280]{1,0:T(8,128)S(1)}, u32[]{:S(2)}, u32[]{:S(2)}) %collective-permute-start.2) | collective-permute-done | bytes 163872 | tf_op jit(solution)/shard_map/ppermute | solution.py:97
  27.6 1.6 %collective-permute-start.5 = (f32[32,2560]{1,0:T(8,128)S(1)}, f32[32,2560]{1,0:T(8,128)S(1)}, u32[]{:S(2)}, u32[]{:S(2)}) collective-permute-start(f32[32,2560]{1,0:T(8,128)S(1)} %shard_map.97.refs_2_.refs_0_), channel_id=1, source_target_pairs={{0,2},{1,5},{2,0},{3,7},{4,6},{5,1},{6,4},{7,3},{8,10},{9,13},{10,... | collective-permute-start | bytes 983048 | tf_op jit(solution)/shard_map/ppermute | solution.py:97
  29.2 2.7 %collective-permute-done.1.refs_1_ = f32[32,1792]{1,0:T(8,128)S(1)} collective-permute-done((f32[32,1792]{1,0:T(8,128)S(1)}, f32[32,1792]{1,0:T(8,128)S(1)}, u32[]{:S(2)}, u32[]{:S(2)}) %collective-permute-start.1) | collective-permute-done | bytes 229408 | tf_op jit(solution)/shard_map/ppermute | solution.py:97
  32.4 2.3 %collective-permute-done.5.refs_1_ = f32[32,2560]{1,0:T(8,128)S(1)} collective-permute-done((f32[32,2560]{1,0:T(8,128)S(1)}, f32[32,2560]{1,0:T(8,128)S(1)}, u32[]{:S(2)}, u32[]{:S(2)}) %collective-permute-start.5) | collective-permute-done | bytes 327712 | tf_op jit(solution)/shard_map/ppermute | solution.py:97
  34.8 1.6 %collective-permute-start.8 = (f32[32,2560]{1,0:T(8,128)S(1)}, f32[32,2560]{1,0:T(8,128)S(1)}, u32[]{:S(2)}, u32[]{:S(2)}) collective-permute-start(f32[32,2560]{1,0:T(8,128)S(1)} %shard_map.99.refs_3_.refs_0_), channel_id=1, source_target_pairs={{0,4},{1,3},{2,6},{3,1},{4,0},{5,7},{6,2},{7,5},{8,12},{9,11},{10,... | collective-permute-start | bytes 983048 | tf_op jit(solution)/shard_map/ppermute | solution.py:97
  36.4 3.7 %collective-permute-done.4.refs_1_ = f32[32,1792]{1,0:T(8,128)S(1)} collective-permute-done((f32[32,1792]{1,0:T(8,128)S(1)}, f32[32,1792]{1,0:T(8,128)S(1)}, u32[]{:S(2)}, u32[]{:S(2)}) %collective-permute-start.4) | collective-permute-done | bytes 229408 | tf_op jit(solution)/shard_map/ppermute | solution.py:97
  40.2 5.1 %shard_map.100 = (f32[32,2688]{1,0:T(8,128)S(1)}, f32[32,1280]{1,0:T(8,128)S(1)}, f32[32,1408]{1,0:T(8,128)S(1)}, bf16[192,1792]{1,0:T(8,128)(2,1)S(1)}) custom-call(f32[32,1792]{1,0:T(8,128)S(1)} %shard_map.98.refs_2_.refs_0_, f32[32,1792]{1,0:T(8,128)S(1)} %collective-permute-done.4.refs_1_, bf16[2560,1792]{1,0:T(8,128)(2,1)S(1)} %get-tuple-element.43.refs_2_.refs_5_, ...), custom_call_target="tpu_custom_call" | custom-call | flops 5750000128 | bytes 1024 | tf_op jit(solution)/shard_map/pallas_call | solution.py:154
  46.0 1.5 %collective-permute-done.6.refs_1_ = f32[32,1280]{1,0:T(8,128)S(1)} collective-permute-done((f32[32,1280]{1,0:T(8,128)S(1)}, f32[32,1280]{1,0:T(8,128)S(1)}, u32[]{:S(2)}, u32[]{:S(2)}) %collective-permute-start.6) | collective-permute-done | bytes 163872 | tf_op jit(solution)/shard_map/ppermute | solution.py:97
  47.6 1.4 %collective-permute-start.12 = (f32[32,2560]{1,0:T(8,128)S(1)}, f32[32,2560]{1,0:T(8,128)S(1)}, u32[]{:S(2)}, u32[]{:S(2)}) collective-permute-start(f32[32,2560]{1,0:T(8,128)S(1)} %get-tuple-element.49.refs_3_.refs_0_), channel_id=1, source_target_pairs={{0,2},{1,5},{2,0},{3,7},{4,6},{5,1},{6,4},{7,3},{8,10},{9,13},{10,... | collective-permute-start | bytes 983048 | tf_op jit(solution)/shard_map/ppermute | solution.py:97
  49.0 1.3 %shard_map.103 = (f32[32,512]{1,0:T(8,128)S(1)}, f32[32,512]{1,0:T(8,128)S(1)}, f32[32,128]{1,0:T(8,128)S(1)}, bf16[192,2560]{1,0:T(8,128)(2,1)S(1)}) custom-call(f32[32,2560]{1,0:T(8,128)S(1)} %shard_map.101.refs_3_.refs_0_, f32[32,2560]{1,0:T(8,128)S(1)} %collective-permute-done.10.refs_1_, ...), custom_call_target="tpu_custom_call" | custom-call | flops 2300000000 | bytes 1024 | tf_op jit(solution)/shard_map/pallas_call | solution.py:154
  50.9 1.9 %shard_map.104 = (f32[32,1280]{1,0:T(8,128)S(1)}, f32[32,1280]{1,0:T(8,128)S(1)}) custom-call(bf16[192,2560]{1,0:T(8,128)(2,1)S(1)} %get-tuple-element.53.refs_0_.refs_4_, bf16[2560,1792]{1,0:T(8,128)(2,1)S(1)} %get-tuple-element.48.refs_2_.refs_1_.refs_5_), custom_call_target="tpu_custom_call" | custom-call | flops 2300000000 | bytes 1024 | tf_op jit(solution)/shard_map/pallas_call | solution.py:154
  52.9 1.6 %collective-permute-start.14 = (f32[32,1280]{1,0:T(8,128)S(1)}, f32[32,1280]{1,0:T(8,128)S(1)}, u32[]{:S(2)}, u32[]{:S(2)}) collective-permute-start(f32[32,1280]{1,0:T(8,128)S(1)} %get-tuple-element.54.refs_2_), channel_id=1, source_target_pairs={{0,4},{1,5},{2,6},{3,7},{4,0},{5,1},{6,2},{7,3},{8,12},{9,13},{10,... | collective-permute-start | bytes 491528 | tf_op jit(solution)/shard_map/ppermute | solution.py:97
  55.6 3.6 %collective-permute-start.13 = (f32[32,640]{1,0:T(8,128)S(1)}, f32[32,640]{1,0:T(8,128)S(1)}, u32[]{:S(2)}, u32[]{:S(2)}) collective-permute-start(f32[32,640]{1,0:T(8,128)S(1)} %shard_map.106.refs_2_.refs_0_), channel_id=1, source_target_pairs={{0,8},{1,9},{2,10},{3,11},{4,12},{5,13},{6,14},{7,15},{8,0},{9,1},... | collective-permute-start | bytes 245768 | tf_op jit(solution)/shard_map/ppermute | solution.py:97
  59.3 3.5 %collective-permute-start.15 = (f32[32,1280]{1,0:T(8,128)S(1)}, f32[32,1280]{1,0:T(8,128)S(1)}, u32[]{:S(2)}, u32[]{:S(2)}) collective-permute-start(f32[32,1280]{1,0:T(8,128)S(1)} %shard_map.107.refs_2_.refs_0_), channel_id=1, source_target_pairs={{0,8},{1,9},{2,10},{3,11},{4,12},{5,13},{6,14},{7,15},{8,0},{9,1},... | collective-permute-start | bytes 491528 | tf_op jit(solution)/shard_map/ppermute | solution.py:97
  62.7 1.5 %collective-permute-done.13.refs_1_ = f32[32,640]{1,0:T(8,128)S(1)} collective-permute-done((f32[32,640]{1,0:T(8,128)S(1)}, f32[32,640]{1,0:T(8,128)S(1)}, u32[]{:S(2)}, u32[]{:S(2)}) %collective-permute-start.13) | collective-permute-done | bytes 81952 | tf_op jit(solution)/shard_map/ppermute | solution.py:97
  64.3 4.0 %shard_map.109 = (bf16[256,1792]{1,0:T(8,128)(2,1)S(1)}, bf16[2560,256]{1,0:T(8,128)(2,1)S(1)}) custom-call(f32[32,128]{1,0:T(8,128)S(1)} %get-tuple-element.47.refs_0_, f32[32,128]{1,0:T(8,128)S(1)} %collective-permute-done.9.refs_1_, f32[32,128]{1,0:T(8,128)S(1)} %get-tuple-element.56.refs_2_, bf16[192,1792]{1,0:T(8,128)(2,1)S(1)} %get-tuple-element.57.refs_3_, ...), custom_call_target="tpu_custom_call" | custom-call | flops 575000000 | bytes 1024 | tf_op jit(solution)/shard_map/pallas_call | solution.py:154
  69.0 4.6 %collective-permute-start.17 = (f32[32,512]{1,0:T(8,128)S(1)}, f32[32,512]{1,0:T(8,128)S(1)}, u32[]{:S(2)}, u32[]{:S(2)}) collective-permute-start(f32[32,512]{1,0:T(8,128)S(1)} %get-tuple-element.59.refs_1_), channel_id=1, source_target_pairs={{0,4},{1,5},{2,6},{3,7},{4,0},{5,1},{6,2},{7,3},{8,12},{9,13},{10,... | collective-permute-start | bytes 196616 | tf_op jit(solution)/shard_map/ppermute | solution.py:97
  73.7 6.2 %shard_map.112 = (bf16[2560,1792]{1,0:T(8,128)(2,1)}, bf16[1280,1792]{1,0:T(8,128)(2,1)}, bf16[2560,256]{1,0:T(8,128)(2,1)S(1)}) custom-call(bf16[256,1792]{1,0:T(8,128)(2,1)S(1)} %get-tuple-element.60.refs_2_.refs_0_, f32[32,1280]{1,0:T(8,128)S(1)} %get-tuple-element.61.refs_2_.refs_1_, f32[32,1280]{1,0:T(8,128)S(1)} %get-tuple-element.62.refs_2_, ...), custom_call_target="tpu_custom_call" | custom-call | flops 9200000000 | bytes 1024 | tf_op jit(solution)/shard_map/pallas_call | solution.py:154
  79.9 6.3 %shard_map.113 = (bf16[2560,1792]{1,0:T(8,128)(2,1)}, bf16[1280,1792]{1,0:T(8,128)(2,1)}, bf16[16,128]{1,0:T(8,128)(2,1)}) custom-call(bf16[2560,256]{1,0:T(8,128)(2,1)S(1)} %get-tuple-element.58.refs_0_, f32[32,512]{1,0:T(8,128)S(1)} %get-tuple-element.59.refs_1_, f32[32,1280]{1,0:T(8,128)S(1)} %shard_map.111.refs_6_.refs_2_, ...), custom_call_target="tpu_custom_call" | custom-call | flops 9200000000 | bytes 1024 | tf_op jit(solution)/shard_map/pallas_call | solution.py:154
  (41 shorter events, 5.2 us)
Async XLA Ops:
  0.6 12.8 %copy-start = (bf16[64,1792]{1,0:T(8,128)(2,1)S(1)}, bf16[64,1792]{1,0:T(8,128)(2,1)}, u32[]{:S(2)}) copy-start(bf16[64,1792]{1,0:T(8,128)(2,1)} %refs_2_.5) | copy-start | bytes 688132
  10.4 8.6 %collective-permute-start = (f32[32,1792]{1,0:T(8,128)S(1)}, f32[32,1792]{1,0:T(8,128)S(1)}, u32[]{:S(2)}, u32[]{:S(2)}) collective-permute-start(f32[32,1792]{1,0:T(8,128)S(1)} %get-tuple-element.37), channel_id=1, source_target_pairs={{0,4},{1,5},{2,6},{3,7},{4,0},{5,1},{6,2},{7,3},{8,12},{9,13},{10,... | collective-permute-start | bytes 688136 | tf_op jit(solution)/shard_map/ppermute | solution.py:97
  19.1 12.8 %collective-permute-start.1 = (f32[32,1792]{1,0:T(8,128)S(1)}, f32[32,1792]{1,0:T(8,128)S(1)}, u32[]{:S(2)}, u32[]{:S(2)}) collective-permute-start(f32[32,1792]{1,0:T(8,128)S(1)} %shard_map.95.refs_5_.refs_0_), channel_id=1, source_target_pairs={{0,8},{1,9},{2,10},{3,11},{4,12},{5,13},{6,14},{7,15},{8,0},{9,1},... | collective-permute-start | bytes 688136 | tf_op jit(solution)/shard_map/ppermute | solution.py:97
  25.9 1.5 %collective-permute-start.2 = (f32[32,1280]{1,0:T(8,128)S(1)}, f32[32,1280]{1,0:T(8,128)S(1)}, u32[]{:S(2)}, u32[]{:S(2)}) collective-permute-start(f32[32,1280]{1,0:T(8,128)S(1)} %get-tuple-element.41), channel_id=1, source_target_pairs={{0,1},{1,0},{2,3},{3,2},{4,5},{5,4},{6,7},{7,6},{8,9},{9,8},{10,11... | collective-permute-start | bytes 491528 | tf_op jit(solution)/shard_map/ppermute | solution.py:97
  26.0 1.6 %collective-permute-start.3 = (f32[32,1280]{1,0:T(8,128)S(1)}, f32[32,1280]{1,0:T(8,128)S(1)}, u32[]{:S(2)}, u32[]{:S(2)}) collective-permute-start(f32[32,1280]{1,0:T(8,128)S(1)} %get-tuple-element.42), channel_id=1, source_target_pairs={{0,1},{1,0},{2,3},{3,2},{4,5},{5,4},{6,7},{7,6},{8,9},{9,8},{10,11... | collective-permute-start | bytes 491528 | tf_op jit(solution)/shard_map/ppermute | solution.py:97
  27.6 7.1 %collective-permute-start.5 = (f32[32,2560]{1,0:T(8,128)S(1)}, f32[32,2560]{1,0:T(8,128)S(1)}, u32[]{:S(2)}, u32[]{:S(2)}) collective-permute-start(f32[32,2560]{1,0:T(8,128)S(1)} %shard_map.97.refs_2_.refs_0_), channel_id=1, source_target_pairs={{0,2},{1,5},{2,0},{3,7},{4,6},{5,1},{6,4},{7,3},{8,10},{9,13},{10,... | collective-permute-start | bytes 983048 | tf_op jit(solution)/shard_map/ppermute | solution.py:97
  31.9 8.3 %collective-permute-start.4 = (f32[32,1792]{1,0:T(8,128)S(1)}, f32[32,1792]{1,0:T(8,128)S(1)}, u32[]{:S(2)}, u32[]{:S(2)}) collective-permute-start(f32[32,1792]{1,0:T(8,128)S(1)} %shard_map.98.refs_2_.refs_0_), channel_id=1, source_target_pairs={{0,4},{1,5},{2,6},{3,7},{4,0},{5,1},{6,2},{7,3},{8,12},{9,13},{10,... | collective-permute-start | bytes 688136 | tf_op jit(solution)/shard_map/ppermute | solution.py:97
  34.8 10.5 %collective-permute-start.8 = (f32[32,2560]{1,0:T(8,128)S(1)}, f32[32,2560]{1,0:T(8,128)S(1)}, u32[]{:S(2)}, u32[]{:S(2)}) collective-permute-start(f32[32,2560]{1,0:T(8,128)S(1)} %shard_map.99.refs_3_.refs_0_), channel_id=1, source_target_pairs={{0,4},{1,3},{2,6},{3,1},{4,0},{5,7},{6,2},{7,5},{8,12},{9,11},{10,... | collective-permute-start | bytes 983048 | tf_op jit(solution)/shard_map/ppermute | solution.py:97
  45.3 3.6 %collective-permute-start.10 = (f32[32,2560]{1,0:T(8,128)S(1)}, f32[32,2560]{1,0:T(8,128)S(1)}, u32[]{:S(2)}, u32[]{:S(2)}) collective-permute-start(f32[32,2560]{1,0:T(8,128)S(1)} %shard_map.101.refs_3_.refs_0_), channel_id=1, source_target_pairs={{0,1},{1,0},{2,3},{3,2},{4,5},{5,4},{6,7},{7,6},{8,9},{9,8},{10,11... | collective-permute-start | bytes 983048 | tf_op jit(solution)/shard_map/ppermute | solution.py:97
  45.4 2.1 %collective-permute-start.7 = (f32[32,1408]{1,0:T(8,128)S(1)}, f32[32,1408]{1,0:T(8,128)S(1)}, u32[]{:S(2)}, u32[]{:S(2)}) collective-permute-start(f32[32,1408]{1,0:T(8,128)S(1)} %get-tuple-element.46), channel_id=1, source_target_pairs={{0,1},{1,0},{2,3},{3,2},{4,5},{5,4},{6,7},{7,6},{8,9},{9,8},{10,11... | collective-permute-start | bytes 540680 | tf_op jit(solution)/shard_map/ppermute | solution.py:97
  45.9 1.6 %collective-permute-start.6 = (f32[32,1280]{1,0:T(8,128)S(1)}, f32[32,1280]{1,0:T(8,128)S(1)}, u32[]{:S(2)}, u32[]{:S(2)}) collective-permute-start(f32[32,1280]{1,0:T(8,128)S(1)} %get-tuple-element.45), channel_id=1, source_target_pairs={{0,1},{1,0},{2,3},{3,2},{4,5},{5,4},{6,7},{7,6},{8,9},{9,8},{10,11... | collective-permute-start | bytes 491528 | tf_op jit(solution)/shard_map/ppermute | solution.py:97
  47.6 7.5 %collective-permute-start.12 = (f32[32,2560]{1,0:T(8,128)S(1)}, f32[32,2560]{1,0:T(8,128)S(1)}, u32[]{:S(2)}, u32[]{:S(2)}) collective-permute-start(f32[32,2560]{1,0:T(8,128)S(1)} %get-tuple-element.49.refs_3_.refs_0_), channel_id=1, source_target_pairs={{0,2},{1,5},{2,0},{3,7},{4,6},{5,1},{6,4},{7,3},{8,10},{9,13},{10,... | collective-permute-start | bytes 983048 | tf_op jit(solution)/shard_map/ppermute | solution.py:97
  50.3 5.3 %collective-permute-start.11 = (f32[32,512]{1,0:T(8,128)S(1)}, f32[32,512]{1,0:T(8,128)S(1)}, u32[]{:S(2)}, u32[]{:S(2)}) collective-permute-start(f32[32,512]{1,0:T(8,128)S(1)} %get-tuple-element.51), channel_id=1, source_target_pairs={{0,4},{1,5},{2,6},{3,7},{4,0},{5,1},{6,2},{7,3},{8,12},{9,13},{10,... | collective-permute-start | bytes 196616 | tf_op jit(solution)/shard_map/ppermute | solution.py:97
  52.9 6.4 %collective-permute-start.14 = (f32[32,1280]{1,0:T(8,128)S(1)}, f32[32,1280]{1,0:T(8,128)S(1)}, u32[]{:S(2)}, u32[]{:S(2)}) collective-permute-start(f32[32,1280]{1,0:T(8,128)S(1)} %get-tuple-element.54.refs_2_), channel_id=1, source_target_pairs={{0,4},{1,5},{2,6},{3,7},{4,0},{5,1},{6,2},{7,3},{8,12},{9,13},{10,... | collective-permute-start | bytes 491528 | tf_op jit(solution)/shard_map/ppermute | solution.py:97
  54.4 9.9 %collective-permute-start.9 = (f32[32,128]{1,0:T(8,128)S(1)}, f32[32,128]{1,0:T(8,128)S(1)}, u32[]{:S(2)}, u32[]{:S(2)}) collective-permute-start(f32[32,128]{1,0:T(8,128)S(1)} %get-tuple-element.47.refs_0_), channel_id=1, source_target_pairs={{0,2},{1,3},{2,0},{3,1},{4,6},{5,7},{6,4},{7,5},{8,10},{9,11},{10,... | collective-permute-start | bytes 49160 | tf_op jit(solution)/shard_map/ppermute | solution.py:97
  55.2 13.2 %collective-permute-start.16 = (f32[32,2560]{1,0:T(8,128)S(1)}, f32[32,2560]{1,0:T(8,128)S(1)}, u32[]{:S(2)}, u32[]{:S(2)}) collective-permute-start(f32[32,2560]{1,0:T(8,128)S(1)} %shard_map.105.refs_3_.refs_0_), channel_id=1, source_target_pairs={{0,4},{1,3},{2,6},{3,1},{4,0},{5,7},{6,2},{7,5},{8,12},{9,11},{10,... | collective-permute-start | bytes 983048 | tf_op jit(solution)/shard_map/ppermute | solution.py:97
  55.6 8.7 %collective-permute-start.13 = (f32[32,640]{1,0:T(8,128)S(1)}, f32[32,640]{1,0:T(8,128)S(1)}, u32[]{:S(2)}, u32[]{:S(2)}) collective-permute-start(f32[32,640]{1,0:T(8,128)S(1)} %shard_map.106.refs_2_.refs_0_), channel_id=1, source_target_pairs={{0,8},{1,9},{2,10},{3,11},{4,12},{5,13},{6,14},{7,15},{8,0},{9,1},... | collective-permute-start | bytes 245768 | tf_op jit(solution)/shard_map/ppermute | solution.py:97
  59.3 14.3 %collective-permute-start.15 = (f32[32,1280]{1,0:T(8,128)S(1)}, f32[32,1280]{1,0:T(8,128)S(1)}, u32[]{:S(2)}, u32[]{:S(2)}) collective-permute-start(f32[32,1280]{1,0:T(8,128)S(1)} %shard_map.107.refs_2_.refs_0_), channel_id=1, source_target_pairs={{0,8},{1,9},{2,10},{3,11},{4,12},{5,13},{6,14},{7,15},{8,0},{9,1},... | collective-permute-start | bytes 491528 | tf_op jit(solution)/shard_map/ppermute | solution.py:97
  68.4 5.3 %collective-permute-start.20 = (f32[32,1280]{1,0:T(8,128)S(1)}, f32[32,1280]{1,0:T(8,128)S(1)}, u32[]{:S(2)}, u32[]{:S(2)}) collective-permute-start(f32[32,1280]{1,0:T(8,128)S(1)} %get-tuple-element.62.refs_2_), channel_id=1, source_target_pairs={{0,1},{1,0},{2,3},{3,2},{4,5},{5,4},{6,7},{7,6},{8,9},{9,8},{10,11... | collective-permute-start | bytes 491528 | tf_op jit(solution)/shard_map/ppermute | solution.py:97
  68.5 5.2 %collective-permute-start.19 = (f32[32,1280]{1,0:T(8,128)S(1)}, f32[32,1280]{1,0:T(8,128)S(1)}, u32[]{:S(2)}, u32[]{:S(2)}) collective-permute-start(f32[32,1280]{1,0:T(8,128)S(1)} %get-tuple-element.61.refs_2_.refs_1_), channel_id=1, source_target_pairs={{0,1},{1,0},{2,3},{3,2},{4,5},{5,4},{6,7},{7,6},{8,9},{9,8},{10,11... | collective-permute-start | bytes 491528 | tf_op jit(solution)/shard_map/ppermute | solution.py:97
  69.0 10.9 %collective-permute-start.17 = (f32[32,512]{1,0:T(8,128)S(1)}, f32[32,512]{1,0:T(8,128)S(1)}, u32[]{:S(2)}, u32[]{:S(2)}) collective-permute-start(f32[32,512]{1,0:T(8,128)S(1)} %get-tuple-element.59.refs_1_), channel_id=1, source_target_pairs={{0,4},{1,5},{2,6},{3,7},{4,0},{5,1},{6,2},{7,3},{8,12},{9,13},{10,... | collective-permute-start | bytes 196616 | tf_op jit(solution)/shard_map/ppermute | solution.py:97
  73.6 6.3 %collective-permute-start.18 = (f32[32,1280]{1,0:T(8,128)S(1)}, f32[32,1280]{1,0:T(8,128)S(1)}, u32[]{:S(2)}, u32[]{:S(2)}) collective-permute-start(f32[32,1280]{1,0:T(8,128)S(1)} %shard_map.111.refs_6_.refs_2_), channel_id=1, source_target_pairs={{0,4},{1,5},{2,6},{3,7},{4,0},{5,1},{6,2},{7,3},{8,12},{9,13},{10,... | collective-permute-start | bytes 491528 | tf_op jit(solution)/shard_map/ppermute | solution.py:97

commit v18 on v15

--- a/solution.py
+++ b/solution.py
@@ -641,7 +641,7 @@
     (gate_b,) = add(run, [gate_b], [got_b], after=(downs[0],))
     other_b = exchange(gate_b, other_replica)
     new_error_down, update_down, turned = rebuild(
-        run, (None, col_stack), downs, others_down, fixed_down, (0, 1), slab // 8, after=(gate_b,)
+        run, (None, col_stack), downs, others_down, fixed_down, (0, 1), slab // 2, after=(gate_b,)
     )
     new_error_gate, update_gate, _ = rebuild(
         run, (row_turned, None), [gate_a, gate_b], [other_a, other_b], fixed_gate, (0, 1), slab // 2,

time: 86.5 us -> 86.2 us (level)
  no operation moved by 1% of the time
where the time goes in v18:
time: 86.2 us; the launch traced here: 86 us
  Pallas kernels  43.7 us (51%)
  starting transfers between devices  26.3 us (31%)
  waiting for transfers between devices  15 us (17%)
  between operations  1.01 us (1%)
    pallas_call x21, Pallas kernels, __call__(): pl.pallas_call(body, out_shape=tuple(((pltpu.VMEM if spec is VMEM else pl...  43.7 us
    ppermute x21, starting transfers between devices, exchange(): return lax.ppermute(x, ('dp', 'tensor'), pairs)  26.3 us
    ppermute x21, waiting for transfers between devices, exchange(): return lax.ppermute(x, ('dp', 'tensor'), pairs)  15 us
  transfers between devices with their start and end apart: 21, of which 9 were waited for; matrix products, arithmetic and copies ran while one was open for 0% of the time, Pallas kernels for 32%

profile of v18, /device:TPU:0, one launch (start us, length us, event | category | flops | bytes accessed | tf_op | source)
XLA Modules:
  0.0 86.0 jit_solution(15133481342467347631)
XLA Ops:
  0.6 9.8 %shard_map.93 = (f32[64,1792]{1,0:T(8,128)}, bf16[2560,1792]{1,0:T(8,128)(2,1)S(1)}, f32[32,1792]{1,0:T(8,128)S(1)}, f32[32,1792]{1,0:T(8,128)S(1)}) custom-call(bf16[2560,1792]{1,0:T(8,128)(2,1)} %refs_0_.3, bf16[2560,1792]{1,0:T(8,128)(2,1)} %refs_1_.3, bf16[64,5120]{1,0:T(8,128)(2,1)} %refs_2_.3), custom_call_target="tpu_custom_call" | custom-call | flops 9200000000 | bytes 1024 | tf_op jit(solution)/shard_map/pallas_call | solution.py:154
  10.4 3.0 %collective-permute-start = (f32[32,1792]{1,0:T(8,128)S(1)}, f32[32,1792]{1,0:T(8,128)S(1)}, u32[]{:S(2)}, u32[]{:S(2)}) collective-permute-start(f32[32,1792]{1,0:T(8,128)S(1)} %get-tuple-element.37), channel_id=1, source_target_pairs={{0,4},{1,5},{2,6},{3,7},{4,0},{5,1},{6,2},{7,3},{8,12},{9,13},{10,... | collective-permute-start | bytes 688136 | tf_op jit(solution)/shard_map/ppermute | solution.py:97
  13.5 5.1 %shard_map.94 = (f32[64,2560]{1,0:T(8,128)S(1)}, bf16[2560,1792]{1,0:T(8,128)(2,1)S(1)}) custom-call(bf16[2560,1792]{1,0:T(8,128)(2,1)} %refs_0_.5, bf16[2560,1792]{1,0:T(8,128)(2,1)} %refs_1_.5, bf16[64,1792]{1,0:T(8,128)(2,1)S(1)} %copy-done, f32[32,1792]{1,0:T(8,128)S(1)} %get-tuple-element.36.refs_3_.refs_0_), custom_call_target="tpu_custom_call" | custom-call | flops 4600000000 | bytes 1024 | tf_op jit(solution)/shard_map/pallas_call | solution.py:154
  19.1 2.8 %collective-permute-start.1 = (f32[32,1792]{1,0:T(8,128)S(1)}, f32[32,1792]{1,0:T(8,128)S(1)}, u32[]{:S(2)}, u32[]{:S(2)}) collective-permute-start(f32[32,1792]{1,0:T(8,128)S(1)} %shard_map.95.refs_5_.refs_0_), channel_id=1, source_target_pairs={{0,8},{1,9},{2,10},{3,11},{4,12},{5,13},{6,14},{7,15},{8,0},{9,1},... | collective-permute-start | bytes 688136 | tf_op jit(solution)/shard_map/ppermute | solution.py:97
  21.9 4.0 %shard_map.96 = (f32[64,2560]{1,0:T(8,128)S(1)}, bf16[2560,1792]{1,0:T(8,128)(2,1)S(1)}, f32[32,2560]{1,0:T(8,128)S(1)}, f32[32,1280]{1,0:T(8,128)S(1)}, f32[32,1280]{1,0:T(8,128)S(1)}) custom-call(bf16[2560,1792]{1,0:T(8,128)(2,1)} %refs_0_.5, bf16[2560,1792]{1,0:T(8,128)(2,1)} %refs_1_.5, ...), custom_call_target="tpu_custom_call", output_to_operand_aliasing={{0}: (3, {}), {1}: (4, {})} | custom-call | flops 4600000000 | bytes 1024 | tf_op jit(solution)/shard_map/pallas_call | solution.py:154
  26.5 0.9 %collective-permute-done.2.refs_1_ = f32[32,1280]{1,0:T(8,128)S(1)} collective-permute-done((f32[32,1280]{1,0:T(8,128)S(1)}, f32[32,1280]{1,0:T(8,128)S(1)}, u32[]{:S(2)}, u32[]{:S(2)}) %collective-permute-start.2) | collective-permute-done | bytes 163872 | tf_op jit(solution)/shard_map/ppermute | solution.py:97
  27.6 1.6 %collective-permute-start.5 = (f32[32,2560]{1,0:T(8,128)S(1)}, f32[32,2560]{1,0:T(8,128)S(1)}, u32[]{:S(2)}, u32[]{:S(2)}) collective-permute-start(f32[32,2560]{1,0:T(8,128)S(1)} %shard_map.97.refs_2_.refs_0_), channel_id=1, source_target_pairs={{0,2},{1,5},{2,0},{3,7},{4,6},{5,1},{6,4},{7,3},{8,10},{9,13},{10,... | collective-permute-start | bytes 983048 | tf_op jit(solution)/shard_map/ppermute | solution.py:97
  29.2 2.7 %collective-permute-done.1.refs_1_ = f32[32,1792]{1,0:T(8,128)S(1)} collective-permute-done((f32[32,1792]{1,0:T(8,128)S(1)}, f32[32,1792]{1,0:T(8,128)S(1)}, u32[]{:S(2)}, u32[]{:S(2)}) %collective-permute-start.1) | collective-permute-done | bytes 229408 | tf_op jit(solution)/shard_map/ppermute | solution.py:97
  32.4 2.3 %collective-permute-done.5.refs_1_ = f32[32,2560]{1,0:T(8,128)S(1)} collective-permute-done((f32[32,2560]{1,0:T(8,128)S(1)}, f32[32,2560]{1,0:T(8,128)S(1)}, u32[]{:S(2)}, u32[]{:S(2)}) %collective-permute-start.5) | collective-permute-done | bytes 327712 | tf_op jit(solution)/shard_map/ppermute | solution.py:97
  34.8 1.6 %collective-permute-start.8 = (f32[32,2560]{1,0:T(8,128)S(1)}, f32[32,2560]{1,0:T(8,128)S(1)}, u32[]{:S(2)}, u32[]{:S(2)}) collective-permute-start(f32[32,2560]{1,0:T(8,128)S(1)} %shard_map.99.refs_3_.refs_0_), channel_id=1, source_target_pairs={{0,4},{1,3},{2,6},{3,1},{4,0},{5,7},{6,2},{7,5},{8,12},{9,11},{10,... | collective-permute-start | bytes 983048 | tf_op jit(solution)/shard_map/ppermute | solution.py:97
  36.4 3.7 %collective-permute-done.4.refs_1_ = f32[32,1792]{1,0:T(8,128)S(1)} collective-permute-done((f32[32,1792]{1,0:T(8,128)S(1)}, f32[32,1792]{1,0:T(8,128)S(1)}, u32[]{:S(2)}, u32[]{:S(2)}) %collective-permute-start.4) | collective-permute-done | bytes 229408 | tf_op jit(solution)/shard_map/ppermute | solution.py:97
  40.2 5.1 %shard_map.100 = (f32[32,2688]{1,0:T(8,128)S(1)}, f32[32,1280]{1,0:T(8,128)S(1)}, f32[32,1408]{1,0:T(8,128)S(1)}, bf16[192,1792]{1,0:T(8,128)(2,1)S(1)}) custom-call(f32[32,1792]{1,0:T(8,128)S(1)} %shard_map.98.refs_2_.refs_0_, f32[32,1792]{1,0:T(8,128)S(1)} %collective-permute-done.4.refs_1_, bf16[2560,1792]{1,0:T(8,128)(2,1)S(1)} %get-tuple-element.43.refs_2_.refs_5_, ...), custom_call_target="tpu_custom_call" | custom-call | flops 5750000128 | bytes 1024 | tf_op jit(solution)/shard_map/pallas_call | solution.py:154
  46.0 1.5 %collective-permute-done.6.refs_1_ = f32[32,1280]{1,0:T(8,128)S(1)} collective-permute-done((f32[32,1280]{1,0:T(8,128)S(1)}, f32[32,1280]{1,0:T(8,128)S(1)}, u32[]{:S(2)}, u32[]{:S(2)}) %collective-permute-start.6) | collective-permute-done | bytes 163872 | tf_op jit(solution)/shard_map/ppermute | solution.py:97
  47.6 1.4 %collective-permute-start.12 = (f32[32,2560]{1,0:T(8,128)S(1)}, f32[32,2560]{1,0:T(8,128)S(1)}, u32[]{:S(2)}, u32[]{:S(2)}) collective-permute-start(f32[32,2560]{1,0:T(8,128)S(1)} %get-tuple-element.49.refs_3_.refs_0_), channel_id=1, source_target_pairs={{0,2},{1,5},{2,0},{3,7},{4,6},{5,1},{6,4},{7,3},{8,10},{9,13},{10,... | collective-permute-start | bytes 983048 | tf_op jit(solution)/shard_map/ppermute | solution.py:97
  49.0 1.7 %shard_map.103 = (f32[32,768]{1,0:T(8,128)S(1)}, f32[32,768]{1,0:T(8,128)S(1)}, f32[32,128]{1,0:T(8,128)S(1)}, bf16[192,2560]{1,0:T(8,128)(2,1)S(1)}) custom-call(f32[32,2560]{1,0:T(8,128)S(1)} %shard_map.101.refs_3_.refs_0_, f32[32,2560]{1,0:T(8,128)S(1)} %collective-permute-done.10.refs_1_, ...), custom_call_target="tpu_custom_call" | custom-call | flops 2300000000 | bytes 1024 | tf_op jit(solution)/shard_map/pallas_call | solution.py:154
  51.3 1.6 %shard_map.104 = (f32[32,1024]{1,0:T(8,128)S(1)}, f32[32,1024]{1,0:T(8,128)S(1)}) custom-call(bf16[192,2560]{1,0:T(8,128)(2,1)S(1)} %get-tuple-element.53.refs_0_.refs_4_, bf16[2560,1792]{1,0:T(8,128)(2,1)S(1)} %get-tuple-element.48.refs_2_.refs_1_.refs_5_), custom_call_target="tpu_custom_call" | custom-call | flops 2300000000 | bytes 1024 | tf_op jit(solution)/shard_map/pallas_call | solution.py:154
  52.9 1.6 %collective-permute-start.14 = (f32[32,1024]{1,0:T(8,128)S(1)}, f32[32,1024]{1,0:T(8,128)S(1)}, u32[]{:S(2)}, u32[]{:S(2)}) collective-permute-start(f32[32,1024]{1,0:T(8,128)S(1)} %get-tuple-element.54.refs_2_), channel_id=1, source_target_pairs={{0,4},{1,5},{2,6},{3,7},{4,0},{5,1},{6,2},{7,3},{8,12},{9,13},{10,... | collective-permute-start | bytes 393224 | tf_op jit(solution)/shard_map/ppermute | solution.py:97
  56.5 2.7 %collective-permute-start.13 = (f32[32,896]{1,0:T(8,128)S(1)}, f32[32,896]{1,0:T(8,128)S(1)}, u32[]{:S(2)}, u32[]{:S(2)}) collective-permute-start(f32[32,896]{1,0:T(8,128)S(1)} %shard_map.106.refs_2_.refs_0_), channel_id=1, source_target_pairs={{0,8},{1,9},{2,10},{3,11},{4,12},{5,13},{6,14},{7,15},{8,0},{9,1},... | collective-permute-start | bytes 344072 | tf_op jit(solution)/shard_map/ppermute | solution.py:97
  59.2 3.3 %collective-permute-start.15 = (f32[32,1024]{1,0:T(8,128)S(1)}, f32[32,1024]{1,0:T(8,128)S(1)}, u32[]{:S(2)}, u32[]{:S(2)}) collective-permute-start(f32[32,1024]{1,0:T(8,128)S(1)} %shard_map.107.refs_2_.refs_0_), channel_id=1, source_target_pairs={{0,8},{1,9},{2,10},{3,11},{4,12},{5,13},{6,14},{7,15},{8,0},{9,1},... | collective-permute-start | bytes 393224 | tf_op jit(solution)/shard_map/ppermute | solution.py:97
  62.5 2.2 %collective-permute-done.13.refs_1_ = f32[32,896]{1,0:T(8,128)S(1)} collective-permute-done((f32[32,896]{1,0:T(8,128)S(1)}, f32[32,896]{1,0:T(8,128)S(1)}, u32[]{:S(2)}, u32[]{:S(2)}) %collective-permute-start.13) | collective-permute-done | bytes 114720 | tf_op jit(solution)/shard_map/ppermute | solution.py:97
  64.8 4.0 %shard_map.109 = (bf16[256,1792]{1,0:T(8,128)(2,1)S(1)}, bf16[2560,256]{1,0:T(8,128)(2,1)S(1)}) custom-call(f32[32,128]{1,0:T(8,128)S(1)} %get-tuple-element.47.refs_0_, f32[32,128]{1,0:T(8,128)S(1)} %collective-permute-done.9.refs_1_, f32[32,128]{1,0:T(8,128)S(1)} %get-tuple-element.56.refs_2_, bf16[192,1792]{1,0:T(8,128)(2,1)S(1)} %get-tuple-element.57.refs_3_, ...), custom_call_target="tpu_custom_call" | custom-call | flops 575000000 | bytes 1024 | tf_op jit(solution)/shard_map/pallas_call | solution.py:154
  69.4 4.1 %collective-permute-start.17 = (f32[32,768]{1,0:T(8,128)S(1)}, f32[32,768]{1,0:T(8,128)S(1)}, u32[]{:S(2)}, u32[]{:S(2)}) collective-permute-start(f32[32,768]{1,0:T(8,128)S(1)} %get-tuple-element.59.refs_1_), channel_id=1, source_target_pairs={{0,4},{1,5},{2,6},{3,7},{4,0},{5,1},{6,2},{7,3},{8,12},{9,13},{10,... | collective-permute-start | bytes 294920 | tf_op jit(solution)/shard_map/ppermute | solution.py:97
  73.7 5.9 %shard_map.112 = (bf16[2560,1792]{1,0:T(8,128)(2,1)}, bf16[1280,1792]{1,0:T(8,128)(2,1)}, bf16[2560,256]{1,0:T(8,128)(2,1)S(1)}) custom-call(bf16[256,1792]{1,0:T(8,128)(2,1)S(1)} %get-tuple-element.60.refs_2_.refs_0_, f32[32,1280]{1,0:T(8,128)S(1)} %get-tuple-element.61.refs_2_.refs_1_, f32[32,1280]{1,0:T(8,128)S(1)} %get-tuple-element.62.refs_2_, ...), custom_call_target="tpu_custom_call" | custom-call | flops 9200000000 | bytes 1024 | tf_op jit(solution)/shard_map/pallas_call | solution.py:154
  79.6 6.3 %shard_map.113 = (bf16[2560,1792]{1,0:T(8,128)(2,1)}, bf16[1280,1792]{1,0:T(8,128)(2,1)}, bf16[16,128]{1,0:T(8,128)(2,1)}) custom-call(bf16[2560,256]{1,0:T(8,128)(2,1)S(1)} %get-tuple-element.58.refs_0_, f32[32,768]{1,0:T(8,128)S(1)} %get-tuple-element.59.refs_1_, f32[32,1024]{1,0:T(8,128)S(1)} %shard_map.111.refs_6_.refs_2_, ...), custom_call_target="tpu_custom_call" | custom-call | flops 9200000000 | bytes 1024 | tf_op jit(solution)/shard_map/pallas_call | solution.py:154
  (41 shorter events, 6.1 us)
Async XLA Ops:
  0.6 12.8 %copy-start = (bf16[64,1792]{1,0:T(8,128)(2,1)S(1)}, bf16[64,1792]{1,0:T(8,128)(2,1)}, u32[]{:S(2)}) copy-start(bf16[64,1792]{1,0:T(8,128)(2,1)} %refs_2_.5) | copy-start | bytes 688132
  10.4 8.6 %collective-permute-start = (f32[32,1792]{1,0:T(8,128)S(1)}, f32[32,1792]{1,0:T(8,128)S(1)}, u32[]{:S(2)}, u32[]{:S(2)}) collective-permute-start(f32[32,1792]{1,0:T(8,128)S(1)} %get-tuple-element.37), channel_id=1, source_target_pairs={{0,4},{1,5},{2,6},{3,7},{4,0},{5,1},{6,2},{7,3},{8,12},{9,13},{10,... | collective-permute-start | bytes 688136 | tf_op jit(solution)/shard_map/ppermute | solution.py:97
  19.1 12.8 %collective-permute-start.1 = (f32[32,1792]{1,0:T(8,128)S(1)}, f32[32,1792]{1,0:T(8,128)S(1)}, u32[]{:S(2)}, u32[]{:S(2)}) collective-permute-start(f32[32,1792]{1,0:T(8,128)S(1)} %shard_map.95.refs_5_.refs_0_), channel_id=1, source_target_pairs={{0,8},{1,9},{2,10},{3,11},{4,12},{5,13},{6,14},{7,15},{8,0},{9,1},... | collective-permute-start | bytes 688136 | tf_op jit(solution)/shard_map/ppermute | solution.py:97
  25.9 1.5 %collective-permute-start.2 = (f32[32,1280]{1,0:T(8,128)S(1)}, f32[32,1280]{1,0:T(8,128)S(1)}, u32[]{:S(2)}, u32[]{:S(2)}) collective-permute-start(f32[32,1280]{1,0:T(8,128)S(1)} %get-tuple-element.41), channel_id=1, source_target_pairs={{0,1},{1,0},{2,3},{3,2},{4,5},{5,4},{6,7},{7,6},{8,9},{9,8},{10,11... | collective-permute-start | bytes 491528 | tf_op jit(solution)/shard_map/ppermute | solution.py:97
  26.0 1.6 %collective-permute-start.3 = (f32[32,1280]{1,0:T(8,128)S(1)}, f32[32,1280]{1,0:T(8,128)S(1)}, u32[]{:S(2)}, u32[]{:S(2)}) collective-permute-start(f32[32,1280]{1,0:T(8,128)S(1)} %get-tuple-element.42), channel_id=1, source_target_pairs={{0,1},{1,0},{2,3},{3,2},{4,5},{5,4},{6,7},{7,6},{8,9},{9,8},{10,11... | collective-permute-start | bytes 491528 | tf_op jit(solution)/shard_map/ppermute | solution.py:97
  27.6 7.1 %collective-permute-start.5 = (f32[32,2560]{1,0:T(8,128)S(1)}, f32[32,2560]{1,0:T(8,128)S(1)}, u32[]{:S(2)}, u32[]{:S(2)}) collective-permute-start(f32[32,2560]{1,0:T(8,128)S(1)} %shard_map.97.refs_2_.refs_0_), channel_id=1, source_target_pairs={{0,2},{1,5},{2,0},{3,7},{4,6},{5,1},{6,4},{7,3},{8,10},{9,13},{10,... | collective-permute-start | bytes 983048 | tf_op jit(solution)/shard_map/ppermute | solution.py:97
  31.9 8.3 %collective-permute-start.4 = (f32[32,1792]{1,0:T(8,128)S(1)}, f32[32,1792]{1,0:T(8,128)S(1)}, u32[]{:S(2)}, u32[]{:S(2)}) collective-permute-start(f32[32,1792]{1,0:T(8,128)S(1)} %shard_map.98.refs_2_.refs_0_), channel_id=1, source_target_pairs={{0,4},{1,5},{2,6},{3,7},{4,0},{5,1},{6,2},{7,3},{8,12},{9,13},{10,... | collective-permute-start | bytes 688136 | tf_op jit(solution)/shard_map/ppermute | solution.py:97
  34.8 10.5 %collective-permute-start.8 = (f32[32,2560]{1,0:T(8,128)S(1)}, f32[32,2560]{1,0:T(8,128)S(1)}, u32[]{:S(2)}, u32[]{:S(2)}) collective-permute-start(f32[32,2560]{1,0:T(8,128)S(1)} %shard_map.99.refs_3_.refs_0_), channel_id=1, source_target_pairs={{0,4},{1,3},{2,6},{3,1},{4,0},{5,7},{6,2},{7,5},{8,12},{9,11},{10,... | collective-permute-start | bytes 983048 | tf_op jit(solution)/shard_map/ppermute | solution.py:97
  45.3 3.6 %collective-permute-start.10 = (f32[32,2560]{1,0:T(8,128)S(1)}, f32[32,2560]{1,0:T(8,128)S(1)}, u32[]{:S(2)}, u32[]{:S(2)}) collective-permute-start(f32[32,2560]{1,0:T(8,128)S(1)} %shard_map.101.refs_3_.refs_0_), channel_id=1, source_target_pairs={{0,1},{1,0},{2,3},{3,2},{4,5},{5,4},{6,7},{7,6},{8,9},{9,8},{10,11... | collective-permute-start | bytes 983048 | tf_op jit(solution)/shard_map/ppermute | solution.py:97
  45.4 2.1 %collective-permute-start.7 = (f32[32,1408]{1,0:T(8,128)S(1)}, f32[32,1408]{1,0:T(8,128)S(1)}, u32[]{:S(2)}, u32[]{:S(2)}) collective-permute-start(f32[32,1408]{1,0:T(8,128)S(1)} %get-tuple-element.46), channel_id=1, source_target_pairs={{0,1},{1,0},{2,3},{3,2},{4,5},{5,4},{6,7},{7,6},{8,9},{9,8},{10,11... | collective-permute-start | bytes 540680 | tf_op jit(solution)/shard_map/ppermute | solution.py:97
  45.9 1.6 %collective-permute-start.6 = (f32[32,1280]{1,0:T(8,128)S(1)}, f32[32,1280]{1,0:T(8,128)S(1)}, u32[]{:S(2)}, u32[]{:S(2)}) collective-permute-start(f32[32,1280]{1,0:T(8,128)S(1)} %get-tuple-element.45), channel_id=1, source_target_pairs={{0,1},{1,0},{2,3},{3,2},{4,5},{5,4},{6,7},{7,6},{8,9},{9,8},{10,11... | collective-permute-start | bytes 491528 | tf_op jit(solution)/shard_map/ppermute | solution.py:97
  47.6 7.5 %collective-permute-start.12 = (f32[32,2560]{1,0:T(8,128)S(1)}, f32[32,2560]{1,0:T(8,128)S(1)}, u32[]{:S(2)}, u32[]{:S(2)}) collective-permute-start(f32[32,2560]{1,0:T(8,128)S(1)} %get-tuple-element.49.refs_3_.refs_0_), channel_id=1, source_target_pairs={{0,2},{1,5},{2,0},{3,7},{4,6},{5,1},{6,4},{7,3},{8,10},{9,13},{10,... | collective-permute-start | bytes 983048 | tf_op jit(solution)/shard_map/ppermute | solution.py:97
  50.7 5.8 %collective-permute-start.11 = (f32[32,768]{1,0:T(8,128)S(1)}, f32[32,768]{1,0:T(8,128)S(1)}, u32[]{:S(2)}, u32[]{:S(2)}) collective-permute-start(f32[32,768]{1,0:T(8,128)S(1)} %get-tuple-element.51), channel_id=1, source_target_pairs={{0,4},{1,5},{2,6},{3,7},{4,0},{5,1},{6,2},{7,3},{8,12},{9,13},{10,... | collective-permute-start | bytes 294920 | tf_op jit(solution)/shard_map/ppermute | solution.py:97
  52.9 6.4 %collective-permute-start.14 = (f32[32,1024]{1,0:T(8,128)S(1)}, f32[32,1024]{1,0:T(8,128)S(1)}, u32[]{:S(2)}, u32[]{:S(2)}) collective-permute-start(f32[32,1024]{1,0:T(8,128)S(1)} %get-tuple-element.54.refs_2_), channel_id=1, source_target_pairs={{0,4},{1,5},{2,6},{3,7},{4,0},{5,1},{6,2},{7,3},{8,12},{9,13},{10,... | collective-permute-start | bytes 393224 | tf_op jit(solution)/shard_map/ppermute | solution.py:97
  54.4 10.3 %collective-permute-start.9 = (f32[32,128]{1,0:T(8,128)S(1)}, f32[32,128]{1,0:T(8,128)S(1)}, u32[]{:S(2)}, u32[]{:S(2)}) collective-permute-start(f32[32,128]{1,0:T(8,128)S(1)} %get-tuple-element.47.refs_0_), channel_id=1, source_target_pairs={{0,2},{1,3},{2,0},{3,1},{4,6},{5,7},{6,4},{7,5},{8,10},{9,11},{10,... | collective-permute-start | bytes 49160 | tf_op jit(solution)/shard_map/ppermute | solution.py:97
  55.2 13.6 %collective-permute-start.16 = (f32[32,2560]{1,0:T(8,128)S(1)}, f32[32,2560]{1,0:T(8,128)S(1)}, u32[]{:S(2)}, u32[]{:S(2)}) collective-permute-start(f32[32,2560]{1,0:T(8,128)S(1)} %shard_map.105.refs_3_.refs_0_), channel_id=1, source_target_pairs={{0,4},{1,3},{2,6},{3,1},{4,0},{5,7},{6,2},{7,5},{8,12},{9,11},{10,... | collective-permute-start | bytes 983048 | tf_op jit(solution)/shard_map/ppermute | solution.py:97
  56.5 8.2 %collective-permute-start.13 = (f32[32,896]{1,0:T(8,128)S(1)}, f32[32,896]{1,0:T(8,128)S(1)}, u32[]{:S(2)}, u32[]{:S(2)}) collective-permute-start(f32[32,896]{1,0:T(8,128)S(1)} %shard_map.106.refs_2_.refs_0_), channel_id=1, source_target_pairs={{0,8},{1,9},{2,10},{3,11},{4,12},{5,13},{6,14},{7,15},{8,0},{9,1},... | collective-permute-start | bytes 344072 | tf_op jit(solution)/shard_map/ppermute | solution.py:97
  59.2 14.3 %collective-permute-start.15 = (f32[32,1024]{1,0:T(8,128)S(1)}, f32[32,1024]{1,0:T(8,128)S(1)}, u32[]{:S(2)}, u32[]{:S(2)}) collective-permute-start(f32[32,1024]{1,0:T(8,128)S(1)} %shard_map.107.refs_2_.refs_0_), channel_id=1, source_target_pairs={{0,8},{1,9},{2,10},{3,11},{4,12},{5,13},{6,14},{7,15},{8,0},{9,1},... | collective-permute-start | bytes 393224 | tf_op jit(solution)/shard_map/ppermute | solution.py:97
  68.8 4.8 %collective-permute-start.20 = (f32[32,1280]{1,0:T(8,128)S(1)}, f32[32,1280]{1,0:T(8,128)S(1)}, u32[]{:S(2)}, u32[]{:S(2)}) collective-permute-start(f32[32,1280]{1,0:T(8,128)S(1)} %get-tuple-element.62.refs_2_), channel_id=1, source_target_pairs={{0,1},{1,0},{2,3},{3,2},{4,5},{5,4},{6,7},{7,6},{8,9},{9,8},{10,11... | collective-permute-start | bytes 491528 | tf_op jit(solution)/shard_map/ppermute | solution.py:97
  68.9 4.8 %collective-permute-start.19 = (f32[32,1280]{1,0:T(8,128)S(1)}, f32[32,1280]{1,0:T(8,128)S(1)}, u32[]{:S(2)}, u32[]{:S(2)}) collective-permute-start(f32[32,1280]{1,0:T(8,128)S(1)} %get-tuple-element.61.refs_2_.refs_1_), channel_id=1, source_target_pairs={{0,1},{1,0},{2,3},{3,2},{4,5},{5,4},{6,7},{7,6},{8,9},{9,8},{10,11... | collective-permute-start | bytes 491528 | tf_op jit(solution)/shard_map/ppermute | solution.py:97
  69.4 10.2 %collective-permute-start.17 = (f32[32,768]{1,0:T(8,128)S(1)}, f32[32,768]{1,0:T(8,128)S(1)}, u32[]{:S(2)}, u32[]{:S(2)}) collective-permute-start(f32[32,768]{1,0:T(8,128)S(1)} %get-tuple-element.59.refs_1_), channel_id=1, source_target_pairs={{0,4},{1,5},{2,6},{3,7},{4,0},{5,1},{6,2},{7,3},{8,12},{9,13},{10,... | collective-permute-start | bytes 294920 | tf_op jit(solution)/shard_map/ppermute | solution.py:97
  73.6 6.0 %collective-permute-start.18 = (f32[32,1024]{1,0:T(8,128)S(1)}, f32[32,1024]{1,0:T(8,128)S(1)}, u32[]{:S(2)}, u32[]{:S(2)}) collective-permute-start(f32[32,1024]{1,0:T(8,128)S(1)} %shard_map.111.refs_6_.refs_2_), channel_id=1, source_target_pairs={{0,4},{1,5},{2,6},{3,7},{4,0},{5,1},{6,2},{7,3},{8,12},{9,13},{10,... | collective-permute-start | bytes 393224 | tf_op jit(solution)/shard_map/ppermute | solution.py:97
